TPU v7x, 32 devices: a whole 2x2x4 slice. The times are simulated.
32 devices in a mesh: groups: 2 (over y), blk: 4 (over z), split: 2 (over x), sub: 2 (over core).
Axes of the slice: x: 2, y: 2, z: 4, core: 2. Of those that a mesh axis runs over, the one named last changes fastest.
Arguments:
- attention_output_rows: bfloat16 [1024, 8192], P(('groups', 'blk'), 'split'), parts along dimension 0, may hold values from -6 to 6
- residual: bfloat16 [1024, 8192], P(('groups', 'split'), ('blk', 'sub')), parts along dimension 0, may hold values from -6 to 6
- output_projection_weight: bfloat16 [8192, 8192], P('split', ('blk', 'sub')), may hold values from -0.0625 to 0.0625
- down_adapter_bank: bfloat16 [4, 64, 8192], P('blk', None, 'split'), may hold values from -0.0625 to 0.0625
- up_adapter_bank: bfloat16 [4, 64, 8192], P('split', None, ('blk', 'sub')), may hold values from -0.75 to 0.75
- rollout_row_tenant: int32 [1024], P('groups'), parts along dimension 0, may hold values from 0 to 3, as said below
- tenant_bank_entry: int32 [4], replicated, may hold values from 0 to 3, each once
- tenant_live_rank: int32 [4], replicated, may hold values from 16 to 64, as said below
Outputs:
- layer_out: bfloat16 [1024, 8192], P(('groups', 'split'), ('blk', 'sub')), parts along dimension 0
There are 2 independent parts, one for each index of `groups`. A program takes and returns all parts, laid end to end along the dimension named above; an argument that names none is the same for every part. Nothing has to cross between parts.
Inputs may be any that keep to these rules, and one draw needn't show every extreme that they name: `rollout_row_tenant`: every tenant owns at least one row of every part. `tenant_live_rank`: some tenant has the full rank 64.
All inputs are finite; a program needn't handle non-finite values.
Results may differ from a plain program's by a relative error of at most 0.0038.
Values may be sent and summed in bfloat16 or wider, within the bound.
No kernel may reach another device: no remote copies, remote signals or barrier semaphores. Data moves between devices by JAX's collectives and lax.ppermute only.
A program may use at most 64 MiB of HBM per device.

v0:
```python
import jax
import jax.numpy as jnp
from jax import lax
from jax.sharding import PartitionSpec as P


def shards(
    attention_output_rows,
    residual,
    output_projection_weight,
    down_adapter_bank,
    up_adapter_bank,
    rollout_row_tenant,
    tenant_bank_entry,
    tenant_live_rank,
):
    out_cols = output_projection_weight.shape[1]
    feat_width = attention_output_rows.shape[1]
    rank_mask_rows = down_adapter_bank.shape[1]
    gathered_down_maps = lax.all_gather(down_adapter_bank, "blk", axis=0, tiled=True)
    tenant_count = gathered_down_maps.shape[0]
    total_rows = rollout_row_tenant.shape[0]
    tenant_ids = jnp.arange(tenant_count, dtype=jnp.int32)
    tenant_hot = (rollout_row_tenant[:, None] == tenant_ids[None, :]).astype(jnp.int32)
    slot_all = jnp.sum(tenant_hot * tenant_bank_entry[None, :], axis=1)
    rank_all = jnp.sum(tenant_hot * tenant_live_rank[None, :], axis=1)
    down_cols = gathered_down_maps.reshape(tenant_count * rank_mask_rows, feat_width).T
    joined = jnp.concatenate([output_projection_weight, down_cols], axis=1)
    own_count = total_rows // lax.axis_size("split")
    own_start = lax.axis_index("split") * own_count
    own_slot = lax.dynamic_slice_in_dim(slot_all, own_start, own_count, 0)
    own_rank = lax.dynamic_slice_in_dim(rank_all, own_start, own_count, 0)
    own_hot = own_slot[:, None] == tenant_ids[None, :]
    full = jnp.dot(
        lax.all_gather(attention_output_rows, "blk", axis=0, tiled=True),
        joined,
        preferred_element_type=jnp.float32,
    )
    piece_hot = slot_all[:, None] == tenant_ids[None, :]
    values = full[:, out_cols:]
    shaped = values.reshape(values.shape[0], tenant_count, rank_mask_rows)
    products = jnp.concatenate(
        [
            full[:, :out_cols],
            jnp.sum(jnp.where(piece_hot[:, :, None], shaped, jnp.zeros((), jnp.float32)), axis=1),
        ],
        axis=1,
    )
    summed = lax.psum_scatter(products, "split", scatter_dimension=0, tiled=True)
    frozen_output_term = summed[:, :out_cols]
    low_rank = summed[:, out_cols:]
    gathered_up_maps = lax.all_gather(up_adapter_bank, "split", axis=0, tiled=True)
    kept_mask = jnp.arange(rank_mask_rows, dtype=jnp.int32)[None, :] < own_rank[:, None]
    scaling = rank_mask_rows / own_rank.astype(jnp.float32)
    low_scaled = jnp.where(
        kept_mask, low_rank * scaling[:, None], jnp.zeros((), jnp.float32)
    ).astype(jnp.bfloat16)
    rank_expanded_rows = jnp.where(
        own_hot[:, :, None], low_scaled[:, None, :], jnp.zeros((), jnp.bfloat16)
    ).reshape(own_count, tenant_count * rank_mask_rows)
    adapter_output_term = jnp.dot(
        rank_expanded_rows,
        gathered_up_maps.reshape(tenant_count * rank_mask_rows, out_cols),
        preferred_element_type=jnp.float32,
    )
    return (residual.astype(jnp.float32) + frozen_output_term + adapter_output_term).astype(
        jnp.bfloat16
    )


def solution(mesh):
    in_specs = (
        P(("groups", "blk"), "split"),
        P(("groups", "split"), ("blk", "sub")),
        P("split", ("blk", "sub")),
        P("blk", None, "split"),
        P("split", None, ("blk", "sub")),
        P("groups"),
        P(),
        P(),
    )
    out_specs = P(("groups", "split"), ("blk", "sub"))
    return jax.shard_map(shards, mesh=mesh, in_specs=in_specs, out_specs=out_specs, check_vma=False)
```

profile of v0, /device:TPU:0, one launch (start us, length us, event | category | flops | bytes accessed | tf_op | source)
XLA Modules:
  0.0 195.2 jit_solution(4081771632402627207)
XLA Ops:
  6.5 0.0 all-gather.3.cloned.1.call-start
  6.5 0.7 all-gather.3.cloned.1.call-update
  7.3 0.0 all-gather.5.cloned.1.call-start
  7.3 0.7 all-gather.5.cloned.1.call-update
  8.0 0.0 reduce-scatter.2.cloned.1.call-start
  8.1 0.8 select_reduce_fusion.1
  8.8 48.8 %all-gather.3.cloned.1.call-done = bf16[4,64,4096]{2,1,0:T(8,128)(2,1)} async-done(((bf16[1,64,4096]{2,1,0:T(8,128)(2,1)}), bf16[4,64,4096]{2,1,0:T(8,128)(2,1)}) %all-gather.3.cloned.1.call-update) | async-done | bytes 2097168 | tf_op jit(solution)/shard_map/all_gather | solution.py:20
  57.6 3.3 %copy.18 = bf16[256,4096]{0,1:T(8,128)(2,1)S(1)} copy(bf16[256,4096]{1,0:T(8,128)(2,1)} %bitcast.14) | data formatting | bytes 4194304 | tf_op jit(solution)/shard_map/reshape | solution.py:27
  60.9 77.8 %all-gather.5.cloned.1.call-done = bf16[512,4096]{1,0:T(8,128)(2,1)} async-done(((bf16[128,4096]{1,0:T(8,128)(2,1)}), bf16[512,4096]{1,0:T(8,128)(2,1)}) %all-gather.5.cloned.1.call-update) | async-done | bytes 4194320 | tf_op jit(solution)/shard_map/all_gather | solution.py:35
  138.7 9.7 %fusion.4 = f32[512,1280]{0,1:T(8,128)S(1)} fusion(bf16[512,4096]{1,0:T(8,128)(2,1)} %all-gather.5.cloned.1.call-done, bf16[4096,256]{1,0:T(8,128)(2,1)S(1)} %bitcast.15, bf16[4096,1024]{1,0:T(8,128)(2,1)} %param.10), kind=kOutput, calls=%fused_computation.4 | convolution fusion | flops 5389680640 | bytes 17301504 | tf_op jit(solution)/shard_map/dot_general | solution.py:34
  148.4 0.2 slice.16
  148.6 0.1 select_reduce_fusion
  148.7 0.0 copy-start
  148.7 1.6 pad_maximum_fusion
  150.3 0.0 copy-start.1
  150.3 0.0 reduce-scatter.2.cloned.1.call-update
  150.3 0.1 dynamic_slice.6
  150.4 0.0 copy-done
  150.4 0.2 copy.17
  150.6 0.1 convert_divide_fusion
  150.7 0.5 copy-done.1
  151.2 13.0 %all_gather.11 = bf16[4,64,1024]{2,1,0:T(8,128)(2,1)S(1)} all-gather(bf16[2,64,1024]{2,1,0:T(8,128)(2,1)S(1)} %copy-done.1), channel_id=1, replica_groups=mesh['groups'=2,'blk'=4,'split'=2,'sub'=2] {'split'}, dimensions={0}, use_global_device_ids=true | all-gather | bytes 786432 | tf_op jit(solution)/shard_map/all_gather | solution.py:52
  164.3 21.0 %reduce-scatter.2.cloned.1.call-done = f32[256,1088]{0,1:T(8,128)} async-done(((f32[512,1088]{0,1:T(8,128)}), f32[256,1088]{0,1:T(8,128)}) %reduce-scatter.2.cloned.1.call-update) | async-done | bytes 1114128 | tf_op jit(solution)/shard_map/reduce_scatter | solution.py:49
  185.2 0.9 fusion.12
  186.1 1.6 fusion.8
  187.7 1.0 copy.20
  (3 shorter events, 0.1 us)
Async XLA Ops:
  6.5 51.1 %all-gather.3.cloned.1.call-start = ((), (), s32[]{:S(2)}) async-start(), calls=%async_computation.1 | async-start | bytes 2621440 | tf_op jit(solution)/shard_map/all_gather | solution.py:20
  7.3 131.4 %all-gather.5.cloned.1.call-start = ((), (), s32[]{:S(2)}) async-start(), calls=%async_computation.2 | async-start | bytes 5242880 | tf_op jit(solution)/shard_map/all_gather | solution.py:35
  8.0 177.2 %reduce-scatter.2.cloned.1.call-start = ((), (), s32[]{:S(2)}) async-start(), calls=%async_computation.3 | async-start | bytes 3342336 | tf_op jit(solution)/shard_map/reduce_scatter | solution.py:49
  148.7 1.7 copy-start
  150.3 0.9 copy-start.1
Sparse Core Ops, SparseCore 0:
  8.9 48.6 all-gather.2
  59.2 79.4 all-gather.4
  150.4 34.7 reduce-scatter.1
where the time goes:
time: 196 us; the launch traced here: 195 us
  waiting for transfers between devices  149 us (76%)
  between operations  13.2 us (7%)
  blocking collectives  13 us (7%)
  matrix products  11.3 us (6%)
  local copies, waits for them, and re-layouts  5.31 us (3%)
  other arithmetic  3.35 us (2%)
    all_gather x1, waiting for transfers between devices, shards(): lax.all_gather(attention_output_rows, 'blk', axis=0, tiled=True)  77.8 us
    all_gather x1, waiting for transfers between devices, shards(): lax.all_gather(down_adapter_bank, 'blk', axis=0, tiled=True)  48.8 us
    reduce_scatter x1, waiting for transfers between devices, shards(): lax.psum_scatter(products, 'split', scatter_dimension=0, tiled=True)  21 us
    all_gather x1, blocking collectives, shards(): lax.all_gather(up_adapter_bank, 'split', axis=0, tiled=True)  13 us
    dot_general x1, matrix products, shards(): jnp.dot(lax.all_gather(attention_output_rows, 'blk', axis=0, tiled=True),...  9.71 us
  transfers between devices with their start and end apart: 3, of which 3 were waited for; matrix products, arithmetic and copies ran while one was open for 2% of the time, Pallas kernels for 0%

commit v1 on v0

v1 whole, which is shorter than its diff:
```python
import jax
import jax.numpy as jnp
from jax import lax
from jax.sharding import PartitionSpec as P

F32 = jnp.float32
BF16 = jnp.bfloat16


def low_rank_weights(low, slot, live, slots, rank_width):
    kept = jnp.arange(rank_width, dtype=jnp.int32)[None, :] < live[:, None]
    scaling = rank_width / live.astype(F32)
    scaled = jnp.where(kept, low * scaling[:, None], jnp.zeros((), F32)).astype(BF16)
    hot = slot[:, None] == jnp.arange(slots, dtype=jnp.int32)[None, :]
    spread = jnp.where(hot[:, :, None], scaled[:, None, :], jnp.zeros((), BF16))
    return spread.reshape(low.shape[0], slots * rank_width)


def tables(tenant, entry, live):
    ids = jnp.arange(entry.shape[0], dtype=jnp.int32)
    hot = (tenant[:, None] == ids[None, :]).astype(jnp.int32)
    return jnp.sum(hot * entry[None, :], axis=1), jnp.sum(hot * live[None, :], axis=1)


def general(rows, residual, weight, down, up, tenant, entry, live):
    own = residual.shape[0]
    cols = weight.shape[1]
    width = down.shape[1]
    slots = entry.shape[0]
    slot_all, live_all = tables(tenant, entry, live)
    part = rows.shape[0] // lax.axis_size("sub")
    mine = lax.dynamic_slice_in_dim(rows, lax.axis_index("sub") * part, part, 0)
    halves = lax.all_gather(lax.all_gather(mine, "blk", axis=0), "sub", axis=1)
    full = halves.reshape(-1, rows.shape[1])
    base = jnp.dot(full, weight, preferred_element_type=F32)
    low = lax.dot_general(
        full, down.reshape(-1, down.shape[2]), (((1,), (1,)), ((), ())), preferred_element_type=F32
    )
    held = down.shape[0]
    places = lax.axis_index("blk") * held + jnp.arange(held, dtype=jnp.int32)
    here = slot_all[:, None] == places[None, :]
    low = jnp.sum(
        jnp.where(here[:, :, None], low.reshape(-1, held, width), jnp.zeros((), F32)), axis=1
    )
    low = lax.psum(lax.psum_scatter(low, "split", scatter_dimension=0, tiled=True), "blk")
    base = lax.psum_scatter(base, "split", scatter_dimension=0, tiled=True)
    start = lax.axis_index("split") * own
    spread = low_rank_weights(
        low,
        lax.dynamic_slice_in_dim(slot_all, start, own, 0),
        lax.dynamic_slice_in_dim(live_all, start, own, 0),
        slots,
        width,
    )
    ups = lax.all_gather(up, "split", axis=0, tiled=True).reshape(slots * width, cols)
    lora = jnp.dot(spread, ups, preferred_element_type=F32)
    return (residual.astype(F32) + base + lora).astype(BF16)


def line(rows, residual, weight, down, up, tenant, entry, live):
    z, x, c = lax.axis_index("blk"), lax.axis_index("split"), lax.axis_index("sub")
    own = residual.shape[0]
    cols = weight.shape[1]
    width = down.shape[1]
    slots = entry.shape[0]
    slot_all, live_all = tables(tenant, entry, live)
    start = x * own

    up_other = lax.ppermute(up, "split", [(0, 1), (1, 0)])
    ups = jnp.where(x == 0, jnp.concatenate([up, up_other]), jnp.concatenate([up_other, up]))
    ups = ups.reshape(slots * width, cols)

    half = rows.shape[0] // 2
    mine = lax.dynamic_slice_in_dim(rows, c * half, half, 0)
    end = (z == 0) | (z == 3)

    pieces = 2
    step = half // pieces
    near, third, fourth = [], [], []
    for p in range(pieces):
        piece = mine[p * step : (p + 1) * step]
        a = lax.ppermute(piece, "blk", [(0, 1), (1, 0), (2, 3), (3, 2)])
        b = lax.ppermute(piece, "blk", [(1, 2), (2, 1)])
        e = lax.ppermute(
            jnp.where(end, piece, b), "blk", [(0, 2), (3, 1), (1, 0), (2, 3)]
        )
        f = lax.ppermute(e, "blk", [(1, 0), (2, 3)])
        near.append(a)
        third.append(jnp.where(end, e, b))
        fourth.append(jnp.where(end, f, e))

    def both(piece):
        other = lax.ppermute(piece, "sub", [(0, 1), (1, 0)])
        return jnp.where(c == 0, jnp.concatenate([piece, other]), jnp.concatenate([other, piece]))

    def whole(parts):
        pairs = [both(part) for part in parts]
        return jnp.concatenate(
            [pair[:step] for pair in pairs] + [pair[step:] for pair in pairs]
        )

    down_map = down[0]

    def products(block):
        base = jnp.dot(block, weight, preferred_element_type=F32)
        low = lax.dot_general(block, down_map, (((1,), (1,)), ((), ())), preferred_element_type=F32)
        return base, low

    blocks = [rows, whole(near), whole(third), whole(fourth)]
    results = [products(block) for block in blocks]
    low_z = z >= 2
    odd = (z % 2) == 1

    def ordered(first, second, swap):
        return jnp.where(swap, jnp.concatenate([second, first]), jnp.concatenate([first, second]))

    early = ordered(results[0][0], results[1][0], odd)
    late = ordered(results[2][0], results[3][0], low_z)
    home = (z // 2) == x
    to_home = [(2 * k + 1 - k // 2, 2 * k + k // 2) for k in range(4)]
    to_away = [(b, a) for a, b in to_home]
    got_early = lax.ppermute(early.astype(BF16), ("blk", "split"), to_home)
    got_late = lax.ppermute(late.astype(BF16), ("blk", "split"), to_away)
    base = jnp.where(home, early, late) + jnp.where(home, got_early, got_late).astype(F32)

    low_early = ordered(results[0][1], results[1][1], odd)
    low_late = ordered(results[2][1], results[3][1], low_z)
    low_keep = jnp.where(home, low_early, low_late)
    low_send = jnp.where(home, low_late, low_early)
    low = low_keep + lax.ppermute(low_send, "split", [(0, 1), (1, 0)])
    slot = lax.dynamic_slice_in_dim(slot_all, start, own, 0)
    low = jnp.where((slot == z)[:, None], low, jnp.zeros((), F32))
    low = low + lax.ppermute(low, "blk", [(0, 1), (1, 0), (2, 3), (3, 2)])
    low = low + lax.ppermute(low, "blk", [(0, 2), (2, 0), (1, 3), (3, 1)])
    spread = low_rank_weights(
        low, slot, lax.dynamic_slice_in_dim(live_all, start, own, 0), slots, width
    )
    lora = jnp.dot(spread, ups, preferred_element_type=F32)
    return (residual.astype(F32) + base + lora).astype(BF16)


def shards(rows, residual, weight, down, up, tenant, entry, live):
    sizes = [lax.axis_size(name) for name in ("blk", "split", "sub")]
    plan = line if sizes == [4, 2, 2] and down.shape[0] == 1 else general
    return plan(rows, residual, weight, down, up, tenant, entry, live)


def solution(mesh):
    in_specs = (
        P(("groups", "blk"), "split"),
        P(("groups", "split"), ("blk", "sub")),
        P("split", ("blk", "sub")),
        P("blk", None, "split"),
        P("split", None, ("blk", "sub")),
        P("groups"),
        P(),
        P(),
    )
    out_specs = P(("groups", "split"), ("blk", "sub"))
    return jax.shard_map(shards, mesh=mesh, in_specs=in_specs, out_specs=out_specs, check_vma=False)
```

time: 196 us -> 68.5 us (0.35)
  waiting for transfers between devices: 149 us -> 23.1 us
  starting transfers between devices: 0.08 us -> 23.7 us
  blocking collectives: 13 us -> 0 us
  between operations: 13.2 us -> 0.41 us
  matrix products: 11.3 us -> 16.5 us
  local copies, waits for them, and re-layouts: 5.31 us -> 1.44 us
    all_gather x2 -> x0, waiting for transfers between devices: 127 us -> none  [the longest x1 77.8 us: shards(): lax.all_gather(attention_output_rows, 'blk', axis=0, tiled=True)]
    ppermute x0 -> x20, starting transfers between devices: none -> 23.7 us  [the longest x2 7.67 us: line(): a = lax.ppermute(piece, 'blk', [(0, 1), (1, 0), (2, 3), (3, 2)])]
    ppermute x0 -> x20, waiting for transfers between devices: none -> 23.1 us  [the longest x2 10.7 us: line(): f = lax.ppermute(e, 'blk', [(1, 0), (2, 3)])]
    reduce_scatter x1 -> x0, waiting for transfers between devices: 21 us -> none  [shards(): lax.psum_scatter(products, 'split', scatter_dimension=0, tiled=True)]
    all_gather x1 -> x0, blocking collectives: 13 us -> none  [shards(): lax.all_gather(up_adapter_bank, 'split', axis=0, tiled=True)]
    dot_general x2 -> x9, matrix products: 11.3 us -> 16.5 us  [the longest x4 12 us: products(): base = jnp.dot(block, weight, preferred_element_type=F32)]
    reshape x1 -> x0, local copies, waits for them, and re-layouts: 3.27 us -> none  [shards(): gathered_down_maps.reshape(tenant_count * rank_mask_rows, feat_width)]
  transfers between devices with their start and end apart: 3 -> 20, of which waited for: 3 -> 9; matrix products, arithmetic and copies ran while one was open for 2% -> 25% of each run, Pallas kernels for 0% -> 0%
where the time goes in v1:
time: 68.5 us; the launch traced here: 68.2 us
  starting transfers between devices  23.7 us (35%)
  waiting for transfers between devices  23.1 us (34%)
  matrix products  16.5 us (24%)
  other arithmetic  3.01 us (4%)
  local copies, waits for them, and re-layouts  1.44 us (2%)
    dot_general x4, matrix products, products(): base = jnp.dot(block, weight, preferred_element_type=F32)  12 us
    ppermute x2, waiting for transfers between devices, line(): f = lax.ppermute(e, 'blk', [(1, 0), (2, 3)])  10.7 us
    ppermute x2, starting transfers between devices, line(): a = lax.ppermute(piece, 'blk', [(0, 1), (1, 0), (2, 3), (3, 2)])  7.67 us
    ppermute x1, waiting for transfers between devices, line(): low = low + lax.ppermute(low, 'blk', [(0, 2), (2, 0), (1, 3), (3, 1)])  5.21 us
    ppermute x1, waiting for transfers between devices, line(): low = low + lax.ppermute(low, 'blk', [(0, 1), (1, 0), (2, 3), (3, 2)])  4.24 us
    ppermute x2, starting transfers between devices, line(): lax.ppermute(jnp.where(end, piece, b), 'blk', [(0, 2), (3, 1), (1, 0), (2...  3.68 us
    ppermute x1, starting transfers between devices, line(): got_late = lax.ppermute(late.astype(BF16), ('blk', 'split'), to_away)  3.06 us
    dot_general x1, matrix products, line(): lora = jnp.dot(spread, ups, preferred_element_type=F32)  2.67 us
  transfers between devices with their start and end apart: 20, of which 9 were waited for; matrix products, arithmetic and copies ran while one was open for 25% of the time, Pallas kernels for 0%

profile of v1, /device:TPU:0, one launch (start us, length us, event | category | flops | bytes accessed | tf_op | source)
XLA Modules:
  0.0 68.2 jit_solution(5477375029678189351)
XLA Ops:
  0.0 1.2 %constant_dynamic-slice_fusion = (bf16[32,4096]{1,0:T(8,128)(2,1)S(1)}, bf16[32,4096]{1,0:T(8,128)(2,1)S(1)}) fusion(bf16[128,4096]{1,0:T(8,128)(2,1)} %param.8, s32[]{:T(128)S(6)} %select_n.149, s32[]{:T(128)S(6)} %add.39), kind=kLoop, calls=%fused_computation.55 | loop fusion | bytes 1048584 | tf_op jit(solution)/shard_map/slice | solution.py:81
  1.2 0.7 collective-permute-start.4
  1.9 5.9 %collective-permute-start = (bf16[32,4096]{1,0:T(8,128)(2,1)S(1)}, bf16[32,4096]{1,0:T(8,128)(2,1)}, u32[]{:S(2)}, u32[]{:S(2)}) collective-permute-start(bf16[32,4096]{1,0:T(8,128)(2,1)S(1)} %get-tuple-element.11), channel_id=1, source_target_pairs={{0,4},{4,0},{8,12},{12,8},{1,5},{5,1},{9,13},{13,9},{2,6},{6,2},{1... | collective-permute-start | bytes 786440 | tf_op jit(solution)/shard_map/ppermute | solution.py:82
  7.8 0.7 collective-permute-start.8
  8.4 1.8 %collective-permute-start.2 = (bf16[32,4096]{1,0:T(8,128)(2,1)S(1)}, bf16[32,4096]{1,0:T(8,128)(2,1)S(1)}, u32[]{:S(2)}, u32[]{:S(2)}) collective-permute-start(bf16[32,4096]{1,0:T(8,128)(2,1)S(1)} %get-tuple-element.12), channel_id=1, source_target_pairs={{0,4},{4,0},{8,12},{12,8},{1,5},{5,1},{9,13},{13,9},{2,6},{6,2},{1... | collective-permute-start | bytes 786440 | tf_op jit(solution)/shard_map/ppermute | solution.py:82
  10.2 1.5 %collective-permute-start.19 = (bf16[2,64,1024]{2,1,0:T(8,128)(2,1)}, bf16[2,64,1024]{2,1,0:T(8,128)(2,1)}, u32[]{:S(2)}, u32[]{:S(2)}) collective-permute-start(bf16[2,64,1024]{2,1,0:T(8,128)(2,1)} %param.12), channel_id=1, source_target_pairs={{0,2},{2,0},{1,3},{3,1},{4,6},{6,4},{5,7},{7,5},{8,10},{10,8},{9,1... | collective-permute-start | bytes 786440 | tf_op jit(solution)/shard_map/ppermute | solution.py:69
  11.7 4.7 %fusion.38 = f32[128,1024]{1,0:T(8,128)S(1)} fusion(bf16[128,4096]{1,0:T(8,128)(2,1)S(1)} %copy-done.1, bf16[4096,1024]{1,0:T(8,128)(2,1)} %param.10), kind=kOutput, calls=%fused_computation.71 | convolution fusion | flops 1073741824 | bytes 9961472 | tf_op jit(solution)/shard_map/dot_general | solution.py:105
  16.4 0.1 select_reduce_fusion
  16.5 0.1 broadcast_compare_fusion
  16.6 0.5 fusion.11
  17.1 1.1 %collective-permute-start.5 = (bf16[32,4096]{1,0:T(8,128)(2,1)S(1)}, bf16[32,4096]{1,0:T(8,128)(2,1)S(1)}, u32[]{:S(2)}, u32[]{:S(2)}) collective-permute-start(bf16[32,4096]{1,0:T(8,128)(2,1)S(1)} %broadcast_select_fusion.5), channel_id=1, source_target_pairs={{0,8},{12,4},{4,0},{8,12},{1,9},{13,5},{5,1},{9,13},{2,10},{14,6},... | collective-permute-start | bytes 786440 | tf_op jit(solution)/shard_map/ppermute | solution.py:84
  18.3 2.5 %collective-permute-start.9 = (bf16[32,4096]{1,0:T(8,128)(2,1)S(1)}, bf16[32,4096]{1,0:T(8,128)(2,1)S(1)}, u32[]{:S(2)}, u32[]{:S(2)}) collective-permute-start(bf16[32,4096]{1,0:T(8,128)(2,1)S(1)} %broadcast_select_fusion.3), channel_id=1, source_target_pairs={{0,8},{12,4},{4,0},{8,12},{1,9},{13,5},{5,1},{9,13},{2,10},{14,6},... | collective-permute-start | bytes 786440 | tf_op jit(solution)/shard_map/ppermute | solution.py:84
  20.9 1.1 %maximum_select_fusion.2 = bf16[64,4096]{1,0:T(8,128)(2,1)S(1)} fusion(bf16[32,4096]{1,0:T(8,128)(2,1)S(1)} %collective-permute-done.1, bf16[32,4096]{1,0:T(8,128)(2,1)} %collective-permute-done, pred[]{:T(512)S(6)} %eq.63), kind=kLoop, calls=%fused_computation.9 | loop fusion | flops 2359296 | bytes 1048577 | tf_op jit(solution)/shard_map/jit(_where)/select_n | solution.py:94
  22.1 0.3 collective-permute-done.3
  22.4 0.1 maximum_select_fusion.3
  22.6 4.8 %fusion.18 = f32[128,1024]{1,0:T(8,128)S(1)} fusion(bf16[4096,1024]{1,0:T(8,128)(2,1)} %param.10, bf16[32,4096]{1,0:T(8,128)(2,1)S(1)} %get-tuple-element.16, bf16[32,4096]{1,0:T(8,128)(2,1)S(1)} %get-tuple-element.14, bf16[32,4096]{1,0:T(8,128)(2,1)S(1)} %get-tuple-element.15, bf16[32,4096]{1,0:T(8,128)(2,1)S(1)} %get-tuple-element.13), kind=kOutput, calls=%fused_computation.38 | convolution fusion | flops 1077936128 | bytes 9961472 | tf_op jit(solution)/shard_map/dot_general | solution.py:105
  27.4 1.3 %collective-permute-start.6 = (bf16[32,4096]{1,0:T(8,128)(2,1)S(1)}, bf16[32,4096]{1,0:T(8,128)(2,1)S(1)}, u32[]{:S(2)}, u32[]{:S(2)}) collective-permute-start(bf16[32,4096]{1,0:T(8,128)(2,1)S(1)} %collective-permute-done.5), channel_id=1, source_target_pairs={{4,0},{8,12},{5,1},{9,13},{6,2},{10,14},{7,3},{11,15},{20,16},{24,... | collective-permute-start | bytes 786440 | tf_op jit(solution)/shard_map/ppermute | solution.py:87
  28.7 0.1 fusion.1
  28.8 1.3 %collective-permute-start.14 = (bf16[256,1024]{1,0:T(8,128)(2,1)S(1)}, bf16[256,1024]{1,0:T(8,128)(2,1)}, u32[]{:S(2)}, u32[]{:S(2)}) collective-permute-start(bf16[256,1024]{1,0:T(8,128)(2,1)S(1)} %fusion.1), channel_id=1, source_target_pairs={{2,0},{6,4},{8,10},{12,14},{3,1},{7,5},{9,11},{13,15},{18,16},{22,... | collective-permute-start | bytes 1572872 | tf_op jit(solution)/shard_map/ppermute | solution.py:122
  30.1 0.6 collective-permute-done.9
  30.7 1.3 %collective-permute-start.10 = (bf16[32,4096]{1,0:T(8,128)(2,1)S(1)}, bf16[32,4096]{1,0:T(8,128)(2,1)S(1)}, u32[]{:S(2)}, u32[]{:S(2)}) collective-permute-start(bf16[32,4096]{1,0:T(8,128)(2,1)S(1)} %collective-permute-done.9), channel_id=1, source_target_pairs={{4,0},{8,12},{5,1},{9,13},{6,2},{10,14},{7,3},{11,15},{20,16},{24,... | collective-permute-start | bytes 786440 | tf_op jit(solution)/shard_map/ppermute | solution.py:87
  31.9 0.5 fusion.13
  32.4 6.0 %collective-permute-done.6 = bf16[32,4096]{1,0:T(8,128)(2,1)S(1)} collective-permute-done((bf16[32,4096]{1,0:T(8,128)(2,1)S(1)}, bf16[32,4096]{1,0:T(8,128)(2,1)S(1)}, u32[]{:S(2)}, u32[]{:S(2)}) %collective-permute-start.6) | collective-permute-done | bytes 262176 | tf_op jit(solution)/shard_map/ppermute | solution.py:87
  38.5 0.1 collective-permute-start.12
  38.5 4.7 %collective-permute-done.10 = bf16[32,4096]{1,0:T(8,128)(2,1)S(1)} collective-permute-done((bf16[32,4096]{1,0:T(8,128)(2,1)S(1)}, bf16[32,4096]{1,0:T(8,128)(2,1)S(1)}, u32[]{:S(2)}, u32[]{:S(2)}) %collective-permute-start.10) | collective-permute-done | bytes 262176 | tf_op jit(solution)/shard_map/ppermute | solution.py:87
  43.3 0.1 collective-permute-start.13
  43.4 0.5 collective-permute-start.7
  43.9 0.1 collective-permute-start.11
  44.0 0.1 maximum_select_fusion.6
  44.1 0.8 %collective-permute-done.13 = bf16[32,4096]{1,0:T(8,128)(2,1)S(1)} collective-permute-done((bf16[32,4096]{1,0:T(8,128)(2,1)S(1)}, bf16[32,4096]{1,0:T(8,128)(2,1)S(1)}, u32[]{:S(2)}, u32[]{:S(2)}) %collective-permute-start.13) | collective-permute-done | bytes 262176 | tf_op jit(solution)/shard_map/ppermute | solution.py:93
  44.9 0.1 maximum_select_fusion.7
  45.1 0.2 collective-permute-done.7
  45.3 0.1 maximum_select_fusion.4
  45.5 1.3 %fusion.16 = f32[128,1024]{1,0:T(8,128)S(1)} fusion(bf16[4096,1024]{1,0:T(8,128)(2,1)S(1)} %bitcast.20, bf16[32,4096]{1,0:T(8,128)(2,1)S(1)} %get-tuple-element.20, bf16[32,4096]{1,0:T(8,128)(2,1)S(1)} %get-tuple-element.18, bf16[32,4096]{1,0:T(8,128)(2,1)S(1)} %get-tuple-element.19, bf16[32,4096]{1,0:T(8,128)(2,1)S(1)} %get-tuple-element.17), kind=kOutput, calls=%fused_computation.36 | convolution fusion | flops 1077936128 | bytes 9961472 | tf_op jit(solution)/shard_map/dot_general | solution.py:105
  46.7 0.5 fusion.7
  47.2 0.1 maximum_select_fusion.5
  47.4 0.5 fusion.9
  47.8 1.3 %fusion.17 = f32[128,1024]{1,0:T(8,128)S(1)} fusion(bf16[4096,1024]{1,0:T(8,128)(2,1)S(1)} %bitcast.20, bf16[32,4096]{1,0:T(8,128)(2,1)S(1)} %get-tuple-element.24, bf16[32,4096]{1,0:T(8,128)(2,1)S(1)} %get-tuple-element.22, bf16[32,4096]{1,0:T(8,128)(2,1)S(1)} %get-tuple-element.23, bf16[32,4096]{1,0:T(8,128)(2,1)S(1)} %get-tuple-element.21), kind=kOutput, calls=%fused_computation.37 | convolution fusion | flops 1077936128 | bytes 9961472 | tf_op jit(solution)/shard_map/dot_general | solution.py:105
  49.1 1.7 %collective-permute-start.16 = (f32[256,64]{0,1:T(8,128)S(1)}, f32[256,64]{0,1:T(8,128)S(1)}, u32[]{:S(2)}, u32[]{:S(2)}) collective-permute-start(f32[256,64]{0,1:T(8,128)S(1)} %fusion.23), channel_id=1, source_target_pairs={{0,2},{2,0},{1,3},{3,1},{4,6},{6,4},{5,7},{7,5},{8,10},{10,8},{9,1... | collective-permute-start | bytes 196616 | tf_op jit(solution)/shard_map/ppermute | solution.py:130
  50.9 0.9 %fusion = bf16[256,1024]{1,0:T(8,128)(2,1)} fusion(f32[128,1024]{1,0:T(8,128)S(1)} %fusion.17, f32[128,1024]{1,0:T(8,128)S(1)} %fusion.16, pred[]{:T(512)S(6)} %ge.3), kind=kLoop, calls=%fused_computation.7 | loop fusion | flops 2359296 | bytes 1572865 | tf_op jit(solution)/shard_map/convert_element_type | solution.py:123
  51.8 3.1 %collective-permute-start.15 = (bf16[256,1024]{1,0:T(8,128)(2,1)}, bf16[256,1024]{1,0:T(8,128)(2,1)}, u32[]{:S(2)}, u32[]{:S(2)}) collective-permute-start(bf16[256,1024]{1,0:T(8,128)(2,1)} %fusion), channel_id=1, source_target_pairs={{0,2},{4,6},{10,8},{14,12},{1,3},{5,7},{11,9},{15,13},{16,18},{20,... | collective-permute-start | bytes 1572872 | tf_op jit(solution)/shard_map/ppermute | solution.py:123
  54.9 0.1 collective-permute-start.17
  54.9 4.2 %collective-permute-done.17 = f32[256,64]{0,1:T(8,128)S(1)} collective-permute-done((f32[256,64]{0,1:T(8,128)S(1)}, f32[256,64]{0,1:T(8,128)S(1)}, u32[]{:S(2)}, u32[]{:S(2)}) %collective-permute-start.17) | collective-permute-done | bytes 65568 | tf_op jit(solution)/shard_map/ppermute | solution.py:133
  59.2 0.1 collective-permute-start.18
  59.3 0.1 convert_divide_fusion
  59.4 5.2 %collective-permute-done.18 = f32[256,64]{0,1:T(8,128)S(1)} collective-permute-done((f32[256,64]{0,1:T(8,128)S(1)}, f32[256,64]{0,1:T(8,128)S(1)}, u32[]{:S(2)}, u32[]{:S(2)}) %collective-permute-start.18) | collective-permute-done | bytes 65568 | tf_op jit(solution)/shard_map/ppermute | solution.py:134
  64.6 0.9 %collective-permute-done.15 = bf16[256,1024]{1,0:T(8,128)(2,1)} collective-permute-done((bf16[256,1024]{1,0:T(8,128)(2,1)}, bf16[256,1024]{1,0:T(8,128)(2,1)}, u32[]{:S(2)}, u32[]{:S(2)}) %collective-permute-start.15) | collective-permute-done | bytes 524320 | tf_op jit(solution)/shard_map/ppermute | solution.py:123
  65.5 2.7 %add_convert_fusion = bf16[256,1024]{1,0:T(8,128)(2,1)} fusion(bf16[256,1024]{1,0:T(8,128)(2,1)} %param.9, f32[128,1024]{1,0:T(8,128)S(1)} %fusion.17, f32[128,1024]{1,0:T(8,128)S(1)} %fusion.16, f32[128,1024]{1,0:T(8,128)S(1)} %fusion.18, f32[128,1024]{1,0:T(8,128)S(1)} %fusion.38, bf16[2,64,1024]{2,1,0:T(8,128)(2,1)} %collective-permute-done.19, ...), kind=kOutput, calls=%fused_computation.6 | convolution fusion | flops 138739712 | bytes 4752388 | tf_op jit(solution)/shard_map/dot_general | solution.py:138
  (45 shorter events, 0.5 us)
Async XLA Ops:
  0.0 16.6 %copy-start = (bf16[1,64,4096]{2,1,0:T(8,128)(2,1)S(1)}, bf16[1,64,4096]{2,1,0:T(8,128)(2,1)}, u32[]{:S(2)}) copy-start(bf16[1,64,4096]{2,1,0:T(8,128)(2,1)} %param.11) | copy-start | bytes 1572868
  0.0 11.7 %copy-start.1 = (bf16[128,4096]{1,0:T(8,128)(2,1)S(1)}, bf16[128,4096]{1,0:T(8,128)(2,1)}, u32[]{:S(2)}) copy-start(bf16[128,4096]{1,0:T(8,128)(2,1)} %param.8) | copy-start | bytes 3145732
  1.2 15.9 %collective-permute-start.4 = (bf16[32,4096]{1,0:T(8,128)(2,1)S(1)}, bf16[32,4096]{1,0:T(8,128)(2,1)S(1)}, u32[]{:S(2)}, u32[]{:S(2)}) collective-permute-start(bf16[32,4096]{1,0:T(8,128)(2,1)S(1)} %get-tuple-element.11), channel_id=1, source_target_pairs={{4,8},{8,4},{5,9},{9,5},{6,10},{10,6},{7,11},{11,7},{20,24},{24,20... | collective-permute-start | bytes 786440 | tf_op jit(solution)/shard_map/ppermute | solution.py:83
  1.9 16.4 %collective-permute-start = (bf16[32,4096]{1,0:T(8,128)(2,1)S(1)}, bf16[32,4096]{1,0:T(8,128)(2,1)}, u32[]{:S(2)}, u32[]{:S(2)}) collective-permute-start(bf16[32,4096]{1,0:T(8,128)(2,1)S(1)} %get-tuple-element.11), channel_id=1, source_target_pairs={{0,4},{4,0},{8,12},{12,8},{1,5},{5,1},{9,13},{13,9},{2,6},{6,2},{1... | collective-permute-start | bytes 786440 | tf_op jit(solution)/shard_map/ppermute | solution.py:82
  7.8 10.5 %collective-permute-start.8 = (bf16[32,4096]{1,0:T(8,128)(2,1)S(1)}, bf16[32,4096]{1,0:T(8,128)(2,1)S(1)}, u32[]{:S(2)}, u32[]{:S(2)}) collective-permute-start(bf16[32,4096]{1,0:T(8,128)(2,1)S(1)} %get-tuple-element.12), channel_id=1, source_target_pairs={{4,8},{8,4},{5,9},{9,5},{6,10},{10,6},{7,11},{11,7},{20,24},{24,20... | collective-permute-start | bytes 786440 | tf_op jit(solution)/shard_map/ppermute | solution.py:83
  8.4 12.4 %collective-permute-start.2 = (bf16[32,4096]{1,0:T(8,128)(2,1)S(1)}, bf16[32,4096]{1,0:T(8,128)(2,1)S(1)}, u32[]{:S(2)}, u32[]{:S(2)}) collective-permute-start(bf16[32,4096]{1,0:T(8,128)(2,1)S(1)} %get-tuple-element.12), channel_id=1, source_target_pairs={{0,4},{4,0},{8,12},{12,8},{1,5},{5,1},{9,13},{13,9},{2,6},{6,2},{1... | collective-permute-start | bytes 786440 | tf_op jit(solution)/shard_map/ppermute | solution.py:82
  10.2 54.4 %collective-permute-start.19 = (bf16[2,64,1024]{2,1,0:T(8,128)(2,1)}, bf16[2,64,1024]{2,1,0:T(8,128)(2,1)}, u32[]{:S(2)}, u32[]{:S(2)}) collective-permute-start(bf16[2,64,1024]{2,1,0:T(8,128)(2,1)} %param.12), channel_id=1, source_target_pairs={{0,2},{2,0},{1,3},{3,1},{4,6},{6,4},{5,7},{7,5},{8,10},{10,8},{9,1... | collective-permute-start | bytes 786440 | tf_op jit(solution)/shard_map/ppermute | solution.py:69
  11.7 4.7 %copy-start.2 = (s32[512]{0:T(512)S(1)}, s32[512]{0:T(512)}, u32[]{:S(2)}) copy-start(s32[512]{0:T(512)} %param.13) | copy-start | bytes 6148
  11.7 4.7 %copy-start.3 = (s32[4]{0:T(128)S(1)}, s32[4]{0:T(128)}, u32[]{:S(2)}) copy-start(s32[4]{0:T(128)} %param.15) | copy-start | bytes 52
  11.7 4.7 %copy-start.4 = (s32[4]{0:T(128)S(1)}, s32[4]{0:T(128)}, u32[]{:S(2)}) copy-start(s32[4]{0:T(128)} %param.14) | copy-start | bytes 52
  17.1 10.2 %collective-permute-start.5 = (bf16[32,4096]{1,0:T(8,128)(2,1)S(1)}, bf16[32,4096]{1,0:T(8,128)(2,1)S(1)}, u32[]{:S(2)}, u32[]{:S(2)}) collective-permute-start(bf16[32,4096]{1,0:T(8,128)(2,1)S(1)} %broadcast_select_fusion.5), channel_id=1, source_target_pairs={{0,8},{12,4},{4,0},{8,12},{1,9},{13,5},{5,1},{9,13},{2,10},{14,6},... | collective-permute-start | bytes 786440 | tf_op jit(solution)/shard_map/ppermute | solution.py:84
  18.3 2.6 %collective-permute-start.1 = (bf16[32,4096]{1,0:T(8,128)(2,1)}, bf16[32,4096]{1,0:T(8,128)(2,1)S(1)}, u32[]{:S(2)}, u32[]{:S(2)}) collective-permute-start(bf16[32,4096]{1,0:T(8,128)(2,1)} %collective-permute-done), channel_id=1, source_target_pairs={{0,1},{1,0},{2,3},{3,2},{4,5},{5,4},{6,7},{7,6},{8,9},{9,8},{10,11... | collective-permute-start | bytes 786440 | tf_op jit(solution)/shard_map/ppermute | solution.py:93
  18.3 12.3 %collective-permute-start.9 = (bf16[32,4096]{1,0:T(8,128)(2,1)S(1)}, bf16[32,4096]{1,0:T(8,128)(2,1)S(1)}, u32[]{:S(2)}, u32[]{:S(2)}) collective-permute-start(bf16[32,4096]{1,0:T(8,128)(2,1)S(1)} %broadcast_select_fusion.3), channel_id=1, source_target_pairs={{0,8},{12,4},{4,0},{8,12},{1,9},{13,5},{5,1},{9,13},{2,10},{14,6},... | collective-permute-start | bytes 786440 | tf_op jit(solution)/shard_map/ppermute | solution.py:84
  20.9 1.5 %collective-permute-start.3 = (bf16[32,4096]{1,0:T(8,128)(2,1)S(1)}, bf16[32,4096]{1,0:T(8,128)(2,1)S(1)}, u32[]{:S(2)}, u32[]{:S(2)}) collective-permute-start(bf16[32,4096]{1,0:T(8,128)(2,1)S(1)} %collective-permute-done.2), channel_id=1, source_target_pairs={{0,1},{1,0},{2,3},{3,2},{4,5},{5,4},{6,7},{7,6},{8,9},{9,8},{10,11... | collective-permute-start | bytes 786440 | tf_op jit(solution)/shard_map/ppermute | solution.py:93
  22.5 22.9 %slice-start = ((s8[8388608]{0:T(1024)(128)(4,1)}), s8[4194304]{0:T(1024)(128)(4,1)S(1)}, s32[]{:S(2)}) async-start(s8[8388608]{0:T(1024)(128)(4,1)} %bitcast.19), calls=%async_computation | async-start | bytes 8388608
  22.6 22.9 %slice-start.1 = ((s8[8388608]{0:T(1024)(128)(4,1)}), s8[4194304]{0:T(1024)(128)(4,1)S(1)}, s32[]{:S(2)}) async-start(s8[8388608]{0:T(1024)(128)(4,1)} %bitcast.19), calls=%async_computation.1 | async-start | bytes 8388608
  27.4 11.0 %collective-permute-start.6 = (bf16[32,4096]{1,0:T(8,128)(2,1)S(1)}, bf16[32,4096]{1,0:T(8,128)(2,1)S(1)}, u32[]{:S(2)}, u32[]{:S(2)}) collective-permute-start(bf16[32,4096]{1,0:T(8,128)(2,1)S(1)} %collective-permute-done.5), channel_id=1, source_target_pairs={{4,0},{8,12},{5,1},{9,13},{6,2},{10,14},{7,3},{11,15},{20,16},{24,... | collective-permute-start | bytes 786440 | tf_op jit(solution)/shard_map/ppermute | solution.py:87
  28.8 35.8 %collective-permute-start.14 = (bf16[256,1024]{1,0:T(8,128)(2,1)S(1)}, bf16[256,1024]{1,0:T(8,128)(2,1)}, u32[]{:S(2)}, u32[]{:S(2)}) collective-permute-start(bf16[256,1024]{1,0:T(8,128)(2,1)S(1)} %fusion.1), channel_id=1, source_target_pairs={{2,0},{6,4},{8,10},{12,14},{3,1},{7,5},{9,11},{13,15},{18,16},{22,... | collective-permute-start | bytes 1572872 | tf_op jit(solution)/shard_map/ppermute | solution.py:122
  30.7 12.6 %collective-permute-start.10 = (bf16[32,4096]{1,0:T(8,128)(2,1)S(1)}, bf16[32,4096]{1,0:T(8,128)(2,1)S(1)}, u32[]{:S(2)}, u32[]{:S(2)}) collective-permute-start(bf16[32,4096]{1,0:T(8,128)(2,1)S(1)} %collective-permute-done.9), channel_id=1, source_target_pairs={{4,0},{8,12},{5,1},{9,13},{6,2},{10,14},{7,3},{11,15},{20,16},{24,... | collective-permute-start | bytes 786440 | tf_op jit(solution)/shard_map/ppermute | solution.py:87
  38.5 5.4 %collective-permute-start.12 = (bf16[32,4096]{1,0:T(8,128)(2,1)S(1)}, bf16[32,4096]{1,0:T(8,128)(2,1)S(1)}, u32[]{:S(2)}, u32[]{:S(2)}) collective-permute-start(bf16[32,4096]{1,0:T(8,128)(2,1)S(1)} %get-tuple-element.25), channel_id=1, source_target_pairs={{0,1},{1,0},{2,3},{3,2},{4,5},{5,4},{6,7},{7,6},{8,9},{9,8},{10,11... | collective-permute-start | bytes 786440 | tf_op jit(solution)/shard_map/ppermute | solution.py:93
  43.3 1.6 %collective-permute-start.13 = (bf16[32,4096]{1,0:T(8,128)(2,1)S(1)}, bf16[32,4096]{1,0:T(8,128)(2,1)S(1)}, u32[]{:S(2)}, u32[]{:S(2)}) collective-permute-start(bf16[32,4096]{1,0:T(8,128)(2,1)S(1)} %get-tuple-element.27), channel_id=1, source_target_pairs={{0,1},{1,0},{2,3},{3,2},{4,5},{5,4},{6,7},{7,6},{8,9},{9,8},{10,11... | collective-permute-start | bytes 786440 | tf_op jit(solution)/shard_map/ppermute | solution.py:93
  43.4 1.9 %collective-permute-start.7 = (bf16[32,4096]{1,0:T(8,128)(2,1)S(1)}, bf16[32,4096]{1,0:T(8,128)(2,1)S(1)}, u32[]{:S(2)}, u32[]{:S(2)}) collective-permute-start(bf16[32,4096]{1,0:T(8,128)(2,1)S(1)} %get-tuple-element.26), channel_id=1, source_target_pairs={{0,1},{1,0},{2,3},{3,2},{4,5},{5,4},{6,7},{7,6},{8,9},{9,8},{10,11... | collective-permute-start | bytes 786440 | tf_op jit(solution)/shard_map/ppermute | solution.py:93
  43.9 3.3 %collective-permute-start.11 = (bf16[32,4096]{1,0:T(8,128)(2,1)S(1)}, bf16[32,4096]{1,0:T(8,128)(2,1)S(1)}, u32[]{:S(2)}, u32[]{:S(2)}) collective-permute-start(bf16[32,4096]{1,0:T(8,128)(2,1)S(1)} %get-tuple-element.28), channel_id=1, source_target_pairs={{0,1},{1,0},{2,3},{3,2},{4,5},{5,4},{6,7},{7,6},{8,9},{9,8},{10,11... | collective-permute-start | bytes 786440 | tf_op jit(solution)/shard_map/ppermute | solution.py:93
  49.1 16.4 %copy-start.5 = (bf16[2,64,1024]{2,1,0:T(8,128)(2,1)S(1)}, bf16[2,64,1024]{2,1,0:T(8,128)(2,1)}, u32[]{:S(2)}) copy-start(bf16[2,64,1024]{2,1,0:T(8,128)(2,1)} %param.12) | copy-start | bytes 786436
  49.1 5.7 %collective-permute-start.16 = (f32[256,64]{0,1:T(8,128)S(1)}, f32[256,64]{0,1:T(8,128)S(1)}, u32[]{:S(2)}, u32[]{:S(2)}) collective-permute-start(f32[256,64]{0,1:T(8,128)S(1)} %fusion.23), channel_id=1, source_target_pairs={{0,2},{2,0},{1,3},{3,1},{4,6},{6,4},{5,7},{7,5},{8,10},{10,8},{9,1... | collective-permute-start | bytes 196616 | tf_op jit(solution)/shard_map/ppermute | solution.py:130
  51.8 13.7 %collective-permute-start.15 = (bf16[256,1024]{1,0:T(8,128)(2,1)}, bf16[256,1024]{1,0:T(8,128)(2,1)}, u32[]{:S(2)}, u32[]{:S(2)}) collective-permute-start(bf16[256,1024]{1,0:T(8,128)(2,1)} %fusion), channel_id=1, source_target_pairs={{0,2},{4,6},{10,8},{14,12},{1,3},{5,7},{11,9},{15,13},{16,18},{20,... | collective-permute-start | bytes 1572872 | tf_op jit(solution)/shard_map/ppermute | solution.py:123
  54.9 4.3 %collective-permute-start.17 = (f32[256,64]{0,1:T(8,128)S(1)}, f32[256,64]{0,1:T(8,128)S(1)}, u32[]{:S(2)}, u32[]{:S(2)}) collective-permute-start(f32[256,64]{0,1:T(8,128)S(1)} %add_select_fusion), channel_id=1, source_target_pairs={{0,4},{4,0},{8,12},{12,8},{1,5},{5,1},{9,13},{13,9},{2,6},{6,2},{1... | collective-permute-start | bytes 196616 | tf_op jit(solution)/shard_map/ppermute | solution.py:133
  59.2 5.4 %collective-permute-start.18 = (f32[256,64]{0,1:T(8,128)S(1)}, f32[256,64]{0,1:T(8,128)S(1)}, u32[]{:S(2)}, u32[]{:S(2)}) collective-permute-start(f32[256,64]{0,1:T(8,128)S(1)} %add.36), channel_id=1, source_target_pairs={{0,8},{8,0},{4,12},{12,4},{1,9},{9,1},{5,13},{13,5},{2,10},{10,2},... | collective-permute-start | bytes 196616 | tf_op jit(solution)/shard_map/ppermute | solution.py:134

commit v2 on v1

v2 whole, which is shorter than its diff:
```python
import jax
import jax.numpy as jnp
from jax import lax
from jax.experimental import pallas as pl
from jax.experimental.pallas import tpu as pltpu
from jax.sharding import PartitionSpec as P

F32 = jnp.float32
BF16 = jnp.bfloat16


def low_rank_weights(low, slot, live, slots, rank_width):
    kept = jnp.arange(rank_width, dtype=jnp.int32)[None, :] < live[:, None]
    scaling = rank_width / live.astype(F32)
    scaled = jnp.where(kept, low * scaling[:, None], jnp.zeros((), F32)).astype(BF16)
    hot = slot[:, None] == jnp.arange(slots, dtype=jnp.int32)[None, :]
    spread = jnp.where(hot[:, :, None], scaled[:, None, :], jnp.zeros((), BF16))
    return spread.reshape(low.shape[0], slots * rank_width)


def tables(tenant, entry, live):
    ids = jnp.arange(entry.shape[0], dtype=jnp.int32)
    hot = (tenant[:, None] == ids[None, :]).astype(jnp.int32)
    return jnp.sum(hot * entry[None, :], axis=1), jnp.sum(hot * live[None, :], axis=1)


def general(rows, residual, weight, down, up, tenant, entry, live):
    own = residual.shape[0]
    cols = weight.shape[1]
    width = down.shape[1]
    slots = entry.shape[0]
    slot_all, live_all = tables(tenant, entry, live)
    part = rows.shape[0] // lax.axis_size("sub")
    mine = lax.dynamic_slice_in_dim(rows, lax.axis_index("sub") * part, part, 0)
    halves = lax.all_gather(lax.all_gather(mine, "blk", axis=0), "sub", axis=1)
    full = halves.reshape(-1, rows.shape[1])
    base = jnp.dot(full, weight, preferred_element_type=F32)
    low = lax.dot_general(
        full, down.reshape(-1, down.shape[2]), (((1,), (1,)), ((), ())), preferred_element_type=F32
    )
    held = down.shape[0]
    places = lax.axis_index("blk") * held + jnp.arange(held, dtype=jnp.int32)
    here = slot_all[:, None] == places[None, :]
    low = jnp.sum(
        jnp.where(here[:, :, None], low.reshape(-1, held, width), jnp.zeros((), F32)), axis=1
    )
    low = lax.psum(lax.psum_scatter(low, "split", scatter_dimension=0, tiled=True), "blk")
    base = lax.psum_scatter(base, "split", scatter_dimension=0, tiled=True)
    start = lax.axis_index("split") * own
    spread = low_rank_weights(
        low,
        lax.dynamic_slice_in_dim(slot_all, start, own, 0),
        lax.dynamic_slice_in_dim(live_all, start, own, 0),
        slots,
        width,
    )
    ups = lax.all_gather(up, "split", axis=0, tiled=True).reshape(slots * width, cols)
    lora = jnp.dot(spread, ups, preferred_element_type=F32)
    return (residual.astype(F32) + base + lora).astype(BF16)


def place_kernel(index_ref, sums_ref, got_ref, *refs):
    refs[-1][...] = (sums_ref[...] + got_ref[...].astype(F32)).astype(refs[-1].dtype)


def place(index, sums, got, step, rows, held=None):
    cols = sums.shape[1]
    piece = pl.BlockSpec((step, cols), lambda i, index: (i, 0))
    operands, in_specs, aliases = [index, sums, got], [piece, piece], {}
    if held is not None:
        operands.append(held)
        in_specs.append(pl.BlockSpec(memory_space=pl.ANY))
        aliases = {3: 0}
    return pl.pallas_call(
        place_kernel,
        out_shape=jax.ShapeDtypeStruct((rows, cols), BF16),
        grid_spec=pltpu.PrefetchScalarGridSpec(
            num_scalar_prefetch=1,
            grid=(sums.shape[0] // step,),
            in_specs=in_specs,
            out_specs=pl.BlockSpec((step, cols), lambda i, index: (index[i], 0)),
        ),
        input_output_aliases=aliases,
    )(*operands)


SWAP = [(0, 1), (1, 0)]
NEIGHBOURS = [(0, 1), (1, 0), (2, 3), (3, 2)]
MIDDLE = [(0, 0), (1, 2), (2, 1), (3, 3)]
ONWARD = [(0, 2), (3, 1), (1, 0), (2, 3)]
INWARD = [(0, 1), (3, 2)]


def line(rows, residual, weight, down, up, tenant, entry, live):
    z, x, c = lax.axis_index("blk"), lax.axis_index("split"), lax.axis_index("sub")
    block_rows, width = rows.shape[0], down.shape[1]
    own, cols = residual.shape
    slots = entry.shape[0]
    slot_all, live_all = tables(tenant, entry, live)
    end = (z == 0) | (z == 3)
    home = (z // 2) == x
    pieces = 2
    step = block_rows // pieces
    half = step // 2

    b, near, third, fourth = [], [], [], []
    mine = [
        lax.dynamic_slice_in_dim(rows, p * step + c * half, half, 0) for p in range(pieces)
    ]
    for piece in mine:
        a = lax.ppermute(piece, "blk", NEIGHBOURS)
        b = lax.ppermute(piece, "blk", MIDDLE)
        e = lax.ppermute(b, "blk", ONWARD)
        f = lax.ppermute(e, "blk", NEIGHBOURS)
        near.append(a)
        third.append(jnp.where(end, e, b))
        fourth.append(jnp.where(end, f, e))

    def both(piece):
        other = lax.ppermute(piece, "sub", SWAP)
        return jnp.where(c == 0, jnp.concatenate([piece, other]), jnp.concatenate([other, piece]))

    near, third, fourth = ([both(piece) for piece in part] for part in (near, third, fourth))
    near, third = jnp.concatenate(near), jnp.concatenate(third)

    down_map = down[0]
    maps = jnp.concatenate([down_map, lax.ppermute(down_map, "blk", INWARD)])
    first_id = jnp.where(end, -1, z)
    second_id = jnp.where(end, -1, jnp.where(z == 1, 0, 3))

    def low_rank(block, place):
        slot = lax.dynamic_slice_in_dim(slot_all, place, block.shape[0], 0)[:, None]
        low = lax.dot_general(block, maps, (((1,), (1,)), ((), ())), preferred_element_type=F32)
        zero = jnp.zeros((), F32)
        return jnp.where(slot == first_id, low[:, :width], zero) + jnp.where(
            slot == second_id, low[:, width:], zero
        )

    near_id = z + 1 - 2 * (z % 2)
    third_id = jnp.where(z < 2, 2, 1)
    fourth_id = jnp.where(z < 2, 3, 0)
    low_near = jnp.concatenate(
        [low_rank(rows, z * block_rows), low_rank(near, near_id * block_rows)]
    )
    low_far = jnp.concatenate(
        [low_rank(third, third_id * block_rows)]
        + [low_rank(fourth[p], fourth_id * block_rows + p * step) for p in range(pieces)]
    )
    low = jnp.where(home, low_near, low_far) + lax.ppermute(
        jnp.where(home, low_far, low_near), "split", SWAP
    )
    low = low + lax.ppermute(low, "blk", MIDDLE)
    low = jnp.where(x == 0, jnp.concatenate([low[block_rows:], low[:block_rows]]), low)
    start = x * own
    slot = lax.dynamic_slice_in_dim(slot_all, start, own, 0)
    rank = lax.dynamic_slice_in_dim(live_all, start, own, 0)
    kept = jnp.arange(width, dtype=jnp.int32)[None, :] < rank[:, None]
    scaling = width / rank.astype(F32)
    scaled = jnp.where(kept, low * scaling[:, None], jnp.zeros((), F32)).astype(BF16)
    scaled = jnp.where(end, lax.ppermute(scaled, "blk", NEIGHBOURS), scaled)
    hot = slot[:, None] == jnp.arange(slots, dtype=jnp.int32)[None, :]
    spread = jnp.where(hot[:, :, None], scaled[:, None, :], jnp.zeros((), BF16))
    spread = spread.reshape(own, slots * width)
    up_other = lax.ppermute(up, "split", SWAP)
    ups = jnp.where(x == 0, jnp.concatenate([up, up_other]), jnp.concatenate([up_other, up]))
    lora = jnp.dot(spread, ups.reshape(slots * width, cols), preferred_element_type=F32)
    rest = residual.astype(F32) + lora

    def product(block):
        return jnp.dot(block, weight, preferred_element_type=F32)

    def exchange(near_sum, far_sum):
        got = lax.ppermute(jnp.where(home, far_sum, near_sum).astype(BF16), "split", SWAP)
        return jnp.where(home, near_sum, far_sum), got

    near_sum = product(near)
    first, first_got = exchange(product(rows), product(third))
    first_place = jnp.where(home, z % 2, z // 2)
    out = None
    kept_sums, gots, places = [first], [first_got], []
    for p in range(pieces):
        kept_sum, got = exchange(near_sum[p * step : (p + 1) * step], product(fourth[p]))
        kept_sums.append(kept_sum)
        gots.append(got)
    places = [first_place * pieces + p for p in range(pieces)] + [
        (1 - first_place) * pieces + p for p in range(pieces)
    ]

    def total(kept_sum, at):
        return kept_sum + lax.dynamic_slice_in_dim(rest, at * step, kept_sum.shape[0], 0)

    early = jnp.concatenate(
        [total(first, first_place * pieces)]
        + [total(kept_sums[p], places[pieces + p - 1]) for p in range(1, pieces)]
    )
    out = place(
        jnp.stack(places[:-1]).astype(jnp.int32),
        early,
        jnp.concatenate(gots[:-1]),
        step,
        own,
    )
    return place(
        jnp.stack(places[-1:]).astype(jnp.int32),
        total(kept_sums[-1], places[-1]),
        gots[-1],
        step,
        own,
        out,
    )


def shards(rows, residual, weight, down, up, tenant, entry, live):
    sizes = [lax.axis_size(name) for name in ("blk", "split", "sub")]
    plan = line if sizes == [4, 2, 2] and down.shape[0] == 1 else general
    return plan(rows, residual, weight, down, up, tenant, entry, live)


def solution(mesh):
    in_specs = (
        P(("groups", "blk"), "split"),
        P(("groups", "split"), ("blk", "sub")),
        P("split", ("blk", "sub")),
        P("blk", None, "split"),
        P("split", None, ("blk", "sub")),
        P("groups"),
        P(),
        P(),
    )
    out_specs = P(("groups", "split"), ("blk", "sub"))
    return jax.shard_map(shards, mesh=mesh, in_specs=in_specs, out_specs=out_specs, check_vma=False)
```

time: 68.5 us -> 93.4 us (1.36)
  starting transfers between devices: 23.7 us -> 35.4 us
  waiting for transfers between devices: 23.1 us -> 30 us
  Pallas kernels: 0 us -> 5.14 us
  other arithmetic: 3.01 us -> 4.18 us
    ppermute x20 -> x22, starting transfers between devices: 23.7 us -> 35.4 us  [the longest x2 7.67 us: line(): a = lax.ppermute(piece, 'blk', NEIGHBOURS)]
    ppermute x20 -> x22, waiting for transfers between devices: 23.1 us -> 30 us  [the longest x2 18.1 us: line(): e = lax.ppermute(b, 'blk', ONWARD)]
    pallas_call x0 -> x2, Pallas kernels: none -> 5.14 us  [place(): pl.pallas_call(place_kernel, out_shape=jax.ShapeDtypeStruct((rows, cols),...]
    concatenate x0 -> x2, other arithmetic: none -> 1.73 us  [the longest x1 0.94 us: line(): jnp.concatenate([total(first, first_place * pieces)] + [total(kept_sums[p...]
    slice x7 -> x1, local copies, waits for them, and re-layouts: 1.4 us -> 0.01 us  [line(): low[block_rows:]]
    dynamic_slice x0 -> x2, local copies, waits for them, and re-layouts: none -> 1.23 us  [the longest x1 1.15 us: line(): lax.dynamic_slice_in_dim(rows, p * step + c * half, half, 0)]
    select_n x6 -> x4, other arithmetic: 1.58 us -> 0.35 us  [both(): jnp.where(c == 0, jnp.concatenate([piece, other]), jnp.concatenate([other...]
    dot_general x9 -> x11, matrix products: 16.5 us -> 15.9 us  [the longest x5 7.88 us: low_rank(): lax.dot_general(block, maps, (((1,), (1,)), ((), ())), preferred_element_...]
  transfers between devices with their start and end apart: 20 -> 22, of which waited for: 9 -> 7; matrix products, arithmetic and copies ran while one was open for 25% -> 20% of each run, Pallas kernels for 0% -> 4%
where the time goes in v2:
time: 93.4 us; the launch traced here: 93 us
  starting transfers between devices  35.4 us (38%)
  waiting for transfers between devices  30 us (32%)
  matrix products  15.9 us (17%)
  Pallas kernels  5.14 us (6%)
  other arithmetic  4.18 us (4%)
  local copies, waits for them, and re-layouts  1.91 us (2%)
    ppermute x2, waiting for transfers between devices, line(): e = lax.ppermute(b, 'blk', ONWARD)  18.1 us
    dot_general x5, matrix products, low_rank(): lax.dot_general(block, maps, (((1,), (1,)), ((), ())), preferred_element_...  7.88 us
    dot_general x5, matrix products, product(): return jnp.dot(block, weight, preferred_element_type=F32)  7.72 us
    ppermute x2, starting transfers between devices, line(): a = lax.ppermute(piece, 'blk', NEIGHBOURS)  7.67 us
    ppermute x2, waiting for transfers between devices, line(): f = lax.ppermute(e, 'blk', NEIGHBOURS)  6.86 us
    ppermute x2, starting transfers between devices, line(): e = lax.ppermute(b, 'blk', ONWARD)  6.51 us
    ppermute x1, starting transfers between devices, line(): scaled = jnp.where(end, lax.ppermute(scaled, 'blk', NEIGHBOURS), scaled)  5.99 us
    pallas_call x2, Pallas kernels, place(): pl.pallas_call(place_kernel, out_shape=jax.ShapeDtypeStruct((rows, cols),...  5.14 us
  transfers between devices with their start and end apart: 22, of which 7 were waited for; matrix products, arithmetic and copies ran while one was open for 20% of the time, Pallas kernels for 4%

profile of v2, /device:TPU:0, one launch (start us, length us, event | category | flops | bytes accessed | tf_op | source)
XLA Modules:
  0.0 93.0 jit_solution(13359333140252367329)
XLA Ops:
  0.0 1.2 %constant_dynamic-slice_fusion.1 = (bf16[32,4096]{1,0:T(8,128)(2,1)S(1)}, bf16[32,4096]{1,0:T(8,128)(2,1)S(1)}) fusion(bf16[128,4096]{1,0:T(8,128)(2,1)} %param.8, s32[]{:T(128)S(6)} %select_n.228, s32[]{:T(128)S(6)} %select_n.230), kind=kLoop, calls=%fused_computation.73 | loop fusion | bytes 1048584 | tf_op jit(solution)/shard_map/dynamic_slice | solution.py:108
  1.2 0.7 collective-permute-start.9
  1.8 5.9 %collective-permute-start = (bf16[32,4096]{1,0:T(8,128)(2,1)S(1)}, bf16[32,4096]{1,0:T(8,128)(2,1)S(1)}, u32[]{:S(2)}, u32[]{:S(2)}) collective-permute-start(bf16[32,4096]{1,0:T(8,128)(2,1)S(1)} %get-tuple-element.11), channel_id=1, source_target_pairs={{0,4},{4,0},{8,12},{12,8},{1,5},{5,1},{9,13},{13,9},{2,6},{6,2},{1... | collective-permute-start | bytes 786440 | tf_op jit(solution)/shard_map/ppermute | solution.py:111
  7.7 0.7 collective-permute-start.4
  8.4 1.8 %collective-permute-start.2 = (bf16[32,4096]{1,0:T(8,128)(2,1)S(1)}, bf16[32,4096]{1,0:T(8,128)(2,1)S(1)}, u32[]{:S(2)}, u32[]{:S(2)}) collective-permute-start(bf16[32,4096]{1,0:T(8,128)(2,1)S(1)} %get-tuple-element.12), channel_id=1, source_target_pairs={{0,4},{4,0},{8,12},{12,8},{1,5},{5,1},{9,13},{13,9},{2,6},{6,2},{1... | collective-permute-start | bytes 786440 | tf_op jit(solution)/shard_map/ppermute | solution.py:111
  10.2 3.0 %collective-permute-start.8 = (bf16[64,4096]{1,0:T(8,128)(2,1)}, bf16[64,4096]{1,0:T(8,128)(2,1)}, u32[]{:S(2)}, u32[]{:S(2)}) collective-permute-start(bf16[64,4096]{1,0:T(8,128)(2,1)} %bitcast.20), channel_id=1, source_target_pairs={{0,4},{12,8},{1,5},{13,9},{2,6},{14,10},{3,7},{15,11},{16,20},{28,... | collective-permute-start | bytes 1572872 | tf_op jit(solution)/shard_map/ppermute | solution.py:127
  13.2 0.8 select_reduce_fusion
  14.0 0.1 convert_divide_fusion
  14.2 2.0 %collective-permute-start.10 = (bf16[32,4096]{1,0:T(8,128)(2,1)S(1)}, bf16[32,4096]{1,0:T(8,128)(2,1)S(1)}, u32[]{:S(2)}, u32[]{:S(2)}) collective-permute-start(bf16[32,4096]{1,0:T(8,128)(2,1)S(1)} %collective-permute-done.9), channel_id=1, source_target_pairs={{0,8},{12,4},{4,0},{8,12},{1,9},{13,5},{5,1},{9,13},{2,10},{14,6},... | collective-permute-start | bytes 786440 | tf_op jit(solution)/shard_map/ppermute | solution.py:113
  16.3 4.5 %collective-permute-start.5 = (bf16[32,4096]{1,0:T(8,128)(2,1)S(1)}, bf16[32,4096]{1,0:T(8,128)(2,1)S(1)}, u32[]{:S(2)}, u32[]{:S(2)}) collective-permute-start(bf16[32,4096]{1,0:T(8,128)(2,1)S(1)} %collective-permute-done.4), channel_id=1, source_target_pairs={{0,8},{12,4},{4,0},{8,12},{1,9},{13,5},{5,1},{9,13},{2,10},{14,6},... | collective-permute-start | bytes 786440 | tf_op jit(solution)/shard_map/ppermute | solution.py:113
  20.8 0.6 pad_add_fusion.index_ref
  21.4 1.6 %collective-permute-start.18 = (bf16[2,64,1024]{2,1,0:T(8,128)(2,1)}, bf16[2,64,1024]{2,1,0:T(8,128)(2,1)S(1)}, u32[]{:S(2)}, u32[]{:S(2)}) collective-permute-start(bf16[2,64,1024]{2,1,0:T(8,128)(2,1)} %param.12), channel_id=1, source_target_pairs={{0,2},{2,0},{1,3},{3,1},{4,6},{6,4},{5,7},{7,5},{8,10},{10,8},{9,1... | collective-permute-start | bytes 786440 | tf_op jit(solution)/shard_map/ppermute | solution.py:164
  23.0 14.0 %collective-permute-done.10 = bf16[32,4096]{1,0:T(8,128)(2,1)S(1)} collective-permute-done((bf16[32,4096]{1,0:T(8,128)(2,1)S(1)}, bf16[32,4096]{1,0:T(8,128)(2,1)S(1)}, u32[]{:S(2)}, u32[]{:S(2)}) %collective-permute-start.10) | collective-permute-done | bytes 262176 | tf_op jit(solution)/shard_map/ppermute | solution.py:113
  37.0 4.1 %collective-permute-done.5 = bf16[32,4096]{1,0:T(8,128)(2,1)S(1)} collective-permute-done((bf16[32,4096]{1,0:T(8,128)(2,1)S(1)}, bf16[32,4096]{1,0:T(8,128)(2,1)S(1)}, u32[]{:S(2)}, u32[]{:S(2)}) %collective-permute-start.5) | collective-permute-done | bytes 262176 | tf_op jit(solution)/shard_map/ppermute | solution.py:113
  41.1 2.4 %collective-permute-start.13 = (bf16[32,4096]{1,0:T(8,128)(2,1)S(1)}, bf16[32,4096]{1,0:T(8,128)(2,1)S(1)}, u32[]{:S(2)}, u32[]{:S(2)}) collective-permute-start(bf16[32,4096]{1,0:T(8,128)(2,1)S(1)} %collective-permute-done.10), channel_id=1, source_target_pairs={{0,4},{4,0},{8,12},{12,8},{1,5},{5,1},{9,13},{13,9},{2,6},{6,2},{1... | collective-permute-start | bytes 786440 | tf_op jit(solution)/shard_map/ppermute | solution.py:114
  43.5 0.1 maximum_select_fusion
  43.6 0.1 maximum_select_fusion.1
  43.7 1.5 %convolution_bitcast_fusion.1 = f32[128,128]{0,1:T(8,128)S(1)} fusion(bf16[128,4096]{1,0:T(8,128)(2,1)S(1)} %copy-done, bf16[64,4096]{1,0:T(8,128)(2,1)} %collective-permute-done.8, bf16[64,4096]{1,0:T(8,128)(2,1)S(1)} %bitcast.21), kind=kOutput, calls=%fused_computation.2 | convolution fusion | flops 136314880 | bytes 2162688 | tf_op jit(solution)/shard_map/dot_general | solution.py:133
  45.2 1.5 %fusion.3 = f32[128,128]{0,1:T(8,128)S(1)} fusion(bf16[64,4096]{1,0:T(8,128)(2,1)S(1)} %maximum_select_fusion.1, bf16[64,4096]{1,0:T(8,128)(2,1)S(1)} %maximum_select_fusion, bf16[64,4096]{1,0:T(8,128)(2,1)} %collective-permute-done.8, bf16[64,4096]{1,0:T(8,128)(2,1)S(1)} %bitcast.22), kind=kOutput, calls=%fused_computation.9 | convolution fusion | flops 138412032 | bytes 2162688 | tf_op jit(solution)/shard_map/dot_general | solution.py:133
  46.7 4.0 %collective-permute-done.13 = bf16[32,4096]{1,0:T(8,128)(2,1)S(1)} collective-permute-done((bf16[32,4096]{1,0:T(8,128)(2,1)S(1)}, bf16[32,4096]{1,0:T(8,128)(2,1)S(1)}, u32[]{:S(2)}, u32[]{:S(2)}) %collective-permute-start.13) | collective-permute-done | bytes 262176 | tf_op jit(solution)/shard_map/ppermute | solution.py:114
  50.8 0.5 collective-permute-start.11
  51.3 2.9 %collective-permute-done.6 = bf16[32,4096]{1,0:T(8,128)(2,1)S(1)} collective-permute-done((bf16[32,4096]{1,0:T(8,128)(2,1)S(1)}, bf16[32,4096]{1,0:T(8,128)(2,1)S(1)}, u32[]{:S(2)}, u32[]{:S(2)}) %collective-permute-start.6) | collective-permute-done | bytes 262176 | tf_op jit(solution)/shard_map/ppermute | solution.py:114
  54.3 0.5 collective-permute-start.7
  54.8 0.1 maximum_select_fusion.3
  54.9 1.8 %fusion.14 = f32[64,128]{0,1:T(8,128)S(1)} fusion(bf16[32,4096]{1,0:T(8,128)(2,1)S(1)} %collective-permute-done.14, bf16[32,4096]{1,0:T(8,128)(2,1)S(1)} %get-tuple-element.16, pred[]{:T(512)S(6)} %eq.116, bf16[64,4096]{1,0:T(8,128)(2,1)} %collective-permute-done.8, bf16[64,4096]{1,0:T(8,128)(2,1)S(1)} %bitcast.23), kind=kOutput, calls=%fused_computation.38 | convolution fusion | flops 71565312 | bytes 1605633 | tf_op jit(solution)/shard_map/dot_general | solution.py:133
  56.8 1.6 %fusion.15 = f32[64,128]{0,1:T(8,128)S(1)} fusion(bf16[32,4096]{1,0:T(8,128)(2,1)S(1)} %collective-permute-done.7, bf16[32,4096]{1,0:T(8,128)(2,1)S(1)} %get-tuple-element.18, pred[]{:T(512)S(6)} %eq.116, bf16[64,4096]{1,0:T(8,128)(2,1)} %collective-permute-done.8, bf16[64,4096]{1,0:T(8,128)(2,1)S(1)} %bitcast.24), kind=kOutput, calls=%fused_computation.39 | convolution fusion | flops 71565312 | bytes 1605633 | tf_op jit(solution)/shard_map/dot_general | solution.py:133
  58.5 0.1 maximum_select_fusion.4
  58.6 1.5 %fusion.2 = f32[128,128]{0,1:T(8,128)S(1)} fusion(bf16[64,4096]{1,0:T(8,128)(2,1)S(1)} %maximum_select_fusion.4, bf16[64,4096]{1,0:T(8,128)(2,1)S(1)} %maximum_select_fusion.3, bf16[64,4096]{1,0:T(8,128)(2,1)} %collective-permute-done.8, bf16[64,4096]{1,0:T(8,128)(2,1)S(1)} %bitcast.25), kind=kOutput, calls=%fused_computation.8 | convolution fusion | flops 138412032 | bytes 2162688 | tf_op jit(solution)/shard_map/dot_general | solution.py:133
  60.2 1.5 %collective-permute-start.15 = (f32[256,64]{0,1:T(8,128)S(1)}, f32[256,64]{0,1:T(8,128)S(1)}, u32[]{:S(2)}, u32[]{:S(2)}) collective-permute-start(f32[256,64]{0,1:T(8,128)S(1)} %fusion.22), channel_id=1, source_target_pairs={{0,2},{2,0},{1,3},{3,1},{4,6},{6,4},{5,7},{7,5},{8,10},{10,8},{9,1... | collective-permute-start | bytes 196616 | tf_op jit(solution)/shard_map/ppermute | solution.py:149
  61.7 1.3 %fusion.4 = f32[128,1024]{1,0:T(8,128)S(1)} fusion(bf16[4096,1024]{1,0:T(8,128)(2,1)S(1)} %bitcast.19, bf16[64,4096]{1,0:T(8,128)(2,1)S(1)} %maximum_select_fusion.1, bf16[64,4096]{1,0:T(8,128)(2,1)S(1)} %maximum_select_fusion), kind=kOutput, calls=%fused_computation.10 | convolution fusion | flops 1075838976 | bytes 9961472 | tf_op jit(solution)/shard_map/dot_general | solution.py:170
  63.0 1.5 %collective-permute-done.15 = f32[256,64]{0,1:T(8,128)S(1)} collective-permute-done((f32[256,64]{0,1:T(8,128)S(1)}, f32[256,64]{0,1:T(8,128)S(1)}, u32[]{:S(2)}, u32[]{:S(2)}) %collective-permute-start.15) | collective-permute-done | bytes 65568 | tf_op jit(solution)/shard_map/ppermute | solution.py:149
  64.5 0.7 collective-permute-start.16
  65.2 1.3 %fusion.1 = f32[128,1024]{1,0:T(8,128)S(1)} fusion(bf16[4096,1024]{1,0:T(8,128)(2,1)S(1)} %bitcast.19, bf16[64,4096]{1,0:T(8,128)(2,1)S(1)} %maximum_select_fusion.4, bf16[64,4096]{1,0:T(8,128)(2,1)S(1)} %maximum_select_fusion.3), kind=kOutput, calls=%fused_computation.7 | convolution fusion | flops 1075838976 | bytes 9961472 | tf_op jit(solution)/shard_map/dot_general | solution.py:170
  66.6 6.0 %collective-permute-start.17 = (bf16[256,64]{0,1:T(8,128)(2,1)S(1)}, bf16[256,64]{0,1:T(8,128)(2,1)S(1)}, u32[]{:S(2)}, u32[]{:S(2)}) collective-permute-start(bf16[256,64]{0,1:T(8,128)(2,1)S(1)} %fusion.19), channel_id=1, source_target_pairs={{0,4},{4,0},{8,12},{12,8},{1,5},{5,1},{9,13},{13,9},{2,6},{6,2},{1... | collective-permute-start | bytes 98312 | tf_op jit(solution)/shard_map/ppermute | solution.py:160
  72.6 1.6 %fusion.16 = f32[64,1024]{1,0:T(8,128)S(1)} fusion(bf16[4096,1024]{1,0:T(8,128)(2,1)S(1)} %bitcast.19, bf16[32,4096]{1,0:T(8,128)(2,1)S(1)} %collective-permute-done.7, bf16[32,4096]{1,0:T(8,128)(2,1)S(1)} %get-tuple-element.18, pred[]{:T(512)S(6)} %eq.116), kind=kOutput, calls=%fused_computation.40 | convolution fusion | flops 539230208 | bytes 9175041 | tf_op jit(solution)/shard_map/dot_general | solution.py:170
  74.2 0.3 collective-permute-done.17
  74.5 0.3 fusion
  74.8 1.4 %dynamic-slice_add_fusion = (f32[128,1024]{1,0:T(8,128)S(1)}, bf16[128,1024]{1,0:T(8,128)(2,1)S(1)}) fusion(f32[256,1024]{1,0:T(8,128)S(1)} %fusion, s32[]{:T(128)S(6)} %select_n.278, f32[128,1024]{1,0:T(8,128)S(1)} %fusion.1, pred[]{:T(512)S(6)} %eq.115, bf16[128,4096]{1,0:T(8,128)(2,1)S(1)} %copy-done, bf16[4096,1024]{1,0:T(8,128)(2,1)S(1)} %bitcast.19), kind=kOutput, calls=%fused_computation.24 | convolution fusion | flops 1074135040 | bytes 11272197 | tf_op jit(solution)/shard_map/dot_general | solution.py:170
  76.3 1.6 %collective-permute-start.20 = (bf16[128,1024]{1,0:T(8,128)(2,1)S(1)}, bf16[128,1024]{1,0:T(8,128)(2,1)S(1)}, u32[]{:S(2)}, u32[]{:S(2)}) collective-permute-start(bf16[128,1024]{1,0:T(8,128)(2,1)S(1)} %select_convert_fusion), channel_id=1, source_target_pairs={{0,2},{2,0},{1,3},{3,1},{4,6},{6,4},{5,7},{7,5},{8,10},{10,8},{9,1... | collective-permute-start | bytes 786440 | tf_op jit(solution)/shard_map/ppermute | solution.py:173
  77.9 2.2 %dynamic-slice_add_fusion.1 = (f32[64,1024]{1,0:T(8,128)S(1)}, f32[64,1024]{1,0:T(8,128)}, bf16[64,1024]{1,0:T(8,128)(2,1)S(1)}) fusion(f32[256,1024]{1,0:T(8,128)S(1)} %fusion, s32[]{:T(128)S(6)} %select_n.280, f32[128,1024]{1,0:T(8,128)S(1)} %fusion.4, pred[]{:T(512)S(6)} %eq.115, s32[]{:T(128)S(6)} %select_n.274, f32[64,1024]{1,0:T(8,128)S(1)} %fusion.16, ...), kind=kOutput, calls=%fused_computation.28 | convolution fusion | flops 539557888 | bytes 10878986 | tf_op jit(solution)/shard_map/dot_general | solution.py:170
  80.1 0.6 collective-permute-start.21
  80.7 1.5 %collective-permute-start.19 = (bf16[64,1024]{1,0:T(8,128)(2,1)S(1)}, bf16[64,1024]{1,0:T(8,128)(2,1)S(1)}, u32[]{:S(2)}, u32[]{:S(2)}) collective-permute-start(bf16[64,1024]{1,0:T(8,128)(2,1)S(1)} %get-tuple-element.14), channel_id=1, source_target_pairs={{0,2},{2,0},{1,3},{3,1},{4,6},{6,4},{5,7},{7,5},{8,10},{10,8},{9,1... | collective-permute-start | bytes 393224 | tf_op jit(solution)/shard_map/ppermute | solution.py:173
  82.2 0.9 %pad_maximum_fusion.3.sums_ref = f32[192,1024]{1,0:T(8,128)} fusion(f32[64,1024]{1,0:T(8,128)S(1)} %get-tuple-element.9, f32[128,1024]{1,0:T(8,128)S(1)} %get-tuple-element.32), kind=kLoop, calls=%fused_computation.6 | loop fusion | flops 196608 | bytes 1572864 | tf_op jit(solution)/shard_map/concatenate | solution.py:192
  83.2 3.2 %collective-permute-done.21 = bf16[64,1024]{1,0:T(8,128)(2,1)S(1)} collective-permute-done((bf16[64,1024]{1,0:T(8,128)(2,1)S(1)}, bf16[64,1024]{1,0:T(8,128)(2,1)S(1)}, u32[]{:S(2)}, u32[]{:S(2)}) %collective-permute-start.21) | collective-permute-done | bytes 131104 | tf_op jit(solution)/shard_map/ppermute | solution.py:173
  86.4 0.8 pad_maximum_fusion.8.got_ref
  87.2 3.5 %shard_map.82.refs_0_ = bf16[256,1024]{1,0:T(8,128)(2,1)} custom-call(s32[3]{0:T(128)} %pad_add_fusion.index_ref, f32[192,1024]{1,0:T(8,128)} %pad_maximum_fusion.3.sums_ref, bf16[192,1024]{1,0:T(8,128)(2,1)} %pad_maximum_fusion.8.got_ref), custom_call_target="tpu_custom_call" | custom-call | tf_op jit(solution)/shard_map/pallas_call | solution.py:74
  90.7 0.6 copy-done.1
  91.3 1.7 %shard_map.83 = bf16[256,1024]{1,0:T(8,128)(2,1)} custom-call(s32[1]{0:T(128)} %bitcast.index_ref, f32[64,1024]{1,0:T(8,128)} %get-tuple-element.10.sums_ref, bf16[64,1024]{1,0:T(8,128)(2,1)} %copy-done.1, bf16[256,1024]{1,0:T(8,128)(2,1)} %shard_map.82.refs_0_), custom_call_target="tpu_custom_call", output_to_operand_aliasing={{}: (3, {})} | custom-call | tf_op jit(solution)/shard_map/pallas_call | solution.py:74
  (52 shorter events, 1.0 us)
Async XLA Ops:
  0.0 43.7 %copy-start = (bf16[128,4096]{1,0:T(8,128)(2,1)S(1)}, bf16[128,4096]{1,0:T(8,128)(2,1)}, u32[]{:S(2)}) copy-start(bf16[128,4096]{1,0:T(8,128)(2,1)} %param.8) | copy-start | bytes 3145732
  1.2 13.1 %collective-permute-start.9 = (bf16[32,4096]{1,0:T(8,128)(2,1)S(1)}, bf16[32,4096]{1,0:T(8,128)(2,1)S(1)}, u32[]{:S(2)}, u32[]{:S(2)}) collective-permute-start(bf16[32,4096]{1,0:T(8,128)(2,1)S(1)} %get-tuple-element.11), channel_id=1, source_target_pairs={{0,0},{4,8},{8,4},{12,12},{1,1},{5,9},{9,5},{13,13},{2,2},{6,10},{... | collective-permute-start | bytes 786440 | tf_op jit(solution)/shard_map/ppermute | solution.py:112
  1.8 18.9 %collective-permute-start = (bf16[32,4096]{1,0:T(8,128)(2,1)S(1)}, bf16[32,4096]{1,0:T(8,128)(2,1)S(1)}, u32[]{:S(2)}, u32[]{:S(2)}) collective-permute-start(bf16[32,4096]{1,0:T(8,128)(2,1)S(1)} %get-tuple-element.11), channel_id=1, source_target_pairs={{0,4},{4,0},{8,12},{12,8},{1,5},{5,1},{9,13},{13,9},{2,6},{6,2},{1... | collective-permute-start | bytes 786440 | tf_op jit(solution)/shard_map/ppermute | solution.py:111
  7.7 8.5 %collective-permute-start.4 = (bf16[32,4096]{1,0:T(8,128)(2,1)S(1)}, bf16[32,4096]{1,0:T(8,128)(2,1)S(1)}, u32[]{:S(2)}, u32[]{:S(2)}) collective-permute-start(bf16[32,4096]{1,0:T(8,128)(2,1)S(1)} %get-tuple-element.12), channel_id=1, source_target_pairs={{0,0},{4,8},{8,4},{12,12},{1,1},{5,9},{9,5},{13,13},{2,2},{6,10},{... | collective-permute-start | bytes 786440 | tf_op jit(solution)/shard_map/ppermute | solution.py:112
  8.4 13.0 %collective-permute-start.2 = (bf16[32,4096]{1,0:T(8,128)(2,1)S(1)}, bf16[32,4096]{1,0:T(8,128)(2,1)S(1)}, u32[]{:S(2)}, u32[]{:S(2)}) collective-permute-start(bf16[32,4096]{1,0:T(8,128)(2,1)S(1)} %get-tuple-element.12), channel_id=1, source_target_pairs={{0,4},{4,0},{8,12},{12,8},{1,5},{5,1},{9,13},{13,9},{2,6},{6,2},{1... | collective-permute-start | bytes 786440 | tf_op jit(solution)/shard_map/ppermute | solution.py:111
  10.2 33.5 %collective-permute-start.8 = (bf16[64,4096]{1,0:T(8,128)(2,1)}, bf16[64,4096]{1,0:T(8,128)(2,1)}, u32[]{:S(2)}, u32[]{:S(2)}) collective-permute-start(bf16[64,4096]{1,0:T(8,128)(2,1)} %bitcast.20), channel_id=1, source_target_pairs={{0,4},{12,8},{1,5},{13,9},{2,6},{14,10},{3,7},{15,11},{16,20},{28,... | collective-permute-start | bytes 1572872 | tf_op jit(solution)/shard_map/ppermute | solution.py:127
  14.2 22.7 %collective-permute-start.10 = (bf16[32,4096]{1,0:T(8,128)(2,1)S(1)}, bf16[32,4096]{1,0:T(8,128)(2,1)S(1)}, u32[]{:S(2)}, u32[]{:S(2)}) collective-permute-start(bf16[32,4096]{1,0:T(8,128)(2,1)S(1)} %collective-permute-done.9), channel_id=1, source_target_pairs={{0,8},{12,4},{4,0},{8,12},{1,9},{13,5},{5,1},{9,13},{2,10},{14,6},... | collective-permute-start | bytes 786440 | tf_op jit(solution)/shard_map/ppermute | solution.py:113
  16.3 24.8 %collective-permute-start.5 = (bf16[32,4096]{1,0:T(8,128)(2,1)S(1)}, bf16[32,4096]{1,0:T(8,128)(2,1)S(1)}, u32[]{:S(2)}, u32[]{:S(2)}) collective-permute-start(bf16[32,4096]{1,0:T(8,128)(2,1)S(1)} %collective-permute-done.4), channel_id=1, source_target_pairs={{0,8},{12,4},{4,0},{8,12},{1,9},{13,5},{5,1},{9,13},{2,10},{14,6},... | collective-permute-start | bytes 786440 | tf_op jit(solution)/shard_map/ppermute | solution.py:113
  20.8 22.7 %collective-permute-start.1 = (bf16[32,4096]{1,0:T(8,128)(2,1)S(1)}, bf16[32,4096]{1,0:T(8,128)(2,1)S(1)}, u32[]{:S(2)}, u32[]{:S(2)}) collective-permute-start(bf16[32,4096]{1,0:T(8,128)(2,1)S(1)} %collective-permute-done), channel_id=1, source_target_pairs={{0,1},{1,0},{2,3},{3,2},{4,5},{5,4},{6,7},{7,6},{8,9},{9,8},{10,11... | collective-permute-start | bytes 786440 | tf_op jit(solution)/shard_map/ppermute | solution.py:120
  21.4 22.3 %copy-start.2 = (bf16[1,64,4096]{2,1,0:T(8,128)(2,1)S(1)}, bf16[1,64,4096]{2,1,0:T(8,128)(2,1)}, u32[]{:S(2)}) copy-start(bf16[1,64,4096]{2,1,0:T(8,128)(2,1)} %param.11) | copy-start | bytes 1572868
  21.4 53.0 %collective-permute-start.18 = (bf16[2,64,1024]{2,1,0:T(8,128)(2,1)}, bf16[2,64,1024]{2,1,0:T(8,128)(2,1)S(1)}, u32[]{:S(2)}, u32[]{:S(2)}) collective-permute-start(bf16[2,64,1024]{2,1,0:T(8,128)(2,1)} %param.12), channel_id=1, source_target_pairs={{0,2},{2,0},{1,3},{3,1},{4,6},{6,4},{5,7},{7,5},{8,10},{10,8},{9,1... | collective-permute-start | bytes 786440 | tf_op jit(solution)/shard_map/ppermute | solution.py:164
  37.0 6.6 %collective-permute-start.3 = (bf16[32,4096]{1,0:T(8,128)(2,1)S(1)}, bf16[32,4096]{1,0:T(8,128)(2,1)S(1)}, u32[]{:S(2)}, u32[]{:S(2)}) collective-permute-start(bf16[32,4096]{1,0:T(8,128)(2,1)S(1)} %collective-permute-done.2), channel_id=1, source_target_pairs={{0,1},{1,0},{2,3},{3,2},{4,5},{5,4},{6,7},{7,6},{8,9},{9,8},{10,11... | collective-permute-start | bytes 786440 | tf_op jit(solution)/shard_map/ppermute | solution.py:120
  41.1 9.6 %collective-permute-start.13 = (bf16[32,4096]{1,0:T(8,128)(2,1)S(1)}, bf16[32,4096]{1,0:T(8,128)(2,1)S(1)}, u32[]{:S(2)}, u32[]{:S(2)}) collective-permute-start(bf16[32,4096]{1,0:T(8,128)(2,1)S(1)} %collective-permute-done.10), channel_id=1, source_target_pairs={{0,4},{4,0},{8,12},{12,8},{1,5},{5,1},{9,13},{13,9},{2,6},{6,2},{1... | collective-permute-start | bytes 786440 | tf_op jit(solution)/shard_map/ppermute | solution.py:114
  43.5 10.7 %collective-permute-start.6 = (bf16[32,4096]{1,0:T(8,128)(2,1)S(1)}, bf16[32,4096]{1,0:T(8,128)(2,1)S(1)}, u32[]{:S(2)}, u32[]{:S(2)}) collective-permute-start(bf16[32,4096]{1,0:T(8,128)(2,1)S(1)} %collective-permute-done.5), channel_id=1, source_target_pairs={{0,4},{4,0},{8,12},{12,8},{1,5},{5,1},{9,13},{13,9},{2,6},{6,2},{1... | collective-permute-start | bytes 786440 | tf_op jit(solution)/shard_map/ppermute | solution.py:114
  50.8 4.2 %collective-permute-start.14 = (bf16[32,4096]{1,0:T(8,128)(2,1)S(1)}, bf16[32,4096]{1,0:T(8,128)(2,1)S(1)}, u32[]{:S(2)}, u32[]{:S(2)}) collective-permute-start(bf16[32,4096]{1,0:T(8,128)(2,1)S(1)} %get-tuple-element.16), channel_id=1, source_target_pairs={{0,1},{1,0},{2,3},{3,2},{4,5},{5,4},{6,7},{7,6},{8,9},{9,8},{10,11... | collective-permute-start | bytes 786440 | tf_op jit(solution)/shard_map/ppermute | solution.py:120
  50.8 4.0 %collective-permute-start.11 = (bf16[32,4096]{1,0:T(8,128)(2,1)S(1)}, bf16[32,4096]{1,0:T(8,128)(2,1)S(1)}, u32[]{:S(2)}, u32[]{:S(2)}) collective-permute-start(bf16[32,4096]{1,0:T(8,128)(2,1)S(1)} %get-tuple-element.15), channel_id=1, source_target_pairs={{0,1},{1,0},{2,3},{3,2},{4,5},{5,4},{6,7},{7,6},{8,9},{9,8},{10,11... | collective-permute-start | bytes 786440 | tf_op jit(solution)/shard_map/ppermute | solution.py:120
  54.2 7.5 %slice-start = ((s8[8388608]{0:T(1024)(128)(4,1)}), s8[4194304]{0:T(1024)(128)(4,1)S(1)}, s32[]{:S(2)}) async-start(s8[8388608]{0:T(1024)(128)(4,1)} %bitcast.18), calls=%async_computation | async-start | bytes 8388608
  54.3 4.2 %collective-permute-start.12 = (bf16[32,4096]{1,0:T(8,128)(2,1)S(1)}, bf16[32,4096]{1,0:T(8,128)(2,1)S(1)}, u32[]{:S(2)}, u32[]{:S(2)}) collective-permute-start(bf16[32,4096]{1,0:T(8,128)(2,1)S(1)} %get-tuple-element.17), channel_id=1, source_target_pairs={{0,1},{1,0},{2,3},{3,2},{4,5},{5,4},{6,7},{7,6},{8,9},{9,8},{10,11... | collective-permute-start | bytes 786440 | tf_op jit(solution)/shard_map/ppermute | solution.py:120
  54.3 2.5 %collective-permute-start.7 = (bf16[32,4096]{1,0:T(8,128)(2,1)S(1)}, bf16[32,4096]{1,0:T(8,128)(2,1)S(1)}, u32[]{:S(2)}, u32[]{:S(2)}) collective-permute-start(bf16[32,4096]{1,0:T(8,128)(2,1)S(1)} %get-tuple-element.18), channel_id=1, source_target_pairs={{0,1},{1,0},{2,3},{3,2},{4,5},{5,4},{6,7},{7,6},{8,9},{9,8},{10,11... | collective-permute-start | bytes 786440 | tf_op jit(solution)/shard_map/ppermute | solution.py:120
  56.8 4.9 %slice-start.1 = ((s8[8388608]{0:T(1024)(128)(4,1)}), s8[4194304]{0:T(1024)(128)(4,1)S(1)}, s32[]{:S(2)}) async-start(s8[8388608]{0:T(1024)(128)(4,1)} %bitcast.18), calls=%async_computation.1 | async-start | bytes 8388608
  60.2 4.3 %collective-permute-start.15 = (f32[256,64]{0,1:T(8,128)S(1)}, f32[256,64]{0,1:T(8,128)S(1)}, u32[]{:S(2)}, u32[]{:S(2)}) collective-permute-start(f32[256,64]{0,1:T(8,128)S(1)} %fusion.22), channel_id=1, source_target_pairs={{0,2},{2,0},{1,3},{3,1},{4,6},{6,4},{5,7},{7,5},{8,10},{10,8},{9,1... | collective-permute-start | bytes 196616 | tf_op jit(solution)/shard_map/ppermute | solution.py:149
  64.5 2.0 %collective-permute-start.16 = (f32[256,64]{0,1:T(8,128)S(1)}, f32[256,64]{0,1:T(8,128)S(1)}, u32[]{:S(2)}, u32[]{:S(2)}) collective-permute-start(f32[256,64]{0,1:T(8,128)S(1)} %select_add_fusion), channel_id=1, source_target_pairs={{0,0},{4,8},{8,4},{12,12},{1,1},{5,9},{9,5},{13,13},{2,2},{6,10},{... | collective-permute-start | bytes 196616 | tf_op jit(solution)/shard_map/ppermute | solution.py:152
  66.6 7.9 %copy-start.3 = (bf16[256,1024]{1,0:T(8,128)(2,1)S(1)}, bf16[256,1024]{1,0:T(8,128)(2,1)}, u32[]{:S(2)}) copy-start(bf16[256,1024]{1,0:T(8,128)(2,1)} %param.9) | copy-start | bytes 1572868
  66.6 7.9 %copy-start.4 = (bf16[2,64,1024]{2,1,0:T(8,128)(2,1)S(1)}, bf16[2,64,1024]{2,1,0:T(8,128)(2,1)}, u32[]{:S(2)}) copy-start(bf16[2,64,1024]{2,1,0:T(8,128)(2,1)} %param.12) | copy-start | bytes 786436
  66.6 7.9 %collective-permute-start.17 = (bf16[256,64]{0,1:T(8,128)(2,1)S(1)}, bf16[256,64]{0,1:T(8,128)(2,1)S(1)}, u32[]{:S(2)}, u32[]{:S(2)}) collective-permute-start(bf16[256,64]{0,1:T(8,128)(2,1)S(1)} %fusion.19), channel_id=1, source_target_pairs={{0,4},{4,0},{8,12},{12,8},{1,5},{5,1},{9,13},{13,9},{2,6},{6,2},{1... | collective-permute-start | bytes 98312 | tf_op jit(solution)/shard_map/ppermute | solution.py:160
  76.3 10.1 %collective-permute-start.20 = (bf16[128,1024]{1,0:T(8,128)(2,1)S(1)}, bf16[128,1024]{1,0:T(8,128)(2,1)S(1)}, u32[]{:S(2)}, u32[]{:S(2)}) collective-permute-start(bf16[128,1024]{1,0:T(8,128)(2,1)S(1)} %select_convert_fusion), channel_id=1, source_target_pairs={{0,2},{2,0},{1,3},{3,1},{4,6},{6,4},{5,7},{7,5},{8,10},{10,8},{9,1... | collective-permute-start | bytes 786440 | tf_op jit(solution)/shard_map/ppermute | solution.py:173
  80.1 6.3 %collective-permute-start.21 = (bf16[64,1024]{1,0:T(8,128)(2,1)S(1)}, bf16[64,1024]{1,0:T(8,128)(2,1)S(1)}, u32[]{:S(2)}, u32[]{:S(2)}) collective-permute-start(bf16[64,1024]{1,0:T(8,128)(2,1)S(1)} %get-tuple-element.13), channel_id=1, source_target_pairs={{0,2},{2,0},{1,3},{3,1},{4,6},{6,4},{5,7},{7,5},{8,10},{10,8},{9,1... | collective-permute-start | bytes 393224 | tf_op jit(solution)/shard_map/ppermute | solution.py:173
  80.7 10.0 %collective-permute-start.19 = (bf16[64,1024]{1,0:T(8,128)(2,1)S(1)}, bf16[64,1024]{1,0:T(8,128)(2,1)S(1)}, u32[]{:S(2)}, u32[]{:S(2)}) collective-permute-start(bf16[64,1024]{1,0:T(8,128)(2,1)S(1)} %get-tuple-element.14), channel_id=1, source_target_pairs={{0,2},{2,0},{1,3},{3,1},{4,6},{6,4},{5,7},{7,5},{8,10},{10,8},{9,1... | collective-permute-start | bytes 393224 | tf_op jit(solution)/shard_map/ppermute | solution.py:173
  90.7 0.6 copy-start.1

commit v3 on v1

v3 whole, which is shorter than its diff:
```python
import functools

import jax
import jax.numpy as jnp
from jax import lax
from jax.experimental import pallas as pl
from jax.experimental.pallas import tpu as pltpu
from jax.sharding import PartitionSpec as P

F32 = jnp.float32
BF16 = jnp.bfloat16


def low_rank_weights(low, slot, live, slots, rank_width):
    kept = jnp.arange(rank_width, dtype=jnp.int32)[None, :] < live[:, None]
    scaling = rank_width / live.astype(F32)
    scaled = jnp.where(kept, low * scaling[:, None], jnp.zeros((), F32)).astype(BF16)
    hot = slot[:, None] == jnp.arange(slots, dtype=jnp.int32)[None, :]
    spread = jnp.where(hot[:, :, None], scaled[:, None, :], jnp.zeros((), BF16))
    return spread.reshape(low.shape[0], slots * rank_width)


def tables(tenant, entry, live):
    ids = jnp.arange(entry.shape[0], dtype=jnp.int32)
    hot = (tenant[:, None] == ids[None, :]).astype(jnp.int32)
    return jnp.sum(hot * entry[None, :], axis=1), jnp.sum(hot * live[None, :], axis=1)


def general(rows, residual, weight, down, up, tenant, entry, live):
    own = residual.shape[0]
    cols = weight.shape[1]
    width = down.shape[1]
    slots = entry.shape[0]
    slot_all, live_all = tables(tenant, entry, live)
    part = rows.shape[0] // lax.axis_size("sub")
    mine = lax.dynamic_slice_in_dim(rows, lax.axis_index("sub") * part, part, 0)
    halves = lax.all_gather(lax.all_gather(mine, "blk", axis=0), "sub", axis=1)
    full = halves.reshape(-1, rows.shape[1])
    base = jnp.dot(full, weight, preferred_element_type=F32)
    low = lax.dot_general(
        full, down.reshape(-1, down.shape[2]), (((1,), (1,)), ((), ())), preferred_element_type=F32
    )
    held = down.shape[0]
    places = lax.axis_index("blk") * held + jnp.arange(held, dtype=jnp.int32)
    here = slot_all[:, None] == places[None, :]
    low = jnp.sum(
        jnp.where(here[:, :, None], low.reshape(-1, held, width), jnp.zeros((), F32)), axis=1
    )
    low = lax.psum(lax.psum_scatter(low, "split", scatter_dimension=0, tiled=True), "blk")
    base = lax.psum_scatter(base, "split", scatter_dimension=0, tiled=True)
    start = lax.axis_index("split") * own
    spread = low_rank_weights(
        low,
        lax.dynamic_slice_in_dim(slot_all, start, own, 0),
        lax.dynamic_slice_in_dim(live_all, start, own, 0),
        slots,
        width,
    )
    ups = lax.all_gather(up, "split", axis=0, tiled=True).reshape(slots * width, cols)
    lora = jnp.dot(spread, ups, preferred_element_type=F32)
    return (residual.astype(F32) + base + lora).astype(BF16)


SWAP = [(0, 1), (1, 0)]
NEAR = [(0, 1), (1, 0), (2, 3), (3, 2)]
FAR = [(0, 2), (2, 0), (1, 3), (3, 1)]
VMEM = pl.BlockSpec(memory_space=pltpu.VMEM)
SMEM = pl.BlockSpec(memory_space=pltpu.SMEM)
COST = pl.CostEstimate(flops=0, bytes_accessed=0, transcendentals=0)
PARAMS = pltpu.CompilerParams(vmem_limit_bytes=16 * 1024 * 1024)


def products(rows, weight_ref, store):
    cols = weight_ref.shape[1]
    tile = 256 if cols % 256 == 0 else cols
    for j in range(0, cols, tile):
        store(j, tile, jnp.dot(rows, weight_ref[:, j : j + tile], preferred_element_type=F32))


def low_product(rows, down_ref):
    return lax.dot_general(
        rows, down_ref[...], (((1,), (1,)), ((), ())), preferred_element_type=F32
    )


def row_pieces(flags_ref, refs):
    c = flags_ref[1]
    ordered = []
    for mine, other in zip(refs[::2], refs[1::2]):
        mine, other = mine[...], other[...]
        ordered += [jnp.where(c == 0, mine, other), jnp.where(c == 0, other, mine)]
    return jnp.concatenate(ordered)


def own_kernel(rows_ref, weight_ref, down_ref, sum_ref, low_ref):
    rows = rows_ref[...]

    def store(j, tile, value):
        sum_ref[:, j : j + tile] = value

    products(rows, weight_ref, store)
    low_ref[...] = low_product(rows, down_ref)


def mix_kernel(plan, flags_ref, weight_ref, down_ref, *refs):
    taken = 0
    groups = []
    for count, begin in plan:
        groups.append((row_pieces(flags_ref, refs[taken : taken + count]), begin))
        taken += count
    refs = list(refs[taken:])
    helds = [refs.pop(0) if begin is not None else None for _, begin in groups]
    home = flags_ref[0] == 1
    low_ref = refs.pop()
    rows = jnp.concatenate([group for group, _ in groups])
    low_ref[...] = low_product(rows, down_ref)
    has_parts = any(begin is not None for _, begin in groups)
    send_ref = refs.pop() if has_parts else None
    keep_ref = refs.pop() if has_parts else None
    sum_ref = refs.pop() if refs else None

    def store(j, tile, value):
        at, sent, summed = 0, 0, 0
        for (group, begin), held_ref in zip(groups, helds):
            count = group.shape[0]
            part = value[at : at + count]
            if begin is None:
                sum_ref[summed : summed + count, j : j + tile] = part
                summed += count
            else:
                held = held_ref[begin : begin + count, j : j + tile]
                keep_ref[sent : sent + count, j : j + tile] = jnp.where(home, held, part)
                send_ref[sent : sent + count, j : j + tile] = jnp.where(home, part, held).astype(
                    BF16
                )
                sent += count
            at += count

    products(rows, weight_ref, store)


def call(kernel, outs, in_specs, operands):
    return pl.pallas_call(
        kernel,
        out_shape=[jax.ShapeDtypeStruct(shape, dtype) for shape, dtype in outs],
        in_specs=in_specs,
        out_specs=[VMEM] * len(outs),
        compiler_params=PARAMS,
        cost_estimate=COST,
    )(*operands)


def final_kernel(flags_ref, residual_ref, spread_ref, ups_ref, *refs):
    *parts, out_ref, rest_ref = refs
    rest_ref[...] = residual_ref[...].astype(F32) + jnp.dot(
        spread_ref[...], ups_ref[...], preferred_element_type=F32
    )
    step = out_ref.shape[0] // 4
    place = flags_ref[2] * (2 * step)
    at = 0
    for keep, got in zip(parts[::2], parts[1::2]):
        for begin in range(0, keep.shape[0], step):
            first = place if at < 2 else 2 * step - place
            rows = pl.ds(pl.multiple_of(first + (at % 2) * step, step), step)
            here = slice(begin, begin + step)
            out_ref[rows, :] = (
                rest_ref[rows, :] + keep[here, :] + got[here, :].astype(F32)
            ).astype(BF16)
            at += 1


def line(rows, residual, weight, down, up, tenant, entry, live):
    z, x, c = lax.axis_index("blk"), lax.axis_index("split"), lax.axis_index("sub")
    block_rows, feats = rows.shape
    width = down.shape[1]
    own, cols = residual.shape
    slots = entry.shape[0]
    slot_all, live_all = tables(tenant, entry, live)
    home = (z // 2) == x
    flags = jnp.stack([home.astype(jnp.int32), c, z % 2])
    unit = 16
    step = block_rows // 2
    half = step // 2
    down_map = down[0]
    barrier = lax.optimization_barrier

    def swapped(piece):
        parts = []
        for at in range(0, piece.shape[0], unit):
            part = piece[at : at + unit]
            parts += [part, lax.ppermute(part, "sub", SWAP)]
        return parts

    def mixed(plan, groups, helds):
        counts = [sum(part.shape[0] for part in group) for group in groups]
        sums = sum(n for n, begin in zip(counts, plan) if begin is None)
        parts = sum(n for n, begin in zip(counts, plan) if begin is not None)
        outs = [((sums, cols), F32)] if sums else []
        outs += [((parts, cols), F32), ((parts, cols), BF16)] if parts else []
        outs.append(((sums + parts, width), F32))
        flat = [part for group in groups for part in group]
        return call(
            functools.partial(mix_kernel, [(len(g), b) for g, b in zip(groups, plan)]),
            outs,
            [SMEM] + [VMEM] * (2 + len(flat) + len(helds)),
            [flags, weight, down_map] + flat + helds,
        )

    def over_x(value):
        return lax.ppermute(value, "split", SWAP)

    mine = lax.dynamic_index_in_dim(
        rows.reshape(block_rows // (2 * unit), 2, unit, feats), c, 1, False
    ).reshape(2, half, feats)
    mine = [mine[0], mine[1]]
    far = [lax.ppermute(piece, "blk", FAR) for piece in mine]
    near = [lax.ppermute(piece, "blk", NEAR) for piece in mine]
    up_other = over_x(up)
    own_sum, own_low = call(
        own_kernel,
        [((block_rows, cols), F32), ((block_rows, width), F32)],
        [VMEM] * 3,
        [rows, weight, down_map],
    )
    far[0], own_sum, own_low, up_other = barrier((far[0], own_sum, own_low, up_other))

    last = [lax.ppermute(far[0], "blk", NEAR)]
    keep_a, send_a, low_a = mixed([0], [swapped(far[0])], [own_sum])
    near_sum, near_low = mixed([None], [swapped(near[0]) + swapped(near[1])], [])
    got_a = over_x(send_a)
    far[1], last[0], got_a, keep_a, near_sum, own_sum = barrier(
        (far[1], last[0], got_a, keep_a, near_sum, own_sum)
    )

    last.append(lax.ppermute(far[1], "blk", NEAR))
    keep_b, send_b, low_b = mixed(
        [step, 0], [swapped(far[1]), swapped(last[0])], [own_sum, near_sum]
    )
    got_b = over_x(send_b)
    last[1], send_b, keep_b, near_sum = barrier((last[1], send_b, keep_b, near_sum))

    keep_c, send_c, low_c = mixed([step], [swapped(last[1])], [near_sum])
    got_c = over_x(send_c)

    odd = z % 2 == 1
    far_low = jnp.concatenate([low_a, low_b[:step]])
    last_low = jnp.concatenate([low_b[step:], low_c])
    near_half = jnp.where(
        odd, jnp.concatenate([near_low, own_low]), jnp.concatenate([own_low, near_low])
    )
    far_half = jnp.where(
        odd, jnp.concatenate([last_low, far_low]), jnp.concatenate([far_low, last_low])
    )
    start = x * own
    slot = lax.dynamic_slice_in_dim(slot_all, start, own, 0)
    rank = lax.dynamic_slice_in_dim(live_all, start, own, 0)
    low = jnp.where(home, near_half, far_half) + over_x(jnp.where(home, far_half, near_half))
    low = jnp.where((slot == z)[:, None], low, jnp.zeros((), F32))
    low, got_b = barrier((low, got_b))
    low = low + lax.ppermute(low, "blk", NEAR)
    low, got_c = barrier((low, got_c))
    low = low + lax.ppermute(low, "blk", FAR)
    spread = low_rank_weights(low, slot, rank, slots, width)
    ups = jnp.where(x == 0, jnp.concatenate([up, up_other]), jnp.concatenate([up_other, up]))
    parts = [keep_a, got_a, keep_b, got_b, keep_c, got_c]
    return pl.pallas_call(
        final_kernel,
        out_shape=jax.ShapeDtypeStruct(residual.shape, BF16),
        in_specs=[SMEM] + [VMEM] * (3 + len(parts)),
        out_specs=VMEM,
        scratch_shapes=[pltpu.VMEM(residual.shape, F32)],
        compiler_params=PARAMS,
        cost_estimate=COST,
    )(flags, residual, spread, ups.reshape(slots * width, cols), *parts)


def shards(rows, residual, weight, down, up, tenant, entry, live):
    sizes = [lax.axis_size(name) for name in ("blk", "split", "sub")]
    plan = line if sizes == [4, 2, 2] and down.shape[0] == 1 else general
    return plan(rows, residual, weight, down, up, tenant, entry, live)


def solution(mesh):
    in_specs = (
        P(("groups", "blk"), "split"),
        P(("groups", "split"), ("blk", "sub")),
        P("split", ("blk", "sub")),
        P("blk", None, "split"),
        P("split", None, ("blk", "sub")),
        P("groups"),
        P(),
        P(),
    )
    out_specs = P(("groups", "split"), ("blk", "sub"))
    return jax.shard_map(shards, mesh=mesh, in_specs=in_specs, out_specs=out_specs, check_vma=False)
```

time: 68.5 us -> 78.8 us (1.15)
  matrix products: 16.5 us -> 0 us
  local copies, waits for them, and re-layouts: 1.44 us -> 14.6 us
  Pallas kernels: 0 us -> 12.9 us
  waiting for transfers between devices: 23.1 us -> 28.7 us
  starting transfers between devices: 23.7 us -> 19.2 us
    dot_general x9 -> x0, matrix products: 16.5 us -> none  [the longest x4 12 us: products(): base = jnp.dot(block, weight, preferred_element_type=F32)]
    pallas_call x0 -> x6, Pallas kernels: none -> 12.9 us  [the longest x5 11.1 us: call(): pl.pallas_call(kernel, out_shape=[jax.ShapeDtypeStruct(shape, dtype) for...]
    unnamed x16 -> x36, local copies, waits for them, and re-layouts: 0.04 us -> 11.3 us
    ppermute x20 -> x25, waiting for transfers between devices: 23.1 us -> 28.7 us  [the longest x2 13.4 us: line(): near = [lax.ppermute(piece, 'blk', NEAR) for piece in mine]]
    ppermute x20 -> x25, starting transfers between devices: 23.7 us -> 19.2 us  [the longest x5 4.76 us: over_x(): return lax.ppermute(value, 'split', SWAP)]
    slice x7 -> x8, local copies, waits for them, and re-layouts: 1.4 us -> 3.16 us  [the longest x6 2.09 us: swapped(): part = piece[at:at + unit]]
    convert_element_type x2 -> x0, other arithmetic: 0.97 us -> none  [the longest x1 0.89 us: line(): got_late = lax.ppermute(late.astype(BF16), ('blk', 'split'), to_away)]
    select_n x1, other arithmetic: 0.02 us -> 0.87 us  [line(): low = jnp.where((slot == z)[:, None], low, jnp.zeros((), F32))]
  transfers between devices with their start and end apart: 20 -> 25, of which waited for: 9 -> 14; matrix products, arithmetic and copies ran while one was open for 25% -> 5% of each run, Pallas kernels for 0% -> 14%
where the time goes in v3:
time: 78.8 us; the launch traced here: 78.4 us
  waiting for transfers between devices  28.7 us (36%)
  starting transfers between devices  19.2 us (24%)
  local copies, waits for them, and re-layouts  14.6 us (19%)
  Pallas kernels  12.9 us (16%)
  other arithmetic  2.71 us (3%)
    ppermute x2, waiting for transfers between devices, line(): near = [lax.ppermute(piece, 'blk', NEAR) for piece in mine]  13.4 us
    unnamed x36, local copies, waits for them, and re-layouts  11.3 us
    pallas_call x5, Pallas kernels, call(): pl.pallas_call(kernel, out_shape=[jax.ShapeDtypeStruct(shape, dtype) for...  11.1 us
    ppermute x5, waiting for transfers between devices, over_x(): return lax.ppermute(value, 'split', SWAP)  6.67 us
    ppermute x5, starting transfers between devices, over_x(): return lax.ppermute(value, 'split', SWAP)  4.76 us
    ppermute x2, starting transfers between devices, line(): far = [lax.ppermute(piece, 'blk', FAR) for piece in mine]  4.44 us
    ppermute x1, waiting for transfers between devices, line(): low = low + lax.ppermute(low, 'blk', NEAR)  2.95 us
    ppermute x12, starting transfers between devices, swapped(): parts += [part, lax.ppermute(part, 'sub', SWAP)]  2.92 us
  transfers between devices with their start and end apart: 25, of which 14 were waited for; matrix products, arithmetic and copies ran while one was open for 5% of the time, Pallas kernels for 14%

profile of v3, /device:TPU:0, one launch (start us, length us, event | category | flops | bytes accessed | tf_op | source)
XLA Modules:
  0.0 78.4 jit_solution(16685847976205860248)
XLA Ops:
  0.0 1.1 %constant_dynamic-slice_fusion.1 = (bf16[2,1,16,4096]{3,2,1,0:T(8,128)(2,1)S(1)}, bf16[2,1,16,4096]{3,2,1,0:T(8,128)(2,1)S(1)}) fusion(bf16[4,2,16,4096]{3,2,1,0:T(8,128)(2,1)} %bitcast.19, s32[]{:T(128)S(6)} %add.31, s32[]{:T(128)S(6)} %select_n.76), kind=kLoop, calls=%fused_computation.16 | loop fusion | bytes 1048584 | tf_op jit(solution)/shard_map/slice | solution.py:215
  1.1 4.1 %collective-permute-start.6 = (bf16[32,4096]{1,0:T(8,128)(2,1)S(1)}, bf16[32,4096]{1,0:T(8,128)(2,1)S(1)}, u32[]{:S(2)}, u32[]{:S(2)}) collective-permute-start(bf16[32,4096]{1,0:T(8,128)(2,1)S(1)} %bitcast.24), channel_id=1, source_target_pairs={{0,8},{8,0},{4,12},{12,4},{1,9},{9,1},{5,13},{13,5},{2,10},{10,2},... | collective-permute-start | bytes 786440 | tf_op jit(solution)/shard_map/ppermute | solution.py:216
  5.2 1.5 %collective-permute-start.7 = (bf16[2,64,1024]{2,1,0:T(8,128)(2,1)}, bf16[2,64,1024]{2,1,0:T(8,128)(2,1)S(1)}, u32[]{:S(2)}, u32[]{:S(2)}) collective-permute-start(bf16[2,64,1024]{2,1,0:T(8,128)(2,1)} %param.12), channel_id=1, source_target_pairs={{0,2},{2,0},{1,3},{3,1},{4,6},{6,4},{5,7},{7,5},{8,10},{10,8},{9,1... | collective-permute-start | bytes 786440 | tf_op jit(solution)/shard_map/ppermute | solution.py:210
  6.7 1.6 %collective-permute-start = (bf16[32,4096]{1,0:T(8,128)(2,1)S(1)}, bf16[32,4096]{1,0:T(8,128)(2,1)S(1)}, u32[]{:S(2)}, u32[]{:S(2)}) collective-permute-start(bf16[32,4096]{1,0:T(8,128)(2,1)S(1)} %bitcast.25), channel_id=1, source_target_pairs={{0,4},{4,0},{8,12},{12,8},{1,5},{5,1},{9,13},{13,9},{2,6},{6,2},{1... | collective-permute-start | bytes 786440 | tf_op jit(solution)/shard_map/ppermute | solution.py:217
  8.2 0.4 collective-permute-start.3
  8.7 0.3 collective-permute-start.8
  9.0 3.4 %copy-done = bf16[4096,1024]{1,0:T(8,128)(2,1)S(1)} copy-done((bf16[4096,1024]{1,0:T(8,128)(2,1)S(1)}, bf16[4096,1024]{1,0:T(8,128)(2,1)}, u32[]{:S(2)}) %copy-start) | copy-done | bytes 8388632
  12.4 1.0 %copy-done.3 = bf16[1,64,4096]{2,1,0:T(8,128)(2,1)S(1)} copy-done((bf16[1,64,4096]{2,1,0:T(8,128)(2,1)S(1)}, bf16[1,64,4096]{2,1,0:T(8,128)(2,1)}, u32[]{:S(2)}) %copy-start.3) | copy-done | bytes 524312
  13.5 1.2 %copy-done.5 = bf16[128,4096]{1,0:T(8,128)(2,1)S(1)} copy-done((bf16[128,4096]{1,0:T(8,128)(2,1)S(1)}, bf16[128,4096]{1,0:T(8,128)(2,1)}, u32[]{:S(2)}) %copy-start.5) | copy-done | bytes 1048600
  14.7 1.6 %shard_map.83 = (f32[128,1024]{1,0:T(8,128)S(1)}, f32[128,64]{1,0:T(8,128)S(1)}) custom-call(bf16[128,4096]{1,0:T(8,128)(2,1)S(1)} %copy-done.5, bf16[4096,1024]{1,0:T(8,128)(2,1)S(1)} %copy-done, bf16[64,4096]{1,0:T(8,128)(2,1)S(1)} %bitcast.14), custom_call_target="tpu_custom_call" | custom-call | tf_op jit(solution)/shard_map/pallas_call | solution.py:143
  16.3 1.7 %collective-permute-done.6 = bf16[32,4096]{1,0:T(8,128)(2,1)S(1)} collective-permute-done((bf16[32,4096]{1,0:T(8,128)(2,1)S(1)}, bf16[32,4096]{1,0:T(8,128)(2,1)S(1)}, u32[]{:S(2)}, u32[]{:S(2)}) %collective-permute-start.6) | collective-permute-done | bytes 262176 | tf_op jit(solution)/shard_map/ppermute | solution.py:216
  18.2 7.8 %collective-permute-done = bf16[32,4096]{1,0:T(8,128)(2,1)S(1)} collective-permute-done((bf16[32,4096]{1,0:T(8,128)(2,1)S(1)}, bf16[32,4096]{1,0:T(8,128)(2,1)S(1)}, u32[]{:S(2)}, u32[]{:S(2)}) %collective-permute-start) | collective-permute-done | bytes 262176 | tf_op jit(solution)/shard_map/ppermute | solution.py:217
  26.0 5.6 %collective-permute-done.3 = bf16[32,4096]{1,0:T(8,128)(2,1)S(1)} collective-permute-done((bf16[32,4096]{1,0:T(8,128)(2,1)S(1)}, bf16[32,4096]{1,0:T(8,128)(2,1)S(1)}, u32[]{:S(2)}, u32[]{:S(2)}) %collective-permute-start.3) | collective-permute-done | bytes 262176 | tf_op jit(solution)/shard_map/ppermute | solution.py:217
  31.6 0.5 collective-permute-start.2
  32.3 2.3 %shard_map.84 = (f32[64,1024]{1,0:T(8,128)S(1)}, bf16[64,1024]{1,0:T(8,128)(2,1)S(1)}, f32[64,64]{1,0:T(8,128)S(1)}) custom-call(s32[3]{0:T(128)S(1)} %pad_add_fusion.flags_ref, bf16[4096,1024]{1,0:T(8,128)(2,1)S(1)} %copy-done.1, bf16[64,4096]{1,0:T(8,128)(2,1)S(1)} %bitcast.15, bf16[16,4096]{1,0:T(8,128)(2,1)S(1)} %get-tuple-element.80.refs_0_, ...), custom_call_target="tpu_custom_call" | custom-call | tf_op jit(solution)/shard_map/pallas_call | solution.py:143
  34.6 0.6 collective-permute-start.5
  35.1 0.6 collective-permute-start.12
  35.7 0.4 collective-permute-done.5.refs_7_
  36.1 2.1 %shard_map.82 = (f32[128,1024]{1,0:T(8,128)S(1)}, f32[128,64]{1,0:T(8,128)S(1)}) custom-call(s32[3]{0:T(128)S(1)} %pad_add_fusion.flags_ref, bf16[4096,1024]{1,0:T(8,128)(2,1)S(1)} %copy-done.1, bf16[64,4096]{1,0:T(8,128)(2,1)S(1)} %bitcast.16, bf16[16,4096]{1,0:T(8,128)(2,1)S(1)} %get-tuple-element.84.refs_0_, ...), custom_call_target="tpu_custom_call" | custom-call | tf_op jit(solution)/shard_map/pallas_call | solution.py:143
  38.2 2.4 %collective-permute-done.12.refs_1_ = bf16[64,1024]{1,0:T(8,128)(2,1)S(1)} collective-permute-done((bf16[64,1024]{1,0:T(8,128)(2,1)S(1)}, bf16[64,1024]{1,0:T(8,128)(2,1)S(1)}, u32[]{:S(2)}, u32[]{:S(2)}) %collective-permute-start.12) | collective-permute-done | bytes 131104 | tf_op jit(solution)/shard_map/ppermute | solution.py:210
  40.6 1.0 %fusion.3 = (bf16[16,4096]{1,0:T(8,128)(2,1)S(1)}, bf16[16,4096]{1,0:T(8,128)(2,1)S(1)}) fusion(bf16[32,4096]{1,0:T(8,128)(2,1)} %collective-permute-done.8), kind=kLoop, calls=%fused_computation.19 | loop fusion | bytes 524288 | tf_op jit(solution)/shard_map/slice | solution.py:190
  41.8 0.5 collective-permute-start.14
  42.3 0.1 collective-permute-start.15
  42.5 0.4 collective-permute-start.16
  43.1 0.2 collective-permute-done.14.refs_3_
  43.3 0.4 collective-permute-done.15.refs_5_
  43.7 0.2 collective-permute-done.16.refs_7_
  43.9 0.7 copy-done.7
  44.6 3.4 %copy-done.2 = bf16[4096,1024]{1,0:T(8,128)(2,1)S(1)} copy-done((bf16[4096,1024]{1,0:T(8,128)(2,1)S(1)}, bf16[4096,1024]{1,0:T(8,128)(2,1)}, u32[]{:S(2)}) %copy-start.2) | copy-done | bytes 8388632
  48.0 0.9 %copy-done.8 = bf16[16,4096]{1,0:T(8,128)(2,1)S(1)} copy-done((bf16[16,4096]{1,0:T(8,128)(2,1)S(1)}, bf16[16,4096]{1,0:T(8,128)(2,1)}, u32[]{:S(2)}) %copy-start.8) | copy-done | bytes 131096
  48.9 2.8 %shard_map.85 = (f32[128,1024]{1,0:T(8,128)S(1)}, bf16[128,1024]{1,0:T(8,128)(2,1)}, f32[128,64]{1,0:T(8,128)S(1)}) custom-call(s32[3]{0:T(128)S(1)} %pad_add_fusion.flags_ref, bf16[4096,1024]{1,0:T(8,128)(2,1)S(1)} %copy-done.2, bf16[64,4096]{1,0:T(8,128)(2,1)S(1)} %bitcast.17, bf16[16,4096]{1,0:T(8,128)(2,1)S(1)} %get-tuple-element.78.refs_0_, ...), custom_call_target="tpu_custom_call" | custom-call | tf_op jit(solution)/shard_map/pallas_call | solution.py:143
  51.7 0.6 collective-permute-start.21
  52.3 1.0 %fusion.1 = (bf16[16,4096]{1,0:T(8,128)(2,1)S(1)}, bf16[16,4096]{1,0:T(8,128)(2,1)S(1)}) fusion(bf16[32,4096]{1,0:T(8,128)(2,1)} %collective-permute-done.17), kind=kLoop, calls=%fused_computation.17 | loop fusion | bytes 524288 | tf_op jit(solution)/shard_map/slice | solution.py:190
  53.4 0.5 collective-permute-start.19
  53.9 0.8 %collective-permute-done.18.refs_1_ = bf16[16,4096]{1,0:T(8,128)(2,1)S(1)} collective-permute-done((bf16[16,4096]{1,0:T(8,128)(2,1)S(1)}, bf16[16,4096]{1,0:T(8,128)(2,1)S(1)}, u32[]{:S(2)}, u32[]{:S(2)}) %collective-permute-start.18) | collective-permute-done | bytes 131104 | tf_op jit(solution)/shard_map/ppermute | solution.py:191
  54.7 0.2 collective-permute-done.19.refs_3_
  54.9 2.3 %shard_map.86 = (f32[64,1024]{1,0:T(8,128)S(1)}, bf16[64,1024]{1,0:T(8,128)(2,1)S(1)}, f32[64,64]{1,0:T(8,128)S(1)}) custom-call(s32[3]{0:T(128)S(1)} %pad_add_fusion.flags_ref, bf16[4096,1024]{1,0:T(8,128)(2,1)S(1)} %copy-done.2, bf16[64,4096]{1,0:T(8,128)(2,1)S(1)} %bitcast.18, bf16[16,4096]{1,0:T(8,128)(2,1)S(1)} %get-tuple-element.74.refs_0_, ...), custom_call_target="tpu_custom_call" | custom-call | tf_op jit(solution)/shard_map/pallas_call | solution.py:143
  57.2 0.6 copy-done.11
  57.9 1.5 %collective-permute-start.20 = (f32[256,64]{1,0:T(8,128)S(1)}, f32[256,64]{1,0:T(8,128)S(1)}, u32[]{:S(2)}, u32[]{:S(2)}) collective-permute-start(f32[256,64]{1,0:T(8,128)S(1)} %fusion), channel_id=1, source_target_pairs={{0,2},{2,0},{1,3},{3,1},{4,6},{6,4},{5,7},{7,5},{8,10},{10,8},{9,1... | collective-permute-start | bytes 196616 | tf_op jit(solution)/shard_map/ppermute | solution.py:210
  59.4 0.6 collective-permute-start.23
  60.0 4.3 %collective-permute-done.20 = f32[256,64]{1,0:T(8,128)S(1)} collective-permute-done((f32[256,64]{1,0:T(8,128)S(1)}, f32[256,64]{1,0:T(8,128)S(1)}, u32[]{:S(2)}, u32[]{:S(2)}) %collective-permute-start.20) | collective-permute-done | bytes 65568 | tf_op jit(solution)/shard_map/ppermute | solution.py:210
  64.2 0.9 %add_select_fusion = f32[256,64]{1,0:T(8,128)S(1)} fusion(f32[256,64]{1,0:T(8,128)S(1)} %collective-permute-done.20, f32[128,64]{1,0:T(8,128)S(1)} %get-tuple-element.35, f32[128,64]{1,0:T(8,128)S(1)} %get-tuple-element.38, pred[256]{0:T(512)(128)(4,1)S(1)} %get-tuple-element.69, pred[]{:T(512)S(6)} %eq.57, pred[]{:T(512)S(6)} %eq.48, ...), kind=kLoop, calls=%fused_computation.4 | loop fusion | flops 196608 | bytes 295170 | tf_op jit(solution)/shard_map/jit(_where)/select_n | solution.py:258
  65.1 2.0 %collective-permute-start.22 = (f32[256,64]{1,0:T(8,128)S(1)}, f32[256,64]{1,0:T(8,128)S(1)}, u32[]{:S(2)}, u32[]{:S(2)}) collective-permute-start(f32[256,64]{1,0:T(8,128)S(1)} %add_select_fusion), channel_id=1, source_target_pairs={{0,4},{4,0},{8,12},{12,8},{1,5},{5,1},{9,13},{13,9},{2,6},{6,2},{1... | collective-permute-start | bytes 196616 | tf_op jit(solution)/shard_map/ppermute | solution.py:260
  67.2 3.0 %collective-permute-done.22 = f32[256,64]{1,0:T(8,128)S(1)} collective-permute-done((f32[256,64]{1,0:T(8,128)S(1)}, f32[256,64]{1,0:T(8,128)S(1)}, u32[]{:S(2)}, u32[]{:S(2)}) %collective-permute-start.22) | collective-permute-done | bytes 65568 | tf_op jit(solution)/shard_map/ppermute | solution.py:260
  70.2 2.9 %collective-permute-start.24 = (f32[256,64]{1,0:T(8,128)S(1)}, f32[256,64]{1,0:T(8,128)S(1)}, u32[]{:S(2)}, u32[]{:S(2)}) collective-permute-start(f32[256,64]{1,0:T(8,128)S(1)} %add.27), channel_id=1, source_target_pairs={{0,8},{8,0},{4,12},{12,4},{1,9},{9,1},{5,13},{13,5},{2,10},{10,2},... | collective-permute-start | bytes 196616 | tf_op jit(solution)/shard_map/ppermute | solution.py:262
  73.1 1.3 %maximum_select_fusion = bf16[4,64,1024]{2,1,0:T(8,128)(2,1)S(1)} fusion(bf16[2,64,1024]{2,1,0:T(8,128)(2,1)} %copy-done.14, bf16[2,64,1024]{2,1,0:T(8,128)(2,1)} %param.12, pred[]{:T(512)S(6)} %eq.58), kind=kLoop, calls=%fused_computation | loop fusion | flops 786432 | bytes 1048577 | tf_op jit(solution)/shard_map/jit(_where)/select_n | solution.py:264
  74.4 1.7 %collective-permute-done.24 = f32[256,64]{1,0:T(8,128)S(1)} collective-permute-done((f32[256,64]{1,0:T(8,128)S(1)}, f32[256,64]{1,0:T(8,128)S(1)}, u32[]{:S(2)}, u32[]{:S(2)}) %collective-permute-start.24) | collective-permute-done | bytes 65568 | tf_op jit(solution)/shard_map/ppermute | solution.py:262
  76.5 1.8 %shard_map.87 = bf16[256,1024]{1,0:T(8,128)(2,1)} custom-call(s32[3]{0:T(128)S(1)} %pad_add_fusion.flags_ref, bf16[256,1024]{1,0:T(8,128)(2,1)S(1)} %copy-done.6, bf16[256,256]{1,0:T(8,128)(2,1)S(1)} %copy.18.spread_ref, bf16[256,1024]{1,0:T(8,128)(2,1)S(1)} %bitcast.20, f32[64,1024]{1,0:T(8,128)S(1)} %get-tuple-element.59.refs_0_, ...), custom_call_target="tpu_custom_call" | custom-call | tf_op jit(solution)/shard_map/pallas_call | solution.py:266
  (65 shorter events, 1.4 us)
Async XLA Ops:
  1.1 17.0 %collective-permute-start.6 = (bf16[32,4096]{1,0:T(8,128)(2,1)S(1)}, bf16[32,4096]{1,0:T(8,128)(2,1)S(1)}, u32[]{:S(2)}, u32[]{:S(2)}) collective-permute-start(bf16[32,4096]{1,0:T(8,128)(2,1)S(1)} %bitcast.24), channel_id=1, source_target_pairs={{0,8},{8,0},{4,12},{12,4},{1,9},{9,1},{5,13},{13,5},{2,10},{10,2},... | collective-permute-start | bytes 786440 | tf_op jit(solution)/shard_map/ppermute | solution.py:216
  5.2 12.9 %collective-permute-start.7 = (bf16[2,64,1024]{2,1,0:T(8,128)(2,1)}, bf16[2,64,1024]{2,1,0:T(8,128)(2,1)S(1)}, u32[]{:S(2)}, u32[]{:S(2)}) collective-permute-start(bf16[2,64,1024]{2,1,0:T(8,128)(2,1)} %param.12), channel_id=1, source_target_pairs={{0,2},{2,0},{1,3},{3,1},{4,6},{6,4},{5,7},{7,5},{8,10},{10,8},{9,1... | collective-permute-start | bytes 786440 | tf_op jit(solution)/shard_map/ppermute | solution.py:210
  6.7 19.3 %collective-permute-start = (bf16[32,4096]{1,0:T(8,128)(2,1)S(1)}, bf16[32,4096]{1,0:T(8,128)(2,1)S(1)}, u32[]{:S(2)}, u32[]{:S(2)}) collective-permute-start(bf16[32,4096]{1,0:T(8,128)(2,1)S(1)} %bitcast.25), channel_id=1, source_target_pairs={{0,4},{4,0},{8,12},{12,8},{1,5},{5,1},{9,13},{13,9},{2,6},{6,2},{1... | collective-permute-start | bytes 786440 | tf_op jit(solution)/shard_map/ppermute | solution.py:217
  8.2 23.4 %collective-permute-start.3 = (bf16[32,4096]{1,0:T(8,128)(2,1)S(1)}, bf16[32,4096]{1,0:T(8,128)(2,1)S(1)}, u32[]{:S(2)}, u32[]{:S(2)}) collective-permute-start(bf16[32,4096]{1,0:T(8,128)(2,1)S(1)} %bitcast.22), channel_id=1, source_target_pairs={{0,4},{4,0},{8,12},{12,8},{1,5},{5,1},{9,13},{13,9},{2,6},{6,2},{1... | collective-permute-start | bytes 786440 | tf_op jit(solution)/shard_map/ppermute | solution.py:217
  8.7 29.5 %collective-permute-start.8 = (bf16[32,4096]{1,0:T(8,128)(2,1)S(1)}, bf16[32,4096]{1,0:T(8,128)(2,1)}, u32[]{:S(2)}, u32[]{:S(2)}) collective-permute-start(bf16[32,4096]{1,0:T(8,128)(2,1)S(1)} %bitcast.23), channel_id=1, source_target_pairs={{0,8},{8,0},{4,12},{12,4},{1,9},{9,1},{5,13},{13,5},{2,10},{10,2},... | collective-permute-start | bytes 786440 | tf_op jit(solution)/shard_map/ppermute | solution.py:216
  9.0 3.4 %copy-start = (bf16[4096,1024]{1,0:T(8,128)(2,1)S(1)}, bf16[4096,1024]{1,0:T(8,128)(2,1)}, u32[]{:S(2)}) copy-start(bf16[4096,1024]{1,0:T(8,128)(2,1)} %weight_ref.9) | copy-start | bytes 25165828
  12.4 1.0 %copy-start.3 = (bf16[1,64,4096]{2,1,0:T(8,128)(2,1)S(1)}, bf16[1,64,4096]{2,1,0:T(8,128)(2,1)}, u32[]{:S(2)}) copy-start(bf16[1,64,4096]{2,1,0:T(8,128)(2,1)} %param.11) | copy-start | bytes 1572868
  13.4 1.2 %copy-start.5 = (bf16[128,4096]{1,0:T(8,128)(2,1)S(1)}, bf16[128,4096]{1,0:T(8,128)(2,1)}, u32[]{:S(2)}) copy-start(bf16[128,4096]{1,0:T(8,128)(2,1)} %rows_ref.1) | copy-start | bytes 3145732
  14.7 17.6 %copy-start.1 = (bf16[4096,1024]{1,0:T(8,128)(2,1)S(1)}, bf16[4096,1024]{1,0:T(8,128)(2,1)}, u32[]{:S(2)}) copy-start(bf16[4096,1024]{1,0:T(8,128)(2,1)} %weight_ref.9) | copy-start | bytes 25165828
  18.0 17.7 %copy-start.14 = (bf16[2,64,1024]{2,1,0:T(8,128)(2,1)}, bf16[2,64,1024]{2,1,0:T(8,128)(2,1)S(1)}, u32[]{:S(2)}) copy-start(bf16[2,64,1024]{2,1,0:T(8,128)(2,1)S(1)} %collective-permute-done.7) | copy-start | bytes 786436
  18.0 22.6 %collective-permute-start.9 = (bf16[32,4096]{1,0:T(8,128)(2,1)S(1)}, bf16[32,4096]{1,0:T(8,128)(2,1)S(1)}, u32[]{:S(2)}, u32[]{:S(2)}) collective-permute-start(bf16[32,4096]{1,0:T(8,128)(2,1)S(1)} %collective-permute-done.6), channel_id=1, source_target_pairs={{0,4},{4,0},{8,12},{12,8},{1,5},{5,1},{9,13},{13,9},{2,6},{6,2},{1... | collective-permute-start | bytes 786440 | tf_op jit(solution)/shard_map/ppermute | solution.py:227
  18.1 13.5 %collective-permute-start.10 = (bf16[16,4096]{1,0:T(8,128)(2,1)S(1)}, bf16[16,4096]{1,0:T(8,128)(2,1)S(1)}, u32[]{:S(2)}, u32[]{:S(2)}) collective-permute-start(bf16[16,4096]{1,0:T(8,128)(2,1)S(1)} %get-tuple-element.80.refs_0_), channel_id=1, source_target_pairs={{0,1},{1,0},{2,3},{3,2},{4,5},{5,4},{6,7},{7,6},{8,9},{9,8},{10,11... | collective-permute-start | bytes 393224 | tf_op jit(solution)/shard_map/ppermute | solution.py:191
  26.0 6.2 %collective-permute-start.11 = (bf16[16,4096]{1,0:T(8,128)(2,1)S(1)}, bf16[16,4096]{1,0:T(8,128)(2,1)S(1)}, u32[]{:S(2)}, u32[]{:S(2)}) collective-permute-start(bf16[16,4096]{1,0:T(8,128)(2,1)S(1)} %get-tuple-element.79.refs_2_), channel_id=1, source_target_pairs={{0,1},{1,0},{2,3},{3,2},{4,5},{5,4},{6,7},{7,6},{8,9},{9,8},{10,11... | collective-permute-start | bytes 393224 | tf_op jit(solution)/shard_map/ppermute | solution.py:191
  31.6 3.0 %collective-permute-start.1 = (bf16[16,4096]{1,0:T(8,128)(2,1)S(1)}, bf16[16,4096]{1,0:T(8,128)(2,1)S(1)}, u32[]{:S(2)}, u32[]{:S(2)}) collective-permute-start(bf16[16,4096]{1,0:T(8,128)(2,1)S(1)} %get-tuple-element.84.refs_0_), channel_id=1, source_target_pairs={{0,1},{1,0},{2,3},{3,2},{4,5},{5,4},{6,7},{7,6},{8,9},{9,8},{10,11... | collective-permute-start | bytes 393224 | tf_op jit(solution)/shard_map/ppermute | solution.py:191
  31.6 3.5 %collective-permute-start.2 = (bf16[16,4096]{1,0:T(8,128)(2,1)S(1)}, bf16[16,4096]{1,0:T(8,128)(2,1)S(1)}, u32[]{:S(2)}, u32[]{:S(2)}) collective-permute-start(bf16[16,4096]{1,0:T(8,128)(2,1)S(1)} %get-tuple-element.83.refs_2_), channel_id=1, source_target_pairs={{0,1},{1,0},{2,3},{3,2},{4,5},{5,4},{6,7},{7,6},{8,9},{9,8},{10,11... | collective-permute-start | bytes 393224 | tf_op jit(solution)/shard_map/ppermute | solution.py:191
  32.1 10.8 %copy-start.15 = (s32[512]{0:T(512)S(1)}, s32[512]{0:T(512)}, u32[]{:S(2)}) copy-start(s32[512]{0:T(512)} %param.13) | copy-start | bytes 6148
  32.2 10.8 %copy-start.16 = (s32[4]{0:T(128)S(1)}, s32[4]{0:T(128)}, u32[]{:S(2)}) copy-start(s32[4]{0:T(128)} %param.15) | copy-start | bytes 52
  32.2 10.7 %copy-start.17 = (s32[4]{0:T(128)S(1)}, s32[4]{0:T(128)}, u32[]{:S(2)}) copy-start(s32[4]{0:T(128)} %param.14) | copy-start | bytes 52
  32.2 12.4 %copy-start.4 = (bf16[1,64,4096]{2,1,0:T(8,128)(2,1)S(1)}, bf16[1,64,4096]{2,1,0:T(8,128)(2,1)}, u32[]{:S(2)}) copy-start(bf16[1,64,4096]{2,1,0:T(8,128)(2,1)} %param.11) | copy-start | bytes 1572868
  32.2 3.5 %collective-permute-start.4 = (bf16[16,4096]{1,0:T(8,128)(2,1)S(1)}, bf16[16,4096]{1,0:T(8,128)(2,1)S(1)}, u32[]{:S(2)}, u32[]{:S(2)}) collective-permute-start(bf16[16,4096]{1,0:T(8,128)(2,1)S(1)} %get-tuple-element.82.refs_4_), channel_id=1, source_target_pairs={{0,1},{1,0},{2,3},{3,2},{4,5},{5,4},{6,7},{7,6},{8,9},{9,8},{10,11... | collective-permute-start | bytes 393224 | tf_op jit(solution)/shard_map/ppermute | solution.py:191
  34.6 1.5 %collective-permute-start.5 = (bf16[16,4096]{1,0:T(8,128)(2,1)S(1)}, bf16[16,4096]{1,0:T(8,128)(2,1)S(1)}, u32[]{:S(2)}, u32[]{:S(2)}) collective-permute-start(bf16[16,4096]{1,0:T(8,128)(2,1)S(1)} %get-tuple-element.81.refs_6_), channel_id=1, source_target_pairs={{0,1},{1,0},{2,3},{3,2},{4,5},{5,4},{6,7},{7,6},{8,9},{9,8},{10,11... | collective-permute-start | bytes 393224 | tf_op jit(solution)/shard_map/ppermute | solution.py:191
  35.1 5.5 %collective-permute-start.12 = (bf16[64,1024]{1,0:T(8,128)(2,1)S(1)}, bf16[64,1024]{1,0:T(8,128)(2,1)S(1)}, u32[]{:S(2)}, u32[]{:S(2)}) collective-permute-start(bf16[64,1024]{1,0:T(8,128)(2,1)S(1)} %get-tuple-element.41), channel_id=1, source_target_pairs={{0,2},{2,0},{1,3},{3,1},{4,6},{6,4},{5,7},{7,5},{8,10},{10,8},{9,1... | collective-permute-start | bytes 393224 | tf_op jit(solution)/shard_map/ppermute | solution.py:210
  40.6 1.9 %copy-start.9 = (bf16[64,1024]{1,0:T(8,128)(2,1)}, bf16[64,1024]{1,0:T(8,128)(2,1)S(1)}, u32[]{:S(2)}) copy-start(bf16[64,1024]{1,0:T(8,128)(2,1)S(1)} %collective-permute-done.12.refs_1_) | copy-start | bytes 393220
  41.7 10.6 %collective-permute-start.17 = (bf16[32,4096]{1,0:T(8,128)(2,1)}, bf16[32,4096]{1,0:T(8,128)(2,1)}, u32[]{:S(2)}, u32[]{:S(2)}) collective-permute-start(bf16[32,4096]{1,0:T(8,128)(2,1)} %collective-permute-done.8), channel_id=1, source_target_pairs={{0,4},{4,0},{8,12},{12,8},{1,5},{5,1},{9,13},{13,9},{2,6},{6,2},{1... | collective-permute-start | bytes 786440 | tf_op jit(solution)/shard_map/ppermute | solution.py:235
  41.7 1.4 %collective-permute-start.13 = (bf16[16,4096]{1,0:T(8,128)(2,1)S(1)}, bf16[16,4096]{1,0:T(8,128)(2,1)S(1)}, u32[]{:S(2)}, u32[]{:S(2)}) collective-permute-start(bf16[16,4096]{1,0:T(8,128)(2,1)S(1)} %get-tuple-element.78.refs_0_), channel_id=1, source_target_pairs={{0,1},{1,0},{2,3},{3,2},{4,5},{5,4},{6,7},{7,6},{8,9},{9,8},{10,11... | collective-permute-start | bytes 393224 | tf_op jit(solution)/shard_map/ppermute | solution.py:191
  41.8 1.5 %collective-permute-start.14 = (bf16[16,4096]{1,0:T(8,128)(2,1)S(1)}, bf16[16,4096]{1,0:T(8,128)(2,1)S(1)}, u32[]{:S(2)}, u32[]{:S(2)}) collective-permute-start(bf16[16,4096]{1,0:T(8,128)(2,1)S(1)} %get-tuple-element.77.refs_2_), channel_id=1, source_target_pairs={{0,1},{1,0},{2,3},{3,2},{4,5},{5,4},{6,7},{7,6},{8,9},{9,8},{10,11... | collective-permute-start | bytes 393224 | tf_op jit(solution)/shard_map/ppermute | solution.py:191
  42.3 1.4 %collective-permute-start.15 = (bf16[16,4096]{1,0:T(8,128)(2,1)S(1)}, bf16[16,4096]{1,0:T(8,128)(2,1)S(1)}, u32[]{:S(2)}, u32[]{:S(2)}) collective-permute-start(bf16[16,4096]{1,0:T(8,128)(2,1)S(1)} %get-tuple-element.76.refs_4_), channel_id=1, source_target_pairs={{0,1},{1,0},{2,3},{3,2},{4,5},{5,4},{6,7},{7,6},{8,9},{9,8},{10,11... | collective-permute-start | bytes 393224 | tf_op jit(solution)/shard_map/ppermute | solution.py:191
  42.5 1.5 %collective-permute-start.16 = (bf16[16,4096]{1,0:T(8,128)(2,1)S(1)}, bf16[16,4096]{1,0:T(8,128)(2,1)S(1)}, u32[]{:S(2)}, u32[]{:S(2)}) collective-permute-start(bf16[16,4096]{1,0:T(8,128)(2,1)S(1)} %get-tuple-element.75.refs_6_), channel_id=1, source_target_pairs={{0,1},{1,0},{2,3},{3,2},{4,5},{5,4},{6,7},{7,6},{8,9},{9,8},{10,11... | collective-permute-start | bytes 393224 | tf_op jit(solution)/shard_map/ppermute | solution.py:191
  43.9 0.7 copy-start.7
  44.6 3.4 %copy-start.2 = (bf16[4096,1024]{1,0:T(8,128)(2,1)S(1)}, bf16[4096,1024]{1,0:T(8,128)(2,1)}, u32[]{:S(2)}) copy-start(bf16[4096,1024]{1,0:T(8,128)(2,1)} %weight_ref.9) | copy-start | bytes 25165828
  48.0 0.9 %copy-start.8 = (bf16[16,4096]{1,0:T(8,128)(2,1)S(1)}, bf16[16,4096]{1,0:T(8,128)(2,1)}, u32[]{:S(2)}) copy-start(bf16[16,4096]{1,0:T(8,128)(2,1)} %copy-done.7) | copy-start | bytes 393220
  51.7 24.8 %copy-start.6 = (bf16[256,1024]{1,0:T(8,128)(2,1)S(1)}, bf16[256,1024]{1,0:T(8,128)(2,1)}, u32[]{:S(2)}) copy-start(bf16[256,1024]{1,0:T(8,128)(2,1)} %residual_ref.1) | copy-start | bytes 1572868
  51.7 24.8 %copy-start.10 = (bf16[64,1024]{1,0:T(8,128)(2,1)S(1)}, bf16[64,1024]{1,0:T(8,128)(2,1)}, u32[]{:S(2)}) copy-start(bf16[64,1024]{1,0:T(8,128)(2,1)} %copy-done.9) | copy-start | bytes 393220
  51.7 13.4 %collective-permute-start.21 = (bf16[128,1024]{1,0:T(8,128)(2,1)}, bf16[128,1024]{1,0:T(8,128)(2,1)S(1)}, u32[]{:S(2)}, u32[]{:S(2)}) collective-permute-start(bf16[128,1024]{1,0:T(8,128)(2,1)} %get-tuple-element.49), channel_id=1, source_target_pairs={{0,2},{2,0},{1,3},{3,1},{4,6},{6,4},{5,7},{7,5},{8,10},{10,8},{9,1... | collective-permute-start | bytes 786440 | tf_op jit(solution)/shard_map/ppermute | solution.py:210
  53.3 1.4 %collective-permute-start.18 = (bf16[16,4096]{1,0:T(8,128)(2,1)S(1)}, bf16[16,4096]{1,0:T(8,128)(2,1)S(1)}, u32[]{:S(2)}, u32[]{:S(2)}) collective-permute-start(bf16[16,4096]{1,0:T(8,128)(2,1)S(1)} %get-tuple-element.74.refs_0_), channel_id=1, source_target_pairs={{0,1},{1,0},{2,3},{3,2},{4,5},{5,4},{6,7},{7,6},{8,9},{9,8},{10,11... | collective-permute-start | bytes 393224 | tf_op jit(solution)/shard_map/ppermute | solution.py:191
  53.4 1.5 %collective-permute-start.19 = (bf16[16,4096]{1,0:T(8,128)(2,1)S(1)}, bf16[16,4096]{1,0:T(8,128)(2,1)S(1)}, u32[]{:S(2)}, u32[]{:S(2)}) collective-permute-start(bf16[16,4096]{1,0:T(8,128)(2,1)S(1)} %get-tuple-element.73.refs_2_), channel_id=1, source_target_pairs={{0,1},{1,0},{2,3},{3,2},{4,5},{5,4},{6,7},{7,6},{8,9},{9,8},{10,11... | collective-permute-start | bytes 393224 | tf_op jit(solution)/shard_map/ppermute | solution.py:191
  53.9 3.9 %copy-start.12 = (f32[64,64]{1,0:T(8,128)}, f32[64,64]{1,0:T(8,128)S(1)}, u32[]{:S(2)}) copy-start(f32[64,64]{1,0:T(8,128)S(1)} %get-tuple-element.85) | copy-start | bytes 49156
  53.9 4.0 %copy-start.13 = (f32[64,64]{1,0:T(8,128)}, f32[64,64]{1,0:T(8,128)S(1)}, u32[]{:S(2)}) copy-start(f32[64,64]{1,0:T(8,128)S(1)} %get-tuple-element.86) | copy-start | bytes 49156
  57.2 0.6 copy-start.11
  57.9 6.4 %collective-permute-start.20 = (f32[256,64]{1,0:T(8,128)S(1)}, f32[256,64]{1,0:T(8,128)S(1)}, u32[]{:S(2)}, u32[]{:S(2)}) collective-permute-start(f32[256,64]{1,0:T(8,128)S(1)} %fusion), channel_id=1, source_target_pairs={{0,2},{2,0},{1,3},{3,1},{4,6},{6,4},{5,7},{7,5},{8,10},{10,8},{9,1... | collective-permute-start | bytes 196616 | tf_op jit(solution)/shard_map/ppermute | solution.py:210
  59.4 10.8 %collective-permute-start.23 = (bf16[64,1024]{1,0:T(8,128)(2,1)}, bf16[64,1024]{1,0:T(8,128)(2,1)S(1)}, u32[]{:S(2)}, u32[]{:S(2)}) collective-permute-start(bf16[64,1024]{1,0:T(8,128)(2,1)} %copy-done.11), channel_id=1, source_target_pairs={{0,2},{2,0},{1,3},{3,1},{4,6},{6,4},{5,7},{7,5},{8,10},{10,8},{9,1... | collective-permute-start | bytes 393224 | tf_op jit(solution)/shard_map/ppermute | solution.py:210
  65.1 5.0 %collective-permute-start.22 = (f32[256,64]{1,0:T(8,128)S(1)}, f32[256,64]{1,0:T(8,128)S(1)}, u32[]{:S(2)}, u32[]{:S(2)}) collective-permute-start(f32[256,64]{1,0:T(8,128)S(1)} %add_select_fusion), channel_id=1, source_target_pairs={{0,4},{4,0},{8,12},{12,8},{1,5},{5,1},{9,13},{13,9},{2,6},{6,2},{1... | collective-permute-start | bytes 196616 | tf_op jit(solution)/shard_map/ppermute | solution.py:260
  70.2 5.9 %collective-permute-start.24 = (f32[256,64]{1,0:T(8,128)S(1)}, f32[256,64]{1,0:T(8,128)S(1)}, u32[]{:S(2)}, u32[]{:S(2)}) collective-permute-start(f32[256,64]{1,0:T(8,128)S(1)} %add.27), channel_id=1, source_target_pairs={{0,8},{8,0},{4,12},{12,4},{1,9},{9,1},{5,13},{13,5},{2,10},{10,2},... | collective-permute-start | bytes 196616 | tf_op jit(solution)/shard_map/ppermute | solution.py:262

commit v4 on v1

v4 whole, which is shorter than its diff:
```python
import functools

import jax
import jax.numpy as jnp
from jax import lax
from jax.experimental import pallas as pl
from jax.experimental.pallas import tpu as pltpu
from jax.sharding import PartitionSpec as P

F32 = jnp.float32
BF16 = jnp.bfloat16


def low_rank_weights(low, slot, live, slots, rank_width):
    kept = jnp.arange(rank_width, dtype=jnp.int32)[None, :] < live[:, None]
    scaling = rank_width / live.astype(F32)
    scaled = jnp.where(kept, low * scaling[:, None], jnp.zeros((), F32)).astype(BF16)
    hot = slot[:, None] == jnp.arange(slots, dtype=jnp.int32)[None, :]
    spread = jnp.where(hot[:, :, None], scaled[:, None, :], jnp.zeros((), BF16))
    return spread.reshape(low.shape[0], slots * rank_width)


def tables(tenant, entry, live):
    ids = jnp.arange(entry.shape[0], dtype=jnp.int32)
    hot = (tenant[:, None] == ids[None, :]).astype(jnp.int32)
    return jnp.sum(hot * entry[None, :], axis=1), jnp.sum(hot * live[None, :], axis=1)


def general(rows, residual, weight, down, up, tenant, entry, live):
    own = residual.shape[0]
    cols = weight.shape[1]
    width = down.shape[1]
    slots = entry.shape[0]
    slot_all, live_all = tables(tenant, entry, live)
    part = rows.shape[0] // lax.axis_size("sub")
    mine = lax.dynamic_slice_in_dim(rows, lax.axis_index("sub") * part, part, 0)
    halves = lax.all_gather(lax.all_gather(mine, "blk", axis=0), "sub", axis=1)
    full = halves.reshape(-1, rows.shape[1])
    base = jnp.dot(full, weight, preferred_element_type=F32)
    low = lax.dot_general(
        full, down.reshape(-1, down.shape[2]), (((1,), (1,)), ((), ())), preferred_element_type=F32
    )
    held = down.shape[0]
    places = lax.axis_index("blk") * held + jnp.arange(held, dtype=jnp.int32)
    here = slot_all[:, None] == places[None, :]
    low = jnp.sum(
        jnp.where(here[:, :, None], low.reshape(-1, held, width), jnp.zeros((), F32)), axis=1
    )
    low = lax.psum(lax.psum_scatter(low, "split", scatter_dimension=0, tiled=True), "blk")
    base = lax.psum_scatter(base, "split", scatter_dimension=0, tiled=True)
    start = lax.axis_index("split") * own
    spread = low_rank_weights(
        low,
        lax.dynamic_slice_in_dim(slot_all, start, own, 0),
        lax.dynamic_slice_in_dim(live_all, start, own, 0),
        slots,
        width,
    )
    ups = lax.all_gather(up, "split", axis=0, tiled=True).reshape(slots * width, cols)
    lora = jnp.dot(spread, ups, preferred_element_type=F32)
    return (residual.astype(F32) + base + lora).astype(BF16)


SWAP = [(0, 1), (1, 0)]
NEAR = [(0, 1), (1, 0), (2, 3), (3, 2)]
FAR = [(0, 2), (2, 0), (1, 3), (3, 1)]
VMEM = pl.BlockSpec(memory_space=pltpu.VMEM)
SMEM = pl.BlockSpec(memory_space=pltpu.SMEM)
HBM = pl.BlockSpec(memory_space=pltpu.HBM)
COST = pl.CostEstimate(flops=0, bytes_accessed=0, transcendentals=0)
PARAMS = pltpu.CompilerParams(vmem_limit_bytes=12 * 1024 * 1024)


def shape(dims, dtype):
    return jax.ShapeDtypeStruct(dims, dtype)


def column_tiles(cols):
    tile = 256 if cols % 256 == 0 else cols
    return [slice(at, at + tile) for at in range(0, cols, tile)]


def dot(a, b):
    return jnp.dot(a, b, preferred_element_type=F32)


def cut_kernel(flags_ref, rows_ref, first_ref, second_ref, half_ref, sems):
    half = half_ref.shape[0]
    step = half // 2
    start = pl.multiple_of(flags_ref[1] * half, half)
    copies = [
        pltpu.make_async_copy(rows_ref.at[pl.ds(start, step)], first_ref, sems.at[0]),
        pltpu.make_async_copy(rows_ref.at[pl.ds(start + step, step)], second_ref, sems.at[1]),
        pltpu.make_async_copy(rows_ref.at[pl.ds(start, half)], half_ref, sems.at[2]),
    ]
    for copy in copies:
        copy.start()
    for copy in copies:
        copy.wait()


def own_kernel(flags_ref, weight_ref, down_ref, rows_ref, sum_ref, low_ref, block):
    step = block.shape[0] // 4
    c = flags_ref[1]
    for i in range(4):
        half = c if i % 2 == 0 else 1 - c
        start = pl.multiple_of(half * (2 * step) + (i // 2) * step, step)
        block[i * step : (i + 1) * step] = rows_ref[pl.ds(start, step)]
    low_ref[...] = dot(block[...], down_ref[...])
    for tile in column_tiles(weight_ref.shape[1]):
        sum_ref[:, tile] = dot(block[...], weight_ref[:, tile])


def part(home, held, value, keep_ref, send_ref, rows, tile):
    @pl.when(home)
    def _():
        keep_ref[rows, tile] = held
        send_ref[rows, tile] = value.astype(BF16)

    @pl.when(jnp.logical_not(home))
    def _():
        keep_ref[rows, tile] = value
        send_ref[rows, tile] = held.astype(BF16)


def piece_kernel(flags_ref, weight_ref, down_ref, held_ref, *refs):
    *pieces, keep_ref, send_ref, low_ref, block = refs
    at = 0
    for ref in pieces:
        block[at : at + ref.shape[0]] = ref[...]
        at += ref.shape[0]
    low_ref[...] = dot(block[...], down_ref[...])
    home = flags_ref[0] == 1
    rows = slice(0, at)
    for tile in column_tiles(weight_ref.shape[1]):
        value = dot(block[...], weight_ref[:, tile])
        part(home, held_ref[rows, tile], value, keep_ref, send_ref, rows, tile)


def end_kernel(
    flags_ref, weight_ref, down_ref, held_ref, own_low, low_a, low_b, *refs
):
    *pieces, keep_ref, send_ref, low_keep_ref, low_send_ref, block = refs
    size = block.shape[0]
    at = 0
    for ref in pieces:
        block[at : at + ref.shape[0]] = ref[...]
        at += ref.shape[0]
    low_c = dot(block[...], down_ref[...])
    home = flags_ref[0] == 1
    near = pl.ds(pl.multiple_of(flags_ref[2] * (2 * size), size), 2 * size)
    far = pl.ds(pl.multiple_of((1 - flags_ref[2]) * (2 * size), size), 2 * size)

    def store(near_ref, far_ref):
        near_ref[near, :] = own_low[...]
        near_ref[far, :] = low_b[: 2 * size]
        far_ref[near, :] = jnp.concatenate([low_a[...], low_b[2 * size : 3 * size]])
        far_ref[far, :] = jnp.concatenate([low_b[3 * size :], low_c])

    @pl.when(home)
    def _():
        store(low_keep_ref, low_send_ref)

    @pl.when(jnp.logical_not(home))
    def _():
        store(low_send_ref, low_keep_ref)

    rows = slice(0, size)
    for tile in column_tiles(weight_ref.shape[1]):
        value = dot(block[...], weight_ref[:, tile])
        part(home, held_ref[rows, tile], value, keep_ref, send_ref, rows, tile)


def blocks_kernel(
    flags_ref, weight_ref, down_ref, held_ref, near_ref, near_other_ref, far_ref, far_other_ref,
    last_ref, last_other_ref, keep_ref, send_ref, hold_ref, low_ref, block,
):
    step = far_ref.shape[0]
    pieces = [
        near_ref[:step], near_other_ref[:step], near_ref[step:], near_other_ref[step:],
        far_ref[...], far_other_ref[...], last_ref[...], last_other_ref[...],
    ]
    for i, piece in enumerate(pieces):
        block[i * step : (i + 1) * step] = piece
    low_ref[...] = dot(block[...], down_ref[...])
    home = flags_ref[0] == 1
    size = 2 * step
    for tile in column_tiles(weight_ref.shape[1]):
        value = dot(block[...], weight_ref[:, tile])
        hold_ref[:, tile] = value[size : 2 * size]
        held = held_ref[size : 2 * size, tile]
        part(home, held, value[2 * size : 3 * size], keep_ref, send_ref, slice(0, size), tile)
        part(home, value[:size], value[3 * size :], keep_ref, send_ref, slice(size, 2 * size), tile)


def final_kernel(flags_ref, residual_ref, low_ref, low_got_ref, factor_ref, ups_ref, *refs):
    *parts, out_ref, lora_ref = refs
    low = low_ref[...] + low_got_ref[...]
    lora = dot((low * factor_ref[0]).astype(BF16), ups_ref[0])
    for slot in range(1, ups_ref.shape[0]):
        lora += dot((low * factor_ref[slot]).astype(BF16), ups_ref[slot])
    lora_ref[...] = lora
    step = out_ref.shape[0] // 8
    odd, c = flags_ref[2], flags_ref[1]
    at = 0
    for keep, got in zip(parts[::2], parts[1::2]):
        for begin in range(0, keep.shape[0], step):
            second, piece, other = at // 4, at // 2 % 2, at % 2
            block = (1 - odd if second else odd) * (4 * step)
            half = (1 - c if other else c) * (2 * step)
            to = pl.ds(pl.multiple_of(block + half + piece * step, step), step)
            lora = pl.ds(pl.multiple_of(block + (2 * piece + other) * step, step), step)
            here = slice(begin, begin + step)
            out_ref[to, :] = (
                residual_ref[to, :].astype(F32)
                + lora_ref[lora, :]
                + keep[here, :]
                + got[here, :].astype(F32)
            ).astype(BF16)
            at += 1


def call(kernel, outs, in_specs, operands, scratch=()):
    return pl.pallas_call(
        kernel,
        out_shape=outs,
        in_specs=in_specs,
        out_specs=jax.tree.map(lambda _: VMEM, outs),
        scratch_shapes=scratch,
        compiler_params=PARAMS,
        cost_estimate=COST,
    )(*operands)


def line(rows, residual, weight, down, up, tenant, entry, live):
    z, x, c = lax.axis_index("blk"), lax.axis_index("split"), lax.axis_index("sub")
    block_rows, feats = rows.shape
    width = down.shape[1]
    own, cols = residual.shape
    slots = entry.shape[0]
    home = (z // 2) == x
    flags = jnp.stack([home.astype(jnp.int32), c, z % 2])
    half, step = block_rows // 2, block_rows // 4
    barrier = lax.optimization_barrier

    def over_core(value):
        return lax.ppermute(value, "sub", SWAP)

    def over_x(value):
        return lax.ppermute(value, "split", SWAP)

    def along(value, pairs):
        return lax.ppermute(value, "blk", pairs)

    def rearranged(value):
        value = lax.dynamic_slice_in_dim(value, x * own, own, 0).reshape(2, 2, 2, step)
        value = jnp.where(c == 0, value, value[:, ::-1])
        return value.transpose(0, 2, 1, 3).reshape(own)

    slot_all, live_all = tables(tenant, entry, live)
    slot, rank = rearranged(slot_all), rearranged(live_all)
    kept = jnp.arange(width, dtype=jnp.int32)[None, :] < rank[:, None]
    scaling = jnp.where(kept, (width / rank.astype(F32))[:, None], jnp.zeros((), F32))
    hot = slot[None, :] == jnp.arange(slots, dtype=jnp.int32)[:, None]
    factor = jnp.where(hot[:, :, None], scaling[None], jnp.zeros((), F32))
    here = jnp.broadcast_to((slot == z)[:, None], (own, width)).astype(F32)
    down_map = down[0].T

    first, second, both = call(
        cut_kernel,
        [shape((step, feats), BF16), shape((step, feats), BF16), shape((half, feats), BF16)],
        [SMEM, HBM],
        [flags, rows],
        [pltpu.SemaphoreType.DMA((3,))],
    )
    far = [along(first, FAR), along(second, FAR)]
    near = along(both, NEAR)
    up_other = over_x(up)
    own_sum, own_low = call(
        own_kernel,
        [shape((block_rows, cols), F32), shape((block_rows, width), F32)],
        [SMEM] + [VMEM] * 3,
        [flags, weight, down_map, rows],
        [pltpu.VMEM((block_rows, feats), BF16)],
    )
    weight, own_sum = barrier((weight, own_sum))
    ups = jnp.where(x == 0, jnp.concatenate([up, up_other]), jnp.concatenate([up_other, up]))
    far[0], own_sum = barrier((far[0], own_sum))

    def in_quarters(piece):
        quarters = [piece[: step // 2], piece[step // 2 :]]
        return quarters + [over_core(quarter) for quarter in quarters]

    def parted(count):
        return [shape((count, cols), F32), shape((count, cols), BF16)]

    last = [along(far[0], NEAR)]
    keep_a, send_a, low_a = call(
        piece_kernel,
        parted(half) + [shape((half, width), F32)],
        [SMEM] + [VMEM] * 7,
        [flags, weight, down_map, own_sum] + in_quarters(far[0]),
        [pltpu.VMEM((half, feats), BF16)],
    )
    got_a = over_x(send_a)
    far[1], last[0], near, got_a, keep_a, own_sum, ups, factor, here = barrier(
        (far[1], last[0], near, got_a, keep_a, own_sum, ups, factor, here)
    )

    last.append(along(far[1], NEAR))
    keep_b, send_b, hold, low_b = call(
        blocks_kernel,
        parted(block_rows) + [shape((half, cols), F32), shape((2 * block_rows, width), F32)],
        [SMEM] + [VMEM] * 9,
        [flags, weight, down_map, own_sum, near, over_core(near), far[1], over_core(far[1])]
        + [last[0], over_core(last[0])],
        [pltpu.VMEM((2 * block_rows, feats), BF16)],
    )
    got_b = over_x(send_b)
    last[1], send_b, keep_b, hold = barrier((last[1], send_b, keep_b, hold))

    keep_c, send_c, low_keep, low_send = call(
        end_kernel,
        parted(half) + [shape((own, width), F32)] * 2,
        [SMEM] + [VMEM] * 10,
        [flags, weight, down_map, hold, own_low, low_a, low_b] + in_quarters(last[1]),
        [pltpu.VMEM((half, feats), BF16)],
    )
    got_c = over_x(send_c)
    low_send, got_b = barrier((low_send, got_b))
    low = (low_keep + over_x(low_send)) * here
    low = low + along(low, NEAR)
    low, got_c = barrier((low, got_c))
    parts = [keep_a, got_a, keep_b, got_b, keep_c, got_c]
    return call(
        final_kernel,
        shape(residual.shape, BF16),
        [SMEM] + [VMEM] * (5 + len(parts)),
        [flags, residual, low, along(low, FAR), factor, ups] + parts,
        [pltpu.VMEM(residual.shape, F32)],
    )


def shards(rows, residual, weight, down, up, tenant, entry, live):
    sizes = [lax.axis_size(name) for name in ("blk", "split", "sub")]
    plan = line if sizes == [4, 2, 2] and down.shape[0] == 1 else general
    return plan(rows, residual, weight, down, up, tenant, entry, live)


def solution(mesh):
    in_specs = (
        P(("groups", "blk"), "split"),
        P(("groups", "split"), ("blk", "sub")),
        P("split", ("blk", "sub")),
        P("blk", None, "split"),
        P("split", None, ("blk", "sub")),
        P("groups"),
        P(),
        P(),
    )
    out_specs = P(("groups", "split"), ("blk", "sub"))
    return jax.shard_map(shards, mesh=mesh, in_specs=in_specs, out_specs=out_specs, check_vma=False)
```

time: 68.5 us -> 79 us (1.15)
  Pallas kernels: 0 us -> 19.9 us
  matrix products: 16.5 us -> 0 us
  local copies, waits for them, and re-layouts: 1.44 us -> 13.1 us
  starting transfers between devices: 23.7 us -> 17.7 us
  waiting for transfers between devices: 23.1 us -> 25.2 us
    pallas_call x0 -> x6, Pallas kernels: none -> 19.9 us  [call(): pl.pallas_call(kernel, out_shape=outs, in_specs=in_specs, out_specs=jax.t...]
    dot_general x9 -> x0, matrix products: 16.5 us -> none  [the longest x4 12 us: products(): base = jnp.dot(block, weight, preferred_element_type=F32)]
    unnamed x16 -> x21, local copies, waits for them, and re-layouts: 0.04 us -> 11.4 us
    ppermute x20 -> x19, starting transfers between devices: 23.7 us -> 17.7 us  [the longest x7 9.48 us: along(): return lax.ppermute(value, 'blk', pairs)]
    ppermute x20 -> x19, waiting for transfers between devices: 23.1 us -> 25.2 us  [the longest x7 14.3 us: along(): return lax.ppermute(value, 'blk', pairs)]
    convert_element_type x3 -> x1, other arithmetic: 0.98 us -> 0.01 us  [line(): here = jnp.broadcast_to((slot == z)[:, None], (own, width)).astype(F32)]
    select_n x12 -> x3, other arithmetic: 1.76 us -> 1.64 us  [the longest x1 1.31 us: line(): jnp.where(x == 0, jnp.concatenate([up, up_other]), jnp.concatenate([up_ot...]
  transfers between devices with their start and end apart: 20 -> 19, of which waited for: 9 -> 12; matrix products, arithmetic and copies ran while one was open for 25% -> 7% of each run, Pallas kernels for 0% -> 21%
where the time goes in v4:
time: 79 us; the launch traced here: 78.7 us
  waiting for transfers between devices  25.2 us (32%)
  Pallas kernels  19.9 us (25%)
  starting transfers between devices  17.7 us (22%)
  local copies, waits for them, and re-layouts  13.1 us (17%)
  other arithmetic  2.56 us (3%)
    pallas_call x6, Pallas kernels, call(): pl.pallas_call(kernel, out_shape=outs, in_specs=in_specs, out_specs=jax.t...  19.9 us
    ppermute x7, waiting for transfers between devices, along(): return lax.ppermute(value, 'blk', pairs)  14.3 us
    unnamed x21, local copies, waits for them, and re-layouts  11.4 us
    ppermute x7, starting transfers between devices, along(): return lax.ppermute(value, 'blk', pairs)  9.48 us
    ppermute x5, waiting for transfers between devices, over_x(): return lax.ppermute(value, 'split', SWAP)  8.48 us
    ppermute x5, starting transfers between devices, over_x(): return lax.ppermute(value, 'split', SWAP)  6.42 us
    ppermute x7, waiting for transfers between devices, over_core(): return lax.ppermute(value, 'sub', SWAP)  2.45 us
    ppermute x7, starting transfers between devices, over_core(): return lax.ppermute(value, 'sub', SWAP)  1.77 us
  transfers between devices with their start and end apart: 19, of which 12 were waited for; matrix products, arithmetic and copies ran while one was open for 7% of the time, Pallas kernels for 21%

profile of v4, /device:TPU:0, one launch (start us, length us, event | category | flops | bytes accessed | tf_op | source)
XLA Modules:
  0.0 78.7 jit_solution(7443440660076733264)
XLA Ops:
  0.1 1.2 %copy-done.3 = bf16[128,4096]{1,0:T(8,128)(2,1)S(1)} copy-done((bf16[128,4096]{1,0:T(8,128)(2,1)S(1)}, bf16[128,4096]{1,0:T(8,128)(2,1)}, u32[]{:S(2)}) %copy-start.3) | copy-done | bytes 1048600
  1.3 1.5 %shard_map.83 = (bf16[32,4096]{1,0:T(8,128)(2,1)S(1)}, bf16[32,4096]{1,0:T(8,128)(2,1)}, bf16[64,4096]{1,0:T(8,128)(2,1)}) custom-call(s32[3]{0:T(128)S(1)} %pad_add_fusion.flags_ref, bf16[128,4096]{1,0:T(8,128)(2,1)S(1)} %copy-done.3), custom_call_target="tpu_custom_call" | custom-call | tf_op jit(solution)/shard_map/pallas_call | solution.py:224
  2.8 4.1 %collective-permute-start.1 = (bf16[32,4096]{1,0:T(8,128)(2,1)S(1)}, bf16[32,4096]{1,0:T(8,128)(2,1)}, u32[]{:S(2)}, u32[]{:S(2)}) collective-permute-start(bf16[32,4096]{1,0:T(8,128)(2,1)S(1)} %get-tuple-element.44), channel_id=1, source_target_pairs={{0,8},{8,0},{4,12},{12,4},{1,9},{9,1},{5,13},{13,5},{2,10},{10,2},... | collective-permute-start | bytes 786440 | tf_op jit(solution)/shard_map/ppermute | solution.py:253
  6.9 1.6 %collective-permute-start.3 = (bf16[64,4096]{1,0:T(8,128)(2,1)}, bf16[64,4096]{1,0:T(8,128)(2,1)S(1)}, u32[]{:S(2)}, u32[]{:S(2)}) collective-permute-start(bf16[64,4096]{1,0:T(8,128)(2,1)} %get-tuple-element.47), channel_id=1, source_target_pairs={{0,4},{4,0},{8,12},{12,8},{1,5},{5,1},{9,13},{13,9},{2,6},{6,2},{1... | collective-permute-start | bytes 1572872 | tf_op jit(solution)/shard_map/ppermute | solution.py:253
  8.5 0.3 collective-permute-start
  8.9 1.5 %collective-permute-start.7 = (bf16[2,64,1024]{2,1,0:T(8,128)(2,1)}, bf16[2,64,1024]{2,1,0:T(8,128)(2,1)}, u32[]{:S(2)}, u32[]{:S(2)}) collective-permute-start(bf16[2,64,1024]{2,1,0:T(8,128)(2,1)} %param.12), channel_id=1, source_target_pairs={{0,2},{2,0},{1,3},{3,1},{4,6},{6,4},{5,7},{7,5},{8,10},{10,8},{9,1... | collective-permute-start | bytes 786440 | tf_op jit(solution)/shard_map/ppermute | solution.py:250
  10.3 0.8 select_reduce_fusion.1
  11.2 0.1 reshape.77
  11.4 0.1 reshape.78
  11.5 0.1 lt.32
  11.6 0.1 eq.60
  11.7 1.5 %copy.14 = bf16[1,64,4096]{1,2,0:T(8,128)(2,1)S(1)} copy(bf16[1,64,4096]{2,1,0:T(8,128)(2,1)} %param.11) | data formatting | bytes 1048576 | tf_op args[3]
  13.2 3.4 %copy-done = bf16[4096,1024]{1,0:T(8,128)(2,1)S(1)} copy-done((bf16[4096,1024]{1,0:T(8,128)(2,1)S(1)}, bf16[4096,1024]{1,0:T(8,128)(2,1)}, u32[]{:S(2)}) %copy-start) | copy-done | bytes 8388632
  16.6 1.2 %copy-done.4 = bf16[128,4096]{1,0:T(8,128)(2,1)S(1)} copy-done((bf16[128,4096]{1,0:T(8,128)(2,1)S(1)}, bf16[128,4096]{1,0:T(8,128)(2,1)}, u32[]{:S(2)}) %copy-start.4) | copy-done | bytes 1048600
  17.8 2.1 %shard_map.82 = (f32[128,1024]{1,0:T(8,128)S(1)}, f32[128,64]{1,0:T(8,128)S(1)}) custom-call(s32[3]{0:T(128)S(1)} %pad_add_fusion.flags_ref, bf16[4096,1024]{1,0:T(8,128)(2,1)S(1)} %copy-done, bf16[4096,64]{1,0:T(8,128)(2,1)S(1)} %bitcast.10, bf16[128,4096]{1,0:T(8,128)(2,1)S(1)} %copy-done.4), custom_call_target="tpu_custom_call" | custom-call | tf_op jit(solution)/shard_map/pallas_call | solution.py:224
  19.9 0.1 fusion
  20.1 1.1 %fusion.4 = (bf16[16,4096]{1,0:T(8,128)(2,1)S(1)}, bf16[16,4096]{1,0:T(8,128)(2,1)S(1)}) fusion(bf16[32,4096]{1,0:T(8,128)(2,1)} %collective-permute-done.1), kind=kLoop, calls=%fused_computation.17 | loop fusion | bytes 524288 | tf_op jit(solution)/shard_map/slice | solution.py:291
  21.3 0.5 collective-permute-start.5
  21.8 0.2 broadcast_select_fusion.factor_ref
  22.0 0.6 collective-permute-done.4.refs_2_
  22.6 0.4 collective-permute-start.2
  23.1 4.3 %shard_map.84 = (f32[64,1024]{1,0:T(8,128)S(1)}, bf16[64,1024]{1,0:T(8,128)(2,1)}, f32[64,64]{1,0:T(8,128)S(1)}) custom-call(s32[3]{0:T(128)S(1)} %pad_add_fusion.flags_ref, bf16[4096,1024]{1,0:T(8,128)(2,1)S(1)} %copy-done.1, bf16[4096,64]{1,0:T(8,128)(2,1)S(1)} %bitcast.11, f32[128,1024]{1,0:T(8,128)S(1)} %get-tuple-element.52.held_ref, ...), custom_call_target="tpu_custom_call" | custom-call | tf_op jit(solution)/shard_map/pallas_call | solution.py:224
  27.4 0.6 copy-done.8
  28.0 1.3 %collective-permute-start.6 = (bf16[64,1024]{1,0:T(8,128)(2,1)}, bf16[64,1024]{1,0:T(8,128)(2,1)S(1)}, u32[]{:S(2)}, u32[]{:S(2)}) collective-permute-start(bf16[64,1024]{1,0:T(8,128)(2,1)} %get-tuple-element.49), channel_id=1, source_target_pairs={{0,2},{2,0},{1,3},{3,1},{4,6},{6,4},{5,7},{7,5},{8,10},{10,8},{9,1... | collective-permute-start | bytes 393224 | tf_op jit(solution)/shard_map/ppermute | solution.py:250
  29.3 1.3 %maximum_select_fusion.ups_ref = bf16[4,64,1024]{2,1,0:T(8,128)(2,1)S(1)} fusion(bf16[2,64,1024]{2,1,0:T(8,128)(2,1)} %collective-permute-done.7, bf16[2,64,1024]{2,1,0:T(8,128)(2,1)} %param.12, pred[]{:T(512)S(6)} %eq.55), kind=kLoop, calls=%fused_computation | loop fusion | flops 786432 | bytes 1048577 | tf_op jit(solution)/shard_map/jit(_where)/select_n | solution.py:287
  30.7 3.0 %collective-permute-done.6.refs_1_ = bf16[64,1024]{1,0:T(8,128)(2,1)S(1)} collective-permute-done((bf16[64,1024]{1,0:T(8,128)(2,1)}, bf16[64,1024]{1,0:T(8,128)(2,1)S(1)}, u32[]{:S(2)}, u32[]{:S(2)}) %collective-permute-start.6) | collective-permute-done | bytes 131104 | tf_op jit(solution)/shard_map/ppermute | solution.py:250
  33.6 2.6 %collective-permute-done.2.last_ref = bf16[32,4096]{1,0:T(8,128)(2,1)S(1)} collective-permute-done((bf16[32,4096]{1,0:T(8,128)(2,1)}, bf16[32,4096]{1,0:T(8,128)(2,1)S(1)}, u32[]{:S(2)}, u32[]{:S(2)}) %collective-permute-start.2) | collective-permute-done | bytes 262176 | tf_op jit(solution)/shard_map/ppermute | solution.py:253
  36.2 0.1 broadcast_in_dim.52
  36.4 0.5 collective-permute-start.10
  37.0 1.3 %collective-permute-start.8 = (bf16[32,4096]{1,0:T(8,128)(2,1)S(1)}, bf16[32,4096]{1,0:T(8,128)(2,1)S(1)}, u32[]{:S(2)}, u32[]{:S(2)}) collective-permute-start(bf16[32,4096]{1,0:T(8,128)(2,1)S(1)} %collective-permute-done.far_ref), channel_id=1, source_target_pairs={{0,4},{4,0},{8,12},{12,8},{1,5},{5,1},{9,13},{13,9},{2,6},{6,2},{1... | collective-permute-start | bytes 786440 | tf_op jit(solution)/shard_map/ppermute | solution.py:253
  38.3 0.4 collective-permute-done.10.far_other_ref
  38.7 0.4 collective-permute-done.11.last_other_ref
  39.1 3.4 %copy-done.2 = bf16[4096,1024]{1,0:T(8,128)(2,1)S(1)} copy-done((bf16[4096,1024]{1,0:T(8,128)(2,1)S(1)}, bf16[4096,1024]{1,0:T(8,128)(2,1)}, u32[]{:S(2)}) %copy-start.2) | copy-done | bytes 8388632
  42.4 6.1 %shard_map.85 = (f32[128,1024]{1,0:T(8,128)S(1)}, bf16[128,1024]{1,0:T(8,128)(2,1)S(1)}, f32[64,1024]{1,0:T(8,128)S(1)}, f32[256,64]{1,0:T(8,128)S(1)}) custom-call(s32[3]{0:T(128)S(1)} %pad_add_fusion.flags_ref, bf16[4096,1024]{1,0:T(8,128)(2,1)S(1)} %copy-done.2, bf16[4096,64]{1,0:T(8,128)(2,1)S(1)} %bitcast.12, ...), custom_call_target="tpu_custom_call" | custom-call | tf_op jit(solution)/shard_map/pallas_call | solution.py:224
  48.5 1.6 %collective-permute-start.14 = (bf16[128,1024]{1,0:T(8,128)(2,1)S(1)}, bf16[128,1024]{1,0:T(8,128)(2,1)S(1)}, u32[]{:S(2)}, u32[]{:S(2)}) collective-permute-start(bf16[128,1024]{1,0:T(8,128)(2,1)S(1)} %get-tuple-element.55), channel_id=1, source_target_pairs={{0,2},{2,0},{1,3},{3,1},{4,6},{6,4},{5,7},{7,5},{8,10},{10,8},{9,1... | collective-permute-start | bytes 786440 | tf_op jit(solution)/shard_map/ppermute | solution.py:250
  50.2 0.5 collective-permute-start.13
  50.7 0.8 %collective-permute-done.12.refs_2_ = bf16[16,4096]{1,0:T(8,128)(2,1)S(1)} collective-permute-done((bf16[16,4096]{1,0:T(8,128)(2,1)S(1)}, bf16[16,4096]{1,0:T(8,128)(2,1)S(1)}, u32[]{:S(2)}, u32[]{:S(2)}) %collective-permute-start.12) | collective-permute-done | bytes 131104 | tf_op jit(solution)/shard_map/ppermute | solution.py:247
  51.6 0.2 collective-permute-done.13.refs_3_
  51.8 3.7 %shard_map.86 = (f32[64,1024]{1,0:T(8,128)S(1)}, bf16[64,1024]{1,0:T(8,128)(2,1)S(1)}, f32[256,64]{1,0:T(8,128)S(1)}, f32[256,64]{1,0:T(8,128)S(1)}) custom-call(s32[3]{0:T(128)S(1)} %pad_add_fusion.flags_ref, bf16[4096,1024]{1,0:T(8,128)(2,1)S(1)} %copy-done.2, bf16[4096,64]{1,0:T(8,128)(2,1)S(1)} %bitcast.13, f32[64,1024]{1,0:T(8,128)S(1)} %get-tuple-element.58.held_ref, ...), custom_call_target="tpu_custom_call" | custom-call | tf_op jit(solution)/shard_map/pallas_call | solution.py:224
  55.5 1.4 %collective-permute-done.14.refs_3_ = bf16[128,1024]{1,0:T(8,128)(2,1)S(1)} collective-permute-done((bf16[128,1024]{1,0:T(8,128)(2,1)S(1)}, bf16[128,1024]{1,0:T(8,128)(2,1)S(1)}, u32[]{:S(2)}, u32[]{:S(2)}) %collective-permute-start.14) | collective-permute-done | bytes 262176 | tf_op jit(solution)/shard_map/ppermute | solution.py:250
  56.9 1.6 %collective-permute-start.15 = (f32[256,64]{1,0:T(8,128)S(1)}, f32[256,64]{1,0:T(8,128)S(1)}, u32[]{:S(2)}, u32[]{:S(2)}) collective-permute-start(f32[256,64]{1,0:T(8,128)S(1)} %get-tuple-element.65), channel_id=1, source_target_pairs={{0,2},{2,0},{1,3},{3,1},{4,6},{6,4},{5,7},{7,5},{8,10},{10,8},{9,1... | collective-permute-start | bytes 196616 | tf_op jit(solution)/shard_map/ppermute | solution.py:250
  58.5 0.5 collective-permute-start.17
  59.0 4.1 %collective-permute-done.15 = f32[256,64]{1,0:T(8,128)S(1)} collective-permute-done((f32[256,64]{1,0:T(8,128)S(1)}, f32[256,64]{1,0:T(8,128)S(1)}, u32[]{:S(2)}, u32[]{:S(2)}) %collective-permute-start.15) | collective-permute-done | bytes 65568 | tf_op jit(solution)/shard_map/ppermute | solution.py:250
  63.1 1.3 %collective-permute-start.16 = (f32[256,64]{1,0:T(8,128)S(1)}, f32[256,64]{1,0:T(8,128)S(1)}, u32[]{:S(2)}, u32[]{:S(2)}) collective-permute-start(f32[256,64]{1,0:T(8,128)S(1)} %add_multiply_fusion), channel_id=1, source_target_pairs={{0,4},{4,0},{8,12},{12,8},{1,5},{5,1},{9,13},{13,9},{2,6},{6,2},{1... | collective-permute-start | bytes 196616 | tf_op jit(solution)/shard_map/ppermute | solution.py:253
  64.4 4.7 %collective-permute-done.16 = f32[256,64]{1,0:T(8,128)S(1)} collective-permute-done((f32[256,64]{1,0:T(8,128)S(1)}, f32[256,64]{1,0:T(8,128)S(1)}, u32[]{:S(2)}, u32[]{:S(2)}) %collective-permute-start.16) | collective-permute-done | bytes 65568 | tf_op jit(solution)/shard_map/ppermute | solution.py:253
  69.1 0.4 collective-permute-start.18
  69.5 6.9 %collective-permute-done.18.low_got_ref = f32[256,64]{1,0:T(8,128)S(1)} collective-permute-done((f32[256,64]{1,0:T(8,128)S(1)}, f32[256,64]{1,0:T(8,128)S(1)}, u32[]{:S(2)}, u32[]{:S(2)}) %collective-permute-start.18) | collective-permute-done | bytes 65568 | tf_op jit(solution)/shard_map/ppermute | solution.py:253
  76.4 2.2 %shard_map.87 = bf16[256,1024]{1,0:T(8,128)(2,1)} custom-call(s32[3]{0:T(128)S(1)} %pad_add_fusion.flags_ref, bf16[256,1024]{1,0:T(8,128)(2,1)S(1)} %copy-done.5, f32[256,64]{1,0:T(8,128)S(1)} %add.18.low_ref, f32[256,64]{1,0:T(8,128)S(1)} %collective-permute-done.18.low_got_ref, f32[4,256,64]{2,1,0:T(8,128)S(1)} %broadcast_select_fusion.factor_ref, ...), custom_call_target="tpu_custom_call" | custom-call | tf_op jit(solution)/shard_map/pallas_call | solution.py:224
  (39 shorter events, 0.7 us)
Async XLA Ops:
  0.1 1.2 %copy-start.3 = (bf16[128,4096]{1,0:T(8,128)(2,1)S(1)}, bf16[128,4096]{1,0:T(8,128)(2,1)}, u32[]{:S(2)}) copy-start(bf16[128,4096]{1,0:T(8,128)(2,1)} %rows_ref.3) | copy-start | bytes 3145732
  2.8 17.2 %collective-permute-start.1 = (bf16[32,4096]{1,0:T(8,128)(2,1)S(1)}, bf16[32,4096]{1,0:T(8,128)(2,1)}, u32[]{:S(2)}, u32[]{:S(2)}) collective-permute-start(bf16[32,4096]{1,0:T(8,128)(2,1)S(1)} %get-tuple-element.44), channel_id=1, source_target_pairs={{0,8},{8,0},{4,12},{12,4},{1,9},{9,1},{5,13},{13,5},{2,10},{10,2},... | collective-permute-start | bytes 786440 | tf_op jit(solution)/shard_map/ppermute | solution.py:253
  6.9 29.3 %collective-permute-start.3 = (bf16[64,4096]{1,0:T(8,128)(2,1)}, bf16[64,4096]{1,0:T(8,128)(2,1)S(1)}, u32[]{:S(2)}, u32[]{:S(2)}) collective-permute-start(bf16[64,4096]{1,0:T(8,128)(2,1)} %get-tuple-element.47), channel_id=1, source_target_pairs={{0,4},{4,0},{8,12},{12,8},{1,5},{5,1},{9,13},{13,9},{2,6},{6,2},{1... | collective-permute-start | bytes 1572872 | tf_op jit(solution)/shard_map/ppermute | solution.py:253
  8.5 22.1 %collective-permute-start = (bf16[32,4096]{1,0:T(8,128)(2,1)}, bf16[32,4096]{1,0:T(8,128)(2,1)S(1)}, u32[]{:S(2)}, u32[]{:S(2)}) collective-permute-start(bf16[32,4096]{1,0:T(8,128)(2,1)} %get-tuple-element.43), channel_id=1, source_target_pairs={{0,8},{8,0},{4,12},{12,4},{1,9},{9,1},{5,13},{13,5},{2,10},{10,2},... | collective-permute-start | bytes 786440 | tf_op jit(solution)/shard_map/ppermute | solution.py:253
  8.9 20.4 %collective-permute-start.7 = (bf16[2,64,1024]{2,1,0:T(8,128)(2,1)}, bf16[2,64,1024]{2,1,0:T(8,128)(2,1)}, u32[]{:S(2)}, u32[]{:S(2)}) collective-permute-start(bf16[2,64,1024]{2,1,0:T(8,128)(2,1)} %param.12), channel_id=1, source_target_pairs={{0,2},{2,0},{1,3},{3,1},{4,6},{6,4},{5,7},{7,5},{8,10},{10,8},{9,1... | collective-permute-start | bytes 786440 | tf_op jit(solution)/shard_map/ppermute | solution.py:250
  13.2 3.4 %copy-start = (bf16[4096,1024]{1,0:T(8,128)(2,1)S(1)}, bf16[4096,1024]{1,0:T(8,128)(2,1)}, u32[]{:S(2)}) copy-start(bf16[4096,1024]{1,0:T(8,128)(2,1)} %weight_ref.4) | copy-start | bytes 25165828
  16.6 1.2 %copy-start.4 = (bf16[128,4096]{1,0:T(8,128)(2,1)S(1)}, bf16[128,4096]{1,0:T(8,128)(2,1)}, u32[]{:S(2)}) copy-start(bf16[128,4096]{1,0:T(8,128)(2,1)} %rows_ref.3) | copy-start | bytes 3145732
  17.8 5.3 %copy-start.1 = (bf16[4096,1024]{1,0:T(8,128)(2,1)S(1)}, bf16[4096,1024]{1,0:T(8,128)(2,1)}, u32[]{:S(2)}) copy-start(bf16[4096,1024]{1,0:T(8,128)(2,1)} %weight_ref.4) | copy-start | bytes 25165828
  19.9 1.4 %copy-start.6 = (f32[128,64]{1,0:T(8,128)}, f32[128,64]{1,0:T(8,128)S(1)}, u32[]{:S(2)}) copy-start(f32[128,64]{1,0:T(8,128)S(1)} %get-tuple-element.59.own_low) | copy-start | bytes 98308
  21.2 1.4 %collective-permute-start.4 = (bf16[16,4096]{1,0:T(8,128)(2,1)S(1)}, bf16[16,4096]{1,0:T(8,128)(2,1)S(1)}, u32[]{:S(2)}, u32[]{:S(2)}) collective-permute-start(bf16[16,4096]{1,0:T(8,128)(2,1)S(1)} %get-tuple-element.82.refs_0_), channel_id=1, source_target_pairs={{0,1},{1,0},{2,3},{3,2},{4,5},{5,4},{6,7},{7,6},{8,9},{9,8},{10,11... | collective-permute-start | bytes 393224 | tf_op jit(solution)/shard_map/ppermute | solution.py:247
  21.3 1.8 %collective-permute-start.5 = (bf16[16,4096]{1,0:T(8,128)(2,1)S(1)}, bf16[16,4096]{1,0:T(8,128)(2,1)S(1)}, u32[]{:S(2)}, u32[]{:S(2)}) collective-permute-start(bf16[16,4096]{1,0:T(8,128)(2,1)S(1)} %get-tuple-element.81.refs_1_), channel_id=1, source_target_pairs={{0,1},{1,0},{2,3},{3,2},{4,5},{5,4},{6,7},{7,6},{8,9},{9,8},{10,11... | collective-permute-start | bytes 393224 | tf_op jit(solution)/shard_map/ppermute | solution.py:247
  22.6 13.6 %collective-permute-start.2 = (bf16[32,4096]{1,0:T(8,128)(2,1)}, bf16[32,4096]{1,0:T(8,128)(2,1)S(1)}, u32[]{:S(2)}, u32[]{:S(2)}) collective-permute-start(bf16[32,4096]{1,0:T(8,128)(2,1)} %collective-permute-done.1), channel_id=1, source_target_pairs={{0,4},{4,0},{8,12},{12,8},{1,5},{5,1},{9,13},{13,9},{2,6},{6,2},{1... | collective-permute-start | bytes 786440 | tf_op jit(solution)/shard_map/ppermute | solution.py:253
  27.4 0.6 copy-start.8
  28.0 5.7 %collective-permute-start.6 = (bf16[64,1024]{1,0:T(8,128)(2,1)}, bf16[64,1024]{1,0:T(8,128)(2,1)S(1)}, u32[]{:S(2)}, u32[]{:S(2)}) collective-permute-start(bf16[64,1024]{1,0:T(8,128)(2,1)} %get-tuple-element.49), channel_id=1, source_target_pairs={{0,2},{2,0},{1,3},{3,1},{4,6},{6,4},{5,7},{7,5},{8,10},{10,8},{9,1... | collective-permute-start | bytes 393224 | tf_op jit(solution)/shard_map/ppermute | solution.py:250
  29.3 22.5 %copy-start.7 = (f32[128,64]{1,0:T(8,128)S(1)}, f32[128,64]{1,0:T(8,128)}, u32[]{:S(2)}) copy-start(f32[128,64]{1,0:T(8,128)} %copy-done.6) | copy-start | bytes 98308
  29.3 22.5 %copy-start.9 = (f32[64,64]{1,0:T(8,128)S(1)}, f32[64,64]{1,0:T(8,128)}, u32[]{:S(2)}) copy-start(f32[64,64]{1,0:T(8,128)} %copy-done.8) | copy-start | bytes 49156
  36.3 2.7 %collective-permute-start.9 = (bf16[64,4096]{1,0:T(8,128)(2,1)S(1)}, bf16[64,4096]{1,0:T(8,128)(2,1)S(1)}, u32[]{:S(2)}, u32[]{:S(2)}) collective-permute-start(bf16[64,4096]{1,0:T(8,128)(2,1)S(1)} %collective-permute-done.3.near_ref), channel_id=1, source_target_pairs={{0,1},{1,0},{2,3},{3,2},{4,5},{5,4},{6,7},{7,6},{8,9},{9,8},{10,11... | collective-permute-start | bytes 1572872 | tf_op jit(solution)/shard_map/ppermute | solution.py:247
  36.4 2.3 %collective-permute-start.10 = (bf16[32,4096]{1,0:T(8,128)(2,1)S(1)}, bf16[32,4096]{1,0:T(8,128)(2,1)S(1)}, u32[]{:S(2)}, u32[]{:S(2)}) collective-permute-start(bf16[32,4096]{1,0:T(8,128)(2,1)S(1)} %collective-permute-done.far_ref), channel_id=1, source_target_pairs={{0,1},{1,0},{2,3},{3,2},{4,5},{5,4},{6,7},{7,6},{8,9},{9,8},{10,11... | collective-permute-start | bytes 786440 | tf_op jit(solution)/shard_map/ppermute | solution.py:247
  36.9 2.1 %collective-permute-start.11 = (bf16[32,4096]{1,0:T(8,128)(2,1)S(1)}, bf16[32,4096]{1,0:T(8,128)(2,1)S(1)}, u32[]{:S(2)}, u32[]{:S(2)}) collective-permute-start(bf16[32,4096]{1,0:T(8,128)(2,1)S(1)} %collective-permute-done.2.last_ref), channel_id=1, source_target_pairs={{0,1},{1,0},{2,3},{3,2},{4,5},{5,4},{6,7},{7,6},{8,9},{9,8},{10,11... | collective-permute-start | bytes 786440 | tf_op jit(solution)/shard_map/ppermute | solution.py:247
  37.0 13.2 %collective-permute-start.8 = (bf16[32,4096]{1,0:T(8,128)(2,1)S(1)}, bf16[32,4096]{1,0:T(8,128)(2,1)S(1)}, u32[]{:S(2)}, u32[]{:S(2)}) collective-permute-start(bf16[32,4096]{1,0:T(8,128)(2,1)S(1)} %collective-permute-done.far_ref), channel_id=1, source_target_pairs={{0,4},{4,0},{8,12},{12,8},{1,5},{5,1},{9,13},{13,9},{2,6},{6,2},{1... | collective-permute-start | bytes 786440 | tf_op jit(solution)/shard_map/ppermute | solution.py:253
  39.1 3.4 %copy-start.2 = (bf16[4096,1024]{1,0:T(8,128)(2,1)S(1)}, bf16[4096,1024]{1,0:T(8,128)(2,1)}, u32[]{:S(2)}) copy-start(bf16[4096,1024]{1,0:T(8,128)(2,1)} %weight_ref.4) | copy-start | bytes 25165828
  48.5 27.9 %copy-start.5 = (bf16[256,1024]{1,0:T(8,128)(2,1)S(1)}, bf16[256,1024]{1,0:T(8,128)(2,1)}, u32[]{:S(2)}) copy-start(bf16[256,1024]{1,0:T(8,128)(2,1)} %residual_ref.1) | copy-start | bytes 1572868
  48.5 8.4 %collective-permute-start.14 = (bf16[128,1024]{1,0:T(8,128)(2,1)S(1)}, bf16[128,1024]{1,0:T(8,128)(2,1)S(1)}, u32[]{:S(2)}, u32[]{:S(2)}) collective-permute-start(bf16[128,1024]{1,0:T(8,128)(2,1)S(1)} %get-tuple-element.55), channel_id=1, source_target_pairs={{0,2},{2,0},{1,3},{3,1},{4,6},{6,4},{5,7},{7,5},{8,10},{10,8},{9,1... | collective-permute-start | bytes 786440 | tf_op jit(solution)/shard_map/ppermute | solution.py:250
  50.2 1.4 %collective-permute-start.12 = (bf16[16,4096]{1,0:T(8,128)(2,1)S(1)}, bf16[16,4096]{1,0:T(8,128)(2,1)S(1)}, u32[]{:S(2)}, u32[]{:S(2)}) collective-permute-start(bf16[16,4096]{1,0:T(8,128)(2,1)S(1)} %get-tuple-element.80.refs_0_), channel_id=1, source_target_pairs={{0,1},{1,0},{2,3},{3,2},{4,5},{5,4},{6,7},{7,6},{8,9},{9,8},{10,11... | collective-permute-start | bytes 393224 | tf_op jit(solution)/shard_map/ppermute | solution.py:247
  50.2 1.5 %collective-permute-start.13 = (bf16[16,4096]{1,0:T(8,128)(2,1)S(1)}, bf16[16,4096]{1,0:T(8,128)(2,1)S(1)}, u32[]{:S(2)}, u32[]{:S(2)}) collective-permute-start(bf16[16,4096]{1,0:T(8,128)(2,1)S(1)} %get-tuple-element.79.refs_1_), channel_id=1, source_target_pairs={{0,1},{1,0},{2,3},{3,2},{4,5},{5,4},{6,7},{7,6},{8,9},{9,8},{10,11... | collective-permute-start | bytes 393224 | tf_op jit(solution)/shard_map/ppermute | solution.py:247
  56.9 6.1 %collective-permute-start.15 = (f32[256,64]{1,0:T(8,128)S(1)}, f32[256,64]{1,0:T(8,128)S(1)}, u32[]{:S(2)}, u32[]{:S(2)}) collective-permute-start(f32[256,64]{1,0:T(8,128)S(1)} %get-tuple-element.65), channel_id=1, source_target_pairs={{0,2},{2,0},{1,3},{3,1},{4,6},{6,4},{5,7},{7,5},{8,10},{10,8},{9,1... | collective-permute-start | bytes 196616 | tf_op jit(solution)/shard_map/ppermute | solution.py:250
  58.5 10.6 %collective-permute-start.17 = (bf16[64,1024]{1,0:T(8,128)(2,1)S(1)}, bf16[64,1024]{1,0:T(8,128)(2,1)S(1)}, u32[]{:S(2)}, u32[]{:S(2)}) collective-permute-start(bf16[64,1024]{1,0:T(8,128)(2,1)S(1)} %get-tuple-element.67), channel_id=1, source_target_pairs={{0,2},{2,0},{1,3},{3,1},{4,6},{6,4},{5,7},{7,5},{8,10},{10,8},{9,1... | collective-permute-start | bytes 393224 | tf_op jit(solution)/shard_map/ppermute | solution.py:250
  63.1 6.0 %collective-permute-start.16 = (f32[256,64]{1,0:T(8,128)S(1)}, f32[256,64]{1,0:T(8,128)S(1)}, u32[]{:S(2)}, u32[]{:S(2)}) collective-permute-start(f32[256,64]{1,0:T(8,128)S(1)} %add_multiply_fusion), channel_id=1, source_target_pairs={{0,4},{4,0},{8,12},{12,8},{1,5},{5,1},{9,13},{13,9},{2,6},{6,2},{1... | collective-permute-start | bytes 196616 | tf_op jit(solution)/shard_map/ppermute | solution.py:253
  69.1 7.3 %collective-permute-start.18 = (f32[256,64]{1,0:T(8,128)S(1)}, f32[256,64]{1,0:T(8,128)S(1)}, u32[]{:S(2)}, u32[]{:S(2)}) collective-permute-start(f32[256,64]{1,0:T(8,128)S(1)} %add.18.low_ref), channel_id=1, source_target_pairs={{0,8},{8,0},{4,12},{12,4},{1,9},{9,1},{5,13},{13,5},{2,10},{10,2},... | collective-permute-start | bytes 196616 | tf_op jit(solution)/shard_map/ppermute | solution.py:253

commit v5 on v1

v5 whole, which is shorter than its diff:
```python
import functools

import jax
import jax.numpy as jnp
from jax import lax
from jax.experimental import pallas as pl
from jax.experimental.pallas import tpu as pltpu
from jax.sharding import PartitionSpec as P

F32 = jnp.float32
BF16 = jnp.bfloat16


def low_rank_weights(low, slot, live, slots, rank_width):
    kept = jnp.arange(rank_width, dtype=jnp.int32)[None, :] < live[:, None]
    scaling = rank_width / live.astype(F32)
    scaled = jnp.where(kept, low * scaling[:, None], jnp.zeros((), F32)).astype(BF16)
    hot = slot[:, None] == jnp.arange(slots, dtype=jnp.int32)[None, :]
    spread = jnp.where(hot[:, :, None], scaled[:, None, :], jnp.zeros((), BF16))
    return spread.reshape(low.shape[0], slots * rank_width)


def tables(tenant, entry, live):
    ids = jnp.arange(entry.shape[0], dtype=jnp.int32)
    hot = (tenant[:, None] == ids[None, :]).astype(jnp.int32)
    return jnp.sum(hot * entry[None, :], axis=1), jnp.sum(hot * live[None, :], axis=1)


def general(rows, residual, weight, down, up, tenant, entry, live):
    own = residual.shape[0]
    cols = weight.shape[1]
    width = down.shape[1]
    slots = entry.shape[0]
    slot_all, live_all = tables(tenant, entry, live)
    part = rows.shape[0] // lax.axis_size("sub")
    mine = lax.dynamic_slice_in_dim(rows, lax.axis_index("sub") * part, part, 0)
    halves = lax.all_gather(lax.all_gather(mine, "blk", axis=0), "sub", axis=1)
    full = halves.reshape(-1, rows.shape[1])
    base = jnp.dot(full, weight, preferred_element_type=F32)
    low = lax.dot_general(
        full, down.reshape(-1, down.shape[2]), (((1,), (1,)), ((), ())), preferred_element_type=F32
    )
    held = down.shape[0]
    places = lax.axis_index("blk") * held + jnp.arange(held, dtype=jnp.int32)
    here = slot_all[:, None] == places[None, :]
    low = jnp.sum(
        jnp.where(here[:, :, None], low.reshape(-1, held, width), jnp.zeros((), F32)), axis=1
    )
    low = lax.psum(lax.psum_scatter(low, "split", scatter_dimension=0, tiled=True), "blk")
    base = lax.psum_scatter(base, "split", scatter_dimension=0, tiled=True)
    start = lax.axis_index("split") * own
    spread = low_rank_weights(
        low,
        lax.dynamic_slice_in_dim(slot_all, start, own, 0),
        lax.dynamic_slice_in_dim(live_all, start, own, 0),
        slots,
        width,
    )
    ups = lax.all_gather(up, "split", axis=0, tiled=True).reshape(slots * width, cols)
    lora = jnp.dot(spread, ups, preferred_element_type=F32)
    return (residual.astype(F32) + base + lora).astype(BF16)


SWAP = [(0, 1), (1, 0)]
NEAR = [(0, 1), (1, 0), (2, 3), (3, 2)]
FAR = [(0, 2), (2, 0), (1, 3), (3, 1)]
VMEM = pl.BlockSpec(memory_space=pltpu.VMEM)
SMEM = pl.BlockSpec(memory_space=pltpu.SMEM)
HBM = pl.BlockSpec(memory_space=pltpu.HBM)
COST = pl.CostEstimate(flops=0, bytes_accessed=0, transcendentals=0)
PARAMS = pltpu.CompilerParams(vmem_limit_bytes=20 * 1024 * 1024)


def shape(dims, dtype):
    return jax.ShapeDtypeStruct(dims, dtype)


def dot(a, b):
    return jnp.dot(a, b, preferred_element_type=F32)


def call(kernel, outs, in_specs, operands, scratch=()):
    return pl.pallas_call(
        kernel,
        out_shape=outs,
        in_specs=in_specs,
        out_specs=jax.tree.map(lambda _: VMEM, outs),
        scratch_shapes=scratch,
        compiler_params=PARAMS,
        cost_estimate=COST,
    )(*operands)


def column_tiles(cols):
    tile = 256 if cols % 256 == 0 else cols
    return [slice(at, at + tile) for at in range(0, cols, tile)]


def streamed_scratch(weight):
    return [
        pltpu.VMEM(weight.shape, weight.dtype),
        pltpu.SemaphoreType.DMA((len(column_tiles(weight.shape[1])),)),
    ]


def streamed(weight_ref, tiles_ref, sems):
    tiles = column_tiles(weight_ref.shape[1])
    copies = [
        pltpu.make_async_copy(weight_ref.at[:, tile], tiles_ref.at[:, tile], sems.at[i])
        for i, tile in enumerate(tiles)
    ]
    for copy in copies:
        copy.start()
    for copy, tile in zip(copies, tiles):
        copy.wait()
        yield tile, tiles_ref[:, tile]


def sum_kernel(weight_ref, *refs):
    *pieces, sum_ref, tiles_ref, sems = refs
    rows = jnp.concatenate([piece[...] for piece in pieces])
    for tile, weights in streamed(weight_ref, tiles_ref, sems):
        sum_ref[:, tile] = dot(rows, weights)


def part(home, held, value, keep_ref, send_ref, tile):
    keep_ref[:, tile] = jnp.where(home, held, value)
    send_ref[:, tile] = jnp.where(home, value, held).astype(BF16)


def part_kernel(begins, flags_ref, weight_ref, *refs):
    count = len(begins)
    *refs, tiles_ref, sems = refs
    pieces, helds, outs = refs[:count], refs[count : 2 * count], refs[2 * count :]
    rows = jnp.concatenate([piece[...] for piece in pieces])
    home = flags_ref[0] == 1
    size = pieces[0].shape[0]
    for tile, weights in streamed(weight_ref, tiles_ref, sems):
        value = dot(rows, weights)
        for i, begin in enumerate(begins):
            held = helds[i][begin : begin + size, tile]
            mine = value[i * size : (i + 1) * size]
            part(home, held, mine, outs[2 * i], outs[2 * i + 1], tile)


def end_kernel(flags_ref, weight_ref, piece_ref, held_ref, keep_ref, send_ref):
    size = piece_ref.shape[0]
    value = dot(piece_ref[...], weight_ref[...])
    part(flags_ref[0] == 1, held_ref[size:, :], value, keep_ref, send_ref, slice(None))


def low_kernel(maps_ref, *refs):
    *pieces, low_ref = refs
    rows = jnp.concatenate([piece[...] for piece in pieces])
    low_ref[...] = lax.dot_general(
        rows, maps_ref[...], (((1,), (1,)), ((), ())), preferred_element_type=F32
    )


def final_kernel(flags_ref, residual_ref, spread_ref, ups_ref, *refs):
    *parts, out_ref = refs
    lora = dot(spread_ref[...], ups_ref[...])
    step = out_ref.shape[0] // 4
    odd = flags_ref[1] == 1
    sums = [
        keep[...] + got[...].astype(F32) for keep, got in zip(parts[::2], parts[1::2])
    ]
    for at in range(4):
        here = slice(at * step, (at + 1) * step)
        base = jnp.where(odd, sums[(at + 2) % 4], sums[at])
        out_ref[here, :] = (residual_ref[here, :].astype(F32) + base + lora[here]).astype(BF16)


def line(rows, residual, weight, down, up, tenant, entry, live):
    z, x, c = lax.axis_index("blk"), lax.axis_index("split"), lax.axis_index("sub")
    y = lax.axis_index("groups")
    block_rows = rows.shape[0]
    width = down.shape[1]
    own, cols = residual.shape
    slots = entry.shape[0]
    home = (z // 2) == x
    odd = z % 2 == 1
    half, step = block_rows // 2, block_rows // 4
    barrier = lax.optimization_barrier

    def over_core(value):
        return lax.ppermute(value, "sub", SWAP)

    def over_x(value):
        return lax.ppermute(value, "split", SWAP)

    def along(value, pairs):
        return lax.ppermute(value, "blk", pairs)

    def by_core(mine, other):
        return jnp.where(c == 0, jnp.concatenate([mine, other]), jnp.concatenate([other, mine]))

    def whole(piece):
        return by_core(piece, over_core(piece))

    mine = [lax.dynamic_slice_in_dim(rows, p * half + c * step, step, 0) for p in range(2)]
    far = [along(mine[0], FAR)]
    near = [along(mine[0], NEAR)]
    rank_half, rank_quarter = width // 2, width // 4
    down_mine = lax.dynamic_slice_in_dim(down[0], c * rank_half, rank_half, 0)
    quarter = lax.dynamic_slice_in_dim(down_mine, y * rank_quarter, rank_quarter, 0)
    quarter = along(quarter, NEAR)
    near.append(along(mine[1], NEAR))
    far.append(along(mine[1], FAR))
    quarter_other = lax.ppermute(quarter, "groups", SWAP)
    maps = jnp.concatenate(
        [
            down_mine,
            jnp.where(
                y == 0,
                jnp.concatenate([quarter, quarter_other]),
                jnp.concatenate([quarter_other, quarter]),
            ),
        ]
    )
    up_other = over_x(up)
    ups = jnp.where(x == 0, jnp.concatenate([up, up_other]), jnp.concatenate([up_other, up]))

    slot_all, live_all = tables(tenant, entry, live)

    flags = jnp.stack([home, odd]).astype(jnp.int32)
    own_sum = call(
        sum_kernel,
        shape((block_rows, cols), F32),
        [HBM, VMEM],
        [weight, rows],
        streamed_scratch(weight),
    )
    own_low = call(low_kernel, shape((block_rows, width), F32), [VMEM] * 2, [maps, rows])

    def masked(low, place):
        slot = lax.dynamic_slice_in_dim(slot_all, place, block_rows, 0)[:, None]
        zero = jnp.zeros((), F32)
        first = jnp.where(slot == z, low[:, :rank_half], zero)
        return first + jnp.where(slot == z + 1 - 2 * (z % 2), low[:, rank_half:], zero)

    own_low = masked(own_low, z * block_rows)
    far[0], own_sum, own_low = barrier((far[0], own_sum, own_low))

    def parted(begins, pieces, helds):
        return call(
            functools.partial(part_kernel, begins),
            [shape((half, cols), F32), shape((half, cols), BF16)] * len(begins),
            [SMEM, HBM] + [VMEM] * (2 * len(begins)),
            [flags, weight] + pieces + helds,
            streamed_scratch(weight),
        )

    last = [along(far[0], NEAR)]
    far_rows = [whole(far[0])]
    kept_a, sent_a = parted([0], [far_rows[0]], [own_sum])
    near_sum = call(
        sum_kernel,
        shape((block_rows, cols), F32),
        [HBM, VMEM, VMEM],
        [weight] + [whole(piece) for piece in near],
        streamed_scratch(weight),
    )
    got_a = over_x(sent_a)
    far[1], last[0], near_sum, kept_a, ups, far_rows[0], own_low, maps = barrier(
        (far[1], last[0], near_sum, kept_a, ups, far_rows[0], own_low, maps)
    )

    last.append(along(far[1], NEAR))
    far_rows.append(whole(far[1]))
    far_low = call(low_kernel, shape((block_rows, width), F32), [VMEM] * 3, [maps] + far_rows)
    far_low = masked(far_low, (z + 2 - 4 * (z // 2)) * block_rows)
    low = jnp.where(home, own_low, far_low) + over_x(jnp.where(home, far_low, own_low))
    low = low + along(low, FAR)

    kept_b, sent_b, kept_c, sent_c = parted(
        [half, 0], [far_rows[1], whole(last[0])], [own_sum, near_sum]
    )
    got_b, got_c = over_x(sent_b), over_x(sent_c)
    last[1], got_a, kept_b, got_b, kept_c, got_c, low, near_sum = barrier(
        (last[1], got_a, kept_b, got_b, kept_c, got_c, low, near_sum)
    )

    kept_d, sent_d = call(
        end_kernel,
        [shape((half, cols), F32), shape((half, cols), BF16)],
        [SMEM] + [VMEM] * 3,
        [flags, weight, whole(last[1]), near_sum],
    )
    low_other, sent_d = barrier((along(low, NEAR), sent_d))
    got_d = over_x(sent_d)
    low = jnp.where(odd, jnp.concatenate([low_other, low]), jnp.concatenate([low, low_other]))
    low_other = over_core(low)
    low = jnp.where(
        c == 0,
        jnp.concatenate([low, low_other], axis=1),
        jnp.concatenate([low_other, low], axis=1),
    )
    start = x * own
    slot = lax.dynamic_slice_in_dim(slot_all, start, own, 0)
    rank = lax.dynamic_slice_in_dim(live_all, start, own, 0)
    spread = low_rank_weights(low, slot, rank, slots, width)
    return call(
        final_kernel,
        shape(residual.shape, BF16),
        [SMEM] + [VMEM] * 11,
        [flags, residual, spread, ups.reshape(slots * width, cols)]
        + [kept_a, got_a, kept_b, got_b, kept_c, got_c, kept_d, got_d],
    )


def shards(rows, residual, weight, down, up, tenant, entry, live):
    sizes = [lax.axis_size(name) for name in ("groups", "blk", "split", "sub")]
    plan = line if sizes == [2, 4, 2, 2] and down.shape[0] == 1 else general
    return plan(rows, residual, weight, down, up, tenant, entry, live)


def solution(mesh):
    in_specs = (
        P(("groups", "blk"), "split"),
        P(("groups", "split"), ("blk", "sub")),
        P("split", ("blk", "sub")),
        P("blk", None, "split"),
        P("split", None, ("blk", "sub")),
        P("groups"),
        P(),
        P(),
    )
    out_specs = P(("groups", "split"), ("blk", "sub"))
    return jax.shard_map(shards, mesh=mesh, in_specs=in_specs, out_specs=out_specs, check_vma=False)
```

time: 68.5 us -> 104 us (1.52)
  Pallas kernels: 0 us -> 21.8 us
  matrix products: 16.5 us -> 0 us
  local copies, waits for them, and re-layouts: 1.44 us -> 15.9 us
  waiting for transfers between devices: 23.1 us -> 33.3 us
  other arithmetic: 3.01 us -> 8.98 us
    pallas_call x0 -> x8, Pallas kernels: none -> 21.8 us  [call(): pl.pallas_call(kernel, out_shape=outs, in_specs=in_specs, out_specs=jax.t...]
    dot_general x9 -> x0, matrix products: 16.5 us -> none  [the longest x4 12 us: products(): base = jnp.dot(block, weight, preferred_element_type=F32)]
    unnamed x16 -> x20, local copies, waits for them, and re-layouts: 0.04 us -> 12 us
    ppermute x20 -> x23, waiting for transfers between devices: 23.1 us -> 33.3 us  [the longest x9 25.8 us: along(): return lax.ppermute(value, 'blk', pairs)]
    select_n x12 -> x11, other arithmetic: 1.76 us -> 7.05 us  [the longest x6 5.97 us: by_core(): jnp.where(c == 0, jnp.concatenate([mine, other]), jnp.concatenate([other,...]
    optimization_barrier x0 -> x2, local copies, waits for them, and re-layouts: none -> 2.44 us  [the longest x1 1.55 us: line(): barrier((last[1], got_a, kept_b, got_b, kept_c, got_c, low, near_sum))]
    slice x7 -> x0, local copies, waits for them, and re-layouts: 1.4 us -> none  [the longest x1 1.18 us: line(): piece = mine[p * step:(p + 1) * step]]
    dynamic_slice x0 -> x4, local copies, waits for them, and re-layouts: none -> 1.33 us  [the longest x1 1.2 us: line(): lax.dynamic_slice_in_dim(rows, p * half + c * step, step, 0)]
  transfers between devices with their start and end apart: 20 -> 23, of which waited for: 9 -> 5; matrix products, arithmetic and copies ran while one was open for 25% -> 10% of each run, Pallas kernels for 0% -> 19%
where the time goes in v5:
time: 104 us; the launch traced here: 103 us
  waiting for transfers between devices  33.3 us (32%)
  starting transfers between devices  22.8 us (22%)
  Pallas kernels  21.8 us (21%)
  local copies, waits for them, and re-layouts  15.9 us (15%)
  other arithmetic  8.98 us (9%)
    ppermute x9, waiting for transfers between devices, along(): return lax.ppermute(value, 'blk', pairs)  25.8 us
    pallas_call x8, Pallas kernels, call(): pl.pallas_call(kernel, out_shape=outs, in_specs=in_specs, out_specs=jax.t...  21.8 us
    ppermute x9, starting transfers between devices, along(): return lax.ppermute(value, 'blk', pairs)  13.1 us
    unnamed x20, local copies, waits for them, and re-layouts  12 us
    ppermute x6, waiting for transfers between devices, over_x(): return lax.ppermute(value, 'split', SWAP)  7.01 us
    ppermute x6, starting transfers between devices, over_x(): return lax.ppermute(value, 'split', SWAP)  6.95 us
    select_n x6, other arithmetic, by_core(): jnp.where(c == 0, jnp.concatenate([mine, other]), jnp.concatenate([other,...  5.97 us
  transfers between devices with their start and end apart: 23, of which 5 were waited for; matrix products, arithmetic and copies ran while one was open for 10% of the time, Pallas kernels for 19%

profile of v5, /device:TPU:0, one launch (start us, length us, event | category | flops | bytes accessed | tf_op | source)
XLA Modules:
  0.0 103.2 jit_solution(16915654335517939556)
XLA Ops:
  0.0 1.2 %constant_dynamic-slice_fusion = (bf16[32,4096]{1,0:T(8,128)(2,1)S(1)}, bf16[32,4096]{1,0:T(8,128)(2,1)S(1)}) fusion(bf16[128,4096]{1,0:T(8,128)(2,1)} %refs_0_.3, s32[]{:T(128)S(6)} %select_n.156, s32[]{:T(128)S(6)} %select_n.155), kind=kLoop, calls=%fused_computation.32 | loop fusion | bytes 1048584 | tf_op jit(solution)/shard_map/dynamic_slice | solution.py:201
  1.2 4.1 %collective-permute-start.1 = (bf16[32,4096]{1,0:T(8,128)(2,1)S(1)}, bf16[32,4096]{1,0:T(8,128)(2,1)}, u32[]{:S(2)}, u32[]{:S(2)}) collective-permute-start(bf16[32,4096]{1,0:T(8,128)(2,1)S(1)} %get-tuple-element.67), channel_id=1, source_target_pairs={{0,8},{8,0},{4,12},{12,4},{1,9},{9,1},{5,13},{13,5},{2,10},{10,2},... | collective-permute-start | bytes 786440 | tf_op jit(solution)/shard_map/ppermute | solution.py:193
  5.3 1.6 %collective-permute-start.5 = (bf16[32,4096]{1,0:T(8,128)(2,1)S(1)}, bf16[32,4096]{1,0:T(8,128)(2,1)}, u32[]{:S(2)}, u32[]{:S(2)}) collective-permute-start(bf16[32,4096]{1,0:T(8,128)(2,1)S(1)} %get-tuple-element.67), channel_id=1, source_target_pairs={{0,4},{4,0},{8,12},{12,8},{1,5},{5,1},{9,13},{13,9},{2,6},{6,2},{1... | collective-permute-start | bytes 786440 | tf_op jit(solution)/shard_map/ppermute | solution.py:193
  6.9 0.4 collective-permute-start.7
  7.5 1.9 %collective-permute-start.2 = (bf16[16,4096]{1,0:T(8,128)(2,1)S(1)}, bf16[16,4096]{1,0:T(8,128)(2,1)S(1)}, u32[]{:S(2)}, u32[]{:S(2)}) collective-permute-start(bf16[16,4096]{1,0:T(8,128)(2,1)S(1)} %dynamic-slice_bitcast_fusion.1), channel_id=1, source_target_pairs={{0,4},{4,0},{8,12},{12,8},{1,5},{5,1},{9,13},{13,9},{2,6},{6,2},{1... | collective-permute-start | bytes 393224 | tf_op jit(solution)/shard_map/ppermute | solution.py:193
  9.4 0.8 select_reduce_fusion
  10.2 21.4 %collective-permute-done.2 = bf16[16,4096]{1,0:T(8,128)(2,1)S(1)} collective-permute-done((bf16[16,4096]{1,0:T(8,128)(2,1)S(1)}, bf16[16,4096]{1,0:T(8,128)(2,1)S(1)}, u32[]{:S(2)}, u32[]{:S(2)}) %collective-permute-start.2) | collective-permute-done | bytes 131104 | tf_op jit(solution)/shard_map/ppermute | solution.py:193
  31.6 1.6 %collective-permute-start.3 = (bf16[16,4096]{1,0:T(8,128)(2,1)S(1)}, bf16[16,4096]{1,0:T(8,128)(2,1)S(1)}, u32[]{:S(2)}, u32[]{:S(2)}) collective-permute-start(bf16[16,4096]{1,0:T(8,128)(2,1)S(1)} %collective-permute-done.2), channel_id=1, source_target_pairs={{0,16},{16,0},{1,17},{17,1},{2,18},{18,2},{3,19},{19,3},{4,20},{20... | collective-permute-start | bytes 393224 | tf_op jit(solution)/shard_map/ppermute | solution.py:210
  33.2 3.4 %copy-done.1 = bf16[4096,1024]{1,0:T(8,128)(2,1)S(1)} copy-done((bf16[4096,1024]{1,0:T(8,128)(2,1)S(1)}, bf16[4096,1024]{1,0:T(8,128)(2,1)}, u32[]{:S(2)}) %copy-start.1) | copy-done | bytes 8388632
  36.6 1.2 %copy-done.5 = bf16[128,4096]{1,0:T(8,128)(2,1)S(1)} copy-done((bf16[128,4096]{1,0:T(8,128)(2,1)S(1)}, bf16[128,4096]{1,0:T(8,128)(2,1)}, u32[]{:S(2)}) %copy-start.5) | copy-done | bytes 1048600
  37.8 3.9 %shard_map.82.refs_1_.refs_2_ = f32[128,1024]{1,0:T(8,128)S(1)} custom-call(bf16[4096,1024]{1,0:T(8,128)(2,1)S(1)} %copy-done.1, bf16[128,4096]{1,0:T(8,128)(2,1)S(1)} %copy-done.5), custom_call_target="tpu_custom_call" | custom-call | tf_op jit(solution)/shard_map/pallas_call | solution.py:83
  41.9 1.6 %collective-permute-start.10 = (bf16[2,64,1024]{2,1,0:T(8,128)(2,1)S(1)}, bf16[2,64,1024]{2,1,0:T(8,128)(2,1)S(1)}, u32[]{:S(2)}, u32[]{:S(2)}) collective-permute-start(bf16[2,64,1024]{2,1,0:T(8,128)(2,1)S(1)} %copy-done.9), channel_id=1, source_target_pairs={{0,2},{2,0},{1,3},{3,1},{4,6},{6,4},{5,7},{7,5},{8,10},{10,8},{9,1... | collective-permute-start | bytes 786440 | tf_op jit(solution)/shard_map/ppermute | solution.py:190
  43.6 0.4 shard_map.83
  44.2 0.6 collective-permute-start.9
  44.8 1.4 %collective-permute-start.4 = (bf16[32,4096]{1,0:T(8,128)(2,1)}, bf16[32,4096]{1,0:T(8,128)(2,1)S(1)}, u32[]{:S(2)}, u32[]{:S(2)}) collective-permute-start(bf16[32,4096]{1,0:T(8,128)(2,1)} %collective-permute-done.1), channel_id=1, source_target_pairs={{0,4},{4,0},{8,12},{12,8},{1,5},{5,1},{9,13},{13,9},{2,6},{6,2},{1... | collective-permute-start | bytes 786440 | tf_op jit(solution)/shard_map/ppermute | solution.py:193
  46.2 2.4 %collective-permute-done.10 = bf16[2,64,1024]{2,1,0:T(8,128)(2,1)S(1)} collective-permute-done((bf16[2,64,1024]{2,1,0:T(8,128)(2,1)S(1)}, bf16[2,64,1024]{2,1,0:T(8,128)(2,1)S(1)}, u32[]{:S(2)}, u32[]{:S(2)}) %collective-permute-start.10) | collective-permute-done | bytes 262176 | tf_op jit(solution)/shard_map/ppermute | solution.py:190
  48.7 1.2 %maximum_select_fusion.refs_0_ = bf16[64,4096]{1,0:T(8,128)(2,1)S(1)} fusion(bf16[32,4096]{1,0:T(8,128)(2,1)S(1)} %collective-permute-done.6, bf16[32,4096]{1,0:T(8,128)(2,1)} %collective-permute-done.5, pred[]{:T(512)S(6)} %eq.87), kind=kLoop, calls=%fused_computation.1 | loop fusion | flops 2359296 | bytes 1048577 | tf_op jit(solution)/shard_map/jit(_where)/select_n | solution.py:196
  49.9 0.5 collective-permute-done.8
  50.4 1.2 %maximum_select_fusion.1.refs_1_ = bf16[64,4096]{1,0:T(8,128)(2,1)S(1)} fusion(bf16[32,4096]{1,0:T(8,128)(2,1)S(1)} %collective-permute-done.8, bf16[32,4096]{1,0:T(8,128)(2,1)} %collective-permute-done.7, pred[]{:T(512)S(6)} %eq.87), kind=kLoop, calls=%fused_computation.2 | loop fusion | flops 2359296 | bytes 1048577 | tf_op jit(solution)/shard_map/jit(_where)/select_n | solution.py:196
  51.6 3.4 %copy-done.2 = bf16[4096,1024]{1,0:T(8,128)(2,1)S(1)} copy-done((bf16[4096,1024]{1,0:T(8,128)(2,1)S(1)}, bf16[4096,1024]{1,0:T(8,128)(2,1)}, u32[]{:S(2)}) %copy-start.2) | copy-done | bytes 8388632
  55.0 3.9 %shard_map.84.refs_3_.held_ref = f32[128,1024]{1,0:T(8,128)S(1)} custom-call(bf16[4096,1024]{1,0:T(8,128)(2,1)S(1)} %copy-done.2, bf16[64,4096]{1,0:T(8,128)(2,1)S(1)} %maximum_select_fusion.refs_0_, bf16[64,4096]{1,0:T(8,128)(2,1)S(1)} %maximum_select_fusion.1.refs_1_), custom_call_target="tpu_custom_call" | custom-call | tf_op jit(solution)/shard_map/pallas_call | solution.py:83
  59.0 1.2 %maximum_select_fusion.2.refs_0_ = bf16[64,4096]{1,0:T(8,128)(2,1)S(1)} fusion(bf16[32,4096]{1,0:T(8,128)(2,1)S(1)} %collective-permute-done.9, bf16[32,4096]{1,0:T(8,128)(2,1)} %collective-permute-done.1, pred[]{:T(512)S(6)} %eq.87), kind=kLoop, calls=%fused_computation.3 | loop fusion | flops 2359296 | bytes 1048577 | tf_op jit(solution)/shard_map/jit(_where)/select_n | solution.py:196
  60.1 4.6 %shard_map.85 = (f32[64,1024]{1,0:T(8,128)S(1)}, bf16[64,1024]{1,0:T(8,128)(2,1)S(1)}) custom-call(s32[2]{0:T(128)S(1)} %add_convert_fusion.flags_ref, bf16[4096,1024]{1,0:T(8,128)(2,1)S(1)} %copy-done.3, bf16[64,4096]{1,0:T(8,128)(2,1)S(1)} %maximum_select_fusion.2.refs_0_, f32[128,1024]{1,0:T(8,128)S(1)} %shard_map.82.refs_1_.refs_2_), custom_call_target="tpu_custom_call" | custom-call | tf_op jit(solution)/shard_map/pallas_call | solution.py:83
  64.8 0.2 collective-permute-start.13
  65.0 1.7 %collective-permute-start.11 = (bf16[32,4096]{1,0:T(8,128)(2,1)}, bf16[32,4096]{1,0:T(8,128)(2,1)}, u32[]{:S(2)}, u32[]{:S(2)}) collective-permute-start(bf16[32,4096]{1,0:T(8,128)(2,1)} %collective-permute-done), channel_id=1, source_target_pairs={{0,4},{4,0},{8,12},{12,8},{1,5},{5,1},{9,13},{13,9},{2,6},{6,2},{1... | collective-permute-start | bytes 786440 | tf_op jit(solution)/shard_map/ppermute | solution.py:193
  66.7 1.5 %collective-permute-start.12 = (bf16[64,1024]{1,0:T(8,128)(2,1)S(1)}, bf16[64,1024]{1,0:T(8,128)(2,1)S(1)}, u32[]{:S(2)}, u32[]{:S(2)}) collective-permute-start(bf16[64,1024]{1,0:T(8,128)(2,1)S(1)} %get-tuple-element.39), channel_id=1, source_target_pairs={{0,2},{2,0},{1,3},{3,1},{4,6},{6,4},{5,7},{7,5},{8,10},{10,8},{9,1... | collective-permute-start | bytes 393224 | tf_op jit(solution)/shard_map/ppermute | solution.py:190
  68.2 1.2 %maximum_select_fusion.4.refs_0_.refs_1_ = bf16[64,4096]{1,0:T(8,128)(2,1)S(1)} fusion(bf16[32,4096]{1,0:T(8,128)(2,1)S(1)} %collective-permute-done.13, bf16[32,4096]{1,0:T(8,128)(2,1)} %collective-permute-done, pred[]{:T(512)S(6)} %eq.87), kind=kLoop, calls=%fused_computation.5 | loop fusion | flops 2359296 | bytes 1048577 | tf_op jit(solution)/shard_map/jit(_where)/select_n | solution.py:196
  69.4 0.4 shard_map.87
  69.9 0.6 collective-permute-start.17
  70.6 4.7 %shard_map.86 = (f32[64,1024]{1,0:T(8,128)S(1)}, bf16[64,1024]{1,0:T(8,128)(2,1)S(1)}, f32[64,1024]{1,0:T(8,128)S(1)}, bf16[64,1024]{1,0:T(8,128)(2,1)S(1)}) custom-call(s32[2]{0:T(128)S(1)} %add_convert_fusion.flags_ref, bf16[4096,1024]{1,0:T(8,128)(2,1)S(1)} %copy-done.3, bf16[64,4096]{1,0:T(8,128)(2,1)S(1)} %maximum_select_fusion.4.refs_0_.refs_1_, ...), custom_call_target="tpu_custom_call" | custom-call | tf_op jit(solution)/shard_map/pallas_call | solution.py:83
  75.3 1.6 %collective-permute-start.15 = (bf16[64,1024]{1,0:T(8,128)(2,1)S(1)}, bf16[64,1024]{1,0:T(8,128)(2,1)S(1)}, u32[]{:S(2)}, u32[]{:S(2)}) collective-permute-start(bf16[64,1024]{1,0:T(8,128)(2,1)S(1)} %get-tuple-element.43), channel_id=1, source_target_pairs={{0,2},{2,0},{1,3},{3,1},{4,6},{6,4},{5,7},{7,5},{8,10},{10,8},{9,1... | collective-permute-start | bytes 393224 | tf_op jit(solution)/shard_map/ppermute | solution.py:190
  76.9 0.5 collective-permute-start.16
  77.4 0.1 select_add_fusion
  77.5 1.5 %collective-permute-start.18 = (f32[128,32]{1,0:T(8,128)S(1)}, f32[128,32]{1,0:T(8,128)S(1)}, u32[]{:S(2)}, u32[]{:S(2)}) collective-permute-start(f32[128,32]{1,0:T(8,128)S(1)} %select_add_fusion), channel_id=1, source_target_pairs={{0,8},{8,0},{4,12},{12,4},{1,9},{9,1},{5,13},{13,5},{2,10},{10,2},... | collective-permute-start | bytes 49160 | tf_op jit(solution)/shard_map/ppermute | solution.py:193
  79.0 4.4 %collective-permute-done.18 = f32[128,32]{1,0:T(8,128)S(1)} collective-permute-done((f32[128,32]{1,0:T(8,128)S(1)}, f32[128,32]{1,0:T(8,128)S(1)}, u32[]{:S(2)}, u32[]{:S(2)}) %collective-permute-start.18) | collective-permute-done | bytes 16416 | tf_op jit(solution)/shard_map/ppermute | solution.py:193
  83.5 0.6 add.67
  84.3 0.4 collective-permute-start.19
  84.7 1.5 %copy.17 = f32[128,32]{0,1:T(8,128)} copy(f32[128,32]{1,0:T(8,128)} %add.67) | data formatting | bytes 32768 | tf_op jit(solution)/shard_map/optimization_barrier | solution.py:280
  86.2 1.2 %maximum_select_fusion.6.piece_ref = bf16[64,4096]{1,0:T(8,128)(2,1)S(1)} fusion(bf16[32,4096]{1,0:T(8,128)(2,1)S(1)} %collective-permute-done.20, bf16[32,4096]{1,0:T(8,128)(2,1)} %collective-permute-done.11, pred[]{:T(512)S(6)} %eq.87), kind=kLoop, calls=%fused_computation.7 | loop fusion | flops 2359296 | bytes 1048577 | tf_op jit(solution)/shard_map/jit(_where)/select_n | solution.py:196
  87.4 3.4 %copy-done.4 = bf16[4096,1024]{1,0:T(8,128)(2,1)S(1)} copy-done((bf16[4096,1024]{1,0:T(8,128)(2,1)S(1)}, bf16[4096,1024]{1,0:T(8,128)(2,1)}, u32[]{:S(2)}) %copy-start.4) | copy-done | bytes 8388632
  90.8 2.1 %shard_map.88 = (f32[64,1024]{1,0:T(8,128)S(1)}, bf16[64,1024]{1,0:T(8,128)(2,1)S(1)}) custom-call(s32[2]{0:T(128)S(1)} %add_convert_fusion.flags_ref, bf16[4096,1024]{1,0:T(8,128)(2,1)S(1)} %copy-done.4, bf16[64,4096]{1,0:T(8,128)(2,1)S(1)} %maximum_select_fusion.6.piece_ref, f32[128,1024]{1,0:T(8,128)S(1)} %shard_map.84.refs_3_.held_ref), custom_call_target="tpu_custom_call" | custom-call | tf_op jit(solution)/shard_map/pallas_call | solution.py:83
  92.9 0.6 copy-done.8
  93.6 0.9 copy.16
  94.5 0.8 maximum_select_fusion.9
  95.3 0.2 collective-permute-start.21
  95.6 1.2 %collective-permute-start.22 = (bf16[64,1024]{1,0:T(8,128)(2,1)}, bf16[64,1024]{1,0:T(8,128)(2,1)S(1)}, u32[]{:S(2)}, u32[]{:S(2)}) collective-permute-start(bf16[64,1024]{1,0:T(8,128)(2,1)} %copy-done.8), channel_id=1, source_target_pairs={{0,2},{2,0},{1,3},{3,1},{4,6},{6,4},{5,7},{7,5},{8,10},{10,8},{9,1... | collective-permute-start | bytes 393224 | tf_op jit(solution)/shard_map/ppermute | solution.py:190
  96.9 4.6 %collective-permute-done.22.refs_7_ = bf16[64,1024]{1,0:T(8,128)(2,1)S(1)} collective-permute-done((bf16[64,1024]{1,0:T(8,128)(2,1)}, bf16[64,1024]{1,0:T(8,128)(2,1)S(1)}, u32[]{:S(2)}, u32[]{:S(2)}) %collective-permute-start.22) | collective-permute-done | bytes 131104 | tf_op jit(solution)/shard_map/ppermute | solution.py:190
  101.5 1.7 %shard_map.89 = bf16[256,1024]{1,0:T(8,128)(2,1)} custom-call(s32[2]{0:T(128)S(1)} %add_convert_fusion.flags_ref, bf16[256,1024]{1,0:T(8,128)(2,1)S(1)} %copy-done.7, bf16[256,256]{1,0:T(8,128)(2,1)S(1)} %copy.20.spread_ref, bf16[256,1024]{1,0:T(8,128)(2,1)S(1)} %bitcast.8, f32[64,1024]{1,0:T(8,128)S(1)} %get-tuple-element.55.refs_0_, ...), custom_call_target="tpu_custom_call" | custom-call | tf_op jit(solution)/shard_map/pallas_call | solution.py:83
  (54 shorter events, 1.4 us)
Async XLA Ops:
  0.0 7.4 %copy-start = (bf16[1,64,4096]{2,1,0:T(8,128)(2,1)S(1)}, bf16[1,64,4096]{2,1,0:T(8,128)(2,1)}, u32[]{:S(2)}) copy-start(bf16[1,64,4096]{2,1,0:T(8,128)(2,1)} %param.11) | copy-start | bytes 1572868
  0.0 43.5 %copy-start.6 = (bf16[128,4096]{1,0:T(8,128)(2,1)S(1)}, bf16[128,4096]{1,0:T(8,128)(2,1)}, u32[]{:S(2)}) copy-start(bf16[128,4096]{1,0:T(8,128)(2,1)} %refs_0_.3) | copy-start | bytes 3145732
  0.0 41.9 %copy-start.9 = (bf16[2,64,1024]{2,1,0:T(8,128)(2,1)S(1)}, bf16[2,64,1024]{2,1,0:T(8,128)(2,1)}, u32[]{:S(2)}) copy-start(bf16[2,64,1024]{2,1,0:T(8,128)(2,1)} %param.12) | copy-start | bytes 786436
  1.2 43.0 %collective-permute-start.1 = (bf16[32,4096]{1,0:T(8,128)(2,1)S(1)}, bf16[32,4096]{1,0:T(8,128)(2,1)}, u32[]{:S(2)}, u32[]{:S(2)}) collective-permute-start(bf16[32,4096]{1,0:T(8,128)(2,1)S(1)} %get-tuple-element.67), channel_id=1, source_target_pairs={{0,8},{8,0},{4,12},{12,4},{1,9},{9,1},{5,13},{13,5},{2,10},{10,2},... | collective-permute-start | bytes 786440 | tf_op jit(solution)/shard_map/ppermute | solution.py:193
  5.3 38.7 %collective-permute-start.5 = (bf16[32,4096]{1,0:T(8,128)(2,1)S(1)}, bf16[32,4096]{1,0:T(8,128)(2,1)}, u32[]{:S(2)}, u32[]{:S(2)}) collective-permute-start(bf16[32,4096]{1,0:T(8,128)(2,1)S(1)} %get-tuple-element.67), channel_id=1, source_target_pairs={{0,4},{4,0},{8,12},{12,8},{1,5},{5,1},{9,13},{13,9},{2,6},{6,2},{1... | collective-permute-start | bytes 786440 | tf_op jit(solution)/shard_map/ppermute | solution.py:193
  6.9 37.9 %collective-permute-start.7 = (bf16[32,4096]{1,0:T(8,128)(2,1)S(1)}, bf16[32,4096]{1,0:T(8,128)(2,1)}, u32[]{:S(2)}, u32[]{:S(2)}) collective-permute-start(bf16[32,4096]{1,0:T(8,128)(2,1)S(1)} %get-tuple-element.68), channel_id=1, source_target_pairs={{0,4},{4,0},{8,12},{12,8},{1,5},{5,1},{9,13},{13,9},{2,6},{6,2},{1... | collective-permute-start | bytes 786440 | tf_op jit(solution)/shard_map/ppermute | solution.py:193
  7.4 57.4 %collective-permute-start = (bf16[32,4096]{1,0:T(8,128)(2,1)S(1)}, bf16[32,4096]{1,0:T(8,128)(2,1)}, u32[]{:S(2)}, u32[]{:S(2)}) collective-permute-start(bf16[32,4096]{1,0:T(8,128)(2,1)S(1)} %get-tuple-element.68), channel_id=1, source_target_pairs={{0,8},{8,0},{4,12},{12,4},{1,9},{9,1},{5,13},{13,5},{2,10},{10,2},... | collective-permute-start | bytes 786440 | tf_op jit(solution)/shard_map/ppermute | solution.py:193
  7.5 24.1 %collective-permute-start.2 = (bf16[16,4096]{1,0:T(8,128)(2,1)S(1)}, bf16[16,4096]{1,0:T(8,128)(2,1)S(1)}, u32[]{:S(2)}, u32[]{:S(2)}) collective-permute-start(bf16[16,4096]{1,0:T(8,128)(2,1)S(1)} %dynamic-slice_bitcast_fusion.1), channel_id=1, source_target_pairs={{0,4},{4,0},{8,12},{12,8},{1,5},{5,1},{9,13},{13,9},{2,6},{6,2},{1... | collective-permute-start | bytes 393224 | tf_op jit(solution)/shard_map/ppermute | solution.py:193
  31.6 10.3 %collective-permute-start.3 = (bf16[16,4096]{1,0:T(8,128)(2,1)S(1)}, bf16[16,4096]{1,0:T(8,128)(2,1)S(1)}, u32[]{:S(2)}, u32[]{:S(2)}) collective-permute-start(bf16[16,4096]{1,0:T(8,128)(2,1)S(1)} %collective-permute-done.2), channel_id=1, source_target_pairs={{0,16},{16,0},{1,17},{17,1},{2,18},{18,2},{3,19},{19,3},{4,20},{20... | collective-permute-start | bytes 393224 | tf_op jit(solution)/shard_map/ppermute | solution.py:210
  33.2 3.4 %copy-start.1 = (bf16[4096,1024]{1,0:T(8,128)(2,1)S(1)}, bf16[4096,1024]{1,0:T(8,128)(2,1)}, u32[]{:S(2)}) copy-start(bf16[4096,1024]{1,0:T(8,128)(2,1)} %weight_ref.9) | copy-start | bytes 25165828
  36.6 1.2 %copy-start.5 = (bf16[128,4096]{1,0:T(8,128)(2,1)S(1)}, bf16[128,4096]{1,0:T(8,128)(2,1)}, u32[]{:S(2)}) copy-start(bf16[128,4096]{1,0:T(8,128)(2,1)} %refs_0_.3) | copy-start | bytes 3145732
  41.9 6.7 %collective-permute-start.10 = (bf16[2,64,1024]{2,1,0:T(8,128)(2,1)S(1)}, bf16[2,64,1024]{2,1,0:T(8,128)(2,1)S(1)}, u32[]{:S(2)}, u32[]{:S(2)}) collective-permute-start(bf16[2,64,1024]{2,1,0:T(8,128)(2,1)S(1)} %copy-done.9), channel_id=1, source_target_pairs={{0,2},{2,0},{1,3},{3,1},{4,6},{6,4},{5,7},{7,5},{8,10},{10,8},{9,1... | collective-permute-start | bytes 786440 | tf_op jit(solution)/shard_map/ppermute | solution.py:190
  44.0 4.7 %collective-permute-start.6 = (bf16[32,4096]{1,0:T(8,128)(2,1)}, bf16[32,4096]{1,0:T(8,128)(2,1)S(1)}, u32[]{:S(2)}, u32[]{:S(2)}) collective-permute-start(bf16[32,4096]{1,0:T(8,128)(2,1)} %collective-permute-done.5), channel_id=1, source_target_pairs={{0,1},{1,0},{2,3},{3,2},{4,5},{5,4},{6,7},{7,6},{8,9},{9,8},{10,11... | collective-permute-start | bytes 786440 | tf_op jit(solution)/shard_map/ppermute | solution.py:187
  44.2 14.7 %collective-permute-start.9 = (bf16[32,4096]{1,0:T(8,128)(2,1)}, bf16[32,4096]{1,0:T(8,128)(2,1)S(1)}, u32[]{:S(2)}, u32[]{:S(2)}) collective-permute-start(bf16[32,4096]{1,0:T(8,128)(2,1)} %collective-permute-done.1), channel_id=1, source_target_pairs={{0,1},{1,0},{2,3},{3,2},{4,5},{5,4},{6,7},{7,6},{8,9},{9,8},{10,11... | collective-permute-start | bytes 786440 | tf_op jit(solution)/shard_map/ppermute | solution.py:187
  44.8 20.0 %collective-permute-start.4 = (bf16[32,4096]{1,0:T(8,128)(2,1)}, bf16[32,4096]{1,0:T(8,128)(2,1)S(1)}, u32[]{:S(2)}, u32[]{:S(2)}) collective-permute-start(bf16[32,4096]{1,0:T(8,128)(2,1)} %collective-permute-done.1), channel_id=1, source_target_pairs={{0,4},{4,0},{8,12},{12,8},{1,5},{5,1},{9,13},{13,9},{2,6},{6,2},{1... | collective-permute-start | bytes 786440 | tf_op jit(solution)/shard_map/ppermute | solution.py:193
  48.6 1.7 %collective-permute-start.8 = (bf16[32,4096]{1,0:T(8,128)(2,1)}, bf16[32,4096]{1,0:T(8,128)(2,1)S(1)}, u32[]{:S(2)}, u32[]{:S(2)}) collective-permute-start(bf16[32,4096]{1,0:T(8,128)(2,1)} %collective-permute-done.7), channel_id=1, source_target_pairs={{0,1},{1,0},{2,3},{3,2},{4,5},{5,4},{6,7},{7,6},{8,9},{9,8},{10,11... | collective-permute-start | bytes 786440 | tf_op jit(solution)/shard_map/ppermute | solution.py:187
  51.6 3.4 %copy-start.2 = (bf16[4096,1024]{1,0:T(8,128)(2,1)S(1)}, bf16[4096,1024]{1,0:T(8,128)(2,1)}, u32[]{:S(2)}) copy-start(bf16[4096,1024]{1,0:T(8,128)(2,1)} %weight_ref.9) | copy-start | bytes 25165828
  55.0 5.1 %copy-start.3 = (bf16[4096,1024]{1,0:T(8,128)(2,1)S(1)}, bf16[4096,1024]{1,0:T(8,128)(2,1)}, u32[]{:S(2)}) copy-start(bf16[4096,1024]{1,0:T(8,128)(2,1)} %weight_ref.9) | copy-start | bytes 25165828
  64.8 3.4 %collective-permute-start.13 = (bf16[32,4096]{1,0:T(8,128)(2,1)}, bf16[32,4096]{1,0:T(8,128)(2,1)S(1)}, u32[]{:S(2)}, u32[]{:S(2)}) collective-permute-start(bf16[32,4096]{1,0:T(8,128)(2,1)} %collective-permute-done), channel_id=1, source_target_pairs={{0,1},{1,0},{2,3},{3,2},{4,5},{5,4},{6,7},{7,6},{8,9},{9,8},{10,11... | collective-permute-start | bytes 786440 | tf_op jit(solution)/shard_map/ppermute | solution.py:187
  65.0 19.1 %collective-permute-start.11 = (bf16[32,4096]{1,0:T(8,128)(2,1)}, bf16[32,4096]{1,0:T(8,128)(2,1)}, u32[]{:S(2)}, u32[]{:S(2)}) collective-permute-start(bf16[32,4096]{1,0:T(8,128)(2,1)} %collective-permute-done), channel_id=1, source_target_pairs={{0,4},{4,0},{8,12},{12,8},{1,5},{5,1},{9,13},{13,9},{2,6},{6,2},{1... | collective-permute-start | bytes 786440 | tf_op jit(solution)/shard_map/ppermute | solution.py:193
  66.6 3.9 %collective-permute-start.14 = (bf16[32,4096]{1,0:T(8,128)(2,1)S(1)}, bf16[32,4096]{1,0:T(8,128)(2,1)S(1)}, u32[]{:S(2)}, u32[]{:S(2)}) collective-permute-start(bf16[32,4096]{1,0:T(8,128)(2,1)S(1)} %collective-permute-done.4), channel_id=1, source_target_pairs={{0,1},{1,0},{2,3},{3,2},{4,5},{5,4},{6,7},{7,6},{8,9},{9,8},{10,11... | collective-permute-start | bytes 786440 | tf_op jit(solution)/shard_map/ppermute | solution.py:187
  66.7 17.4 %collective-permute-start.12 = (bf16[64,1024]{1,0:T(8,128)(2,1)S(1)}, bf16[64,1024]{1,0:T(8,128)(2,1)S(1)}, u32[]{:S(2)}, u32[]{:S(2)}) collective-permute-start(bf16[64,1024]{1,0:T(8,128)(2,1)S(1)} %get-tuple-element.39), channel_id=1, source_target_pairs={{0,2},{2,0},{1,3},{3,1},{4,6},{6,4},{5,7},{7,5},{8,10},{10,8},{9,1... | collective-permute-start | bytes 393224 | tf_op jit(solution)/shard_map/ppermute | solution.py:190
  69.9 7.5 %collective-permute-start.17 = (f32[128,32]{1,0:T(8,128)S(1)}, f32[128,32]{1,0:T(8,128)S(1)}, u32[]{:S(2)}, u32[]{:S(2)}) collective-permute-start(f32[128,32]{1,0:T(8,128)S(1)} %broadcast_select_fusion.1), channel_id=1, source_target_pairs={{0,2},{2,0},{1,3},{3,1},{4,6},{6,4},{5,7},{7,5},{8,10},{10,8},{9,1... | collective-permute-start | bytes 49160 | tf_op jit(solution)/shard_map/ppermute | solution.py:190
  75.3 26.2 %copy-start.7 = (bf16[256,1024]{1,0:T(8,128)(2,1)S(1)}, bf16[256,1024]{1,0:T(8,128)(2,1)}, u32[]{:S(2)}) copy-start(bf16[256,1024]{1,0:T(8,128)(2,1)} %residual_ref.1) | copy-start | bytes 1572868
  75.3 8.8 %collective-permute-start.15 = (bf16[64,1024]{1,0:T(8,128)(2,1)S(1)}, bf16[64,1024]{1,0:T(8,128)(2,1)S(1)}, u32[]{:S(2)}, u32[]{:S(2)}) collective-permute-start(bf16[64,1024]{1,0:T(8,128)(2,1)S(1)} %get-tuple-element.43), channel_id=1, source_target_pairs={{0,2},{2,0},{1,3},{3,1},{4,6},{6,4},{5,7},{7,5},{8,10},{10,8},{9,1... | collective-permute-start | bytes 393224 | tf_op jit(solution)/shard_map/ppermute | solution.py:190
  76.9 7.2 %collective-permute-start.16 = (bf16[64,1024]{1,0:T(8,128)(2,1)S(1)}, bf16[64,1024]{1,0:T(8,128)(2,1)S(1)}, u32[]{:S(2)}, u32[]{:S(2)}) collective-permute-start(bf16[64,1024]{1,0:T(8,128)(2,1)S(1)} %get-tuple-element.45), channel_id=1, source_target_pairs={{0,2},{2,0},{1,3},{3,1},{4,6},{6,4},{5,7},{7,5},{8,10},{10,8},{9,1... | collective-permute-start | bytes 393224 | tf_op jit(solution)/shard_map/ppermute | solution.py:190
  77.5 5.9 %collective-permute-start.18 = (f32[128,32]{1,0:T(8,128)S(1)}, f32[128,32]{1,0:T(8,128)S(1)}, u32[]{:S(2)}, u32[]{:S(2)}) collective-permute-start(f32[128,32]{1,0:T(8,128)S(1)} %select_add_fusion), channel_id=1, source_target_pairs={{0,8},{8,0},{4,12},{12,4},{1,9},{9,1},{5,13},{13,5},{2,10},{10,2},... | collective-permute-start | bytes 49160 | tf_op jit(solution)/shard_map/ppermute | solution.py:193
  84.1 2.1 %collective-permute-start.20 = (bf16[32,4096]{1,0:T(8,128)(2,1)}, bf16[32,4096]{1,0:T(8,128)(2,1)S(1)}, u32[]{:S(2)}, u32[]{:S(2)}) collective-permute-start(bf16[32,4096]{1,0:T(8,128)(2,1)} %collective-permute-done.11), channel_id=1, source_target_pairs={{0,1},{1,0},{2,3},{3,2},{4,5},{5,4},{6,7},{7,6},{8,9},{9,8},{10,11... | collective-permute-start | bytes 786440 | tf_op jit(solution)/shard_map/ppermute | solution.py:187
  84.3 9.3 %collective-permute-start.19 = (f32[128,32]{1,0:T(8,128)}, f32[128,32]{1,0:T(8,128)}, u32[]{:S(2)}, u32[]{:S(2)}) collective-permute-start(f32[128,32]{1,0:T(8,128)} %add.67), channel_id=1, source_target_pairs={{0,4},{4,0},{8,12},{12,8},{1,5},{5,1},{9,13},{13,9},{2,6},{6,2},{1... | collective-permute-start | bytes 49160 | tf_op jit(solution)/shard_map/ppermute | solution.py:193
  87.4 3.4 %copy-start.4 = (bf16[4096,1024]{1,0:T(8,128)(2,1)S(1)}, bf16[4096,1024]{1,0:T(8,128)(2,1)}, u32[]{:S(2)}) copy-start(bf16[4096,1024]{1,0:T(8,128)(2,1)} %weight_ref.9) | copy-start | bytes 25165828
  92.9 0.7 copy-start.8
  95.3 1.5 %collective-permute-start.21 = (f32[256,32]{0,1:T(8,128)S(1)}, f32[256,32]{0,1:T(8,128)S(1)}, u32[]{:S(2)}, u32[]{:S(2)}) collective-permute-start(f32[256,32]{0,1:T(8,128)S(1)} %maximum_select_fusion.9), channel_id=1, source_target_pairs={{0,1},{1,0},{2,3},{3,2},{4,5},{5,4},{6,7},{7,6},{8,9},{9,8},{10,11... | collective-permute-start | bytes 98312 | tf_op jit(solution)/shard_map/ppermute | solution.py:187
  95.6 5.9 %collective-permute-start.22 = (bf16[64,1024]{1,0:T(8,128)(2,1)}, bf16[64,1024]{1,0:T(8,128)(2,1)S(1)}, u32[]{:S(2)}, u32[]{:S(2)}) collective-permute-start(bf16[64,1024]{1,0:T(8,128)(2,1)} %copy-done.8), channel_id=1, source_target_pairs={{0,2},{2,0},{1,3},{3,1},{4,6},{6,4},{5,7},{7,5},{8,10},{10,8},{9,1... | collective-permute-start | bytes 393224 | tf_op jit(solution)/shard_map/ppermute | solution.py:190

commit v6 on v1

v6 whole, which is shorter than its diff:
```python
import jax
import jax.numpy as jnp
from jax import lax
from jax.sharding import PartitionSpec as P

F32 = jnp.float32
BF16 = jnp.bfloat16


def low_rank_weights(low, slot, live, slots, rank_width):
    kept = jnp.arange(rank_width, dtype=jnp.int32)[None, :] < live[:, None]
    scaling = rank_width / live.astype(F32)
    scaled = jnp.where(kept, low * scaling[:, None], jnp.zeros((), F32)).astype(BF16)
    hot = slot[:, None] == jnp.arange(slots, dtype=jnp.int32)[None, :]
    spread = jnp.where(hot[:, :, None], scaled[:, None, :], jnp.zeros((), BF16))
    return spread.reshape(low.shape[0], slots * rank_width)


def tables(tenant, entry, live):
    ids = jnp.arange(entry.shape[0], dtype=jnp.int32)
    hot = (tenant[:, None] == ids[None, :]).astype(jnp.int32)
    return jnp.sum(hot * entry[None, :], axis=1), jnp.sum(hot * live[None, :], axis=1)


def general(rows, residual, weight, down, up, tenant, entry, live):
    own = residual.shape[0]
    cols = weight.shape[1]
    width = down.shape[1]
    slots = entry.shape[0]
    slot_all, live_all = tables(tenant, entry, live)
    part = rows.shape[0] // lax.axis_size("sub")
    mine = lax.dynamic_slice_in_dim(rows, lax.axis_index("sub") * part, part, 0)
    halves = lax.all_gather(lax.all_gather(mine, "blk", axis=0), "sub", axis=1)
    full = halves.reshape(-1, rows.shape[1])
    base = jnp.dot(full, weight, preferred_element_type=F32)
    low = lax.dot_general(
        full, down.reshape(-1, down.shape[2]), (((1,), (1,)), ((), ())), preferred_element_type=F32
    )
    held = down.shape[0]
    places = lax.axis_index("blk") * held + jnp.arange(held, dtype=jnp.int32)
    here = slot_all[:, None] == places[None, :]
    low = jnp.sum(
        jnp.where(here[:, :, None], low.reshape(-1, held, width), jnp.zeros((), F32)), axis=1
    )
    low = lax.psum(lax.psum_scatter(low, "split", scatter_dimension=0, tiled=True), "blk")
    base = lax.psum_scatter(base, "split", scatter_dimension=0, tiled=True)
    start = lax.axis_index("split") * own
    spread = low_rank_weights(
        low,
        lax.dynamic_slice_in_dim(slot_all, start, own, 0),
        lax.dynamic_slice_in_dim(live_all, start, own, 0),
        slots,
        width,
    )
    ups = lax.all_gather(up, "split", axis=0, tiled=True).reshape(slots * width, cols)
    lora = jnp.dot(spread, ups, preferred_element_type=F32)
    return (residual.astype(F32) + base + lora).astype(BF16)


SWAP = [(0, 1), (1, 0)]
NEAR = [(0, 1), (1, 0), (2, 3), (3, 2)]
FAR = [(0, 2), (2, 0), (1, 3), (3, 1)]


def line(rows, residual, weight, down, up, tenant, entry, live):
    z, x, c = lax.axis_index("blk"), lax.axis_index("split"), lax.axis_index("sub")
    block_rows = rows.shape[0]
    width = down.shape[1]
    own, cols = residual.shape
    slots = entry.shape[0]
    home = (z // 2) == x
    odd = z % 2 == 1
    half, step = block_rows // 2, block_rows // 4
    barrier = lax.optimization_barrier

    def over_core(value):
        return lax.ppermute(value, "sub", SWAP)

    def over_x(value):
        return lax.ppermute(value, "split", SWAP)

    def along(value, pairs):
        return lax.ppermute(value, "blk", pairs)

    def product(block):
        return jnp.dot(block, weight, preferred_element_type=F32)

    def low_rank(block):
        return lax.dot_general(
            block, down[0], (((1,), (1,)), ((), ())), preferred_element_type=F32
        )

    def joined(piece, other):
        return jnp.where(
            c == 0, jnp.concatenate([piece, other]), jnp.concatenate([other, piece])
        )

    def whole(piece):
        return joined(piece, over_core(piece))

    def in_order(first, second):
        return jnp.where(
            odd, jnp.concatenate([second, first]), jnp.concatenate([first, second])
        )

    def exchange(near_sum, far_sum):
        got = over_x(jnp.where(home, far_sum, near_sum).astype(BF16))
        return jnp.where(home, near_sum, far_sum), got

    slot_all, live_all = tables(tenant, entry, live)
    slot = lax.dynamic_slice_in_dim(slot_all, x * own, own, 0)
    rank = lax.dynamic_slice_in_dim(live_all, x * own, own, 0)

    mine = lax.dynamic_slice_in_dim(rows, c * half, half, 0)
    near, far = along(mine, NEAR), along(mine, FAR)
    up_other = over_x(up)
    ups = jnp.where(x == 0, jnp.concatenate([up, up_other]), jnp.concatenate([up_other, up]))
    own_sum, own_low = product(rows), low_rank(rows)
    near, far, own_sum, own_low, ups = barrier((near, far, own_sum, own_low, ups))

    last = along(far, NEAR)

    def doubled(piece):
        return joined(
            piece, jnp.concatenate([over_core(piece[:step]), over_core(piece[step:])])
        )

    far = doubled(far)
    far_sum, far_low = product(far), low_rank(far)
    kept, got = exchange(own_sum, far_sum)
    first = kept + got.astype(F32)
    near = doubled(near)
    near_sum, near_low = product(near), low_rank(near)
    last, first, far_low, near_sum, near_low = barrier((last, first, far_low, near_sum, near_low))

    pieces = [whole(last[:step]), whole(last[step:])]
    last_low = low_rank(jnp.concatenate(pieces)).reshape(2, 2, step, width)
    last_low = last_low.transpose(1, 0, 2, 3).reshape(block_rows, width)
    near_low, far_low = in_order(own_low, near_low), in_order(far_low, last_low)
    low = jnp.where(home, near_low, far_low) + over_x(jnp.where(home, far_low, near_low))
    low = jnp.where((slot == z)[:, None], low, jnp.zeros((), F32))
    near_parts = near_sum.reshape(2, 2, step, cols)
    second = []
    for p, pairs in enumerate((NEAR, FAR)):
        kept, got = exchange(near_parts[:, p].reshape(half, cols), product(pieces[p]))
        low, kept, got = barrier((low, kept, got)) if p else (low, kept, got)
        low = low + along(low, pairs)
        second.append((kept + got.astype(F32)).reshape(2, step, cols))
    second = jnp.stack(second, axis=1).reshape(block_rows, cols)
    spread = low_rank_weights(low, slot, rank, slots, width)
    lora = jnp.dot(spread, ups.reshape(slots * width, cols), preferred_element_type=F32)
    return (residual.astype(F32) + in_order(first, second) + lora).astype(BF16)


def shards(rows, residual, weight, down, up, tenant, entry, live):
    sizes = [lax.axis_size(name) for name in ("blk", "split", "sub")]
    plan = line if sizes == [4, 2, 2] and down.shape[0] == 1 else general
    return plan(rows, residual, weight, down, up, tenant, entry, live)


def solution(mesh):
    in_specs = (
        P(("groups", "blk"), "split"),
        P(("groups", "split"), ("blk", "sub")),
        P("split", ("blk", "sub")),
        P("blk", None, "split"),
        P("split", None, ("blk", "sub")),
        P("groups"),
        P(),
        P(),
    )
    out_specs = P(("groups", "split"), ("blk", "sub"))
    return jax.shard_map(shards, mesh=mesh, in_specs=in_specs, out_specs=out_specs, check_vma=False)
```

time: 68.5 us -> 75.2 us (1.098)
  matrix products: 16.5 us -> 25 us
  starting transfers between devices: 23.7 us -> 18.9 us
  waiting for transfers between devices: 23.1 us -> 24.9 us
  local copies, waits for them, and re-layouts: 1.44 us -> 2.31 us
    dot_general x9 -> x10, matrix products: 16.5 us -> 25 us  [the longest x5 22 us: product(): return jnp.dot(block, weight, preferred_element_type=F32)]
    ppermute x20 -> x16, starting transfers between devices: 23.7 us -> 18.9 us  [the longest x5 10.5 us: along(): return lax.ppermute(value, 'blk', pairs)]
    ppermute x20 -> x16, waiting for transfers between devices: 23.1 us -> 24.9 us  [the longest x5 16.7 us: along(): return lax.ppermute(value, 'blk', pairs)]
    slice x7 -> x4, local copies, waits for them, and re-layouts: 1.4 us -> 0.14 us  [the longest x2 0.07 us: doubled(): piece[:step]]
    unnamed x16 -> x24, local copies, waits for them, and re-layouts: 0.04 us -> 1.28 us
    add x1 -> x4, other arithmetic: 0.01 us -> 0.97 us  [the longest x1 0.88 us: line(): first = kept + got.astype(F32)]
    convert_element_type x2 -> x1, other arithmetic: 0.97 us -> 0.03 us  [exchange(): got = over_x(jnp.where(home, far_sum, near_sum).astype(BF16))]
    dynamic_slice x0 -> x1, local copies, waits for them, and re-layouts: none -> 0.83 us  [line(): mine = lax.dynamic_slice_in_dim(rows, c * half, half, 0)]
  transfers between devices with their start and end apart: 20 -> 16, of which waited for: 9 -> 10; matrix products, arithmetic and copies ran while one was open for 25% -> 37% of each run, Pallas kernels for 0% -> 0%
where the time goes in v6:
time: 75.2 us; the launch traced here: 74.9 us
  matrix products  25 us (33%)
  waiting for transfers between devices  24.9 us (33%)
  starting transfers between devices  18.9 us (25%)
  other arithmetic  3.51 us (5%)
  local copies, waits for them, and re-layouts  2.31 us (3%)
    dot_general x5, matrix products, product(): return jnp.dot(block, weight, preferred_element_type=F32)  22 us
    ppermute x5, waiting for transfers between devices, along(): return lax.ppermute(value, 'blk', pairs)  16.7 us
    ppermute x5, starting transfers between devices, along(): return lax.ppermute(value, 'blk', pairs)  10.5 us
    ppermute x5, starting transfers between devices, over_x(): return lax.ppermute(value, 'split', SWAP)  6.76 us
    ppermute x5, waiting for transfers between devices, over_x(): return lax.ppermute(value, 'split', SWAP)  6.47 us
    select_n x1, other arithmetic, line(): jnp.where(x == 0, jnp.concatenate([up, up_other]), jnp.concatenate([up_ot...  1.91 us
    dot_general x4, matrix products, low_rank(): lax.dot_general(block, down[0], (((1,), (1,)), ((), ())), preferred_eleme...  1.86 us
    ppermute x6, waiting for transfers between devices, over_core(): return lax.ppermute(value, 'sub', SWAP)  1.68 us
  transfers between devices with their start and end apart: 16, of which 10 were waited for; matrix products, arithmetic and copies ran while one was open for 37% of the time, Pallas kernels for 0%

profile of v6, /device:TPU:0, one launch (start us, length us, event | category | flops | bytes accessed | tf_op | source)
XLA Modules:
  0.0 74.9 jit_solution(13577943883124707699)
XLA Ops:
  0.0 1.2 %copy-done = bf16[128,4096]{1,0:T(8,128)(2,1)S(1)} copy-done((bf16[128,4096]{1,0:T(8,128)(2,1)S(1)}, bf16[128,4096]{1,0:T(8,128)(2,1)}, u32[]{:S(2)}) %copy-start) | copy-done | bytes 1048600
  1.2 0.8 %constant_dynamic-slice_fusion = bf16[64,4096]{1,0:T(8,128)(2,1)} fusion(bf16[128,4096]{1,0:T(8,128)(2,1)S(1)} %copy-done, s32[]{:T(128)S(6)} %select_n.128), kind=kLoop, calls=%fused_computation.46 | loop fusion | bytes 1048580 | tf_op jit(solution)/shard_map/dynamic_slice | solution.py:114
  2.1 3.0 %collective-permute-start = (bf16[64,4096]{1,0:T(8,128)(2,1)}, bf16[64,4096]{1,0:T(8,128)(2,1)S(1)}, u32[]{:S(2)}, u32[]{:S(2)}) collective-permute-start(bf16[64,4096]{1,0:T(8,128)(2,1)} %constant_dynamic-slice_fusion), channel_id=1, source_target_pairs={{0,4},{4,0},{8,12},{12,8},{1,5},{5,1},{9,13},{13,9},{2,6},{6,2},{1... | collective-permute-start | bytes 1572872 | tf_op jit(solution)/shard_map/ppermute | solution.py:83
  5.1 2.6 %collective-permute-start.1 = (bf16[64,4096]{1,0:T(8,128)(2,1)}, bf16[64,4096]{1,0:T(8,128)(2,1)S(1)}, u32[]{:S(2)}, u32[]{:S(2)}) collective-permute-start(bf16[64,4096]{1,0:T(8,128)(2,1)} %constant_dynamic-slice_fusion), channel_id=1, source_target_pairs={{0,8},{8,0},{4,12},{12,4},{1,9},{9,1},{5,13},{13,5},{2,10},{10,2},... | collective-permute-start | bytes 1572872 | tf_op jit(solution)/shard_map/ppermute | solution.py:83
  7.7 1.5 %collective-permute-start.2 = (bf16[2,64,1024]{2,1,0:T(8,128)(2,1)}, bf16[2,64,1024]{2,1,0:T(8,128)(2,1)}, u32[]{:S(2)}, u32[]{:S(2)}) collective-permute-start(bf16[2,64,1024]{2,1,0:T(8,128)(2,1)} %param.12), channel_id=1, source_target_pairs={{0,2},{2,0},{1,3},{3,1},{4,6},{6,4},{5,7},{7,5},{8,10},{10,8},{9,1... | collective-permute-start | bytes 786440 | tf_op jit(solution)/shard_map/ppermute | solution.py:80
  9.2 4.7 %fusion.25 = f32[128,1024]{1,0:T(8,128)S(1)} fusion(bf16[128,4096]{1,0:T(8,128)(2,1)S(1)} %copy-done, bf16[4096,1024]{1,0:T(8,128)(2,1)} %param.10), kind=kOutput, calls=%fused_computation.54 | convolution fusion | flops 1073741824 | bytes 9961472 | tf_op jit(solution)/shard_map/dot_general | solution.py:86
  13.9 0.1 select_reduce_fusion
  14.0 0.1 broadcast_compare_fusion
  14.1 0.5 fusion.8
  14.6 0.9 %collective-permute-done.2 = bf16[2,64,1024]{2,1,0:T(8,128)(2,1)} collective-permute-done((bf16[2,64,1024]{2,1,0:T(8,128)(2,1)}, bf16[2,64,1024]{2,1,0:T(8,128)(2,1)}, u32[]{:S(2)}, u32[]{:S(2)}) %collective-permute-start.2) | collective-permute-done | bytes 262176 | tf_op jit(solution)/shard_map/ppermute | solution.py:80
  15.5 1.9 %maximum_select_fusion.3 = bf16[4,64,1024]{2,1,0:T(8,128)(2,1)} fusion(bf16[2,64,1024]{2,1,0:T(8,128)(2,1)} %collective-permute-done.2, bf16[2,64,1024]{2,1,0:T(8,128)(2,1)S(1)} %copy-done.5, pred[]{:T(512)S(6)} %eq.55), kind=kLoop, calls=%fused_computation.9 | loop fusion | flops 786432 | bytes 1048577 | tf_op jit(solution)/shard_map/jit(_where)/select_n | solution.py:117
  17.4 10.9 %collective-permute-done = bf16[64,4096]{1,0:T(8,128)(2,1)S(1)} collective-permute-done((bf16[64,4096]{1,0:T(8,128)(2,1)}, bf16[64,4096]{1,0:T(8,128)(2,1)S(1)}, u32[]{:S(2)}, u32[]{:S(2)}) %collective-permute-start) | collective-permute-done | bytes 524320 | tf_op jit(solution)/shard_map/ppermute | solution.py:83
  28.3 2.6 %collective-permute-done.1 = bf16[64,4096]{1,0:T(8,128)(2,1)S(1)} collective-permute-done((bf16[64,4096]{1,0:T(8,128)(2,1)}, bf16[64,4096]{1,0:T(8,128)(2,1)S(1)}, u32[]{:S(2)}, u32[]{:S(2)}) %collective-permute-start.1) | collective-permute-done | bytes 524320 | tf_op jit(solution)/shard_map/ppermute | solution.py:83
  30.9 0.5 collective-permute-start.3
  31.4 0.5 collective-permute-start.5
  32.0 0.1 collective-permute-start.7
  32.0 0.0 slice-start.1
  32.0 0.5 collective-permute-start.8
  32.5 0.4 collective-permute-done.4
  32.9 0.4 collective-permute-done.5
  33.3 5.3 %select_convert_fusion = (bf16[128,1024]{1,0:T(8,128)(2,1)S(1)}, f32[128,1024]{1,0:T(8,128)S(1)}) fusion(f32[128,1024]{1,0:T(8,128)S(1)} %fusion.25, pred[]{:T(512)S(6)} %eq.54, bf16[4096,1024]{1,0:T(8,128)(2,1)} %param.10, bf16[32,4096]{1,0:T(8,128)(2,1)S(1)} %collective-permute-done.5, bf16[32,4096]{1,0:T(8,128)(2,1)S(1)} %collective-permute-done.4, ...), kind=kOutput, calls=%fused_computation.21 | convolution fusion | flops 1080688640 | bytes 10747906 | tf_op jit(solution)/shard_map/dot_general | solution.py:86
  38.6 1.6 %collective-permute-start.6 = (bf16[128,1024]{1,0:T(8,128)(2,1)S(1)}, bf16[128,1024]{1,0:T(8,128)(2,1)S(1)}, u32[]{:S(2)}, u32[]{:S(2)}) collective-permute-start(bf16[128,1024]{1,0:T(8,128)(2,1)S(1)} %get-tuple-element.45), channel_id=1, source_target_pairs={{0,2},{2,0},{1,3},{3,1},{4,6},{6,4},{5,7},{7,5},{8,10},{10,8},{9,1... | collective-permute-start | bytes 786440 | tf_op jit(solution)/shard_map/ppermute | solution.py:80
  40.2 0.5 fusion.6
  40.7 2.1 %fusion.19 = f32[128,1024]{1,0:T(8,128)} fusion(bf16[4096,1024]{1,0:T(8,128)(2,1)S(1)} %bitcast.55, bf16[32,4096]{1,0:T(8,128)(2,1)S(1)} %collective-permute-done.8, bf16[32,4096]{1,0:T(8,128)(2,1)S(1)} %collective-permute-done.7, bf16[64,4096]{1,0:T(8,128)(2,1)S(1)} %collective-permute-done, pred[]{:T(512)S(6)} %eq.56), kind=kOutput, calls=%fused_computation.48 | convolution fusion | flops 1080557568 | bytes 9961473 | tf_op jit(solution)/shard_map/dot_general | solution.py:86
  42.8 0.5 fusion.4
  43.3 3.8 %collective-permute-done.6 = bf16[128,1024]{1,0:T(8,128)(2,1)S(1)} collective-permute-done((bf16[128,1024]{1,0:T(8,128)(2,1)S(1)}, bf16[128,1024]{1,0:T(8,128)(2,1)S(1)}, u32[]{:S(2)}, u32[]{:S(2)}) %collective-permute-start.6) | collective-permute-done | bytes 262176 | tf_op jit(solution)/shard_map/ppermute | solution.py:80
  47.1 0.9 %convert_add_fusion = f32[128,1024]{1,0:T(8,128)} fusion(bf16[128,1024]{1,0:T(8,128)(2,1)S(1)} %collective-permute-done.6, f32[128,1024]{1,0:T(8,128)S(1)} %fusion.25, f32[128,1024]{1,0:T(8,128)S(1)} %get-tuple-element.46, pred[]{:T(512)S(6)} %eq.54), kind=kLoop, calls=%fused_computation.20 | loop fusion | flops 393216 | bytes 1835009 | tf_op jit(solution)/shard_map/add | solution.py:131
  48.0 0.1 collective-permute-start.11
  48.1 0.1 convert_divide_fusion
  48.2 0.5 collective-permute-start.9
  48.7 0.9 %collective-permute-done.11 = bf16[32,4096]{1,0:T(8,128)(2,1)S(1)} collective-permute-done((bf16[32,4096]{1,0:T(8,128)(2,1)S(1)}, bf16[32,4096]{1,0:T(8,128)(2,1)S(1)}, u32[]{:S(2)}, u32[]{:S(2)}) %collective-permute-start.11) | collective-permute-done | bytes 262176 | tf_op jit(solution)/shard_map/ppermute | solution.py:77
  49.6 0.1 maximum_select_fusion.5
  49.7 5.0 %bitcast_select_fusion.1 = (f32[64,1024]{1,0:T(8,128)S(1)}, bf16[64,1024]{1,0:T(8,128)(2,1)S(1)}) fusion(f32[2,1,32,1024]{3,2,1,0:T(8,128)S(1)} %get-tuple-element.38, pred[]{:T(512)S(6)} %eq.54, bf16[64,4096]{1,0:T(8,128)(2,1)S(1)} %maximum_select_fusion.5, bf16[4096,1024]{1,0:T(8,128)(2,1)} %param.10), kind=kOutput, calls=%fused_computation.23 | convolution fusion | flops 537001984 | bytes 9568257 | tf_op jit(solution)/shard_map/dot_general | solution.py:86
  54.7 1.6 %collective-permute-start.14 = (bf16[64,1024]{1,0:T(8,128)(2,1)S(1)}, bf16[64,1024]{1,0:T(8,128)(2,1)S(1)}, u32[]{:S(2)}, u32[]{:S(2)}) collective-permute-start(bf16[64,1024]{1,0:T(8,128)(2,1)S(1)} %fusion.10), channel_id=1, source_target_pairs={{0,2},{2,0},{1,3},{3,1},{4,6},{6,4},{5,7},{7,5},{8,10},{10,8},{9,1... | collective-permute-start | bytes 393224 | tf_op jit(solution)/shard_map/ppermute | solution.py:80
  56.3 0.1 maximum_select_fusion.4
  56.4 0.1 pad_maximum_fusion
  56.5 0.4 convolution_bitcast_fusion.1
  56.9 0.1 copy.18
  57.0 0.6 collective-permute-start.12
  57.6 5.0 %fusion.12 = (bf16[64,1024]{1,0:T(8,128)(2,1)S(1)}, f32[64,1024]{1,0:T(8,128)S(1)}) fusion(f32[2,1,32,1024]{3,2,1,0:T(8,128)S(1)} %get-tuple-element.37, pred[]{:T(512)S(6)} %eq.54, bf16[64,4096]{1,0:T(8,128)(2,1)S(1)} %maximum_select_fusion.4, bf16[4096,1024]{1,0:T(8,128)(2,1)} %param.10), kind=kOutput, calls=%fused_computation.28 | convolution fusion | flops 536936448 | bytes 9568257 | tf_op jit(solution)/shard_map/dot_general | solution.py:86
  62.6 1.6 %collective-permute-start.10 = (bf16[64,1024]{1,0:T(8,128)(2,1)S(1)}, bf16[64,1024]{1,0:T(8,128)(2,1)S(1)}, u32[]{:S(2)}, u32[]{:S(2)}) collective-permute-start(bf16[64,1024]{1,0:T(8,128)(2,1)S(1)} %get-tuple-element.49), channel_id=1, source_target_pairs={{0,2},{2,0},{1,3},{3,1},{4,6},{6,4},{5,7},{7,5},{8,10},{10,8},{9,1... | collective-permute-start | bytes 393224 | tf_op jit(solution)/shard_map/ppermute | solution.py:80
  64.2 1.7 %collective-permute-start.13 = (f32[256,64]{0,1:T(8,128)S(1)}, f32[256,64]{0,1:T(8,128)S(1)}, u32[]{:S(2)}, u32[]{:S(2)}) collective-permute-start(f32[256,64]{0,1:T(8,128)S(1)} %add_select_fusion), channel_id=1, source_target_pairs={{0,4},{4,0},{8,12},{12,8},{1,5},{5,1},{9,13},{13,9},{2,6},{6,2},{1... | collective-permute-start | bytes 196616 | tf_op jit(solution)/shard_map/ppermute | solution.py:83
  65.8 1.8 %collective-permute-done.10 = bf16[64,1024]{1,0:T(8,128)(2,1)S(1)} collective-permute-done((bf16[64,1024]{1,0:T(8,128)(2,1)S(1)}, bf16[64,1024]{1,0:T(8,128)(2,1)S(1)}, u32[]{:S(2)}, u32[]{:S(2)}) %collective-permute-start.10) | collective-permute-done | bytes 131104 | tf_op jit(solution)/shard_map/ppermute | solution.py:80
  67.6 0.1 fusion.11
  67.7 0.8 %collective-permute-done.13 = f32[256,64]{0,1:T(8,128)S(1)} collective-permute-done((f32[256,64]{0,1:T(8,128)S(1)}, f32[256,64]{0,1:T(8,128)S(1)}, u32[]{:S(2)}, u32[]{:S(2)}) %collective-permute-start.13) | collective-permute-done | bytes 65568 | tf_op jit(solution)/shard_map/ppermute | solution.py:83
  68.5 2.7 %collective-permute-start.15 = (f32[256,64]{0,1:T(8,128)S(1)}, f32[256,64]{0,1:T(8,128)S(1)}, u32[]{:S(2)}, u32[]{:S(2)}) collective-permute-start(f32[256,64]{0,1:T(8,128)S(1)} %add.42), channel_id=1, source_target_pairs={{0,8},{8,0},{4,12},{12,4},{1,9},{9,1},{5,13},{13,5},{2,10},{10,2},... | collective-permute-start | bytes 196616 | tf_op jit(solution)/shard_map/ppermute | solution.py:83
  71.3 2.4 %collective-permute-done.15 = f32[256,64]{0,1:T(8,128)S(1)} collective-permute-done((f32[256,64]{0,1:T(8,128)S(1)}, f32[256,64]{0,1:T(8,128)S(1)}, u32[]{:S(2)}, u32[]{:S(2)}) %collective-permute-start.15) | collective-permute-done | bytes 65568 | tf_op jit(solution)/shard_map/ppermute | solution.py:83
  73.8 1.1 %fusion.1 = bf16[256,1024]{1,0:T(8,128)(2,1)} fusion(bf16[4,64,1024]{2,1,0:T(8,128)(2,1)S(1)} %copy-done.3, f32[128,1024]{1,0:T(8,128)S(1)} %copy-done.4, f32[128,1024]{1,0:T(8,128)S(1)} %bitcast.60, bf16[256,1024]{1,0:T(8,128)(2,1)S(1)} %copy-done.9, pred[]{:T(512)S(6)} %eq.53, pred[256,4]{0,1:T(4,128)(4,1)S(1)} %iota_compare_fusion.2, ...), kind=kOutput, calls=%fused_computation.2 | convolution fusion | flops 136118272 | bytes 2655233 | tf_op jit(solution)/shard_map/dot_general | solution.py:151
  (43 shorter events, 0.4 us)
Async XLA Ops:
  0.0 1.2 %copy-start = (bf16[128,4096]{1,0:T(8,128)(2,1)S(1)}, bf16[128,4096]{1,0:T(8,128)(2,1)}, u32[]{:S(2)}) copy-start(bf16[128,4096]{1,0:T(8,128)(2,1)} %param.8) | copy-start | bytes 3145732
  2.1 26.3 %collective-permute-start = (bf16[64,4096]{1,0:T(8,128)(2,1)}, bf16[64,4096]{1,0:T(8,128)(2,1)S(1)}, u32[]{:S(2)}, u32[]{:S(2)}) collective-permute-start(bf16[64,4096]{1,0:T(8,128)(2,1)} %constant_dynamic-slice_fusion), channel_id=1, source_target_pairs={{0,4},{4,0},{8,12},{12,8},{1,5},{5,1},{9,13},{13,9},{2,6},{6,2},{1... | collective-permute-start | bytes 1572872 | tf_op jit(solution)/shard_map/ppermute | solution.py:83
  5.1 25.8 %collective-permute-start.1 = (bf16[64,4096]{1,0:T(8,128)(2,1)}, bf16[64,4096]{1,0:T(8,128)(2,1)S(1)}, u32[]{:S(2)}, u32[]{:S(2)}) collective-permute-start(bf16[64,4096]{1,0:T(8,128)(2,1)} %constant_dynamic-slice_fusion), channel_id=1, source_target_pairs={{0,8},{8,0},{4,12},{12,4},{1,9},{9,1},{5,13},{13,5},{2,10},{10,2},... | collective-permute-start | bytes 1572872 | tf_op jit(solution)/shard_map/ppermute | solution.py:83
  7.7 7.8 %collective-permute-start.2 = (bf16[2,64,1024]{2,1,0:T(8,128)(2,1)}, bf16[2,64,1024]{2,1,0:T(8,128)(2,1)}, u32[]{:S(2)}, u32[]{:S(2)}) collective-permute-start(bf16[2,64,1024]{2,1,0:T(8,128)(2,1)} %param.12), channel_id=1, source_target_pairs={{0,2},{2,0},{1,3},{3,1},{4,6},{6,4},{5,7},{7,5},{8,10},{10,8},{9,1... | collective-permute-start | bytes 786440 | tf_op jit(solution)/shard_map/ppermute | solution.py:80
  9.2 4.7 %copy-start.6 = (s32[512]{0:T(512)S(1)}, s32[512]{0:T(512)}, u32[]{:S(2)}) copy-start(s32[512]{0:T(512)} %param.13) | copy-start | bytes 6148
  9.2 4.7 %copy-start.7 = (s32[4]{0:T(128)S(1)}, s32[4]{0:T(128)}, u32[]{:S(2)}) copy-start(s32[4]{0:T(128)} %param.15) | copy-start | bytes 52
  9.2 4.8 %copy-start.8 = (s32[4]{0:T(128)S(1)}, s32[4]{0:T(128)}, u32[]{:S(2)}) copy-start(s32[4]{0:T(128)} %param.14) | copy-start | bytes 52
  9.2 4.9 %copy-start.1 = (bf16[1,64,4096]{2,1,0:T(8,128)(2,1)S(1)}, bf16[1,64,4096]{2,1,0:T(8,128)(2,1)}, u32[]{:S(2)}) copy-start(bf16[1,64,4096]{2,1,0:T(8,128)(2,1)} %param.11) | copy-start | bytes 1572868
  9.2 6.3 %copy-start.5 = (bf16[2,64,1024]{2,1,0:T(8,128)(2,1)S(1)}, bf16[2,64,1024]{2,1,0:T(8,128)(2,1)}, u32[]{:S(2)}) copy-start(bf16[2,64,1024]{2,1,0:T(8,128)(2,1)} %param.12) | copy-start | bytes 786436
  30.9 17.1 %collective-permute-start.3 = (bf16[64,4096]{1,0:T(8,128)(2,1)S(1)}, bf16[64,4096]{1,0:T(8,128)(2,1)S(1)}, u32[]{:S(2)}, u32[]{:S(2)}) collective-permute-start(bf16[64,4096]{1,0:T(8,128)(2,1)S(1)} %collective-permute-done.1), channel_id=1, source_target_pairs={{0,4},{4,0},{8,12},{12,8},{1,5},{5,1},{9,13},{13,9},{2,6},{6,2},{1... | collective-permute-start | bytes 1572872 | tf_op jit(solution)/shard_map/ppermute | solution.py:83
  31.4 1.5 %collective-permute-start.4 = (bf16[32,4096]{1,0:T(8,128)(2,1)S(1)}, bf16[32,4096]{1,0:T(8,128)(2,1)S(1)}, u32[]{:S(2)}, u32[]{:S(2)}) collective-permute-start(bf16[32,4096]{1,0:T(8,128)(2,1)S(1)} %get-tuple-element.43), channel_id=1, source_target_pairs={{0,1},{1,0},{2,3},{3,2},{4,5},{5,4},{6,7},{7,6},{8,9},{9,8},{10,11... | collective-permute-start | bytes 786440 | tf_op jit(solution)/shard_map/ppermute | solution.py:77
  31.4 1.9 %collective-permute-start.5 = (bf16[32,4096]{1,0:T(8,128)(2,1)S(1)}, bf16[32,4096]{1,0:T(8,128)(2,1)S(1)}, u32[]{:S(2)}, u32[]{:S(2)}) collective-permute-start(bf16[32,4096]{1,0:T(8,128)(2,1)S(1)} %get-tuple-element.44), channel_id=1, source_target_pairs={{0,1},{1,0},{2,3},{3,2},{4,5},{5,4},{6,7},{7,6},{8,9},{9,8},{10,11... | collective-permute-start | bytes 786440 | tf_op jit(solution)/shard_map/ppermute | solution.py:77
  31.9 8.8 %slice-start = ((s8[8388608]{0:T(1024)(128)(4,1)}), s8[4194304]{0:T(1024)(128)(4,1)S(1)}, s32[]{:S(2)}) async-start(s8[8388608]{0:T(1024)(128)(4,1)} %bitcast.54), calls=%async_computation | async-start | bytes 8388608
  32.0 8.7 %collective-permute-start.7 = (bf16[32,4096]{1,0:T(8,128)(2,1)S(1)}, bf16[32,4096]{1,0:T(8,128)(2,1)S(1)}, u32[]{:S(2)}, u32[]{:S(2)}) collective-permute-start(bf16[32,4096]{1,0:T(8,128)(2,1)S(1)} %get-tuple-element.41), channel_id=1, source_target_pairs={{0,1},{1,0},{2,3},{3,2},{4,5},{5,4},{6,7},{7,6},{8,9},{9,8},{10,11... | collective-permute-start | bytes 786440 | tf_op jit(solution)/shard_map/ppermute | solution.py:77
  32.0 8.7 %slice-start.1 = ((s8[8388608]{0:T(1024)(128)(4,1)}), s8[4194304]{0:T(1024)(128)(4,1)S(1)}, s32[]{:S(2)}) async-start(s8[8388608]{0:T(1024)(128)(4,1)} %bitcast.54), calls=%async_computation.1 | async-start | bytes 8388608
  32.0 8.6 %collective-permute-start.8 = (bf16[32,4096]{1,0:T(8,128)(2,1)S(1)}, bf16[32,4096]{1,0:T(8,128)(2,1)S(1)}, u32[]{:S(2)}, u32[]{:S(2)}) collective-permute-start(bf16[32,4096]{1,0:T(8,128)(2,1)S(1)} %get-tuple-element.42), channel_id=1, source_target_pairs={{0,1},{1,0},{2,3},{3,2},{4,5},{5,4},{6,7},{7,6},{8,9},{9,8},{10,11... | collective-permute-start | bytes 786440 | tf_op jit(solution)/shard_map/ppermute | solution.py:77
  38.6 8.5 %collective-permute-start.6 = (bf16[128,1024]{1,0:T(8,128)(2,1)S(1)}, bf16[128,1024]{1,0:T(8,128)(2,1)S(1)}, u32[]{:S(2)}, u32[]{:S(2)}) collective-permute-start(bf16[128,1024]{1,0:T(8,128)(2,1)S(1)} %get-tuple-element.45), channel_id=1, source_target_pairs={{0,2},{2,0},{1,3},{3,1},{4,6},{6,4},{5,7},{7,5},{8,10},{10,8},{9,1... | collective-permute-start | bytes 786440 | tf_op jit(solution)/shard_map/ppermute | solution.py:80
  43.3 5.4 %copy-start.2 = (f32[128,1024]{1,0:T(8,128)S(1)}, f32[128,1024]{1,0:T(8,128)}, u32[]{:S(2)}) copy-start(f32[128,1024]{1,0:T(8,128)} %fusion.19) | copy-start | bytes 1572868
  48.0 1.6 %collective-permute-start.11 = (bf16[32,4096]{1,0:T(8,128)(2,1)S(1)}, bf16[32,4096]{1,0:T(8,128)(2,1)S(1)}, u32[]{:S(2)}, u32[]{:S(2)}) collective-permute-start(bf16[32,4096]{1,0:T(8,128)(2,1)S(1)} %get-tuple-element.40), channel_id=1, source_target_pairs={{0,1},{1,0},{2,3},{3,2},{4,5},{5,4},{6,7},{7,6},{8,9},{9,8},{10,11... | collective-permute-start | bytes 786440 | tf_op jit(solution)/shard_map/ppermute | solution.py:77
  48.2 8.1 %collective-permute-start.9 = (bf16[32,4096]{1,0:T(8,128)(2,1)S(1)}, bf16[32,4096]{1,0:T(8,128)(2,1)S(1)}, u32[]{:S(2)}, u32[]{:S(2)}) collective-permute-start(bf16[32,4096]{1,0:T(8,128)(2,1)S(1)} %get-tuple-element.39), channel_id=1, source_target_pairs={{0,1},{1,0},{2,3},{3,2},{4,5},{5,4},{6,7},{7,6},{8,9},{9,8},{10,11... | collective-permute-start | bytes 786440 | tf_op jit(solution)/shard_map/ppermute | solution.py:77
  54.7 13.8 %collective-permute-start.14 = (bf16[64,1024]{1,0:T(8,128)(2,1)S(1)}, bf16[64,1024]{1,0:T(8,128)(2,1)S(1)}, u32[]{:S(2)}, u32[]{:S(2)}) collective-permute-start(bf16[64,1024]{1,0:T(8,128)(2,1)S(1)} %fusion.10), channel_id=1, source_target_pairs={{0,2},{2,0},{1,3},{3,1},{4,6},{6,4},{5,7},{7,5},{8,10},{10,8},{9,1... | collective-permute-start | bytes 393224 | tf_op jit(solution)/shard_map/ppermute | solution.py:80
  57.0 7.2 %collective-permute-start.12 = (f32[256,64]{0,1:T(8,128)S(1)}, f32[256,64]{0,1:T(8,128)S(1)}, u32[]{:S(2)}, u32[]{:S(2)}) collective-permute-start(f32[256,64]{0,1:T(8,128)S(1)} %fusion.17), channel_id=1, source_target_pairs={{0,2},{2,0},{1,3},{3,1},{4,6},{6,4},{5,7},{7,5},{8,10},{10,8},{9,1... | collective-permute-start | bytes 196616 | tf_op jit(solution)/shard_map/ppermute | solution.py:80
  62.6 11.2 %copy-start.3 = (bf16[4,64,1024]{2,1,0:T(8,128)(2,1)S(1)}, bf16[4,64,1024]{2,1,0:T(8,128)(2,1)}, u32[]{:S(2)}) copy-start(bf16[4,64,1024]{2,1,0:T(8,128)(2,1)} %maximum_select_fusion.3) | copy-start | bytes 1572868
  62.6 11.2 %copy-start.4 = (f32[128,1024]{1,0:T(8,128)S(1)}, f32[128,1024]{1,0:T(8,128)}, u32[]{:S(2)}) copy-start(f32[128,1024]{1,0:T(8,128)} %convert_add_fusion) | copy-start | bytes 1572868
  62.6 11.2 %copy-start.9 = (bf16[256,1024]{1,0:T(8,128)(2,1)S(1)}, bf16[256,1024]{1,0:T(8,128)(2,1)}, u32[]{:S(2)}) copy-start(bf16[256,1024]{1,0:T(8,128)(2,1)} %param.9) | copy-start | bytes 1572868
  62.6 5.0 %collective-permute-start.10 = (bf16[64,1024]{1,0:T(8,128)(2,1)S(1)}, bf16[64,1024]{1,0:T(8,128)(2,1)S(1)}, u32[]{:S(2)}, u32[]{:S(2)}) collective-permute-start(bf16[64,1024]{1,0:T(8,128)(2,1)S(1)} %get-tuple-element.49), channel_id=1, source_target_pairs={{0,2},{2,0},{1,3},{3,1},{4,6},{6,4},{5,7},{7,5},{8,10},{10,8},{9,1... | collective-permute-start | bytes 393224 | tf_op jit(solution)/shard_map/ppermute | solution.py:80
  64.2 4.3 %collective-permute-start.13 = (f32[256,64]{0,1:T(8,128)S(1)}, f32[256,64]{0,1:T(8,128)S(1)}, u32[]{:S(2)}, u32[]{:S(2)}) collective-permute-start(f32[256,64]{0,1:T(8,128)S(1)} %add_select_fusion), channel_id=1, source_target_pairs={{0,4},{4,0},{8,12},{12,8},{1,5},{5,1},{9,13},{13,9},{2,6},{6,2},{1... | collective-permute-start | bytes 196616 | tf_op jit(solution)/shard_map/ppermute | solution.py:83
  68.5 5.2 %collective-permute-start.15 = (f32[256,64]{0,1:T(8,128)S(1)}, f32[256,64]{0,1:T(8,128)S(1)}, u32[]{:S(2)}, u32[]{:S(2)}) collective-permute-start(f32[256,64]{0,1:T(8,128)S(1)} %add.42), channel_id=1, source_target_pairs={{0,8},{8,0},{4,12},{12,4},{1,9},{9,1},{5,13},{13,5},{2,10},{10,2},... | collective-permute-start | bytes 196616 | tf_op jit(solution)/shard_map/ppermute | solution.py:83

commit v7 on v6

--- a/solution.py
+++ b/solution.py
@@ -1,6 +1,8 @@
 import jax
 import jax.numpy as jnp
 from jax import lax
+from jax.experimental import pallas as pl
+from jax.experimental.pallas import tpu as pltpu
 from jax.sharding import PartitionSpec as P
 
 F32 = jnp.float32
@@ -62,6 +64,23 @@
 FAR = [(0, 2), (2, 0), (1, 3), (3, 1)]
 
 
+def hold_kernel(array_ref, held_ref, sem):
+    copy = pltpu.make_async_copy(array_ref, held_ref, sem)
+    copy.start()
+    copy.wait()
+
+
+def hold(array):
+    return pl.pallas_call(
+        hold_kernel,
+        out_shape=jax.ShapeDtypeStruct(array.shape, array.dtype),
+        in_specs=[pl.BlockSpec(memory_space=pltpu.HBM)],
+        out_specs=pl.BlockSpec(memory_space=pltpu.VMEM),
+        scratch_shapes=[pltpu.SemaphoreType.DMA],
+        compiler_params=pltpu.CompilerParams(vmem_limit_bytes=1024 * 1024),
+    )(array)
+
+
 def line(rows, residual, weight, down, up, tenant, entry, live):
     z, x, c = lax.axis_index("blk"), lax.axis_index("split"), lax.axis_index("sub")
     block_rows = rows.shape[0]
@@ -82,8 +101,10 @@
     def along(value, pairs):
         return lax.ppermute(value, "blk", pairs)
 
+    held = hold(weight)
+
     def product(block):
-        return jnp.dot(block, weight, preferred_element_type=F32)
+        return jnp.dot(block, held, preferred_element_type=F32)
 
     def low_rank(block):
         return lax.dot_general(

time: 75.2 us -> 77.5 us (1.031)
  local copies, waits for them, and re-layouts: 2.31 us -> 9.5 us
  matrix products: 25 us -> 19.6 us
  other arithmetic: 3.51 us -> 4.8 us
  waiting for transfers between devices: 24.9 us -> 24 us
    unnamed x24 -> x28, local copies, waits for them, and re-layouts: 1.28 us -> 8.42 us
    dot_general x5, matrix products: 22 us -> 15.4 us  [product(): return jnp.dot(block, held, preferred_element_type=F32)]
    ppermute x5, waiting for transfers between devices: 16.7 us -> 12.6 us  [along(): return lax.ppermute(value, 'blk', pairs)]
    ppermute x5, waiting for transfers between devices: 6.47 us -> 9.54 us  [over_x(): return lax.ppermute(value, 'split', SWAP)]
    dot_general x1, matrix products: 1.13 us -> 2.33 us  [line(): jnp.dot(spread, ups.reshape(slots * width, cols), preferred_element_type=...]
    select_n x2, other arithmetic: 0.18 us -> 1.22 us  [joined(): jnp.where(c == 0, jnp.concatenate([piece, other]), jnp.concatenate([other...]
  transfers between devices with their start and end apart: 16 -> 16, of which waited for: 10 -> 9; matrix products, arithmetic and copies ran while one was open for 37% -> 26% of each run, Pallas kernels for 0% -> 1%
where the time goes in v7:
time: 77.5 us; the launch traced here: 77.2 us
  waiting for transfers between devices  24 us (31%)
  matrix products  19.6 us (25%)
  starting transfers between devices  18.4 us (24%)
  local copies, waits for them, and re-layouts  9.5 us (12%)
  other arithmetic  4.8 us (6%)
    dot_general x5, matrix products, product(): return jnp.dot(block, held, preferred_element_type=F32)  15.4 us
    ppermute x5, waiting for transfers between devices, along(): return lax.ppermute(value, 'blk', pairs)  12.6 us
    ppermute x5, starting transfers between devices, along(): return lax.ppermute(value, 'blk', pairs)  10.1 us
    ppermute x5, waiting for transfers between devices, over_x(): return lax.ppermute(value, 'split', SWAP)  9.54 us
    unnamed x28, local copies, waits for them, and re-layouts  8.42 us
    ppermute x5, starting transfers between devices, over_x(): return lax.ppermute(value, 'split', SWAP)  6.7 us
    dot_general x1, matrix products, line(): jnp.dot(spread, ups.reshape(slots * width, cols), preferred_element_type=...  2.33 us
    select_n x1, other arithmetic, line(): jnp.where(x == 0, jnp.concatenate([up, up_other]), jnp.concatenate([up_ot...  2.1 us
  transfers between devices with their start and end apart: 16, of which 9 were waited for; matrix products, arithmetic and copies ran while one was open for 26% of the time, Pallas kernels for 1%

profile of v7, /device:TPU:0, one launch (start us, length us, event | category | flops | bytes accessed | tf_op | source)
XLA Modules:
  0.0 77.2 jit_solution(8542490357298388230)
XLA Ops:
  0.0 1.2 %copy-done = bf16[128,4096]{1,0:T(8,128)(2,1)S(1)} copy-done((bf16[128,4096]{1,0:T(8,128)(2,1)S(1)}, bf16[128,4096]{1,0:T(8,128)(2,1)}, u32[]{:S(2)}) %copy-start) | copy-done | bytes 1048600
  1.2 0.9 %constant_dynamic-slice_fusion = bf16[64,4096]{1,0:T(8,128)(2,1)} fusion(bf16[128,4096]{1,0:T(8,128)(2,1)S(1)} %copy-done, s32[]{:T(128)S(6)} %select_n.128), kind=kLoop, calls=%fused_computation.46 | loop fusion | bytes 1048580 | tf_op jit(solution)/shard_map/dynamic_slice | solution.py:135
  2.1 4.0 %collective-permute-start.1 = (bf16[64,4096]{1,0:T(8,128)(2,1)}, bf16[64,4096]{1,0:T(8,128)(2,1)S(1)}, u32[]{:S(2)}, u32[]{:S(2)}) collective-permute-start(bf16[64,4096]{1,0:T(8,128)(2,1)} %constant_dynamic-slice_fusion), channel_id=1, source_target_pairs={{0,8},{8,0},{4,12},{12,4},{1,9},{9,1},{5,13},{13,5},{2,10},{10,2},... | collective-permute-start | bytes 1572872 | tf_op jit(solution)/shard_map/ppermute | solution.py:102
  6.1 1.6 %collective-permute-start = (bf16[64,4096]{1,0:T(8,128)(2,1)}, bf16[64,4096]{1,0:T(8,128)(2,1)S(1)}, u32[]{:S(2)}, u32[]{:S(2)}) collective-permute-start(bf16[64,4096]{1,0:T(8,128)(2,1)} %constant_dynamic-slice_fusion), channel_id=1, source_target_pairs={{0,4},{4,0},{8,12},{12,8},{1,5},{5,1},{9,13},{13,9},{2,6},{6,2},{1... | collective-permute-start | bytes 1572872 | tf_op jit(solution)/shard_map/ppermute | solution.py:102
  7.7 1.5 %collective-permute-start.2 = (bf16[2,64,1024]{2,1,0:T(8,128)(2,1)}, bf16[2,64,1024]{2,1,0:T(8,128)(2,1)}, u32[]{:S(2)}, u32[]{:S(2)}) collective-permute-start(bf16[2,64,1024]{2,1,0:T(8,128)(2,1)} %param.12), channel_id=1, source_target_pairs={{0,2},{2,0},{1,3},{3,1},{4,6},{6,4},{5,7},{7,5},{8,10},{10,8},{9,1... | collective-permute-start | bytes 786440 | tf_op jit(solution)/shard_map/ppermute | solution.py:99
  9.2 3.4 %copy-done.2 = bf16[4096,1024]{1,0:T(8,128)(2,1)S(1)} copy-done((bf16[4096,1024]{1,0:T(8,128)(2,1)S(1)}, bf16[4096,1024]{1,0:T(8,128)(2,1)}, u32[]{:S(2)}) %copy-start.2) | copy-done | bytes 8388632
  12.6 0.6 shard_map.82
  13.2 3.3 %copy-done.1 = bf16[4096,1024]{1,0:T(8,128)(2,1)} copy-done((bf16[4096,1024]{1,0:T(8,128)(2,1)}, bf16[4096,1024]{1,0:T(8,128)(2,1)S(1)}, u32[]{:S(2)}) %copy-start.1) | copy-done | bytes 8388632
  16.4 1.3 %fusion.25 = f32[128,1024]{1,0:T(8,128)S(1)} fusion(bf16[128,4096]{1,0:T(8,128)(2,1)S(1)} %copy-done, bf16[4096,1024]{1,0:T(8,128)(2,1)S(1)} %shard_map.82), kind=kOutput, calls=%fused_computation.54 | convolution fusion | flops 1073741824 | bytes 9961472 | tf_op jit(solution)/shard_map/dot_general | solution.py:107
  17.8 0.1 select_reduce_fusion
  17.9 0.1 broadcast_compare_fusion
  18.0 0.5 fusion.8
  18.5 2.1 %maximum_select_fusion.3 = bf16[4,64,1024]{2,1,0:T(8,128)(2,1)} fusion(bf16[2,64,1024]{2,1,0:T(8,128)(2,1)} %collective-permute-done.2, bf16[2,64,1024]{2,1,0:T(8,128)(2,1)} %param.12, pred[]{:T(512)S(6)} %eq.55), kind=kLoop, calls=%fused_computation.9 | loop fusion | flops 786432 | bytes 1048577 | tf_op jit(solution)/shard_map/jit(_where)/select_n | solution.py:138
  20.6 9.0 %collective-permute-done.1 = bf16[64,4096]{1,0:T(8,128)(2,1)S(1)} collective-permute-done((bf16[64,4096]{1,0:T(8,128)(2,1)}, bf16[64,4096]{1,0:T(8,128)(2,1)S(1)}, u32[]{:S(2)}, u32[]{:S(2)}) %collective-permute-start.1) | collective-permute-done | bytes 524320 | tf_op jit(solution)/shard_map/ppermute | solution.py:102
  29.6 0.2 collective-permute-done
  29.8 1.6 %collective-permute-start.3 = (bf16[64,4096]{1,0:T(8,128)(2,1)S(1)}, bf16[64,4096]{1,0:T(8,128)(2,1)S(1)}, u32[]{:S(2)}, u32[]{:S(2)}) collective-permute-start(bf16[64,4096]{1,0:T(8,128)(2,1)S(1)} %collective-permute-done.1), channel_id=1, source_target_pairs={{0,4},{4,0},{8,12},{12,8},{1,5},{5,1},{9,13},{13,9},{2,6},{6,2},{1... | collective-permute-start | bytes 1572872 | tf_op jit(solution)/shard_map/ppermute | solution.py:102
  31.4 0.5 collective-permute-start.5
  31.9 0.1 collective-permute-start.7
  32.0 0.5 collective-permute-start.8
  32.5 0.4 collective-permute-done.4
  32.9 0.4 collective-permute-done.5
  33.3 5.3 %select_convert_fusion = (bf16[128,1024]{1,0:T(8,128)(2,1)S(1)}, f32[128,1024]{1,0:T(8,128)S(1)}) fusion(f32[128,1024]{1,0:T(8,128)S(1)} %fusion.25, pred[]{:T(512)S(6)} %eq.54, bf16[4096,1024]{1,0:T(8,128)(2,1)} %copy-done.1, bf16[32,4096]{1,0:T(8,128)(2,1)S(1)} %collective-permute-done.5, bf16[32,4096]{1,0:T(8,128)(2,1)S(1)} %collective-permute-done.4, ...), kind=kOutput, calls=%fused_computation.21 | convolution fusion | flops 1080688640 | bytes 10747906 | tf_op jit(solution)/shard_map/dot_general | solution.py:107
  38.6 1.6 %collective-permute-start.6 = (bf16[128,1024]{1,0:T(8,128)(2,1)S(1)}, bf16[128,1024]{1,0:T(8,128)(2,1)S(1)}, u32[]{:S(2)}, u32[]{:S(2)}) collective-permute-start(bf16[128,1024]{1,0:T(8,128)(2,1)S(1)} %get-tuple-element.45), channel_id=1, source_target_pairs={{0,2},{2,0},{1,3},{3,1},{4,6},{6,4},{5,7},{7,5},{8,10},{10,8},{9,1... | collective-permute-start | bytes 786440 | tf_op jit(solution)/shard_map/ppermute | solution.py:99
  40.2 0.5 fusion.4
  40.7 2.1 %fusion.19 = f32[128,1024]{1,0:T(8,128)} fusion(bf16[4096,1024]{1,0:T(8,128)(2,1)S(1)} %bitcast.55, bf16[32,4096]{1,0:T(8,128)(2,1)S(1)} %collective-permute-done.8, bf16[32,4096]{1,0:T(8,128)(2,1)S(1)} %collective-permute-done.7, bf16[64,4096]{1,0:T(8,128)(2,1)S(1)} %collective-permute-done, pred[]{:T(512)S(6)} %eq.56), kind=kOutput, calls=%fused_computation.48 | convolution fusion | flops 1080557568 | bytes 9961473 | tf_op jit(solution)/shard_map/dot_general | solution.py:107
  42.7 0.5 fusion.6
  43.2 3.8 %collective-permute-done.6 = bf16[128,1024]{1,0:T(8,128)(2,1)S(1)} collective-permute-done((bf16[128,1024]{1,0:T(8,128)(2,1)S(1)}, bf16[128,1024]{1,0:T(8,128)(2,1)S(1)}, u32[]{:S(2)}, u32[]{:S(2)}) %collective-permute-start.6) | collective-permute-done | bytes 262176 | tf_op jit(solution)/shard_map/ppermute | solution.py:99
  47.1 0.9 %convert_add_fusion = f32[128,1024]{1,0:T(8,128)} fusion(bf16[128,1024]{1,0:T(8,128)(2,1)S(1)} %collective-permute-done.6, f32[128,1024]{1,0:T(8,128)S(1)} %fusion.25, f32[128,1024]{1,0:T(8,128)S(1)} %get-tuple-element.46, pred[]{:T(512)S(6)} %eq.54), kind=kLoop, calls=%fused_computation.20 | loop fusion | flops 393216 | bytes 1835009 | tf_op jit(solution)/shard_map/add | solution.py:152
  48.0 0.1 collective-permute-start.11
  48.1 0.1 convert_divide_fusion
  48.2 0.5 collective-permute-start.9
  48.7 1.0 %collective-permute-done.11 = bf16[32,4096]{1,0:T(8,128)(2,1)} collective-permute-done((bf16[32,4096]{1,0:T(8,128)(2,1)S(1)}, bf16[32,4096]{1,0:T(8,128)(2,1)}, u32[]{:S(2)}, u32[]{:S(2)}) %collective-permute-start.11) | collective-permute-done | bytes 262176 | tf_op jit(solution)/shard_map/ppermute | solution.py:96
  49.8 1.1 %maximum_select_fusion.5 = bf16[64,4096]{1,0:T(8,128)(2,1)S(1)} fusion(bf16[32,4096]{1,0:T(8,128)(2,1)} %collective-permute-done.11, bf16[32,4096]{1,0:T(8,128)(2,1)S(1)} %get-tuple-element.40, pred[]{:T(512)S(6)} %eq.56), kind=kLoop, calls=%fused_computation.11 | loop fusion | flops 2359296 | bytes 1048577 | tf_op jit(solution)/shard_map/jit(_where)/select_n | solution.py:115
  50.9 5.1 %bitcast_select_fusion.1 = (f32[64,1024]{1,0:T(8,128)S(1)}, bf16[64,1024]{1,0:T(8,128)(2,1)S(1)}) fusion(f32[2,1,32,1024]{3,2,1,0:T(8,128)S(1)} %get-tuple-element.38, pred[]{:T(512)S(6)} %eq.54, bf16[64,4096]{1,0:T(8,128)(2,1)S(1)} %maximum_select_fusion.5, bf16[4096,1024]{1,0:T(8,128)(2,1)} %copy-done.1), kind=kOutput, calls=%fused_computation.23 | convolution fusion | flops 537001984 | bytes 9568257 | tf_op jit(solution)/shard_map/dot_general | solution.py:107
  56.0 0.1 maximum_select_fusion.4
  56.1 0.1 pad_maximum_fusion
  56.3 0.5 slice-done.3
  56.7 1.6 %fusion.12 = (bf16[64,1024]{1,0:T(8,128)(2,1)S(1)}, f32[64,1024]{1,0:T(8,128)S(1)}) fusion(f32[2,1,32,1024]{3,2,1,0:T(8,128)S(1)} %get-tuple-element.37, pred[]{:T(512)S(6)} %eq.54, bf16[64,4096]{1,0:T(8,128)(2,1)S(1)} %maximum_select_fusion.4, bf16[4096,1024]{1,0:T(8,128)(2,1)S(1)} %bitcast.57), kind=kOutput, calls=%fused_computation.28 | convolution fusion | flops 536936448 | bytes 9568257 | tf_op jit(solution)/shard_map/dot_general | solution.py:107
  58.3 0.4 convolution_bitcast_fusion.1
  58.9 1.6 %collective-permute-start.12 = (f32[256,64]{0,1:T(8,128)S(1)}, f32[256,64]{0,1:T(8,128)S(1)}, u32[]{:S(2)}, u32[]{:S(2)}) collective-permute-start(f32[256,64]{0,1:T(8,128)S(1)} %fusion.17), channel_id=1, source_target_pairs={{0,2},{2,0},{1,3},{3,1},{4,6},{6,4},{5,7},{7,5},{8,10},{10,8},{9,1... | collective-permute-start | bytes 196616 | tf_op jit(solution)/shard_map/ppermute | solution.py:99
  60.5 0.6 collective-permute-start.14
  61.1 1.5 %collective-permute-start.10 = (bf16[64,1024]{1,0:T(8,128)(2,1)S(1)}, bf16[64,1024]{1,0:T(8,128)(2,1)S(1)}, u32[]{:S(2)}, u32[]{:S(2)}) collective-permute-start(bf16[64,1024]{1,0:T(8,128)(2,1)S(1)} %get-tuple-element.49), channel_id=1, source_target_pairs={{0,2},{2,0},{1,3},{3,1},{4,6},{6,4},{5,7},{7,5},{8,10},{10,8},{9,1... | collective-permute-start | bytes 393224 | tf_op jit(solution)/shard_map/ppermute | solution.py:99
  62.6 1.0 %collective-permute-done.12 = f32[256,64]{0,1:T(8,128)S(1)} collective-permute-done((f32[256,64]{0,1:T(8,128)S(1)}, f32[256,64]{0,1:T(8,128)S(1)}, u32[]{:S(2)}, u32[]{:S(2)}) %collective-permute-start.12) | collective-permute-done | bytes 65568 | tf_op jit(solution)/shard_map/ppermute | solution.py:99
  63.6 0.5 collective-permute-start.13
  64.1 4.8 %collective-permute-done.10 = bf16[64,1024]{1,0:T(8,128)(2,1)S(1)} collective-permute-done((bf16[64,1024]{1,0:T(8,128)(2,1)S(1)}, bf16[64,1024]{1,0:T(8,128)(2,1)S(1)}, u32[]{:S(2)}, u32[]{:S(2)}) %collective-permute-start.10) | collective-permute-done | bytes 131104 | tf_op jit(solution)/shard_map/ppermute | solution.py:99
  68.9 2.4 %collective-permute-start.15 = (f32[256,64]{0,1:T(8,128)S(1)}, f32[256,64]{0,1:T(8,128)S(1)}, u32[]{:S(2)}, u32[]{:S(2)}) collective-permute-start(f32[256,64]{0,1:T(8,128)S(1)} %add.42), channel_id=1, source_target_pairs={{0,8},{8,0},{4,12},{12,4},{1,9},{9,1},{5,13},{13,5},{2,10},{10,2},... | collective-permute-start | bytes 196616 | tf_op jit(solution)/shard_map/ppermute | solution.py:102
  71.4 3.4 %collective-permute-done.15 = f32[256,64]{0,1:T(8,128)S(1)} collective-permute-done((f32[256,64]{0,1:T(8,128)S(1)}, f32[256,64]{0,1:T(8,128)S(1)}, u32[]{:S(2)}, u32[]{:S(2)}) %collective-permute-start.15) | collective-permute-done | bytes 65568 | tf_op jit(solution)/shard_map/ppermute | solution.py:102
  74.9 2.3 %fusion.1 = bf16[256,1024]{1,0:T(8,128)(2,1)} fusion(bf16[4,64,1024]{2,1,0:T(8,128)(2,1)S(1)} %copy-done.5, f32[128,1024]{1,0:T(8,128)} %convert_add_fusion, f32[128,1024]{1,0:T(8,128)S(1)} %bitcast.62, bf16[256,1024]{1,0:T(8,128)(2,1)S(1)} %copy-done.9, pred[]{:T(512)S(6)} %eq.53, pred[256,4]{0,1:T(4,128)(4,1)S(1)} %iota_compare_fusion.2, ...), kind=kOutput, calls=%fused_computation.2 | convolution fusion | flops 136118272 | bytes 2655233 | tf_op jit(solution)/shard_map/dot_general | solution.py:172
  (49 shorter events, 0.5 us)
Async XLA Ops:
  0.0 1.2 %copy-start = (bf16[128,4096]{1,0:T(8,128)(2,1)S(1)}, bf16[128,4096]{1,0:T(8,128)(2,1)}, u32[]{:S(2)}) copy-start(bf16[128,4096]{1,0:T(8,128)(2,1)} %param.8) | copy-start | bytes 3145732
  2.1 27.5 %collective-permute-start.1 = (bf16[64,4096]{1,0:T(8,128)(2,1)}, bf16[64,4096]{1,0:T(8,128)(2,1)S(1)}, u32[]{:S(2)}, u32[]{:S(2)}) collective-permute-start(bf16[64,4096]{1,0:T(8,128)(2,1)} %constant_dynamic-slice_fusion), channel_id=1, source_target_pairs={{0,8},{8,0},{4,12},{12,4},{1,9},{9,1},{5,13},{13,5},{2,10},{10,2},... | collective-permute-start | bytes 1572872 | tf_op jit(solution)/shard_map/ppermute | solution.py:102
  6.1 23.7 %collective-permute-start = (bf16[64,4096]{1,0:T(8,128)(2,1)}, bf16[64,4096]{1,0:T(8,128)(2,1)S(1)}, u32[]{:S(2)}, u32[]{:S(2)}) collective-permute-start(bf16[64,4096]{1,0:T(8,128)(2,1)} %constant_dynamic-slice_fusion), channel_id=1, source_target_pairs={{0,4},{4,0},{8,12},{12,8},{1,5},{5,1},{9,13},{13,9},{2,6},{6,2},{1... | collective-permute-start | bytes 1572872 | tf_op jit(solution)/shard_map/ppermute | solution.py:102
  7.7 10.8 %collective-permute-start.2 = (bf16[2,64,1024]{2,1,0:T(8,128)(2,1)}, bf16[2,64,1024]{2,1,0:T(8,128)(2,1)}, u32[]{:S(2)}, u32[]{:S(2)}) collective-permute-start(bf16[2,64,1024]{2,1,0:T(8,128)(2,1)} %param.12), channel_id=1, source_target_pairs={{0,2},{2,0},{1,3},{3,1},{4,6},{6,4},{5,7},{7,5},{8,10},{10,8},{9,1... | collective-permute-start | bytes 786440 | tf_op jit(solution)/shard_map/ppermute | solution.py:99
  9.2 3.4 %copy-start.2 = (bf16[4096,1024]{1,0:T(8,128)(2,1)S(1)}, bf16[4096,1024]{1,0:T(8,128)(2,1)}, u32[]{:S(2)}) copy-start(bf16[4096,1024]{1,0:T(8,128)(2,1)} %array_ref.1) | copy-start | bytes 25165828
  13.2 3.3 %copy-start.1 = (bf16[4096,1024]{1,0:T(8,128)(2,1)}, bf16[4096,1024]{1,0:T(8,128)(2,1)S(1)}, u32[]{:S(2)}) copy-start(bf16[4096,1024]{1,0:T(8,128)(2,1)S(1)} %shard_map.82) | copy-start | bytes 25165828
  16.4 1.4 %copy-start.6 = (s32[512]{0:T(512)S(1)}, s32[512]{0:T(512)}, u32[]{:S(2)}) copy-start(s32[512]{0:T(512)} %param.13) | copy-start | bytes 6148
  16.4 1.4 %copy-start.7 = (s32[4]{0:T(128)S(1)}, s32[4]{0:T(128)}, u32[]{:S(2)}) copy-start(s32[4]{0:T(128)} %param.15) | copy-start | bytes 52
  16.4 1.4 %copy-start.8 = (s32[4]{0:T(128)S(1)}, s32[4]{0:T(128)}, u32[]{:S(2)}) copy-start(s32[4]{0:T(128)} %param.14) | copy-start | bytes 52
  16.4 1.6 %copy-start.3 = (bf16[1,64,4096]{2,1,0:T(8,128)(2,1)S(1)}, bf16[1,64,4096]{2,1,0:T(8,128)(2,1)}, u32[]{:S(2)}) copy-start(bf16[1,64,4096]{2,1,0:T(8,128)(2,1)} %param.11) | copy-start | bytes 1572868
  29.8 18.1 %collective-permute-start.3 = (bf16[64,4096]{1,0:T(8,128)(2,1)S(1)}, bf16[64,4096]{1,0:T(8,128)(2,1)S(1)}, u32[]{:S(2)}, u32[]{:S(2)}) collective-permute-start(bf16[64,4096]{1,0:T(8,128)(2,1)S(1)} %collective-permute-done.1), channel_id=1, source_target_pairs={{0,4},{4,0},{8,12},{12,8},{1,5},{5,1},{9,13},{13,9},{2,6},{6,2},{1... | collective-permute-start | bytes 1572872 | tf_op jit(solution)/shard_map/ppermute | solution.py:102
  31.4 1.5 %collective-permute-start.4 = (bf16[32,4096]{1,0:T(8,128)(2,1)S(1)}, bf16[32,4096]{1,0:T(8,128)(2,1)S(1)}, u32[]{:S(2)}, u32[]{:S(2)}) collective-permute-start(bf16[32,4096]{1,0:T(8,128)(2,1)S(1)} %get-tuple-element.43), channel_id=1, source_target_pairs={{0,1},{1,0},{2,3},{3,2},{4,5},{5,4},{6,7},{7,6},{8,9},{9,8},{10,11... | collective-permute-start | bytes 786440 | tf_op jit(solution)/shard_map/ppermute | solution.py:96
  31.4 1.9 %collective-permute-start.5 = (bf16[32,4096]{1,0:T(8,128)(2,1)S(1)}, bf16[32,4096]{1,0:T(8,128)(2,1)S(1)}, u32[]{:S(2)}, u32[]{:S(2)}) collective-permute-start(bf16[32,4096]{1,0:T(8,128)(2,1)S(1)} %get-tuple-element.44), channel_id=1, source_target_pairs={{0,1},{1,0},{2,3},{3,2},{4,5},{5,4},{6,7},{7,6},{8,9},{9,8},{10,11... | collective-permute-start | bytes 786440 | tf_op jit(solution)/shard_map/ppermute | solution.py:96
  31.9 8.7 %slice-start = ((s8[8388608]{0:T(1024)(128)(4,1)}), s8[4194304]{0:T(1024)(128)(4,1)S(1)}, s32[]{:S(2)}) async-start(s8[8388608]{0:T(1024)(128)(4,1)} %bitcast.54), calls=%async_computation | async-start | bytes 8388608
  31.9 8.2 %collective-permute-start.7 = (bf16[32,4096]{1,0:T(8,128)(2,1)S(1)}, bf16[32,4096]{1,0:T(8,128)(2,1)S(1)}, u32[]{:S(2)}, u32[]{:S(2)}) collective-permute-start(bf16[32,4096]{1,0:T(8,128)(2,1)S(1)} %get-tuple-element.41), channel_id=1, source_target_pairs={{0,1},{1,0},{2,3},{3,2},{4,5},{5,4},{6,7},{7,6},{8,9},{9,8},{10,11... | collective-permute-start | bytes 786440 | tf_op jit(solution)/shard_map/ppermute | solution.py:96
  32.0 8.6 %slice-start.1 = ((s8[8388608]{0:T(1024)(128)(4,1)}), s8[4194304]{0:T(1024)(128)(4,1)S(1)}, s32[]{:S(2)}) async-start(s8[8388608]{0:T(1024)(128)(4,1)} %bitcast.54), calls=%async_computation.1 | async-start | bytes 8388608
  32.0 8.1 %collective-permute-start.8 = (bf16[32,4096]{1,0:T(8,128)(2,1)S(1)}, bf16[32,4096]{1,0:T(8,128)(2,1)S(1)}, u32[]{:S(2)}, u32[]{:S(2)}) collective-permute-start(bf16[32,4096]{1,0:T(8,128)(2,1)S(1)} %get-tuple-element.42), channel_id=1, source_target_pairs={{0,1},{1,0},{2,3},{3,2},{4,5},{5,4},{6,7},{7,6},{8,9},{9,8},{10,11... | collective-permute-start | bytes 786440 | tf_op jit(solution)/shard_map/ppermute | solution.py:96
  38.6 8.5 %collective-permute-start.6 = (bf16[128,1024]{1,0:T(8,128)(2,1)S(1)}, bf16[128,1024]{1,0:T(8,128)(2,1)S(1)}, u32[]{:S(2)}, u32[]{:S(2)}) collective-permute-start(bf16[128,1024]{1,0:T(8,128)(2,1)S(1)} %get-tuple-element.45), channel_id=1, source_target_pairs={{0,2},{2,0},{1,3},{3,1},{4,6},{6,4},{5,7},{7,5},{8,10},{10,8},{9,1... | collective-permute-start | bytes 786440 | tf_op jit(solution)/shard_map/ppermute | solution.py:99
  43.2 5.5 %copy-start.4 = (f32[128,1024]{1,0:T(8,128)S(1)}, f32[128,1024]{1,0:T(8,128)}, u32[]{:S(2)}) copy-start(f32[128,1024]{1,0:T(8,128)} %fusion.19) | copy-start | bytes 1572868
  48.0 1.7 %collective-permute-start.11 = (bf16[32,4096]{1,0:T(8,128)(2,1)S(1)}, bf16[32,4096]{1,0:T(8,128)(2,1)}, u32[]{:S(2)}, u32[]{:S(2)}) collective-permute-start(bf16[32,4096]{1,0:T(8,128)(2,1)S(1)} %get-tuple-element.40), channel_id=1, source_target_pairs={{0,1},{1,0},{2,3},{3,2},{4,5},{5,4},{6,7},{7,6},{8,9},{9,8},{10,11... | collective-permute-start | bytes 786440 | tf_op jit(solution)/shard_map/ppermute | solution.py:96
  48.2 7.9 %collective-permute-start.9 = (bf16[32,4096]{1,0:T(8,128)(2,1)S(1)}, bf16[32,4096]{1,0:T(8,128)(2,1)S(1)}, u32[]{:S(2)}, u32[]{:S(2)}) collective-permute-start(bf16[32,4096]{1,0:T(8,128)(2,1)S(1)} %get-tuple-element.39), channel_id=1, source_target_pairs={{0,1},{1,0},{2,3},{3,2},{4,5},{5,4},{6,7},{7,6},{8,9},{9,8},{10,11... | collective-permute-start | bytes 786440 | tf_op jit(solution)/shard_map/ppermute | solution.py:96
  50.9 5.4 %slice-start.2 = ((s8[8388608]{0:T(1024)(128)(4,1)}), s8[4194304]{0:T(1024)(128)(4,1)S(1)}, s32[]{:S(2)}) async-start(s8[8388608]{0:T(1024)(128)(4,1)} %bitcast.56), calls=%async_computation.2 | async-start | bytes 8388608
  50.9 5.8 %slice-start.3 = ((s8[8388608]{0:T(1024)(128)(4,1)}), s8[4194304]{0:T(1024)(128)(4,1)S(1)}, s32[]{:S(2)}) async-start(s8[8388608]{0:T(1024)(128)(4,1)} %bitcast.56), calls=%async_computation.3 | async-start | bytes 8388608
  58.8 16.1 %copy-start.5 = (bf16[4,64,1024]{2,1,0:T(8,128)(2,1)S(1)}, bf16[4,64,1024]{2,1,0:T(8,128)(2,1)}, u32[]{:S(2)}) copy-start(bf16[4,64,1024]{2,1,0:T(8,128)(2,1)} %maximum_select_fusion.3) | copy-start | bytes 1572868
  58.9 16.0 %copy-start.9 = (bf16[256,1024]{1,0:T(8,128)(2,1)S(1)}, bf16[256,1024]{1,0:T(8,128)(2,1)}, u32[]{:S(2)}) copy-start(bf16[256,1024]{1,0:T(8,128)(2,1)} %param.9) | copy-start | bytes 1572868
  58.9 4.6 %collective-permute-start.12 = (f32[256,64]{0,1:T(8,128)S(1)}, f32[256,64]{0,1:T(8,128)S(1)}, u32[]{:S(2)}, u32[]{:S(2)}) collective-permute-start(f32[256,64]{0,1:T(8,128)S(1)} %fusion.17), channel_id=1, source_target_pairs={{0,2},{2,0},{1,3},{3,1},{4,6},{6,4},{5,7},{7,5},{8,10},{10,8},{9,1... | collective-permute-start | bytes 196616 | tf_op jit(solution)/shard_map/ppermute | solution.py:99
  60.5 8.4 %collective-permute-start.14 = (bf16[64,1024]{1,0:T(8,128)(2,1)S(1)}, bf16[64,1024]{1,0:T(8,128)(2,1)S(1)}, u32[]{:S(2)}, u32[]{:S(2)}) collective-permute-start(bf16[64,1024]{1,0:T(8,128)(2,1)S(1)} %fusion.10), channel_id=1, source_target_pairs={{0,2},{2,0},{1,3},{3,1},{4,6},{6,4},{5,7},{7,5},{8,10},{10,8},{9,1... | collective-permute-start | bytes 393224 | tf_op jit(solution)/shard_map/ppermute | solution.py:99
  61.1 7.8 %collective-permute-start.10 = (bf16[64,1024]{1,0:T(8,128)(2,1)S(1)}, bf16[64,1024]{1,0:T(8,128)(2,1)S(1)}, u32[]{:S(2)}, u32[]{:S(2)}) collective-permute-start(bf16[64,1024]{1,0:T(8,128)(2,1)S(1)} %get-tuple-element.49), channel_id=1, source_target_pairs={{0,2},{2,0},{1,3},{3,1},{4,6},{6,4},{5,7},{7,5},{8,10},{10,8},{9,1... | collective-permute-start | bytes 393224 | tf_op jit(solution)/shard_map/ppermute | solution.py:99
  63.6 5.3 %collective-permute-start.13 = (f32[256,64]{0,1:T(8,128)S(1)}, f32[256,64]{0,1:T(8,128)S(1)}, u32[]{:S(2)}, u32[]{:S(2)}) collective-permute-start(f32[256,64]{0,1:T(8,128)S(1)} %add_select_fusion), channel_id=1, source_target_pairs={{0,4},{4,0},{8,12},{12,8},{1,5},{5,1},{9,13},{13,9},{2,6},{6,2},{1... | collective-permute-start | bytes 196616 | tf_op jit(solution)/shard_map/ppermute | solution.py:102
  68.9 5.9 %collective-permute-start.15 = (f32[256,64]{0,1:T(8,128)S(1)}, f32[256,64]{0,1:T(8,128)S(1)}, u32[]{:S(2)}, u32[]{:S(2)}) collective-permute-start(f32[256,64]{0,1:T(8,128)S(1)} %add.42), channel_id=1, source_target_pairs={{0,8},{8,0},{4,12},{12,4},{1,9},{9,1},{5,13},{13,5},{2,10},{10,2},... | collective-permute-start | bytes 196616 | tf_op jit(solution)/shard_map/ppermute | solution.py:102

commit v8 on v6

--- a/solution.py
+++ b/solution.py
@@ -1,6 +1,8 @@
 import jax
 import jax.numpy as jnp
 from jax import lax
+from jax.experimental import pallas as pl
+from jax.experimental.pallas import tpu as pltpu
 from jax.sharding import PartitionSpec as P
 
 F32 = jnp.float32
@@ -60,6 +62,151 @@
 SWAP = [(0, 1), (1, 0)]
 NEAR = [(0, 1), (1, 0), (2, 3), (3, 2)]
 FAR = [(0, 2), (2, 0), (1, 3), (3, 1)]
+VMEM = pl.BlockSpec(memory_space=pltpu.VMEM)
+SMEM = pl.BlockSpec(memory_space=pltpu.SMEM)
+HBM = pl.BlockSpec(memory_space=pltpu.HBM)
+COST = pl.CostEstimate(flops=0, bytes_accessed=0, transcendentals=0)
+PARAMS = pltpu.CompilerParams(vmem_limit_bytes=50 * 1024 * 1024)
+
+
+def shape(dims, dtype):
+    return jax.ShapeDtypeStruct(dims, dtype)
+
+
+def dot(a, b):
+    return jnp.dot(a, b, preferred_element_type=F32)
+
+
+def call(kernel, outs, in_specs, operands, scratch=()):
+    return pl.pallas_call(
+        kernel,
+        out_shape=outs,
+        in_specs=in_specs,
+        out_specs=jax.tree.map(lambda _: VMEM, outs),
+        scratch_shapes=scratch,
+        compiler_params=PARAMS,
+        cost_estimate=COST,
+    )(*operands)
+
+
+def column_tiles(cols):
+    tile = 256 if cols % 256 == 0 else cols
+    return [slice(at, at + tile) for at in range(0, cols, tile)]
+
+
+def streamed_scratch(weight):
+    return [
+        pltpu.VMEM(weight.shape, weight.dtype),
+        pltpu.SemaphoreType.DMA((len(column_tiles(weight.shape[1])),)),
+    ]
+
+
+def streaming(weight_ref, tiles_ref, sems):
+    tiles = column_tiles(weight_ref.shape[1])
+    copies = [
+        pltpu.make_async_copy(weight_ref.at[:, tile], tiles_ref.at[:, tile], sems.at[i])
+        for i, tile in enumerate(tiles)
+    ]
+    for copy in copies:
+        copy.start()
+
+    def come():
+        for copy, tile in zip(copies, tiles):
+            copy.wait()
+            yield tile, tiles_ref[:, tile]
+
+    return come()
+
+
+def joined(flags_ref, mine, other):
+    first = flags_ref[1] == 0
+    return jnp.concatenate([jnp.where(first, mine, other), jnp.where(first, other, mine)])
+
+
+def low_product(rows, down_ref):
+    return lax.dot_general(
+        rows, down_ref[...], (((1,), (1,)), ((), ())), preferred_element_type=F32
+    )
+
+
+def part(flags_ref, held, value, keep_ref, send_ref, tile):
+    home = flags_ref[0] == 1
+    keep_ref[:, tile] = jnp.where(home, held, value)
+    send_ref[:, tile] = jnp.where(home, value, held).astype(BF16)
+
+
+def own_kernel(weight_ref, down_ref, rows_ref, sum_ref, low_ref, tiles_ref, sems):
+    stream = streaming(weight_ref, tiles_ref, sems)
+    rows = rows_ref[...]
+    low_ref[...] = low_product(rows, down_ref)
+    for tile, weights in stream:
+        sum_ref[:, tile] = dot(rows, weights)
+
+
+def far_kernel(
+    flags_ref, weight_ref, down_ref, held_ref, mine_ref, first_ref, second_ref,
+    keep_ref, send_ref, keep_more_ref, send_more_ref, low_ref, tiles_ref, sems,
+):
+    stream = streaming(weight_ref, tiles_ref, sems)
+    other = jnp.concatenate([first_ref[...], second_ref[...]])
+    rows = joined(flags_ref, mine_ref[...], other)
+    low_ref[...] = low_product(rows, down_ref)
+    half = keep_ref.shape[0]
+    for tile, weights in stream:
+        value = dot(rows, weights)
+        part(flags_ref, held_ref[:half, tile], value[:half], keep_ref, send_ref, tile)
+        part(flags_ref, held_ref[half:, tile], value[half:], keep_more_ref, send_more_ref, tile)
+
+
+def near_kernel(
+    flags_ref, weight_ref, down_ref, mine_ref, first_ref, second_ref, last_ref, third_ref,
+    fourth_ref, keep_ref, send_ref, hold_ref, low_ref, tiles_ref, sems,
+):
+    stream = streaming(weight_ref, tiles_ref, sems)
+    other = jnp.concatenate([first_ref[...], second_ref[...]])
+    near = joined(flags_ref, mine_ref[...], other)
+    last = joined(flags_ref, last_ref[...], jnp.concatenate([third_ref[...], fourth_ref[...]]))
+    rows = jnp.concatenate([near, last])
+    low_ref[...] = low_product(rows, down_ref)
+    step = last_ref.shape[0]
+    for tile, weights in stream:
+        value = dot(rows, weights)
+        held = jnp.concatenate([value[:step], value[2 * step : 3 * step]])
+        part(flags_ref, held, value[4 * step :], keep_ref, send_ref, tile)
+        hold_ref[:, tile] = jnp.concatenate(
+            [value[step : 2 * step], value[3 * step : 4 * step]]
+        )
+
+
+def last_kernel(
+    flags_ref, weight_ref, down_ref, held_ref, mine_ref, first_ref, second_ref,
+    keep_ref, send_ref, low_ref, tiles_ref, sems,
+):
+    stream = streaming(weight_ref, tiles_ref, sems)
+    other = jnp.concatenate([first_ref[...], second_ref[...]])
+    rows = joined(flags_ref, mine_ref[...], other)
+    low_ref[...] = low_product(rows, down_ref)
+    for tile, weights in stream:
+        part(flags_ref, held_ref[:, tile], dot(rows, weights), keep_ref, send_ref, tile)
+
+
+def final_kernel(flags_ref, residual_ref, low_ref, low_got_ref, factor_ref, ups_ref, *refs):
+    *parts, out_ref = refs
+    low = low_ref[...] + low_got_ref[...]
+    lora = dot((low * factor_ref[0]).astype(BF16), ups_ref[0])
+    for slot in range(1, ups_ref.shape[0]):
+        lora += dot((low * factor_ref[slot]).astype(BF16), ups_ref[slot])
+    odd = flags_ref[2] == 1
+    sums = [keep[...] + got[...].astype(F32) for keep, got in zip(parts[::2], parts[1::2])]
+    step = sums[2].shape[0] // 2
+    first = jnp.concatenate(sums[:2])
+    second = jnp.concatenate(
+        [sums[2][:step], sums[3][:step], sums[2][step:], sums[3][step:]]
+    )
+    block = first.shape[0]
+    for at, base in ((0, jnp.where(odd, second, first)), (block, jnp.where(odd, first, second))):
+        here = slice(at, at + block)
+        out_ref[here, :] = (residual_ref[here, :].astype(F32) + base + lora[here]).astype(BF16)
 
 
 def line(rows, residual, weight, down, up, tenant, entry, live):
@@ -82,74 +229,91 @@
     def along(value, pairs):
         return lax.ppermute(value, "blk", pairs)
 
-    def product(block):
-        return jnp.dot(block, weight, preferred_element_type=F32)
-
-    def low_rank(block):
-        return lax.dot_general(
-            block, down[0], (((1,), (1,)), ((), ())), preferred_element_type=F32
-        )
-
-    def joined(piece, other):
-        return jnp.where(
-            c == 0, jnp.concatenate([piece, other]), jnp.concatenate([other, piece])
-        )
-
-    def whole(piece):
-        return joined(piece, over_core(piece))
+    def over_core_in_two(piece):
+        count = piece.shape[0] // 2
+        return [over_core(piece[:count]), over_core(piece[count:])]
 
     def in_order(first, second):
         return jnp.where(
             odd, jnp.concatenate([second, first]), jnp.concatenate([first, second])
         )
 
-    def exchange(near_sum, far_sum):
-        got = over_x(jnp.where(home, far_sum, near_sum).astype(BF16))
-        return jnp.where(home, near_sum, far_sum), got
+    def parted(count):
+        return [shape((count, cols), F32), shape((count, cols), BF16)]
+
+    def lows(count):
+        return [shape((count, width), F32)]
 
     slot_all, live_all = tables(tenant, entry, live)
     slot = lax.dynamic_slice_in_dim(slot_all, x * own, own, 0)
     rank = lax.dynamic_slice_in_dim(live_all, x * own, own, 0)
+
+    flags = jnp.stack([home, c, odd]).astype(jnp.int32)
+    kept = jnp.arange(width, dtype=jnp.int32)[None, :] < rank[:, None]
+    scaling = jnp.where(kept, (width / rank.astype(F32))[:, None], jnp.zeros((), F32))
+    hot = slot[None, :] == jnp.arange(slots, dtype=jnp.int32)[:, None]
+    factor = jnp.where(hot[:, :, None], scaling[None], jnp.zeros((), F32))
 
     mine = lax.dynamic_slice_in_dim(rows, c * half, half, 0)
     near, far = along(mine, NEAR), along(mine, FAR)
     up_other = over_x(up)
     ups = jnp.where(x == 0, jnp.concatenate([up, up_other]), jnp.concatenate([up_other, up]))
-    own_sum, own_low = product(rows), low_rank(rows)
-    near, far, own_sum, own_low, ups = barrier((near, far, own_sum, own_low, ups))
-
-    last = along(far, NEAR)
-
-    def doubled(piece):
-        return joined(
-            piece, jnp.concatenate([over_core(piece[:step]), over_core(piece[step:])])
-        )
-
-    far = doubled(far)
-    far_sum, far_low = product(far), low_rank(far)
-    kept, got = exchange(own_sum, far_sum)
-    first = kept + got.astype(F32)
-    near = doubled(near)
-    near_sum, near_low = product(near), low_rank(near)
-    last, first, far_low, near_sum, near_low = barrier((last, first, far_low, near_sum, near_low))
-
-    pieces = [whole(last[:step]), whole(last[step:])]
-    last_low = low_rank(jnp.concatenate(pieces)).reshape(2, 2, step, width)
-    last_low = last_low.transpose(1, 0, 2, 3).reshape(block_rows, width)
-    near_low, far_low = in_order(own_low, near_low), in_order(far_low, last_low)
+    own_sum, own_low = call(
+        own_kernel,
+        [shape((block_rows, cols), F32)] + lows(block_rows),
+        [HBM, VMEM, VMEM],
+        [weight, down[0], rows],
+        streamed_scratch(weight),
+    )
+    near, far, own_sum, own_low, ups, factor = barrier((near, far, own_sum, own_low, ups, factor))
+
+    last = [along(far[:step], NEAR), along(far[step:], NEAR)]
+    kept_a, sent_a, kept_b, sent_b, far_low = call(
+        far_kernel,
+        parted(half) * 2 + lows(block_rows),
+        [SMEM, HBM] + [VMEM] * 5,
+        [flags, weight, down[0], own_sum, far] + over_core_in_two(far),
+        streamed_scratch(weight),
+    )
+    got_a, got_b = over_x(sent_a), over_x(sent_b)
+    last[0], kept_a = barrier((last[0], kept_a))
+
+    kept_c, sent_c, hold, near_low = call(
+        near_kernel,
+        parted(half) + [shape((half, cols), F32)] + lows(block_rows + half),
+        [SMEM, HBM] + [VMEM] * 7,
+        [flags, weight, down[0], near] + over_core_in_two(near)
+        + [last[0]] + over_core_in_two(last[0]),
+        streamed_scratch(weight),
+    )
+    got_c = over_x(sent_c)
+    last[1], hold, got_a, got_b, near_low = barrier((last[1], hold, got_a, got_b, near_low))
+
+    others = over_core_in_two(last[1])
+    others, got_c = barrier((others, got_c))
+    kept_d, sent_d, last_low = call(
+        last_kernel,
+        parted(half) + lows(half),
+        [SMEM, HBM] + [VMEM] * 5,
+        [flags, weight, down[0], hold, last[1]] + others,
+        streamed_scratch(weight),
+    )
+    got_d = over_x(sent_d)
+
+    pair = [near_low[block_rows:], last_low]
+    last_low = jnp.concatenate([low[at : at + step] for at in (0, step) for low in pair])
+    near_low, far_low = in_order(own_low, near_low[:block_rows]), in_order(far_low, last_low)
     low = jnp.where(home, near_low, far_low) + over_x(jnp.where(home, far_low, near_low))
     low = jnp.where((slot == z)[:, None], low, jnp.zeros((), F32))
-    near_parts = near_sum.reshape(2, 2, step, cols)
-    second = []
-    for p, pairs in enumerate((NEAR, FAR)):
-        kept, got = exchange(near_parts[:, p].reshape(half, cols), product(pieces[p]))
-        low, kept, got = barrier((low, kept, got)) if p else (low, kept, got)
-        low = low + along(low, pairs)
-        second.append((kept + got.astype(F32)).reshape(2, step, cols))
-    second = jnp.stack(second, axis=1).reshape(block_rows, cols)
-    spread = low_rank_weights(low, slot, rank, slots, width)
-    lora = jnp.dot(spread, ups.reshape(slots * width, cols), preferred_element_type=F32)
-    return (residual.astype(F32) + in_order(first, second) + lora).astype(BF16)
+    low = low + along(low, NEAR)
+    low, got_d = barrier((low, got_d))
+    parts = [kept_a, got_a, kept_b, got_b, kept_c, got_c, kept_d, got_d]
+    return call(
+        final_kernel,
+        shape(residual.shape, BF16),
+        [SMEM] + [VMEM] * 13,
+        [flags, residual, low, along(low, FAR), factor, ups] + parts,
+    )
 
 
 def shards(rows, residual, weight, down, up, tenant, entry, live):

time: 75.2 us -> 80.7 us (1.073)
  matrix products: 25 us -> 0 us
  Pallas kernels: 0 us -> 23.6 us
  waiting for transfers between devices: 24.9 us -> 32.3 us
  other arithmetic: 3.51 us -> 1.58 us
  local copies, waits for them, and re-layouts: 2.31 us -> 3.57 us
    dot_general x10 -> x0, matrix products: 25 us -> none  [the longest x5 22 us: product(): return jnp.dot(block, weight, preferred_element_type=F32)]
    pallas_call x0 -> x5, Pallas kernels: none -> 23.6 us  [call(): pl.pallas_call(kernel, out_shape=outs, in_specs=in_specs, out_specs=jax.t...]
    ppermute x5 -> x6, waiting for transfers between devices: 16.7 us -> 24.3 us  [along(): return lax.ppermute(value, 'blk', pairs)]
    select_n x1, other arithmetic: 1.91 us -> 0.08 us  [line(): jnp.where(x == 0, jnp.concatenate([up, up_other]), jnp.concatenate([up_ot...]
    ppermute x6 -> x8, waiting for transfers between devices: 1.68 us -> 0.02 us  [over_core(): return lax.ppermute(value, 'sub', SWAP)]
    ppermute x5 -> x6, waiting for transfers between devices: 6.47 us -> 7.99 us  [over_x(): return lax.ppermute(value, 'split', SWAP)]
    unnamed x24 -> x14, local copies, waits for them, and re-layouts: 1.28 us -> 2.3 us
    add x4 -> x1, other arithmetic: 0.97 us -> 0.02 us  [line(): low = low + along(low, NEAR)]
  transfers between devices with their start and end apart: 16 -> 20, of which waited for: 10 -> 7; matrix products, arithmetic and copies ran while one was open for 37% -> 2% of each run, Pallas kernels for 0% -> 20%
where the time goes in v8:
time: 80.7 us; the launch traced here: 80.5 us
  waiting for transfers between devices  32.3 us (40%)
  Pallas kernels  23.6 us (29%)
  starting transfers between devices  19.2 us (24%)
  local copies, waits for them, and re-layouts  3.57 us (4%)
  other arithmetic  1.58 us (2%)
    ppermute x6, waiting for transfers between devices, along(): return lax.ppermute(value, 'blk', pairs)  24.3 us
    pallas_call x5, Pallas kernels, call(): pl.pallas_call(kernel, out_shape=outs, in_specs=in_specs, out_specs=jax.t...  23.6 us
    ppermute x6, starting transfers between devices, along(): return lax.ppermute(value, 'blk', pairs)  10.1 us
    ppermute x6, waiting for transfers between devices, over_x(): return lax.ppermute(value, 'split', SWAP)  7.99 us
    ppermute x6, starting transfers between devices, over_x(): return lax.ppermute(value, 'split', SWAP)  7.1 us
    unnamed x14, local copies, waits for them, and re-layouts  2.3 us
    ppermute x8, starting transfers between devices, over_core(): return lax.ppermute(value, 'sub', SWAP)  1.95 us
  transfers between devices with their start and end apart: 20, of which 7 were waited for; matrix products, arithmetic and copies ran while one was open for 2% of the time, Pallas kernels for 20%

profile of v8, /device:TPU:0, one launch (start us, length us, event | category | flops | bytes accessed | tf_op | source)
XLA Modules:
  0.0 80.5 jit_solution(984346668585795337)
XLA Ops:
  0.0 1.1 %constant_dynamic-slice_fusion = bf16[64,4096]{1,0:T(8,128)(2,1)S(1)} fusion(bf16[128,4096]{1,0:T(8,128)(2,1)} %rows_ref.1, s32[]{:T(128)S(6)} %select_n.69), kind=kLoop, calls=%fused_computation.25 | loop fusion | bytes 1048580 | tf_op jit(solution)/shard_map/dynamic_slice | solution.py:257
  1.2 3.1 %collective-permute-start = (bf16[64,4096]{1,0:T(8,128)(2,1)S(1)}, bf16[64,4096]{1,0:T(8,128)(2,1)S(1)}, u32[]{:S(2)}, u32[]{:S(2)}) collective-permute-start(bf16[64,4096]{1,0:T(8,128)(2,1)S(1)} %constant_dynamic-slice_fusion), channel_id=1, source_target_pairs={{0,4},{4,0},{8,12},{12,8},{1,5},{5,1},{9,13},{13,9},{2,6},{6,2},{1... | collective-permute-start | bytes 1572872 | tf_op jit(solution)/shard_map/ppermute | solution.py:230
  4.2 2.6 %collective-permute-start.1 = (bf16[64,4096]{1,0:T(8,128)(2,1)S(1)}, bf16[64,4096]{1,0:T(8,128)(2,1)S(1)}, u32[]{:S(2)}, u32[]{:S(2)}) collective-permute-start(bf16[64,4096]{1,0:T(8,128)(2,1)S(1)} %constant_dynamic-slice_fusion), channel_id=1, source_target_pairs={{0,8},{8,0},{4,12},{12,4},{1,9},{9,1},{5,13},{13,5},{2,10},{10,2},... | collective-permute-start | bytes 1572872 | tf_op jit(solution)/shard_map/ppermute | solution.py:230
  6.8 1.5 %collective-permute-start.2 = (bf16[2,64,1024]{2,1,0:T(8,128)(2,1)}, bf16[2,64,1024]{2,1,0:T(8,128)(2,1)S(1)}, u32[]{:S(2)}, u32[]{:S(2)}) collective-permute-start(bf16[2,64,1024]{2,1,0:T(8,128)(2,1)} %param.12), channel_id=1, source_target_pairs={{0,2},{2,0},{1,3},{3,1},{4,6},{6,4},{5,7},{7,5},{8,10},{10,8},{9,1... | collective-permute-start | bytes 786440 | tf_op jit(solution)/shard_map/ppermute | solution.py:227
  8.3 0.8 select_reduce_fusion.1
  9.1 0.1 convert_divide_fusion
  9.2 0.1 fusion
  9.3 0.1 broadcast_compare_fusion
  9.4 0.1 pad_add_fusion.flags_ref
  9.5 1.0 %copy-done = bf16[1,64,4096]{2,1,0:T(8,128)(2,1)S(1)} copy-done((bf16[1,64,4096]{2,1,0:T(8,128)(2,1)S(1)}, bf16[1,64,4096]{2,1,0:T(8,128)(2,1)}, u32[]{:S(2)}) %copy-start) | copy-done | bytes 524312
  10.5 1.2 %copy-done.2 = bf16[128,4096]{1,0:T(8,128)(2,1)S(1)} copy-done((bf16[128,4096]{1,0:T(8,128)(2,1)S(1)}, bf16[128,4096]{1,0:T(8,128)(2,1)}, u32[]{:S(2)}) %copy-start.2) | copy-done | bytes 1048600
  11.8 4.7 %shard_map.82 = (f32[128,1024]{1,0:T(8,128)S(1)}, f32[128,64]{1,0:T(8,128)S(1)}) custom-call(bf16[4096,1024]{1,0:T(8,128)(2,1)} %weight_ref.7, bf16[64,4096]{1,0:T(8,128)(2,1)S(1)} %bitcast.4, bf16[128,4096]{1,0:T(8,128)(2,1)S(1)} %copy-done.2), custom_call_target="tpu_custom_call" | custom-call | tf_op jit(solution)/shard_map/pallas_call | solution.py:81
  16.4 0.2 broadcast_select_fusion.factor_ref
  16.7 0.1 maximum_select_fusion.ups_ref
  16.8 10.5 %collective-permute-done.mine_ref = bf16[64,4096]{1,0:T(8,128)(2,1)S(1)} collective-permute-done((bf16[64,4096]{1,0:T(8,128)(2,1)S(1)}, bf16[64,4096]{1,0:T(8,128)(2,1)S(1)}, u32[]{:S(2)}, u32[]{:S(2)}) %collective-permute-start) | collective-permute-done | bytes 524320 | tf_op jit(solution)/shard_map/ppermute | solution.py:230
  27.3 2.5 %collective-permute-done.1.mine_ref = bf16[64,4096]{1,0:T(8,128)(2,1)S(1)} collective-permute-done((bf16[64,4096]{1,0:T(8,128)(2,1)S(1)}, bf16[64,4096]{1,0:T(8,128)(2,1)S(1)}, u32[]{:S(2)}, u32[]{:S(2)}) %collective-permute-start.1) | collective-permute-done | bytes 524320 | tf_op jit(solution)/shard_map/ppermute | solution.py:230
  29.9 0.1 collective-permute-start.7
  29.9 0.5 collective-permute-start.6
  30.4 0.2 collective-permute-start.8
  30.6 1.6 %collective-permute-start.3 = (bf16[32,4096]{1,0:T(8,128)(2,1)S(1)}, bf16[32,4096]{1,0:T(8,128)(2,1)S(1)}, u32[]{:S(2)}, u32[]{:S(2)}) collective-permute-start(bf16[32,4096]{1,0:T(8,128)(2,1)S(1)} %get-tuple-element.76), channel_id=1, source_target_pairs={{0,4},{4,0},{8,12},{12,8},{1,5},{5,1},{9,13},{13,9},{2,6},{6,2},{1... | collective-permute-start | bytes 786440 | tf_op jit(solution)/shard_map/ppermute | solution.py:230
  32.2 0.1 collective-permute-start.4
  32.4 0.0 collective-permute-done.7.first_ref
  32.4 0.4 collective-permute-start.5
  32.8 0.0 collective-permute-done.8.second_ref
  32.8 5.2 %shard_map.83 = (f32[64,1024]{1,0:T(8,128)S(1)}, bf16[64,1024]{1,0:T(8,128)(2,1)S(1)}, f32[64,1024]{1,0:T(8,128)S(1)}, bf16[64,1024]{1,0:T(8,128)(2,1)S(1)}, f32[128,64]{1,0:T(8,128)S(1)}) custom-call(s32[3]{0:T(128)S(1)} %pad_add_fusion.flags_ref, bf16[4096,1024]{1,0:T(8,128)(2,1)} %weight_ref.7, bf16[64,4096]{1,0:T(8,128)(2,1)S(1)} %bitcast.5, ...), custom_call_target="tpu_custom_call" | custom-call | tf_op jit(solution)/shard_map/pallas_call | solution.py:81
  38.1 1.1 %collective-permute-done.6.last_ref = bf16[32,4096]{1,0:T(8,128)(2,1)S(1)} collective-permute-done((bf16[32,4096]{1,0:T(8,128)(2,1)S(1)}, bf16[32,4096]{1,0:T(8,128)(2,1)S(1)}, u32[]{:S(2)}, u32[]{:S(2)}) %collective-permute-start.6) | collective-permute-done | bytes 262176 | tf_op jit(solution)/shard_map/ppermute | solution.py:230
  39.1 0.1 collective-permute-start.10
  39.2 0.5 collective-permute-start.9
  39.7 1.5 %collective-permute-start.11 = (bf16[64,1024]{1,0:T(8,128)(2,1)S(1)}, bf16[64,1024]{1,0:T(8,128)(2,1)S(1)}, u32[]{:S(2)}, u32[]{:S(2)}) collective-permute-start(bf16[64,1024]{1,0:T(8,128)(2,1)S(1)} %get-tuple-element.45), channel_id=1, source_target_pairs={{0,2},{2,0},{1,3},{3,1},{4,6},{6,4},{5,7},{7,5},{8,10},{10,8},{9,1... | collective-permute-start | bytes 393224 | tf_op jit(solution)/shard_map/ppermute | solution.py:227
  41.2 0.5 collective-permute-start.12
  41.7 0.0 collective-permute-done.9.third_ref
  41.8 6.4 %shard_map.84 = (f32[64,1024]{1,0:T(8,128)S(1)}, bf16[64,1024]{1,0:T(8,128)(2,1)S(1)}, f32[64,1024]{1,0:T(8,128)S(1)}, f32[192,64]{1,0:T(8,128)S(1)}) custom-call(s32[3]{0:T(128)S(1)} %pad_add_fusion.flags_ref, bf16[4096,1024]{1,0:T(8,128)(2,1)} %weight_ref.7, bf16[64,4096]{1,0:T(8,128)(2,1)S(1)} %bitcast.6, ...), custom_call_target="tpu_custom_call" | custom-call | tf_op jit(solution)/shard_map/pallas_call | solution.py:81
  48.2 0.0 copy-start.3
  48.2 0.0 collective-permute-done.11.refs_1_
  48.3 0.1 collective-permute-start.13
  48.3 0.5 collective-permute-start.14
  48.8 1.5 %collective-permute-start.15 = (bf16[64,1024]{1,0:T(8,128)(2,1)S(1)}, bf16[64,1024]{1,0:T(8,128)(2,1)S(1)}, u32[]{:S(2)}, u32[]{:S(2)}) collective-permute-start(bf16[64,1024]{1,0:T(8,128)(2,1)S(1)} %get-tuple-element.52), channel_id=1, source_target_pairs={{0,2},{2,0},{1,3},{3,1},{4,6},{6,4},{5,7},{7,5},{8,10},{10,8},{9,1... | collective-permute-start | bytes 393224 | tf_op jit(solution)/shard_map/ppermute | solution.py:227
  50.4 4.0 %collective-permute-done.15.refs_5_ = bf16[64,1024]{1,0:T(8,128)(2,1)S(1)} collective-permute-done((bf16[64,1024]{1,0:T(8,128)(2,1)S(1)}, bf16[64,1024]{1,0:T(8,128)(2,1)S(1)}, u32[]{:S(2)}, u32[]{:S(2)}) %collective-permute-start.15) | collective-permute-done | bytes 131104 | tf_op jit(solution)/shard_map/ppermute | solution.py:227
  54.3 5.2 %shard_map.85 = (f32[64,1024]{1,0:T(8,128)S(1)}, bf16[64,1024]{1,0:T(8,128)(2,1)S(1)}, f32[64,64]{1,0:T(8,128)S(1)}) custom-call(s32[3]{0:T(128)S(1)} %pad_add_fusion.flags_ref, bf16[4096,1024]{1,0:T(8,128)(2,1)} %weight_ref.7, bf16[64,4096]{1,0:T(8,128)(2,1)S(1)} %bitcast.7, f32[64,1024]{1,0:T(8,128)S(1)} %get-tuple-element.50.held_ref, ...), custom_call_target="tpu_custom_call" | custom-call | tf_op jit(solution)/shard_map/pallas_call | solution.py:81
  59.6 1.6 %collective-permute-start.16 = (f32[256,64]{1,0:T(8,128)S(1)}, f32[256,64]{1,0:T(8,128)S(1)}, u32[]{:S(2)}, u32[]{:S(2)}) collective-permute-start(f32[256,64]{1,0:T(8,128)S(1)} %fusion.1), channel_id=1, source_target_pairs={{0,2},{2,0},{1,3},{3,1},{4,6},{6,4},{5,7},{7,5},{8,10},{10,8},{9,1... | collective-permute-start | bytes 196616 | tf_op jit(solution)/shard_map/ppermute | solution.py:227
  61.2 0.5 collective-permute-start.18
  61.7 4.0 %collective-permute-done.16 = f32[256,64]{1,0:T(8,128)S(1)} collective-permute-done((f32[256,64]{1,0:T(8,128)S(1)}, f32[256,64]{1,0:T(8,128)S(1)}, u32[]{:S(2)}, u32[]{:S(2)}) %collective-permute-start.16) | collective-permute-done | bytes 65568 | tf_op jit(solution)/shard_map/ppermute | solution.py:227
  65.7 0.1 add_select_fusion
  65.8 0.5 collective-permute-start.17
  66.4 4.8 %collective-permute-done.17 = f32[256,64]{1,0:T(8,128)S(1)} collective-permute-done((f32[256,64]{1,0:T(8,128)S(1)}, f32[256,64]{1,0:T(8,128)S(1)}, u32[]{:S(2)}, u32[]{:S(2)}) %collective-permute-start.17) | collective-permute-done | bytes 65568 | tf_op jit(solution)/shard_map/ppermute | solution.py:230
  71.2 1.9 %collective-permute-start.19 = (f32[256,64]{1,0:T(8,128)S(1)}, f32[256,64]{1,0:T(8,128)S(1)}, u32[]{:S(2)}, u32[]{:S(2)}) collective-permute-start(f32[256,64]{1,0:T(8,128)S(1)} %add.22.low_ref), channel_id=1, source_target_pairs={{0,8},{8,0},{4,12},{12,4},{1,9},{9,1},{5,13},{13,5},{2,10},{10,2},... | collective-permute-start | bytes 196616 | tf_op jit(solution)/shard_map/ppermute | solution.py:230
  73.0 5.4 %collective-permute-done.19.low_got_ref = f32[256,64]{1,0:T(8,128)S(1)} collective-permute-done((f32[256,64]{1,0:T(8,128)S(1)}, f32[256,64]{1,0:T(8,128)S(1)}, u32[]{:S(2)}, u32[]{:S(2)}) %collective-permute-start.19) | collective-permute-done | bytes 65568 | tf_op jit(solution)/shard_map/ppermute | solution.py:230
  78.4 2.1 %shard_map.86 = bf16[256,1024]{1,0:T(8,128)(2,1)} custom-call(s32[3]{0:T(128)S(1)} %pad_add_fusion.flags_ref, bf16[256,1024]{1,0:T(8,128)(2,1)S(1)} %copy-done.3, f32[256,64]{1,0:T(8,128)S(1)} %add.22.low_ref, f32[256,64]{1,0:T(8,128)S(1)} %collective-permute-done.19.low_got_ref, f32[4,256,64]{2,1,0:T(8,128)S(1)} %broadcast_select_fusion.factor_ref, ...), custom_call_target="tpu_custom_call" | custom-call | tf_op jit(solution)/shard_map/pallas_call | solution.py:81
  (30 shorter events, 0.2 us)
Async XLA Ops:
  0.0 16.7 %copy-start.4 = (bf16[2,64,1024]{2,1,0:T(8,128)(2,1)S(1)}, bf16[2,64,1024]{2,1,0:T(8,128)(2,1)}, u32[]{:S(2)}) copy-start(bf16[2,64,1024]{2,1,0:T(8,128)(2,1)} %param.12) | copy-start | bytes 786436
  0.0 32.8 %copy-start.1 = (bf16[1,64,4096]{2,1,0:T(8,128)(2,1)S(1)}, bf16[1,64,4096]{2,1,0:T(8,128)(2,1)}, u32[]{:S(2)}) copy-start(bf16[1,64,4096]{2,1,0:T(8,128)(2,1)} %param.11) | copy-start | bytes 1572868
  1.2 26.1 %collective-permute-start = (bf16[64,4096]{1,0:T(8,128)(2,1)S(1)}, bf16[64,4096]{1,0:T(8,128)(2,1)S(1)}, u32[]{:S(2)}, u32[]{:S(2)}) collective-permute-start(bf16[64,4096]{1,0:T(8,128)(2,1)S(1)} %constant_dynamic-slice_fusion), channel_id=1, source_target_pairs={{0,4},{4,0},{8,12},{12,8},{1,5},{5,1},{9,13},{13,9},{2,6},{6,2},{1... | collective-permute-start | bytes 1572872 | tf_op jit(solution)/shard_map/ppermute | solution.py:230
  4.2 25.6 %collective-permute-start.1 = (bf16[64,4096]{1,0:T(8,128)(2,1)S(1)}, bf16[64,4096]{1,0:T(8,128)(2,1)S(1)}, u32[]{:S(2)}, u32[]{:S(2)}) collective-permute-start(bf16[64,4096]{1,0:T(8,128)(2,1)S(1)} %constant_dynamic-slice_fusion), channel_id=1, source_target_pairs={{0,8},{8,0},{4,12},{12,4},{1,9},{9,1},{5,13},{13,5},{2,10},{10,2},... | collective-permute-start | bytes 1572872 | tf_op jit(solution)/shard_map/ppermute | solution.py:230
  6.8 9.8 %collective-permute-start.2 = (bf16[2,64,1024]{2,1,0:T(8,128)(2,1)}, bf16[2,64,1024]{2,1,0:T(8,128)(2,1)S(1)}, u32[]{:S(2)}, u32[]{:S(2)}) collective-permute-start(bf16[2,64,1024]{2,1,0:T(8,128)(2,1)} %param.12), channel_id=1, source_target_pairs={{0,2},{2,0},{1,3},{3,1},{4,6},{6,4},{5,7},{7,5},{8,10},{10,8},{9,1... | collective-permute-start | bytes 786440 | tf_op jit(solution)/shard_map/ppermute | solution.py:227
  9.5 1.0 %copy-start = (bf16[1,64,4096]{2,1,0:T(8,128)(2,1)S(1)}, bf16[1,64,4096]{2,1,0:T(8,128)(2,1)}, u32[]{:S(2)}) copy-start(bf16[1,64,4096]{2,1,0:T(8,128)(2,1)} %param.11) | copy-start | bytes 1572868
  10.5 1.2 %copy-start.2 = (bf16[128,4096]{1,0:T(8,128)(2,1)S(1)}, bf16[128,4096]{1,0:T(8,128)(2,1)}, u32[]{:S(2)}) copy-start(bf16[128,4096]{1,0:T(8,128)(2,1)} %rows_ref.1) | copy-start | bytes 3145732
  29.9 2.5 %collective-permute-start.7 = (bf16[32,4096]{1,0:T(8,128)(2,1)S(1)}, bf16[32,4096]{1,0:T(8,128)(2,1)S(1)}, u32[]{:S(2)}, u32[]{:S(2)}) collective-permute-start(bf16[32,4096]{1,0:T(8,128)(2,1)S(1)} %get-tuple-element.75), channel_id=1, source_target_pairs={{0,1},{1,0},{2,3},{3,2},{4,5},{5,4},{6,7},{7,6},{8,9},{9,8},{10,11... | collective-permute-start | bytes 786440 | tf_op jit(solution)/shard_map/ppermute | solution.py:224
  29.9 9.2 %collective-permute-start.6 = (bf16[32,4096]{1,0:T(8,128)(2,1)S(1)}, bf16[32,4096]{1,0:T(8,128)(2,1)S(1)}, u32[]{:S(2)}, u32[]{:S(2)}) collective-permute-start(bf16[32,4096]{1,0:T(8,128)(2,1)S(1)} %get-tuple-element.75), channel_id=1, source_target_pairs={{0,4},{4,0},{8,12},{12,8},{1,5},{5,1},{9,13},{13,9},{2,6},{6,2},{1... | collective-permute-start | bytes 786440 | tf_op jit(solution)/shard_map/ppermute | solution.py:230
  30.4 2.4 %collective-permute-start.8 = (bf16[32,4096]{1,0:T(8,128)(2,1)S(1)}, bf16[32,4096]{1,0:T(8,128)(2,1)S(1)}, u32[]{:S(2)}, u32[]{:S(2)}) collective-permute-start(bf16[32,4096]{1,0:T(8,128)(2,1)S(1)} %get-tuple-element.76), channel_id=1, source_target_pairs={{0,1},{1,0},{2,3},{3,2},{4,5},{5,4},{6,7},{7,6},{8,9},{9,8},{10,11... | collective-permute-start | bytes 786440 | tf_op jit(solution)/shard_map/ppermute | solution.py:224
  30.6 17.6 %collective-permute-start.3 = (bf16[32,4096]{1,0:T(8,128)(2,1)S(1)}, bf16[32,4096]{1,0:T(8,128)(2,1)S(1)}, u32[]{:S(2)}, u32[]{:S(2)}) collective-permute-start(bf16[32,4096]{1,0:T(8,128)(2,1)S(1)} %get-tuple-element.76), channel_id=1, source_target_pairs={{0,4},{4,0},{8,12},{12,8},{1,5},{5,1},{9,13},{13,9},{2,6},{6,2},{1... | collective-permute-start | bytes 786440 | tf_op jit(solution)/shard_map/ppermute | solution.py:230
  32.2 7.5 %collective-permute-start.4 = (bf16[32,4096]{1,0:T(8,128)(2,1)S(1)}, bf16[32,4096]{1,0:T(8,128)(2,1)S(1)}, u32[]{:S(2)}, u32[]{:S(2)}) collective-permute-start(bf16[32,4096]{1,0:T(8,128)(2,1)S(1)} %get-tuple-element.78), channel_id=1, source_target_pairs={{0,1},{1,0},{2,3},{3,2},{4,5},{5,4},{6,7},{7,6},{8,9},{9,8},{10,11... | collective-permute-start | bytes 786440 | tf_op jit(solution)/shard_map/ppermute | solution.py:224
  32.4 8.8 %collective-permute-start.5 = (bf16[32,4096]{1,0:T(8,128)(2,1)S(1)}, bf16[32,4096]{1,0:T(8,128)(2,1)S(1)}, u32[]{:S(2)}, u32[]{:S(2)}) collective-permute-start(bf16[32,4096]{1,0:T(8,128)(2,1)S(1)} %get-tuple-element.77), channel_id=1, source_target_pairs={{0,1},{1,0},{2,3},{3,2},{4,5},{5,4},{6,7},{7,6},{8,9},{9,8},{10,11... | collective-permute-start | bytes 786440 | tf_op jit(solution)/shard_map/ppermute | solution.py:224
  39.1 2.6 %collective-permute-start.10 = (bf16[16,4096]{1,0:T(8,128)(2,1)S(1)}, bf16[16,4096]{1,0:T(8,128)(2,1)S(1)}, u32[]{:S(2)}, u32[]{:S(2)}) collective-permute-start(bf16[16,4096]{1,0:T(8,128)(2,1)S(1)} %get-tuple-element.81), channel_id=1, source_target_pairs={{0,1},{1,0},{2,3},{3,2},{4,5},{5,4},{6,7},{7,6},{8,9},{9,8},{10,11... | collective-permute-start | bytes 393224 | tf_op jit(solution)/shard_map/ppermute | solution.py:224
  39.2 2.5 %collective-permute-start.9 = (bf16[16,4096]{1,0:T(8,128)(2,1)S(1)}, bf16[16,4096]{1,0:T(8,128)(2,1)S(1)}, u32[]{:S(2)}, u32[]{:S(2)}) collective-permute-start(bf16[16,4096]{1,0:T(8,128)(2,1)S(1)} %get-tuple-element.82), channel_id=1, source_target_pairs={{0,1},{1,0},{2,3},{3,2},{4,5},{5,4},{6,7},{7,6},{8,9},{9,8},{10,11... | collective-permute-start | bytes 393224 | tf_op jit(solution)/shard_map/ppermute | solution.py:224
  39.7 8.5 %collective-permute-start.11 = (bf16[64,1024]{1,0:T(8,128)(2,1)S(1)}, bf16[64,1024]{1,0:T(8,128)(2,1)S(1)}, u32[]{:S(2)}, u32[]{:S(2)}) collective-permute-start(bf16[64,1024]{1,0:T(8,128)(2,1)S(1)} %get-tuple-element.45), channel_id=1, source_target_pairs={{0,2},{2,0},{1,3},{3,1},{4,6},{6,4},{5,7},{7,5},{8,10},{10,8},{9,1... | collective-permute-start | bytes 393224 | tf_op jit(solution)/shard_map/ppermute | solution.py:227
  41.2 7.0 %collective-permute-start.12 = (bf16[64,1024]{1,0:T(8,128)(2,1)S(1)}, bf16[64,1024]{1,0:T(8,128)(2,1)S(1)}, u32[]{:S(2)}, u32[]{:S(2)}) collective-permute-start(bf16[64,1024]{1,0:T(8,128)(2,1)S(1)} %get-tuple-element.46), channel_id=1, source_target_pairs={{0,2},{2,0},{1,3},{3,1},{4,6},{6,4},{5,7},{7,5},{8,10},{10,8},{9,1... | collective-permute-start | bytes 393224 | tf_op jit(solution)/shard_map/ppermute | solution.py:227
  48.2 30.2 %copy-start.3 = (bf16[256,1024]{1,0:T(8,128)(2,1)S(1)}, bf16[256,1024]{1,0:T(8,128)(2,1)}, u32[]{:S(2)}) copy-start(bf16[256,1024]{1,0:T(8,128)(2,1)} %residual_ref.1) | copy-start | bytes 1572868
  48.3 2.1 %collective-permute-start.13 = (bf16[16,4096]{1,0:T(8,128)(2,1)S(1)}, bf16[16,4096]{1,0:T(8,128)(2,1)S(1)}, u32[]{:S(2)}, u32[]{:S(2)}) collective-permute-start(bf16[16,4096]{1,0:T(8,128)(2,1)S(1)} %get-tuple-element.80), channel_id=1, source_target_pairs={{0,1},{1,0},{2,3},{3,2},{4,5},{5,4},{6,7},{7,6},{8,9},{9,8},{10,11... | collective-permute-start | bytes 393224 | tf_op jit(solution)/shard_map/ppermute | solution.py:224
  48.3 2.0 %collective-permute-start.14 = (bf16[16,4096]{1,0:T(8,128)(2,1)S(1)}, bf16[16,4096]{1,0:T(8,128)(2,1)S(1)}, u32[]{:S(2)}, u32[]{:S(2)}) collective-permute-start(bf16[16,4096]{1,0:T(8,128)(2,1)S(1)} %get-tuple-element.79), channel_id=1, source_target_pairs={{0,1},{1,0},{2,3},{3,2},{4,5},{5,4},{6,7},{7,6},{8,9},{9,8},{10,11... | collective-permute-start | bytes 393224 | tf_op jit(solution)/shard_map/ppermute | solution.py:224
  48.8 5.5 %collective-permute-start.15 = (bf16[64,1024]{1,0:T(8,128)(2,1)S(1)}, bf16[64,1024]{1,0:T(8,128)(2,1)S(1)}, u32[]{:S(2)}, u32[]{:S(2)}) collective-permute-start(bf16[64,1024]{1,0:T(8,128)(2,1)S(1)} %get-tuple-element.52), channel_id=1, source_target_pairs={{0,2},{2,0},{1,3},{3,1},{4,6},{6,4},{5,7},{7,5},{8,10},{10,8},{9,1... | collective-permute-start | bytes 393224 | tf_op jit(solution)/shard_map/ppermute | solution.py:227
  59.6 6.1 %collective-permute-start.16 = (f32[256,64]{1,0:T(8,128)S(1)}, f32[256,64]{1,0:T(8,128)S(1)}, u32[]{:S(2)}, u32[]{:S(2)}) collective-permute-start(f32[256,64]{1,0:T(8,128)S(1)} %fusion.1), channel_id=1, source_target_pairs={{0,2},{2,0},{1,3},{3,1},{4,6},{6,4},{5,7},{7,5},{8,10},{10,8},{9,1... | collective-permute-start | bytes 196616 | tf_op jit(solution)/shard_map/ppermute | solution.py:227
  61.2 10.0 %collective-permute-start.18 = (bf16[64,1024]{1,0:T(8,128)(2,1)S(1)}, bf16[64,1024]{1,0:T(8,128)(2,1)S(1)}, u32[]{:S(2)}, u32[]{:S(2)}) collective-permute-start(bf16[64,1024]{1,0:T(8,128)(2,1)S(1)} %get-tuple-element.57), channel_id=1, source_target_pairs={{0,2},{2,0},{1,3},{3,1},{4,6},{6,4},{5,7},{7,5},{8,10},{10,8},{9,1... | collective-permute-start | bytes 393224 | tf_op jit(solution)/shard_map/ppermute | solution.py:227
  65.8 5.3 %collective-permute-start.17 = (f32[256,64]{1,0:T(8,128)S(1)}, f32[256,64]{1,0:T(8,128)S(1)}, u32[]{:S(2)}, u32[]{:S(2)}) collective-permute-start(f32[256,64]{1,0:T(8,128)S(1)} %add_select_fusion), channel_id=1, source_target_pairs={{0,4},{4,0},{8,12},{12,8},{1,5},{5,1},{9,13},{13,9},{2,6},{6,2},{1... | collective-permute-start | bytes 196616 | tf_op jit(solution)/shard_map/ppermute | solution.py:230
  71.2 7.3 %collective-permute-start.19 = (f32[256,64]{1,0:T(8,128)S(1)}, f32[256,64]{1,0:T(8,128)S(1)}, u32[]{:S(2)}, u32[]{:S(2)}) collective-permute-start(f32[256,64]{1,0:T(8,128)S(1)} %add.22.low_ref), channel_id=1, source_target_pairs={{0,8},{8,0},{4,12},{12,4},{1,9},{9,1},{5,13},{13,5},{2,10},{10,2},... | collective-permute-start | bytes 196616 | tf_op jit(solution)/shard_map/ppermute | solution.py:230

commit v9 on v8

--- a/solution.py
+++ b/solution.py
@@ -66,7 +66,8 @@
 SMEM = pl.BlockSpec(memory_space=pltpu.SMEM)
 HBM = pl.BlockSpec(memory_space=pltpu.HBM)
 COST = pl.CostEstimate(flops=0, bytes_accessed=0, transcendentals=0)
-PARAMS = pltpu.CompilerParams(vmem_limit_bytes=50 * 1024 * 1024)
+PARAMS = pltpu.CompilerParams(vmem_limit_bytes=16 * 1024 * 1024)
+FROM_HBM = pltpu.CompilerParams(vmem_limit_bytes=40 * 1024 * 1024)
 
 
 def shape(dims, dtype):
@@ -77,14 +78,14 @@
     return jnp.dot(a, b, preferred_element_type=F32)
 
 
-def call(kernel, outs, in_specs, operands, scratch=()):
+def call(kernel, outs, in_specs, operands, scratch=(), params=PARAMS):
     return pl.pallas_call(
         kernel,
         out_shape=outs,
         in_specs=in_specs,
         out_specs=jax.tree.map(lambda _: VMEM, outs),
         scratch_shapes=scratch,
-        compiler_params=PARAMS,
+        compiler_params=params,
         cost_estimate=COST,
     )(*operands)
 
@@ -94,83 +95,66 @@
     return [slice(at, at + tile) for at in range(0, cols, tile)]
 
 
-def streamed_scratch(weight):
-    return [
-        pltpu.VMEM(weight.shape, weight.dtype),
-        pltpu.SemaphoreType.DMA((len(column_tiles(weight.shape[1])),)),
-    ]
-
-
-def streaming(weight_ref, tiles_ref, sems):
+def joined(flags_ref, mine, other):
+    first = flags_ref[1] == 0
+    return jnp.concatenate([jnp.where(first, mine, other), jnp.where(first, other, mine)])
+
+
+def low_product(rows, down_ref):
+    return lax.dot_general(
+        rows, down_ref[...], (((1,), (1,)), ((), ())), preferred_element_type=F32
+    )
+
+
+def part(flags_ref, held, value, keep_ref, send_ref, tile):
+    home = flags_ref[0] == 1
+    keep_ref[:, tile] = jnp.where(home, held, value)
+    send_ref[:, tile] = jnp.where(home, value, held).astype(BF16)
+
+
+def own_kernel(
+    weight_ref, down_ref, rows_ref, held_ref, sum_ref, low_ref, sems
+):
     tiles = column_tiles(weight_ref.shape[1])
     copies = [
-        pltpu.make_async_copy(weight_ref.at[:, tile], tiles_ref.at[:, tile], sems.at[i])
+        pltpu.make_async_copy(weight_ref.at[:, tile], held_ref.at[:, tile], sems.at[i])
         for i, tile in enumerate(tiles)
     ]
     for copy in copies:
         copy.start()
-
-    def come():
-        for copy, tile in zip(copies, tiles):
-            copy.wait()
-            yield tile, tiles_ref[:, tile]
-
-    return come()
-
-
-def joined(flags_ref, mine, other):
-    first = flags_ref[1] == 0
-    return jnp.concatenate([jnp.where(first, mine, other), jnp.where(first, other, mine)])
-
-
-def low_product(rows, down_ref):
-    return lax.dot_general(
-        rows, down_ref[...], (((1,), (1,)), ((), ())), preferred_element_type=F32
-    )
-
-
-def part(flags_ref, held, value, keep_ref, send_ref, tile):
-    home = flags_ref[0] == 1
-    keep_ref[:, tile] = jnp.where(home, held, value)
-    send_ref[:, tile] = jnp.where(home, value, held).astype(BF16)
-
-
-def own_kernel(weight_ref, down_ref, rows_ref, sum_ref, low_ref, tiles_ref, sems):
-    stream = streaming(weight_ref, tiles_ref, sems)
     rows = rows_ref[...]
     low_ref[...] = low_product(rows, down_ref)
-    for tile, weights in stream:
-        sum_ref[:, tile] = dot(rows, weights)
+    for copy, tile in zip(copies, tiles):
+        copy.wait()
+        sum_ref[:, tile] = dot(rows, held_ref[:, tile])
 
 
 def far_kernel(
     flags_ref, weight_ref, down_ref, held_ref, mine_ref, first_ref, second_ref,
-    keep_ref, send_ref, keep_more_ref, send_more_ref, low_ref, tiles_ref, sems,
+    keep_ref, send_ref, keep_more_ref, send_more_ref, low_ref,
 ):
-    stream = streaming(weight_ref, tiles_ref, sems)
     other = jnp.concatenate([first_ref[...], second_ref[...]])
     rows = joined(flags_ref, mine_ref[...], other)
     low_ref[...] = low_product(rows, down_ref)
     half = keep_ref.shape[0]
-    for tile, weights in stream:
-        value = dot(rows, weights)
+    for tile in column_tiles(weight_ref.shape[1]):
+        value = dot(rows, weight_ref[:, tile])
         part(flags_ref, held_ref[:half, tile], value[:half], keep_ref, send_ref, tile)
         part(flags_ref, held_ref[half:, tile], value[half:], keep_more_ref, send_more_ref, tile)
 
 
 def near_kernel(
     flags_ref, weight_ref, down_ref, mine_ref, first_ref, second_ref, last_ref, third_ref,
-    fourth_ref, keep_ref, send_ref, hold_ref, low_ref, tiles_ref, sems,
+    fourth_ref, keep_ref, send_ref, hold_ref, low_ref,
 ):
-    stream = streaming(weight_ref, tiles_ref, sems)
     other = jnp.concatenate([first_ref[...], second_ref[...]])
     near = joined(flags_ref, mine_ref[...], other)
     last = joined(flags_ref, last_ref[...], jnp.concatenate([third_ref[...], fourth_ref[...]]))
     rows = jnp.concatenate([near, last])
     low_ref[...] = low_product(rows, down_ref)
     step = last_ref.shape[0]
-    for tile, weights in stream:
-        value = dot(rows, weights)
+    for tile in column_tiles(weight_ref.shape[1]):
+        value = dot(rows, weight_ref[:, tile])
         held = jnp.concatenate([value[:step], value[2 * step : 3 * step]])
         part(flags_ref, held, value[4 * step :], keep_ref, send_ref, tile)
         hold_ref[:, tile] = jnp.concatenate(
@@ -179,23 +163,41 @@
 
 
 def last_kernel(
-    flags_ref, weight_ref, down_ref, held_ref, mine_ref, first_ref, second_ref,
-    keep_ref, send_ref, low_ref, tiles_ref, sems,
+    flags_ref, weight_ref, down_ref, held_ref, own_low, far_low, near_low, mine_ref, first_ref,
+    second_ref, keep_ref, send_ref, low_keep_ref, low_send_ref,
 ):
-    stream = streaming(weight_ref, tiles_ref, sems)
     other = jnp.concatenate([first_ref[...], second_ref[...]])
     rows = joined(flags_ref, mine_ref[...], other)
-    low_ref[...] = low_product(rows, down_ref)
-    for tile, weights in stream:
-        part(flags_ref, held_ref[:, tile], dot(rows, weights), keep_ref, send_ref, tile)
-
-
-def final_kernel(flags_ref, residual_ref, low_ref, low_got_ref, factor_ref, ups_ref, *refs):
+    low = low_product(rows, down_ref)
+    block, width = own_low.shape
+    step = mine_ref.shape[0]
+    last_low = jnp.concatenate(
+        [
+            near_low[block : block + step], low[:step],
+            near_low[block + step :], low[step:],
+        ]
+    )
+    odd, home = flags_ref[2] == 1, flags_ref[0] == 1
+    near = own_low[...], near_low[:block]
+    far = far_low[...], last_low
+    for side, here in ((0, slice(0, width)), (1, slice(width, 2 * width))):
+        near_side = jnp.where(odd, near[1 - side], near[side])
+        far_side = jnp.where(odd, far[1 - side], far[side])
+        low_keep_ref[:, here] = jnp.where(home, near_side, far_side)
+        low_send_ref[:, here] = jnp.where(home, far_side, near_side)
+    for tile in column_tiles(weight_ref.shape[1]):
+        value = dot(rows, weight_ref[:, tile])
+        part(flags_ref, held_ref[:, tile], value, keep_ref, send_ref, tile)
+
+
+def final_kernel(flags_ref, residual_ref, scaled_ref, scaled_got_ref, hot_ref, ups_ref, *refs):
     *parts, out_ref = refs
-    low = low_ref[...] + low_got_ref[...]
-    lora = dot((low * factor_ref[0]).astype(BF16), ups_ref[0])
+    scaled = scaled_ref[...] + scaled_got_ref[...]
+    width = ups_ref.shape[1]
+    scaled = jnp.concatenate([scaled[:, :width], scaled[:, width:]])
+    lora = dot(scaled * hot_ref[0], ups_ref[0])
     for slot in range(1, ups_ref.shape[0]):
-        lora += dot((low * factor_ref[slot]).astype(BF16), ups_ref[slot])
+        lora += dot(scaled * hot_ref[slot], ups_ref[slot])
     odd = flags_ref[2] == 1
     sums = [keep[...] + got[...].astype(F32) for keep, got in zip(parts[::2], parts[1::2])]
     step = sums[2].shape[0] // 2
@@ -233,11 +235,6 @@
         count = piece.shape[0] // 2
         return [over_core(piece[:count]), over_core(piece[count:])]
 
-    def in_order(first, second):
-        return jnp.where(
-            odd, jnp.concatenate([second, first]), jnp.concatenate([first, second])
-        )
-
     def parted(count):
         return [shape((count, cols), F32), shape((count, cols), BF16)]
 
@@ -250,30 +247,34 @@
 
     flags = jnp.stack([home, c, odd]).astype(jnp.int32)
     kept = jnp.arange(width, dtype=jnp.int32)[None, :] < rank[:, None]
-    scaling = jnp.where(kept, (width / rank.astype(F32))[:, None], jnp.zeros((), F32))
+    scale = jnp.where(kept, (width / rank.astype(F32))[:, None], jnp.zeros((), F32))
+    scale = jnp.where((slot == z)[:, None], scale, jnp.zeros((), F32))
+    scale = jnp.concatenate([scale[:block_rows], scale[block_rows:]], axis=1)
     hot = slot[None, :] == jnp.arange(slots, dtype=jnp.int32)[:, None]
-    factor = jnp.where(hot[:, :, None], scaling[None], jnp.zeros((), F32))
+    hot = jnp.broadcast_to(hot[:, :, None], (slots, own, width)).astype(BF16)
 
     mine = lax.dynamic_slice_in_dim(rows, c * half, half, 0)
     near, far = along(mine, NEAR), along(mine, FAR)
     up_other = over_x(up)
     ups = jnp.where(x == 0, jnp.concatenate([up, up_other]), jnp.concatenate([up_other, up]))
-    own_sum, own_low = call(
+    held, own_sum, own_low = call(
         own_kernel,
-        [shape((block_rows, cols), F32)] + lows(block_rows),
+        [shape(weight.shape, BF16), shape((block_rows, cols), F32)] + lows(block_rows),
         [HBM, VMEM, VMEM],
         [weight, down[0], rows],
-        streamed_scratch(weight),
-    )
-    near, far, own_sum, own_low, ups, factor = barrier((near, far, own_sum, own_low, ups, factor))
+        [pltpu.SemaphoreType.DMA((len(column_tiles(cols)),))],
+        FROM_HBM,
+    )
+    near, far, own_sum, own_low, ups, hot, scale = barrier(
+        (near, far, own_sum, own_low, ups, hot, scale)
+    )
 
     last = [along(far[:step], NEAR), along(far[step:], NEAR)]
     kept_a, sent_a, kept_b, sent_b, far_low = call(
         far_kernel,
         parted(half) * 2 + lows(block_rows),
-        [SMEM, HBM] + [VMEM] * 5,
-        [flags, weight, down[0], own_sum, far] + over_core_in_two(far),
-        streamed_scratch(weight),
+        [SMEM] + [VMEM] * 6,
+        [flags, held, down[0], own_sum, far] + over_core_in_two(far),
     )
     got_a, got_b = over_x(sent_a), over_x(sent_b)
     last[0], kept_a = barrier((last[0], kept_a))
@@ -281,38 +282,32 @@
     kept_c, sent_c, hold, near_low = call(
         near_kernel,
         parted(half) + [shape((half, cols), F32)] + lows(block_rows + half),
-        [SMEM, HBM] + [VMEM] * 7,
-        [flags, weight, down[0], near] + over_core_in_two(near)
+        [SMEM] + [VMEM] * 8,
+        [flags, held, down[0], near] + over_core_in_two(near)
         + [last[0]] + over_core_in_two(last[0]),
-        streamed_scratch(weight),
     )
     got_c = over_x(sent_c)
     last[1], hold, got_a, got_b, near_low = barrier((last[1], hold, got_a, got_b, near_low))
 
-    others = over_core_in_two(last[1])
-    others, got_c = barrier((others, got_c))
-    kept_d, sent_d, last_low = call(
+    kept_d, sent_d, low, low_sent = call(
         last_kernel,
-        parted(half) + lows(half),
-        [SMEM, HBM] + [VMEM] * 5,
-        [flags, weight, down[0], hold, last[1]] + others,
-        streamed_scratch(weight),
-    )
+        parted(half) + [shape((block_rows, 2 * width), F32)] * 2,
+        [SMEM] + [VMEM] * 9,
+        [flags, held, down[0], hold, own_low, far_low, near_low, last[1]]
+        + over_core_in_two(last[1]),
+    )
+    low_sent, got_c = barrier((low_sent, got_c))
     got_d = over_x(sent_d)
 
-    pair = [near_low[block_rows:], last_low]
-    last_low = jnp.concatenate([low[at : at + step] for at in (0, step) for low in pair])
-    near_low, far_low = in_order(own_low, near_low[:block_rows]), in_order(far_low, last_low)
-    low = jnp.where(home, near_low, far_low) + over_x(jnp.where(home, far_low, near_low))
-    low = jnp.where((slot == z)[:, None], low, jnp.zeros((), F32))
-    low = low + along(low, NEAR)
-    low, got_d = barrier((low, got_d))
+    scaled = ((low + over_x(low_sent)) * scale).astype(BF16)
+    scaled = scaled + along(scaled, NEAR)
+    scaled, got_d = barrier((scaled, got_d))
     parts = [kept_a, got_a, kept_b, got_b, kept_c, got_c, kept_d, got_d]
     return call(
         final_kernel,
         shape(residual.shape, BF16),
         [SMEM] + [VMEM] * 13,
-        [flags, residual, low, along(low, FAR), factor, ups] + parts,
+        [flags, residual, scaled, along(scaled, FAR), hot, ups] + parts,
     )
 
 

time: 80.7 us -> 69.3 us (0.86)
  Pallas kernels: 23.6 us -> 13.5 us
  waiting for transfers between devices: 32.3 us -> 29.7 us
  starting transfers between devices: 19.2 us -> 20.5 us
    pallas_call x5, Pallas kernels: 23.6 us -> 13.5 us  [call(): pl.pallas_call(kernel, out_shape=outs, in_specs=in_specs, out_specs=jax.t...]
    ppermute x6, waiting for transfers between devices: 24.3 us -> 21.5 us  [along(): return lax.ppermute(value, 'blk', pairs)]
    ppermute x6, starting transfers between devices: 10.1 us -> 11.4 us  [along(): return lax.ppermute(value, 'blk', pairs)]
    unnamed x14 -> x8, local copies, waits for them, and re-layouts: 2.3 us -> 2.27 us
  transfers between devices with their start and end apart: 20 -> 20, of which waited for: 7 -> 10; matrix products, arithmetic and copies ran while one was open for 2% -> 2% of each run, Pallas kernels for 20% -> 17%
where the time goes in v9:
time: 69.3 us; the launch traced here: 69 us
  waiting for transfers between devices  29.7 us (43%)
  starting transfers between devices  20.5 us (30%)
  Pallas kernels  13.5 us (19%)
  local copies, waits for them, and re-layouts  3.71 us (5%)
  other arithmetic  1.38 us (2%)
    ppermute x6, waiting for transfers between devices, along(): return lax.ppermute(value, 'blk', pairs)  21.5 us
    pallas_call x5, Pallas kernels, call(): pl.pallas_call(kernel, out_shape=outs, in_specs=in_specs, out_specs=jax.t...  13.5 us
    ppermute x6, starting transfers between devices, along(): return lax.ppermute(value, 'blk', pairs)  11.4 us
    ppermute x6, waiting for transfers between devices, over_x(): return lax.ppermute(value, 'split', SWAP)  8.04 us
    ppermute x6, starting transfers between devices, over_x(): return lax.ppermute(value, 'split', SWAP)  7.08 us
    unnamed x8, local copies, waits for them, and re-layouts  2.27 us
    ppermute x8, starting transfers between devices, over_core(): return lax.ppermute(value, 'sub', SWAP)  1.95 us
  transfers between devices with their start and end apart: 20, of which 10 were waited for; matrix products, arithmetic and copies ran while one was open for 2% of the time, Pallas kernels for 17%

profile of v9, /device:TPU:0, one launch (start us, length us, event | category | flops | bytes accessed | tf_op | source)
XLA Modules:
  0.0 69.0 jit_solution(6401841826734536570)
XLA Ops:
  0.0 1.1 %constant_dynamic-slice_fusion = bf16[64,4096]{1,0:T(8,128)(2,1)S(1)} fusion(bf16[128,4096]{1,0:T(8,128)(2,1)} %rows_ref.1, s32[]{:T(128)S(6)} %select_n.36), kind=kLoop, calls=%fused_computation.13 | loop fusion | bytes 1048580 | tf_op jit(solution)/shard_map/dynamic_slice | solution.py:256
  1.1 4.1 %collective-permute-start.1 = (bf16[64,4096]{1,0:T(8,128)(2,1)S(1)}, bf16[64,4096]{1,0:T(8,128)(2,1)S(1)}, u32[]{:S(2)}, u32[]{:S(2)}) collective-permute-start(bf16[64,4096]{1,0:T(8,128)(2,1)S(1)} %constant_dynamic-slice_fusion), channel_id=1, source_target_pairs={{0,8},{8,0},{4,12},{12,4},{1,9},{9,1},{5,13},{13,5},{2,10},{10,2},... | collective-permute-start | bytes 1572872 | tf_op jit(solution)/shard_map/ppermute | solution.py:232
  5.2 1.6 %collective-permute-start = (bf16[64,4096]{1,0:T(8,128)(2,1)S(1)}, bf16[64,4096]{1,0:T(8,128)(2,1)S(1)}, u32[]{:S(2)}, u32[]{:S(2)}) collective-permute-start(bf16[64,4096]{1,0:T(8,128)(2,1)S(1)} %constant_dynamic-slice_fusion), channel_id=1, source_target_pairs={{0,4},{4,0},{8,12},{12,8},{1,5},{5,1},{9,13},{13,9},{2,6},{6,2},{1... | collective-permute-start | bytes 1572872 | tf_op jit(solution)/shard_map/ppermute | solution.py:232
  6.8 1.5 %collective-permute-start.2 = (bf16[2,64,1024]{2,1,0:T(8,128)(2,1)}, bf16[2,64,1024]{2,1,0:T(8,128)(2,1)S(1)}, u32[]{:S(2)}, u32[]{:S(2)}) collective-permute-start(bf16[2,64,1024]{2,1,0:T(8,128)(2,1)} %param.12), channel_id=1, source_target_pairs={{0,2},{2,0},{1,3},{3,1},{4,6},{6,4},{5,7},{7,5},{8,10},{10,8},{9,1... | collective-permute-start | bytes 786440 | tf_op jit(solution)/shard_map/ppermute | solution.py:229
  8.3 0.8 %select_reduce_fusion = (s32[512]{0:T(512)S(1)}, s32[512]{0:T(512)S(1)}) fusion(s32[4]{0:T(128)} %param.15, s32[512]{0:T(512)} %param.13, s32[4]{0:T(128)} %param.14), kind=kLoop, calls=%fused_computation.5 | loop fusion | flops 9216 | bytes 6176 | tf_op jit(solution)/shard_map/reduce_sum | solution.py:24
  9.1 0.1 convert_divide_fusion
  9.2 0.1 broadcast_compare_fusion
  9.2 0.2 select_select_fusion
  9.4 0.1 pad_maximum_fusion
  9.5 0.1 pad_add_fusion.flags_ref
  9.6 1.0 %copy-done = bf16[1,64,4096]{2,1,0:T(8,128)(2,1)S(1)} copy-done((bf16[1,64,4096]{2,1,0:T(8,128)(2,1)S(1)}, bf16[1,64,4096]{2,1,0:T(8,128)(2,1)}, u32[]{:S(2)}) %copy-start) | copy-done | bytes 524312
  10.6 1.2 %copy-done.1 = bf16[128,4096]{1,0:T(8,128)(2,1)S(1)} copy-done((bf16[128,4096]{1,0:T(8,128)(2,1)S(1)}, bf16[128,4096]{1,0:T(8,128)(2,1)}, u32[]{:S(2)}) %copy-start.1) | copy-done | bytes 1048600
  11.9 4.4 %shard_map.82 = (bf16[4096,1024]{1,0:T(8,128)(2,1)S(1)}, f32[128,1024]{1,0:T(8,128)S(1)}, f32[128,64]{1,0:T(8,128)S(1)}) custom-call(bf16[4096,1024]{1,0:T(8,128)(2,1)} %weight_ref.1, bf16[64,4096]{1,0:T(8,128)(2,1)S(1)} %bitcast.4, bf16[128,4096]{1,0:T(8,128)(2,1)S(1)} %copy-done.1), custom_call_target="tpu_custom_call" | custom-call | tf_op jit(solution)/shard_map/pallas_call | solution.py:82
  16.3 0.0 collective-permute-done.2
  16.3 0.1 maximum_select_fusion.ups_ref
  16.4 12.1 %collective-permute-done.1.mine_ref = bf16[64,4096]{1,0:T(8,128)(2,1)S(1)} collective-permute-done((bf16[64,4096]{1,0:T(8,128)(2,1)S(1)}, bf16[64,4096]{1,0:T(8,128)(2,1)S(1)}, u32[]{:S(2)}, u32[]{:S(2)}) %collective-permute-start.1) | collective-permute-done | bytes 524320 | tf_op jit(solution)/shard_map/ppermute | solution.py:232
  28.5 0.2 collective-permute-done.mine_ref
  28.7 0.2 broadcast_in_dim.24.hot_ref
  28.9 0.1 collective-permute-start.7
  29.0 1.6 %collective-permute-start.6 = (bf16[32,4096]{1,0:T(8,128)(2,1)S(1)}, bf16[32,4096]{1,0:T(8,128)(2,1)S(1)}, u32[]{:S(2)}, u32[]{:S(2)}) collective-permute-start(bf16[32,4096]{1,0:T(8,128)(2,1)S(1)} %get-tuple-element.79), channel_id=1, source_target_pairs={{0,4},{4,0},{8,12},{12,8},{1,5},{5,1},{9,13},{13,9},{2,6},{6,2},{1... | collective-permute-start | bytes 786440 | tf_op jit(solution)/shard_map/ppermute | solution.py:232
  30.6 0.2 collective-permute-start.8
  30.7 0.5 collective-permute-start.3
  31.3 0.1 collective-permute-start.5
  31.4 0.4 collective-permute-start.4
  31.9 0.2 collective-permute-done.8.second_ref
  32.1 2.1 %shard_map.83 = (f32[64,1024]{1,0:T(8,128)S(1)}, bf16[64,1024]{1,0:T(8,128)(2,1)S(1)}, f32[64,1024]{1,0:T(8,128)S(1)}, bf16[64,1024]{1,0:T(8,128)(2,1)S(1)}, f32[128,64]{1,0:T(8,128)S(1)}) custom-call(s32[3]{0:T(128)S(1)} %pad_add_fusion.flags_ref, bf16[4096,1024]{1,0:T(8,128)(2,1)S(1)} %get-tuple-element.39.weight_ref, bf16[64,4096]{1,0:T(8,128)(2,1)S(1)} %bitcast.5, ...), custom_call_target="tpu_custom_call" | custom-call | tf_op jit(solution)/shard_map/pallas_call | solution.py:82
  34.2 4.0 %collective-permute-done.6.last_ref = bf16[32,4096]{1,0:T(8,128)(2,1)S(1)} collective-permute-done((bf16[32,4096]{1,0:T(8,128)(2,1)S(1)}, bf16[32,4096]{1,0:T(8,128)(2,1)S(1)}, u32[]{:S(2)}, u32[]{:S(2)}) %collective-permute-start.6) | collective-permute-done | bytes 262176 | tf_op jit(solution)/shard_map/ppermute | solution.py:232
  38.2 0.1 collective-permute-start.10
  38.3 0.5 collective-permute-start.9
  38.8 0.0 collective-permute-done.5.second_ref
  38.8 1.5 %collective-permute-start.11 = (bf16[64,1024]{1,0:T(8,128)(2,1)S(1)}, bf16[64,1024]{1,0:T(8,128)(2,1)S(1)}, u32[]{:S(2)}, u32[]{:S(2)}) collective-permute-start(bf16[64,1024]{1,0:T(8,128)(2,1)S(1)} %get-tuple-element.48), channel_id=1, source_target_pairs={{0,2},{2,0},{1,3},{3,1},{4,6},{6,4},{5,7},{7,5},{8,10},{10,8},{9,1... | collective-permute-start | bytes 393224 | tf_op jit(solution)/shard_map/ppermute | solution.py:229
  40.3 0.5 collective-permute-start.12
  40.8 2.7 %shard_map.84 = (f32[64,1024]{1,0:T(8,128)S(1)}, bf16[64,1024]{1,0:T(8,128)(2,1)S(1)}, f32[64,1024]{1,0:T(8,128)S(1)}, f32[192,64]{1,0:T(8,128)S(1)}) custom-call(s32[3]{0:T(128)S(1)} %pad_add_fusion.flags_ref, bf16[4096,1024]{1,0:T(8,128)(2,1)S(1)} %get-tuple-element.39.weight_ref, bf16[64,4096]{1,0:T(8,128)(2,1)S(1)} %bitcast.6, ...), custom_call_target="tpu_custom_call" | custom-call | tf_op jit(solution)/shard_map/pallas_call | solution.py:82
  43.6 1.6 %collective-permute-done.11.refs_1_ = bf16[64,1024]{1,0:T(8,128)(2,1)S(1)} collective-permute-done((bf16[64,1024]{1,0:T(8,128)(2,1)S(1)}, bf16[64,1024]{1,0:T(8,128)(2,1)S(1)}, u32[]{:S(2)}, u32[]{:S(2)}) %collective-permute-start.11) | collective-permute-done | bytes 131104 | tf_op jit(solution)/shard_map/ppermute | solution.py:229
  45.1 1.9 %collective-permute-done.12.refs_3_ = bf16[64,1024]{1,0:T(8,128)(2,1)S(1)} collective-permute-done((bf16[64,1024]{1,0:T(8,128)(2,1)S(1)}, bf16[64,1024]{1,0:T(8,128)(2,1)S(1)}, u32[]{:S(2)}, u32[]{:S(2)}) %collective-permute-start.12) | collective-permute-done | bytes 131104 | tf_op jit(solution)/shard_map/ppermute | solution.py:229
  47.1 0.1 collective-permute-start.14
  47.2 0.5 collective-permute-start.13
  47.7 1.5 %collective-permute-start.15 = (bf16[64,1024]{1,0:T(8,128)(2,1)S(1)}, bf16[64,1024]{1,0:T(8,128)(2,1)S(1)}, u32[]{:S(2)}, u32[]{:S(2)}) collective-permute-start(bf16[64,1024]{1,0:T(8,128)(2,1)S(1)} %get-tuple-element.58), channel_id=1, source_target_pairs={{0,2},{2,0},{1,3},{3,1},{4,6},{6,4},{5,7},{7,5},{8,10},{10,8},{9,1... | collective-permute-start | bytes 393224 | tf_op jit(solution)/shard_map/ppermute | solution.py:229
  49.2 2.3 %shard_map.85 = (f32[64,1024]{1,0:T(8,128)S(1)}, bf16[64,1024]{1,0:T(8,128)(2,1)S(1)}, f32[128,128]{1,0:T(8,128)S(1)}, f32[128,128]{1,0:T(8,128)S(1)}) custom-call(s32[3]{0:T(128)S(1)} %pad_add_fusion.flags_ref, bf16[4096,1024]{1,0:T(8,128)(2,1)S(1)} %get-tuple-element.39.weight_ref, bf16[64,4096]{1,0:T(8,128)(2,1)S(1)} %bitcast.7, ...), custom_call_target="tpu_custom_call" | custom-call | tf_op jit(solution)/shard_map/pallas_call | solution.py:82
  51.5 1.7 %collective-permute-done.15.refs_5_ = bf16[64,1024]{1,0:T(8,128)(2,1)S(1)} collective-permute-done((bf16[64,1024]{1,0:T(8,128)(2,1)S(1)}, bf16[64,1024]{1,0:T(8,128)(2,1)S(1)}, u32[]{:S(2)}, u32[]{:S(2)}) %collective-permute-start.15) | collective-permute-done | bytes 131104 | tf_op jit(solution)/shard_map/ppermute | solution.py:229
  53.2 1.5 %collective-permute-start.16 = (f32[128,128]{1,0:T(8,128)S(1)}, f32[128,128]{1,0:T(8,128)S(1)}, u32[]{:S(2)}, u32[]{:S(2)}) collective-permute-start(f32[128,128]{1,0:T(8,128)S(1)} %get-tuple-element.59), channel_id=1, source_target_pairs={{0,2},{2,0},{1,3},{3,1},{4,6},{6,4},{5,7},{7,5},{8,10},{10,8},{9,1... | collective-permute-start | bytes 196616 | tf_op jit(solution)/shard_map/ppermute | solution.py:229
  54.7 0.5 collective-permute-start.18
  55.2 2.9 %collective-permute-done.16 = f32[128,128]{1,0:T(8,128)S(1)} collective-permute-done((f32[128,128]{1,0:T(8,128)S(1)}, f32[128,128]{1,0:T(8,128)S(1)}, u32[]{:S(2)}, u32[]{:S(2)}) %collective-permute-start.16) | collective-permute-done | bytes 65568 | tf_op jit(solution)/shard_map/ppermute | solution.py:229
  58.1 1.6 %collective-permute-start.17 = (bf16[128,128]{1,0:T(8,128)(2,1)S(1)}, bf16[128,128]{1,0:T(8,128)(2,1)S(1)}, u32[]{:S(2)}, u32[]{:S(2)}) collective-permute-start(bf16[128,128]{1,0:T(8,128)(2,1)S(1)} %multiply_convert_fusion), channel_id=1, source_target_pairs={{0,4},{4,0},{8,12},{12,8},{1,5},{5,1},{9,13},{13,9},{2,6},{6,2},{1... | collective-permute-start | bytes 98312 | tf_op jit(solution)/shard_map/ppermute | solution.py:232
  59.6 2.4 %collective-permute-done.17 = bf16[128,128]{1,0:T(8,128)(2,1)S(1)} collective-permute-done((bf16[128,128]{1,0:T(8,128)(2,1)S(1)}, bf16[128,128]{1,0:T(8,128)(2,1)S(1)}, u32[]{:S(2)}, u32[]{:S(2)}) %collective-permute-start.17) | collective-permute-done | bytes 32800 | tf_op jit(solution)/shard_map/ppermute | solution.py:232
  62.1 2.1 %collective-permute-start.19 = (bf16[128,128]{1,0:T(8,128)(2,1)S(1)}, bf16[128,128]{1,0:T(8,128)(2,1)S(1)}, u32[]{:S(2)}, u32[]{:S(2)}) collective-permute-start(bf16[128,128]{1,0:T(8,128)(2,1)S(1)} %add.22.scaled_ref), channel_id=1, source_target_pairs={{0,8},{8,0},{4,12},{12,4},{1,9},{9,1},{5,13},{13,5},{2,10},{10,2},... | collective-permute-start | bytes 98312 | tf_op jit(solution)/shard_map/ppermute | solution.py:232
  64.2 2.8 %collective-permute-done.19.scaled_got_ref = bf16[128,128]{1,0:T(8,128)(2,1)S(1)} collective-permute-done((bf16[128,128]{1,0:T(8,128)(2,1)S(1)}, bf16[128,128]{1,0:T(8,128)(2,1)S(1)}, u32[]{:S(2)}, u32[]{:S(2)}) %collective-permute-start.19) | collective-permute-done | bytes 32800 | tf_op jit(solution)/shard_map/ppermute | solution.py:232
  66.9 2.1 %shard_map.86 = bf16[256,1024]{1,0:T(8,128)(2,1)} custom-call(s32[3]{0:T(128)S(1)} %pad_add_fusion.flags_ref, bf16[256,1024]{1,0:T(8,128)(2,1)S(1)} %copy-done.2, bf16[128,128]{1,0:T(8,128)(2,1)S(1)} %add.22.scaled_ref, bf16[128,128]{1,0:T(8,128)(2,1)S(1)} %collective-permute-done.19.scaled_got_ref, bf16[4,256,64]{2,1,0:T(8,128)(2,1)S(1)} %broadcast_in_dim.24.hot_ref, ...), custom_call_target="tpu_custom_call" | custom-call | tf_op jit(solution)/shard_map/pallas_call | solution.py:82
  (22 shorter events, 0.2 us)
Async XLA Ops:
  0.0 16.3 %copy-start.3 = (bf16[2,64,1024]{2,1,0:T(8,128)(2,1)S(1)}, bf16[2,64,1024]{2,1,0:T(8,128)(2,1)}, u32[]{:S(2)}) copy-start(bf16[2,64,1024]{2,1,0:T(8,128)(2,1)} %param.12) | copy-start | bytes 786436
  1.1 27.4 %collective-permute-start.1 = (bf16[64,4096]{1,0:T(8,128)(2,1)S(1)}, bf16[64,4096]{1,0:T(8,128)(2,1)S(1)}, u32[]{:S(2)}, u32[]{:S(2)}) collective-permute-start(bf16[64,4096]{1,0:T(8,128)(2,1)S(1)} %constant_dynamic-slice_fusion), channel_id=1, source_target_pairs={{0,8},{8,0},{4,12},{12,4},{1,9},{9,1},{5,13},{13,5},{2,10},{10,2},... | collective-permute-start | bytes 1572872 | tf_op jit(solution)/shard_map/ppermute | solution.py:232
  5.2 23.5 %collective-permute-start = (bf16[64,4096]{1,0:T(8,128)(2,1)S(1)}, bf16[64,4096]{1,0:T(8,128)(2,1)S(1)}, u32[]{:S(2)}, u32[]{:S(2)}) collective-permute-start(bf16[64,4096]{1,0:T(8,128)(2,1)S(1)} %constant_dynamic-slice_fusion), channel_id=1, source_target_pairs={{0,4},{4,0},{8,12},{12,8},{1,5},{5,1},{9,13},{13,9},{2,6},{6,2},{1... | collective-permute-start | bytes 1572872 | tf_op jit(solution)/shard_map/ppermute | solution.py:232
  6.8 9.5 %collective-permute-start.2 = (bf16[2,64,1024]{2,1,0:T(8,128)(2,1)}, bf16[2,64,1024]{2,1,0:T(8,128)(2,1)S(1)}, u32[]{:S(2)}, u32[]{:S(2)}) collective-permute-start(bf16[2,64,1024]{2,1,0:T(8,128)(2,1)} %param.12), channel_id=1, source_target_pairs={{0,2},{2,0},{1,3},{3,1},{4,6},{6,4},{5,7},{7,5},{8,10},{10,8},{9,1... | collective-permute-start | bytes 786440 | tf_op jit(solution)/shard_map/ppermute | solution.py:229
  9.6 1.0 %copy-start = (bf16[1,64,4096]{2,1,0:T(8,128)(2,1)S(1)}, bf16[1,64,4096]{2,1,0:T(8,128)(2,1)}, u32[]{:S(2)}) copy-start(bf16[1,64,4096]{2,1,0:T(8,128)(2,1)} %param.11) | copy-start | bytes 1572868
  10.6 1.2 %copy-start.1 = (bf16[128,4096]{1,0:T(8,128)(2,1)S(1)}, bf16[128,4096]{1,0:T(8,128)(2,1)}, u32[]{:S(2)}) copy-start(bf16[128,4096]{1,0:T(8,128)(2,1)} %rows_ref.1) | copy-start | bytes 3145732
  28.9 2.5 %collective-permute-start.7 = (bf16[32,4096]{1,0:T(8,128)(2,1)S(1)}, bf16[32,4096]{1,0:T(8,128)(2,1)S(1)}, u32[]{:S(2)}, u32[]{:S(2)}) collective-permute-start(bf16[32,4096]{1,0:T(8,128)(2,1)S(1)} %get-tuple-element.79), channel_id=1, source_target_pairs={{0,1},{1,0},{2,3},{3,2},{4,5},{5,4},{6,7},{7,6},{8,9},{9,8},{10,11... | collective-permute-start | bytes 786440 | tf_op jit(solution)/shard_map/ppermute | solution.py:226
  29.0 9.2 %collective-permute-start.6 = (bf16[32,4096]{1,0:T(8,128)(2,1)S(1)}, bf16[32,4096]{1,0:T(8,128)(2,1)S(1)}, u32[]{:S(2)}, u32[]{:S(2)}) collective-permute-start(bf16[32,4096]{1,0:T(8,128)(2,1)S(1)} %get-tuple-element.79), channel_id=1, source_target_pairs={{0,4},{4,0},{8,12},{12,8},{1,5},{5,1},{9,13},{13,9},{2,6},{6,2},{1... | collective-permute-start | bytes 786440 | tf_op jit(solution)/shard_map/ppermute | solution.py:232
  30.6 1.5 %collective-permute-start.8 = (bf16[32,4096]{1,0:T(8,128)(2,1)S(1)}, bf16[32,4096]{1,0:T(8,128)(2,1)S(1)}, u32[]{:S(2)}, u32[]{:S(2)}) collective-permute-start(bf16[32,4096]{1,0:T(8,128)(2,1)S(1)} %get-tuple-element.80), channel_id=1, source_target_pairs={{0,1},{1,0},{2,3},{3,2},{4,5},{5,4},{6,7},{7,6},{8,9},{9,8},{10,11... | collective-permute-start | bytes 786440 | tf_op jit(solution)/shard_map/ppermute | solution.py:226
  30.7 12.8 %collective-permute-start.3 = (bf16[32,4096]{1,0:T(8,128)(2,1)S(1)}, bf16[32,4096]{1,0:T(8,128)(2,1)S(1)}, u32[]{:S(2)}, u32[]{:S(2)}) collective-permute-start(bf16[32,4096]{1,0:T(8,128)(2,1)S(1)} %get-tuple-element.80), channel_id=1, source_target_pairs={{0,4},{4,0},{8,12},{12,8},{1,5},{5,1},{9,13},{13,9},{2,6},{6,2},{1... | collective-permute-start | bytes 786440 | tf_op jit(solution)/shard_map/ppermute | solution.py:232
  31.3 7.5 %collective-permute-start.5 = (bf16[32,4096]{1,0:T(8,128)(2,1)S(1)}, bf16[32,4096]{1,0:T(8,128)(2,1)S(1)}, u32[]{:S(2)}, u32[]{:S(2)}) collective-permute-start(bf16[32,4096]{1,0:T(8,128)(2,1)S(1)} %get-tuple-element.81), channel_id=1, source_target_pairs={{0,1},{1,0},{2,3},{3,2},{4,5},{5,4},{6,7},{7,6},{8,9},{9,8},{10,11... | collective-permute-start | bytes 786440 | tf_op jit(solution)/shard_map/ppermute | solution.py:226
  31.4 8.9 %collective-permute-start.4 = (bf16[32,4096]{1,0:T(8,128)(2,1)S(1)}, bf16[32,4096]{1,0:T(8,128)(2,1)S(1)}, u32[]{:S(2)}, u32[]{:S(2)}) collective-permute-start(bf16[32,4096]{1,0:T(8,128)(2,1)S(1)} %get-tuple-element.82), channel_id=1, source_target_pairs={{0,1},{1,0},{2,3},{3,2},{4,5},{5,4},{6,7},{7,6},{8,9},{9,8},{10,11... | collective-permute-start | bytes 786440 | tf_op jit(solution)/shard_map/ppermute | solution.py:226
  38.2 2.6 %collective-permute-start.10 = (bf16[16,4096]{1,0:T(8,128)(2,1)S(1)}, bf16[16,4096]{1,0:T(8,128)(2,1)S(1)}, u32[]{:S(2)}, u32[]{:S(2)}) collective-permute-start(bf16[16,4096]{1,0:T(8,128)(2,1)S(1)} %get-tuple-element.85), channel_id=1, source_target_pairs={{0,1},{1,0},{2,3},{3,2},{4,5},{5,4},{6,7},{7,6},{8,9},{9,8},{10,11... | collective-permute-start | bytes 393224 | tf_op jit(solution)/shard_map/ppermute | solution.py:226
  38.3 2.5 %collective-permute-start.9 = (bf16[16,4096]{1,0:T(8,128)(2,1)S(1)}, bf16[16,4096]{1,0:T(8,128)(2,1)S(1)}, u32[]{:S(2)}, u32[]{:S(2)}) collective-permute-start(bf16[16,4096]{1,0:T(8,128)(2,1)S(1)} %get-tuple-element.86), channel_id=1, source_target_pairs={{0,1},{1,0},{2,3},{3,2},{4,5},{5,4},{6,7},{7,6},{8,9},{9,8},{10,11... | collective-permute-start | bytes 393224 | tf_op jit(solution)/shard_map/ppermute | solution.py:226
  38.8 6.4 %collective-permute-start.11 = (bf16[64,1024]{1,0:T(8,128)(2,1)S(1)}, bf16[64,1024]{1,0:T(8,128)(2,1)S(1)}, u32[]{:S(2)}, u32[]{:S(2)}) collective-permute-start(bf16[64,1024]{1,0:T(8,128)(2,1)S(1)} %get-tuple-element.48), channel_id=1, source_target_pairs={{0,2},{2,0},{1,3},{3,1},{4,6},{6,4},{5,7},{7,5},{8,10},{10,8},{9,1... | collective-permute-start | bytes 393224 | tf_op jit(solution)/shard_map/ppermute | solution.py:229
  40.3 26.6 %copy-start.2 = (bf16[256,1024]{1,0:T(8,128)(2,1)S(1)}, bf16[256,1024]{1,0:T(8,128)(2,1)}, u32[]{:S(2)}) copy-start(bf16[256,1024]{1,0:T(8,128)(2,1)} %residual_ref.1) | copy-start | bytes 1572868
  40.3 6.7 %collective-permute-start.12 = (bf16[64,1024]{1,0:T(8,128)(2,1)S(1)}, bf16[64,1024]{1,0:T(8,128)(2,1)S(1)}, u32[]{:S(2)}, u32[]{:S(2)}) collective-permute-start(bf16[64,1024]{1,0:T(8,128)(2,1)S(1)} %get-tuple-element.49), channel_id=1, source_target_pairs={{0,2},{2,0},{1,3},{3,1},{4,6},{6,4},{5,7},{7,5},{8,10},{10,8},{9,1... | collective-permute-start | bytes 393224 | tf_op jit(solution)/shard_map/ppermute | solution.py:229
  47.1 2.1 %collective-permute-start.14 = (bf16[16,4096]{1,0:T(8,128)(2,1)S(1)}, bf16[16,4096]{1,0:T(8,128)(2,1)S(1)}, u32[]{:S(2)}, u32[]{:S(2)}) collective-permute-start(bf16[16,4096]{1,0:T(8,128)(2,1)S(1)} %get-tuple-element.83), channel_id=1, source_target_pairs={{0,1},{1,0},{2,3},{3,2},{4,5},{5,4},{6,7},{7,6},{8,9},{9,8},{10,11... | collective-permute-start | bytes 393224 | tf_op jit(solution)/shard_map/ppermute | solution.py:226
  47.2 2.0 %collective-permute-start.13 = (bf16[16,4096]{1,0:T(8,128)(2,1)S(1)}, bf16[16,4096]{1,0:T(8,128)(2,1)S(1)}, u32[]{:S(2)}, u32[]{:S(2)}) collective-permute-start(bf16[16,4096]{1,0:T(8,128)(2,1)S(1)} %get-tuple-element.84), channel_id=1, source_target_pairs={{0,1},{1,0},{2,3},{3,2},{4,5},{5,4},{6,7},{7,6},{8,9},{9,8},{10,11... | collective-permute-start | bytes 393224 | tf_op jit(solution)/shard_map/ppermute | solution.py:226
  47.7 5.5 %collective-permute-start.15 = (bf16[64,1024]{1,0:T(8,128)(2,1)S(1)}, bf16[64,1024]{1,0:T(8,128)(2,1)S(1)}, u32[]{:S(2)}, u32[]{:S(2)}) collective-permute-start(bf16[64,1024]{1,0:T(8,128)(2,1)S(1)} %get-tuple-element.58), channel_id=1, source_target_pairs={{0,2},{2,0},{1,3},{3,1},{4,6},{6,4},{5,7},{7,5},{8,10},{10,8},{9,1... | collective-permute-start | bytes 393224 | tf_op jit(solution)/shard_map/ppermute | solution.py:229
  53.2 4.9 %collective-permute-start.16 = (f32[128,128]{1,0:T(8,128)S(1)}, f32[128,128]{1,0:T(8,128)S(1)}, u32[]{:S(2)}, u32[]{:S(2)}) collective-permute-start(f32[128,128]{1,0:T(8,128)S(1)} %get-tuple-element.59), channel_id=1, source_target_pairs={{0,2},{2,0},{1,3},{3,1},{4,6},{6,4},{5,7},{7,5},{8,10},{10,8},{9,1... | collective-permute-start | bytes 196616 | tf_op jit(solution)/shard_map/ppermute | solution.py:229
  54.7 7.4 %collective-permute-start.18 = (bf16[64,1024]{1,0:T(8,128)(2,1)S(1)}, bf16[64,1024]{1,0:T(8,128)(2,1)S(1)}, u32[]{:S(2)}, u32[]{:S(2)}) collective-permute-start(bf16[64,1024]{1,0:T(8,128)(2,1)S(1)} %get-tuple-element.61), channel_id=1, source_target_pairs={{0,2},{2,0},{1,3},{3,1},{4,6},{6,4},{5,7},{7,5},{8,10},{10,8},{9,1... | collective-permute-start | bytes 393224 | tf_op jit(solution)/shard_map/ppermute | solution.py:229
  58.1 4.0 %collective-permute-start.17 = (bf16[128,128]{1,0:T(8,128)(2,1)S(1)}, bf16[128,128]{1,0:T(8,128)(2,1)S(1)}, u32[]{:S(2)}, u32[]{:S(2)}) collective-permute-start(bf16[128,128]{1,0:T(8,128)(2,1)S(1)} %multiply_convert_fusion), channel_id=1, source_target_pairs={{0,4},{4,0},{8,12},{12,8},{1,5},{5,1},{9,13},{13,9},{2,6},{6,2},{1... | collective-permute-start | bytes 98312 | tf_op jit(solution)/shard_map/ppermute | solution.py:232
  62.1 4.9 %collective-permute-start.19 = (bf16[128,128]{1,0:T(8,128)(2,1)S(1)}, bf16[128,128]{1,0:T(8,128)(2,1)S(1)}, u32[]{:S(2)}, u32[]{:S(2)}) collective-permute-start(bf16[128,128]{1,0:T(8,128)(2,1)S(1)} %add.22.scaled_ref), channel_id=1, source_target_pairs={{0,8},{8,0},{4,12},{12,4},{1,9},{9,1},{5,13},{13,5},{2,10},{10,2},... | collective-permute-start | bytes 98312 | tf_op jit(solution)/shard_map/ppermute | solution.py:232

commit v10 on v9

--- a/solution.py
+++ b/solution.py
@@ -131,16 +131,14 @@
 
 def far_kernel(
     flags_ref, weight_ref, down_ref, held_ref, mine_ref, first_ref, second_ref,
-    keep_ref, send_ref, keep_more_ref, send_more_ref, low_ref,
+    keep_ref, send_ref, low_ref,
 ):
     other = jnp.concatenate([first_ref[...], second_ref[...]])
     rows = joined(flags_ref, mine_ref[...], other)
     low_ref[...] = low_product(rows, down_ref)
-    half = keep_ref.shape[0]
     for tile in column_tiles(weight_ref.shape[1]):
         value = dot(rows, weight_ref[:, tile])
-        part(flags_ref, held_ref[:half, tile], value[:half], keep_ref, send_ref, tile)
-        part(flags_ref, held_ref[half:, tile], value[half:], keep_more_ref, send_more_ref, tile)
+        part(flags_ref, held_ref[:, tile], value, keep_ref, send_ref, tile)
 
 
 def near_kernel(
@@ -190,25 +188,28 @@
         part(flags_ref, held_ref[:, tile], value, keep_ref, send_ref, tile)
 
 
-def final_kernel(flags_ref, residual_ref, scaled_ref, scaled_got_ref, hot_ref, ups_ref, *refs):
+def base_kernel(flags_ref, residual_ref, *refs):
     *parts, out_ref = refs
+    odd = flags_ref[2] == 1
+    first, left, right = [
+        keep[...] + got[...].astype(F32) for keep, got in zip(parts[::2], parts[1::2])
+    ]
+    step = left.shape[0] // 2
+    second = jnp.concatenate([left[:step], right[:step], left[step:], right[step:]])
+    block = first.shape[0]
+    for at, base in ((0, jnp.where(odd, second, first)), (block, jnp.where(odd, first, second))):
+        here = slice(at, at + block)
+        out_ref[here, :] = residual_ref[here, :].astype(F32) + base
+
+
+def final_kernel(base_ref, scaled_ref, scaled_got_ref, hot_ref, ups_ref, out_ref):
     scaled = scaled_ref[...] + scaled_got_ref[...]
     width = ups_ref.shape[1]
     scaled = jnp.concatenate([scaled[:, :width], scaled[:, width:]])
     lora = dot(scaled * hot_ref[0], ups_ref[0])
     for slot in range(1, ups_ref.shape[0]):
         lora += dot(scaled * hot_ref[slot], ups_ref[slot])
-    odd = flags_ref[2] == 1
-    sums = [keep[...] + got[...].astype(F32) for keep, got in zip(parts[::2], parts[1::2])]
-    step = sums[2].shape[0] // 2
-    first = jnp.concatenate(sums[:2])
-    second = jnp.concatenate(
-        [sums[2][:step], sums[3][:step], sums[2][step:], sums[3][step:]]
-    )
-    block = first.shape[0]
-    for at, base in ((0, jnp.where(odd, second, first)), (block, jnp.where(odd, first, second))):
-        here = slice(at, at + block)
-        out_ref[here, :] = (residual_ref[here, :].astype(F32) + base + lora[here]).astype(BF16)
+    out_ref[...] = (base_ref[...] + lora).astype(BF16)
 
 
 def line(rows, residual, weight, down, up, tenant, entry, live):
@@ -269,14 +270,17 @@
         (near, far, own_sum, own_low, ups, hot, scale)
     )
 
-    last = [along(far[:step], NEAR), along(far[step:], NEAR)]
-    kept_a, sent_a, kept_b, sent_b, far_low = call(
+    last = [along(far[:step], NEAR)]
+    far_others = over_core_in_two(far)
+    far_second, far_others[0] = barrier((far[step:], far_others[0]))
+    last.append(along(far_second, NEAR))
+    kept_a, sent_a, far_low = call(
         far_kernel,
-        parted(half) * 2 + lows(block_rows),
+        parted(block_rows) + lows(block_rows),
         [SMEM] + [VMEM] * 6,
-        [flags, held, down[0], own_sum, far] + over_core_in_two(far),
-    )
-    got_a, got_b = over_x(sent_a), over_x(sent_b)
+        [flags, held, down[0], own_sum, far] + far_others,
+    )
+    got_a = over_x(sent_a)
     last[0], kept_a = barrier((last[0], kept_a))
 
     kept_c, sent_c, hold, near_low = call(
@@ -287,7 +291,7 @@
         + [last[0]] + over_core_in_two(last[0]),
     )
     got_c = over_x(sent_c)
-    last[1], hold, got_a, got_b, near_low = barrier((last[1], hold, got_a, got_b, near_low))
+    last[1], hold, got_a, near_low = barrier((last[1], hold, got_a, near_low))
 
     kept_d, sent_d, low, low_sent = call(
         last_kernel,
@@ -296,18 +300,22 @@
         [flags, held, down[0], hold, own_low, far_low, near_low, last[1]]
         + over_core_in_two(last[1]),
     )
-    low_sent, got_c = barrier((low_sent, got_c))
     got_d = over_x(sent_d)
 
     scaled = ((low + over_x(low_sent)) * scale).astype(BF16)
     scaled = scaled + along(scaled, NEAR)
-    scaled, got_d = barrier((scaled, got_d))
-    parts = [kept_a, got_a, kept_b, got_b, kept_c, got_c, kept_d, got_d]
+    scaled, got_c, got_d = barrier((scaled, got_c, got_d))
+    base = call(
+        base_kernel,
+        shape(residual.shape, F32),
+        [SMEM] + [VMEM] * 7,
+        [flags, residual, kept_a, got_a, kept_c, got_c, kept_d, got_d],
+    )
     return call(
         final_kernel,
         shape(residual.shape, BF16),
-        [SMEM] + [VMEM] * 13,
-        [flags, residual, scaled, along(scaled, FAR), hot, ups] + parts,
+        [VMEM] * 5,
+        [base, scaled, along(scaled, FAR), hot, ups],
     )
 
 

time: 69.3 us -> 64.3 us (0.928)
  waiting for transfers between devices: 29.7 us -> 26.1 us
  starting transfers between devices: 20.5 us -> 19 us
    ppermute x6 -> x5, waiting for transfers between devices: 8.04 us -> 3.37 us  [over_x(): return lax.ppermute(value, 'split', SWAP)]
    ppermute x8, waiting for transfers between devices: 0.23 us -> 2.8 us  [over_core(): return lax.ppermute(value, 'sub', SWAP)]
    ppermute x6, waiting for transfers between devices: 21.5 us -> 19.9 us  [along(): return lax.ppermute(value, 'blk', pairs)]
    ppermute x6 -> x5, starting transfers between devices: 7.08 us -> 6.19 us  [over_x(): return lax.ppermute(value, 'split', SWAP)]
    pallas_call x5 -> x6, Pallas kernels: 13.5 us -> 13.7 us  [call(): pl.pallas_call(kernel, out_shape=outs, in_specs=in_specs, out_specs=jax.t...]
  transfers between devices with their start and end apart: 20 -> 19, of which waited for: 10 -> 14; matrix products, arithmetic and copies ran while one was open for 2% -> 2% of each run, Pallas kernels for 17% -> 16%
where the time goes in v10:
time: 64.3 us; the launch traced here: 64 us
  waiting for transfers between devices  26.1 us (41%)
  starting transfers between devices  19 us (30%)
  Pallas kernels  13.7 us (21%)
  local copies, waits for them, and re-layouts  3.71 us (6%)
  other arithmetic  1.38 us (2%)
    ppermute x6, waiting for transfers between devices, along(): return lax.ppermute(value, 'blk', pairs)  19.9 us
    pallas_call x6, Pallas kernels, call(): pl.pallas_call(kernel, out_shape=outs, in_specs=in_specs, out_specs=jax.t...  13.7 us
    ppermute x6, starting transfers between devices, along(): return lax.ppermute(value, 'blk', pairs)  10.9 us
    ppermute x5, starting transfers between devices, over_x(): return lax.ppermute(value, 'split', SWAP)  6.19 us
    ppermute x5, waiting for transfers between devices, over_x(): return lax.ppermute(value, 'split', SWAP)  3.37 us
    ppermute x8, waiting for transfers between devices, over_core(): return lax.ppermute(value, 'sub', SWAP)  2.8 us
    unnamed x8, local copies, waits for them, and re-layouts  2.28 us
    ppermute x8, starting transfers between devices, over_core(): return lax.ppermute(value, 'sub', SWAP)  1.93 us
  transfers between devices with their start and end apart: 19, of which 14 were waited for; matrix products, arithmetic and copies ran while one was open for 2% of the time, Pallas kernels for 16%

profile of v10, /device:TPU:0, one launch (start us, length us, event | category | flops | bytes accessed | tf_op | source)
XLA Modules:
  0.0 64.0 jit_solution(14693825108273444834)
XLA Ops:
  0.0 1.1 %constant_dynamic-slice_fusion = bf16[64,4096]{1,0:T(8,128)(2,1)S(1)} fusion(bf16[128,4096]{1,0:T(8,128)(2,1)} %rows_ref.1, s32[]{:T(128)S(6)} %select_n.36), kind=kLoop, calls=%fused_computation.13 | loop fusion | bytes 1048580 | tf_op jit(solution)/shard_map/dynamic_slice | solution.py:257
  1.1 4.1 %collective-permute-start.1 = (bf16[64,4096]{1,0:T(8,128)(2,1)S(1)}, bf16[64,4096]{1,0:T(8,128)(2,1)S(1)}, u32[]{:S(2)}, u32[]{:S(2)}) collective-permute-start(bf16[64,4096]{1,0:T(8,128)(2,1)S(1)} %constant_dynamic-slice_fusion), channel_id=1, source_target_pairs={{0,8},{8,0},{4,12},{12,4},{1,9},{9,1},{5,13},{13,5},{2,10},{10,2},... | collective-permute-start | bytes 1572872 | tf_op jit(solution)/shard_map/ppermute | solution.py:233
  5.2 1.6 %collective-permute-start = (bf16[64,4096]{1,0:T(8,128)(2,1)S(1)}, bf16[64,4096]{1,0:T(8,128)(2,1)S(1)}, u32[]{:S(2)}, u32[]{:S(2)}) collective-permute-start(bf16[64,4096]{1,0:T(8,128)(2,1)S(1)} %constant_dynamic-slice_fusion), channel_id=1, source_target_pairs={{0,4},{4,0},{8,12},{12,8},{1,5},{5,1},{9,13},{13,9},{2,6},{6,2},{1... | collective-permute-start | bytes 1572872 | tf_op jit(solution)/shard_map/ppermute | solution.py:233
  6.8 1.5 %collective-permute-start.2 = (bf16[2,64,1024]{2,1,0:T(8,128)(2,1)}, bf16[2,64,1024]{2,1,0:T(8,128)(2,1)S(1)}, u32[]{:S(2)}, u32[]{:S(2)}) collective-permute-start(bf16[2,64,1024]{2,1,0:T(8,128)(2,1)} %param.12), channel_id=1, source_target_pairs={{0,2},{2,0},{1,3},{3,1},{4,6},{6,4},{5,7},{7,5},{8,10},{10,8},{9,1... | collective-permute-start | bytes 786440 | tf_op jit(solution)/shard_map/ppermute | solution.py:230
  8.3 0.8 %select_reduce_fusion = (s32[512]{0:T(512)S(1)}, s32[512]{0:T(512)S(1)}) fusion(s32[4]{0:T(128)} %param.15, s32[512]{0:T(512)} %param.13, s32[4]{0:T(128)} %param.14), kind=kLoop, calls=%fused_computation.5 | loop fusion | flops 9216 | bytes 6176 | tf_op jit(solution)/shard_map/reduce_sum | solution.py:24
  9.1 0.1 convert_divide_fusion
  9.2 0.1 broadcast_compare_fusion
  9.2 0.2 select_select_fusion
  9.4 0.1 pad_maximum_fusion
  9.5 0.1 pad_add_fusion.flags_ref
  9.6 1.0 %copy-done = bf16[1,64,4096]{2,1,0:T(8,128)(2,1)S(1)} copy-done((bf16[1,64,4096]{2,1,0:T(8,128)(2,1)S(1)}, bf16[1,64,4096]{2,1,0:T(8,128)(2,1)}, u32[]{:S(2)}) %copy-start) | copy-done | bytes 524312
  10.6 1.2 %copy-done.1 = bf16[128,4096]{1,0:T(8,128)(2,1)S(1)} copy-done((bf16[128,4096]{1,0:T(8,128)(2,1)S(1)}, bf16[128,4096]{1,0:T(8,128)(2,1)}, u32[]{:S(2)}) %copy-start.1) | copy-done | bytes 1048600
  11.9 4.4 %shard_map.82 = (bf16[4096,1024]{1,0:T(8,128)(2,1)S(1)}, f32[128,1024]{1,0:T(8,128)S(1)}, f32[128,64]{1,0:T(8,128)S(1)}) custom-call(bf16[4096,1024]{1,0:T(8,128)(2,1)} %weight_ref.1, bf16[64,4096]{1,0:T(8,128)(2,1)S(1)} %bitcast.4, bf16[128,4096]{1,0:T(8,128)(2,1)S(1)} %copy-done.1), custom_call_target="tpu_custom_call" | custom-call | tf_op jit(solution)/shard_map/pallas_call | solution.py:82
  16.3 0.1 maximum_select_fusion.ups_ref
  16.4 12.1 %collective-permute-done.1.mine_ref = bf16[64,4096]{1,0:T(8,128)(2,1)S(1)} collective-permute-done((bf16[64,4096]{1,0:T(8,128)(2,1)S(1)}, bf16[64,4096]{1,0:T(8,128)(2,1)S(1)}, u32[]{:S(2)}, u32[]{:S(2)}) %collective-permute-start.1) | collective-permute-done | bytes 524320 | tf_op jit(solution)/shard_map/ppermute | solution.py:233
  28.5 0.2 collective-permute-done.mine_ref
  28.7 0.2 broadcast_in_dim.24.hot_ref
  28.9 0.1 collective-permute-start.4
  29.0 1.6 %collective-permute-start.3 = (bf16[32,4096]{1,0:T(8,128)(2,1)S(1)}, bf16[32,4096]{1,0:T(8,128)(2,1)S(1)}, u32[]{:S(2)}, u32[]{:S(2)}) collective-permute-start(bf16[32,4096]{1,0:T(8,128)(2,1)S(1)} %get-tuple-element.78), channel_id=1, source_target_pairs={{0,4},{4,0},{8,12},{12,8},{1,5},{5,1},{9,13},{13,9},{2,6},{6,2},{1... | collective-permute-start | bytes 786440 | tf_op jit(solution)/shard_map/ppermute | solution.py:233
  30.6 0.2 collective-permute-start.5
  30.8 0.4 collective-permute-start.8
  31.2 0.2 collective-permute-start.7
  31.3 0.7 %collective-permute-done.5.second_ref = bf16[32,4096]{1,0:T(8,128)(2,1)S(1)} collective-permute-done((bf16[32,4096]{1,0:T(8,128)(2,1)S(1)}, bf16[32,4096]{1,0:T(8,128)(2,1)S(1)}, u32[]{:S(2)}, u32[]{:S(2)}) %collective-permute-start.5) | collective-permute-done | bytes 262176 | tf_op jit(solution)/shard_map/ppermute | solution.py:227
  32.1 2.1 %shard_map.83 = (f32[128,1024]{1,0:T(8,128)S(1)}, bf16[128,1024]{1,0:T(8,128)(2,1)S(1)}, f32[128,64]{1,0:T(8,128)S(1)}) custom-call(s32[3]{0:T(128)S(1)} %pad_add_fusion.flags_ref, bf16[4096,1024]{1,0:T(8,128)(2,1)S(1)} %get-tuple-element.40.weight_ref, bf16[64,4096]{1,0:T(8,128)(2,1)S(1)} %bitcast.5, f32[128,1024]{1,0:T(8,128)S(1)} %get-tuple-element.41.held_ref, ...), custom_call_target="tpu_custom_call" | custom-call | tf_op jit(solution)/shard_map/pallas_call | solution.py:82
  34.2 1.6 %collective-permute-start.11 = (bf16[128,1024]{1,0:T(8,128)(2,1)S(1)}, bf16[128,1024]{1,0:T(8,128)(2,1)S(1)}, u32[]{:S(2)}, u32[]{:S(2)}) collective-permute-start(bf16[128,1024]{1,0:T(8,128)(2,1)S(1)} %get-tuple-element.49), channel_id=1, source_target_pairs={{0,2},{2,0},{1,3},{3,1},{4,6},{6,4},{5,7},{7,5},{8,10},{10,8},{9,1... | collective-permute-start | bytes 786440 | tf_op jit(solution)/shard_map/ppermute | solution.py:230
  35.7 0.6 collective-permute-start.6
  36.3 1.4 %collective-permute-done.3.last_ref = bf16[32,4096]{1,0:T(8,128)(2,1)S(1)} collective-permute-done((bf16[32,4096]{1,0:T(8,128)(2,1)S(1)}, bf16[32,4096]{1,0:T(8,128)(2,1)S(1)}, u32[]{:S(2)}, u32[]{:S(2)}) %collective-permute-start.3) | collective-permute-done | bytes 262176 | tf_op jit(solution)/shard_map/ppermute | solution.py:233
  37.9 0.5 collective-permute-start.9
  38.3 0.8 %collective-permute-done.10.fourth_ref = bf16[16,4096]{1,0:T(8,128)(2,1)S(1)} collective-permute-done((bf16[16,4096]{1,0:T(8,128)(2,1)S(1)}, bf16[16,4096]{1,0:T(8,128)(2,1)S(1)}, u32[]{:S(2)}, u32[]{:S(2)}) %collective-permute-start.10) | collective-permute-done | bytes 131104 | tf_op jit(solution)/shard_map/ppermute | solution.py:227
  39.2 0.2 collective-permute-done.9.third_ref
  39.4 2.7 %shard_map.84 = (f32[64,1024]{1,0:T(8,128)S(1)}, bf16[64,1024]{1,0:T(8,128)(2,1)S(1)}, f32[64,1024]{1,0:T(8,128)S(1)}, f32[192,64]{1,0:T(8,128)S(1)}) custom-call(s32[3]{0:T(128)S(1)} %pad_add_fusion.flags_ref, bf16[4096,1024]{1,0:T(8,128)(2,1)S(1)} %get-tuple-element.40.weight_ref, bf16[64,4096]{1,0:T(8,128)(2,1)S(1)} %bitcast.6, ...), custom_call_target="tpu_custom_call" | custom-call | tf_op jit(solution)/shard_map/pallas_call | solution.py:82
  42.1 0.5 collective-permute-done.11.refs_1_
  42.6 1.2 %collective-permute-done.6.mine_ref = bf16[32,4096]{1,0:T(8,128)(2,1)S(1)} collective-permute-done((bf16[32,4096]{1,0:T(8,128)(2,1)S(1)}, bf16[32,4096]{1,0:T(8,128)(2,1)S(1)}, u32[]{:S(2)}, u32[]{:S(2)}) %collective-permute-start.6) | collective-permute-done | bytes 262176 | tf_op jit(solution)/shard_map/ppermute | solution.py:233
  43.9 0.5 collective-permute-start.12
  44.4 0.8 %collective-permute-done.13.second_ref = bf16[16,4096]{1,0:T(8,128)(2,1)S(1)} collective-permute-done((bf16[16,4096]{1,0:T(8,128)(2,1)S(1)}, bf16[16,4096]{1,0:T(8,128)(2,1)S(1)}, u32[]{:S(2)}, u32[]{:S(2)}) %collective-permute-start.13) | collective-permute-done | bytes 131104 | tf_op jit(solution)/shard_map/ppermute | solution.py:227
  45.3 0.2 collective-permute-done.12.first_ref
  45.5 2.3 %shard_map.85 = (f32[64,1024]{1,0:T(8,128)S(1)}, bf16[64,1024]{1,0:T(8,128)(2,1)S(1)}, f32[128,128]{1,0:T(8,128)S(1)}, f32[128,128]{1,0:T(8,128)S(1)}) custom-call(s32[3]{0:T(128)S(1)} %pad_add_fusion.flags_ref, bf16[4096,1024]{1,0:T(8,128)(2,1)S(1)} %get-tuple-element.40.weight_ref, bf16[64,4096]{1,0:T(8,128)(2,1)S(1)} %bitcast.7, ...), custom_call_target="tpu_custom_call" | custom-call | tf_op jit(solution)/shard_map/pallas_call | solution.py:82
  47.7 1.1 %collective-permute-start.14 = (f32[128,128]{1,0:T(8,128)S(1)}, f32[128,128]{1,0:T(8,128)S(1)}, u32[]{:S(2)}, u32[]{:S(2)}) collective-permute-start(f32[128,128]{1,0:T(8,128)S(1)} %get-tuple-element.59), channel_id=1, source_target_pairs={{0,2},{2,0},{1,3},{3,1},{4,6},{6,4},{5,7},{7,5},{8,10},{10,8},{9,1... | collective-permute-start | bytes 196616 | tf_op jit(solution)/shard_map/ppermute | solution.py:230
  48.8 1.0 %collective-permute-start.16 = (bf16[64,1024]{1,0:T(8,128)(2,1)S(1)}, bf16[64,1024]{1,0:T(8,128)(2,1)S(1)}, u32[]{:S(2)}, u32[]{:S(2)}) collective-permute-start(bf16[64,1024]{1,0:T(8,128)(2,1)S(1)} %get-tuple-element.61), channel_id=1, source_target_pairs={{0,2},{2,0},{1,3},{3,1},{4,6},{6,4},{5,7},{7,5},{8,10},{10,8},{9,1... | collective-permute-start | bytes 393224 | tf_op jit(solution)/shard_map/ppermute | solution.py:230
  49.8 1.1 %collective-permute-start.17 = (bf16[64,1024]{1,0:T(8,128)(2,1)S(1)}, bf16[64,1024]{1,0:T(8,128)(2,1)S(1)}, u32[]{:S(2)}, u32[]{:S(2)}) collective-permute-start(bf16[64,1024]{1,0:T(8,128)(2,1)S(1)} %get-tuple-element.62), channel_id=1, source_target_pairs={{0,2},{2,0},{1,3},{3,1},{4,6},{6,4},{5,7},{7,5},{8,10},{10,8},{9,1... | collective-permute-start | bytes 393224 | tf_op jit(solution)/shard_map/ppermute | solution.py:230
  50.9 1.8 %collective-permute-done.14 = f32[128,128]{1,0:T(8,128)S(1)} collective-permute-done((f32[128,128]{1,0:T(8,128)S(1)}, f32[128,128]{1,0:T(8,128)S(1)}, u32[]{:S(2)}, u32[]{:S(2)}) %collective-permute-start.14) | collective-permute-done | bytes 65568 | tf_op jit(solution)/shard_map/ppermute | solution.py:230
  52.7 0.7 %collective-permute-start.15 = (bf16[128,128]{1,0:T(8,128)(2,1)S(1)}, bf16[128,128]{1,0:T(8,128)(2,1)S(1)}, u32[]{:S(2)}, u32[]{:S(2)}) collective-permute-start(bf16[128,128]{1,0:T(8,128)(2,1)S(1)} %multiply_convert_fusion), channel_id=1, source_target_pairs={{0,4},{4,0},{8,12},{12,8},{1,5},{5,1},{9,13},{13,9},{2,6},{6,2},{1... | collective-permute-start | bytes 98312 | tf_op jit(solution)/shard_map/ppermute | solution.py:233
  53.4 3.3 %collective-permute-done.15 = bf16[128,128]{1,0:T(8,128)(2,1)S(1)} collective-permute-done((bf16[128,128]{1,0:T(8,128)(2,1)S(1)}, bf16[128,128]{1,0:T(8,128)(2,1)S(1)}, u32[]{:S(2)}, u32[]{:S(2)}) %collective-permute-start.15) | collective-permute-done | bytes 32800 | tf_op jit(solution)/shard_map/ppermute | solution.py:233
  56.7 1.0 %collective-permute-done.17.refs_5_ = bf16[64,1024]{1,0:T(8,128)(2,1)S(1)} collective-permute-done((bf16[64,1024]{1,0:T(8,128)(2,1)S(1)}, bf16[64,1024]{1,0:T(8,128)(2,1)S(1)}, u32[]{:S(2)}, u32[]{:S(2)}) %collective-permute-start.17) | collective-permute-done | bytes 131104 | tf_op jit(solution)/shard_map/ppermute | solution.py:230
  57.7 2.3 %collective-permute-start.18 = (bf16[128,128]{1,0:T(8,128)(2,1)S(1)}, bf16[128,128]{1,0:T(8,128)(2,1)S(1)}, u32[]{:S(2)}, u32[]{:S(2)}) collective-permute-start(bf16[128,128]{1,0:T(8,128)(2,1)S(1)} %add.22.scaled_ref), channel_id=1, source_target_pairs={{0,8},{8,0},{4,12},{12,4},{1,9},{9,1},{5,13},{13,5},{2,10},{10,2},... | collective-permute-start | bytes 98312 | tf_op jit(solution)/shard_map/ppermute | solution.py:233
  60.0 0.7 %shard_map.86.base_ref = f32[256,1024]{1,0:T(8,128)S(1)} custom-call(s32[3]{0:T(128)S(1)} %pad_add_fusion.flags_ref, bf16[256,1024]{1,0:T(8,128)(2,1)S(1)} %copy-done.2, f32[128,1024]{1,0:T(8,128)S(1)} %get-tuple-element.44.refs_0_, bf16[128,1024]{1,0:T(8,128)(2,1)S(1)} %collective-permute-done.11.refs_1_, f32[64,1024]{1,0:T(8,128)S(1)} %get-tuple-element.52.refs_2_, ...), custom_call_target="tpu_custom_call" | custom-call | tf_op jit(solution)/shard_map/pallas_call | solution.py:82
  60.8 1.8 %collective-permute-done.18.scaled_got_ref = bf16[128,128]{1,0:T(8,128)(2,1)S(1)} collective-permute-done((bf16[128,128]{1,0:T(8,128)(2,1)S(1)}, bf16[128,128]{1,0:T(8,128)(2,1)S(1)}, u32[]{:S(2)}, u32[]{:S(2)}) %collective-permute-start.18) | collective-permute-done | bytes 32800 | tf_op jit(solution)/shard_map/ppermute | solution.py:233
  62.5 1.5 %shard_map.87 = bf16[256,1024]{1,0:T(8,128)(2,1)} custom-call(f32[256,1024]{1,0:T(8,128)S(1)} %shard_map.86.base_ref, bf16[128,128]{1,0:T(8,128)(2,1)S(1)} %add.22.scaled_ref, bf16[128,128]{1,0:T(8,128)(2,1)S(1)} %collective-permute-done.18.scaled_got_ref, bf16[4,256,64]{2,1,0:T(8,128)(2,1)S(1)} %broadcast_in_dim.24.hot_ref, ...), custom_call_target="tpu_custom_call" | custom-call | tf_op jit(solution)/shard_map/pallas_call | solution.py:82
  (21 shorter events, 0.3 us)
Async XLA Ops:
  0.0 16.3 %copy-start.3 = (bf16[2,64,1024]{2,1,0:T(8,128)(2,1)S(1)}, bf16[2,64,1024]{2,1,0:T(8,128)(2,1)}, u32[]{:S(2)}) copy-start(bf16[2,64,1024]{2,1,0:T(8,128)(2,1)} %param.12) | copy-start | bytes 786436
  1.1 27.4 %collective-permute-start.1 = (bf16[64,4096]{1,0:T(8,128)(2,1)S(1)}, bf16[64,4096]{1,0:T(8,128)(2,1)S(1)}, u32[]{:S(2)}, u32[]{:S(2)}) collective-permute-start(bf16[64,4096]{1,0:T(8,128)(2,1)S(1)} %constant_dynamic-slice_fusion), channel_id=1, source_target_pairs={{0,8},{8,0},{4,12},{12,4},{1,9},{9,1},{5,13},{13,5},{2,10},{10,2},... | collective-permute-start | bytes 1572872 | tf_op jit(solution)/shard_map/ppermute | solution.py:233
  5.2 23.5 %collective-permute-start = (bf16[64,4096]{1,0:T(8,128)(2,1)S(1)}, bf16[64,4096]{1,0:T(8,128)(2,1)S(1)}, u32[]{:S(2)}, u32[]{:S(2)}) collective-permute-start(bf16[64,4096]{1,0:T(8,128)(2,1)S(1)} %constant_dynamic-slice_fusion), channel_id=1, source_target_pairs={{0,4},{4,0},{8,12},{12,8},{1,5},{5,1},{9,13},{13,9},{2,6},{6,2},{1... | collective-permute-start | bytes 1572872 | tf_op jit(solution)/shard_map/ppermute | solution.py:233
  6.8 9.5 %collective-permute-start.2 = (bf16[2,64,1024]{2,1,0:T(8,128)(2,1)}, bf16[2,64,1024]{2,1,0:T(8,128)(2,1)S(1)}, u32[]{:S(2)}, u32[]{:S(2)}) collective-permute-start(bf16[2,64,1024]{2,1,0:T(8,128)(2,1)} %param.12), channel_id=1, source_target_pairs={{0,2},{2,0},{1,3},{3,1},{4,6},{6,4},{5,7},{7,5},{8,10},{10,8},{9,1... | collective-permute-start | bytes 786440 | tf_op jit(solution)/shard_map/ppermute | solution.py:230
  9.6 1.0 %copy-start = (bf16[1,64,4096]{2,1,0:T(8,128)(2,1)S(1)}, bf16[1,64,4096]{2,1,0:T(8,128)(2,1)}, u32[]{:S(2)}) copy-start(bf16[1,64,4096]{2,1,0:T(8,128)(2,1)} %param.11) | copy-start | bytes 1572868
  10.6 1.2 %copy-start.1 = (bf16[128,4096]{1,0:T(8,128)(2,1)S(1)}, bf16[128,4096]{1,0:T(8,128)(2,1)}, u32[]{:S(2)}) copy-start(bf16[128,4096]{1,0:T(8,128)(2,1)} %rows_ref.1) | copy-start | bytes 3145732
  28.9 2.4 %collective-permute-start.4 = (bf16[32,4096]{1,0:T(8,128)(2,1)S(1)}, bf16[32,4096]{1,0:T(8,128)(2,1)S(1)}, u32[]{:S(2)}, u32[]{:S(2)}) collective-permute-start(bf16[32,4096]{1,0:T(8,128)(2,1)S(1)} %get-tuple-element.78), channel_id=1, source_target_pairs={{0,1},{1,0},{2,3},{3,2},{4,5},{5,4},{6,7},{7,6},{8,9},{9,8},{10,11... | collective-permute-start | bytes 786440 | tf_op jit(solution)/shard_map/ppermute | solution.py:227
  29.0 8.7 %collective-permute-start.3 = (bf16[32,4096]{1,0:T(8,128)(2,1)S(1)}, bf16[32,4096]{1,0:T(8,128)(2,1)S(1)}, u32[]{:S(2)}, u32[]{:S(2)}) collective-permute-start(bf16[32,4096]{1,0:T(8,128)(2,1)S(1)} %get-tuple-element.78), channel_id=1, source_target_pairs={{0,4},{4,0},{8,12},{12,8},{1,5},{5,1},{9,13},{13,9},{2,6},{6,2},{1... | collective-permute-start | bytes 786440 | tf_op jit(solution)/shard_map/ppermute | solution.py:233
  30.6 1.5 %collective-permute-start.5 = (bf16[32,4096]{1,0:T(8,128)(2,1)S(1)}, bf16[32,4096]{1,0:T(8,128)(2,1)S(1)}, u32[]{:S(2)}, u32[]{:S(2)}) collective-permute-start(bf16[32,4096]{1,0:T(8,128)(2,1)S(1)} %get-tuple-element.45), channel_id=1, source_target_pairs={{0,1},{1,0},{2,3},{3,2},{4,5},{5,4},{6,7},{7,6},{8,9},{9,8},{10,11... | collective-permute-start | bytes 786440 | tf_op jit(solution)/shard_map/ppermute | solution.py:227
  30.8 7.1 %collective-permute-start.8 = (bf16[32,4096]{1,0:T(8,128)(2,1)S(1)}, bf16[32,4096]{1,0:T(8,128)(2,1)S(1)}, u32[]{:S(2)}, u32[]{:S(2)}) collective-permute-start(bf16[32,4096]{1,0:T(8,128)(2,1)S(1)} %get-tuple-element.75), channel_id=1, source_target_pairs={{0,1},{1,0},{2,3},{3,2},{4,5},{5,4},{6,7},{7,6},{8,9},{9,8},{10,11... | collective-permute-start | bytes 786440 | tf_op jit(solution)/shard_map/ppermute | solution.py:227
  31.2 7.2 %collective-permute-start.7 = (bf16[32,4096]{1,0:T(8,128)(2,1)S(1)}, bf16[32,4096]{1,0:T(8,128)(2,1)S(1)}, u32[]{:S(2)}, u32[]{:S(2)}) collective-permute-start(bf16[32,4096]{1,0:T(8,128)(2,1)S(1)} %get-tuple-element.76), channel_id=1, source_target_pairs={{0,1},{1,0},{2,3},{3,2},{4,5},{5,4},{6,7},{7,6},{8,9},{9,8},{10,11... | collective-permute-start | bytes 786440 | tf_op jit(solution)/shard_map/ppermute | solution.py:227
  34.2 8.4 %collective-permute-start.11 = (bf16[128,1024]{1,0:T(8,128)(2,1)S(1)}, bf16[128,1024]{1,0:T(8,128)(2,1)S(1)}, u32[]{:S(2)}, u32[]{:S(2)}) collective-permute-start(bf16[128,1024]{1,0:T(8,128)(2,1)S(1)} %get-tuple-element.49), channel_id=1, source_target_pairs={{0,2},{2,0},{1,3},{3,1},{4,6},{6,4},{5,7},{7,5},{8,10},{10,8},{9,1... | collective-permute-start | bytes 786440 | tf_op jit(solution)/shard_map/ppermute | solution.py:230
  35.7 8.1 %collective-permute-start.6 = (bf16[32,4096]{1,0:T(8,128)(2,1)S(1)}, bf16[32,4096]{1,0:T(8,128)(2,1)S(1)}, u32[]{:S(2)}, u32[]{:S(2)}) collective-permute-start(bf16[32,4096]{1,0:T(8,128)(2,1)S(1)} %get-tuple-element.45), channel_id=1, source_target_pairs={{0,4},{4,0},{8,12},{12,8},{1,5},{5,1},{9,13},{13,9},{2,6},{6,2},{1... | collective-permute-start | bytes 786440 | tf_op jit(solution)/shard_map/ppermute | solution.py:233
  37.8 1.4 %collective-permute-start.10 = (bf16[16,4096]{1,0:T(8,128)(2,1)S(1)}, bf16[16,4096]{1,0:T(8,128)(2,1)S(1)}, u32[]{:S(2)}, u32[]{:S(2)}) collective-permute-start(bf16[16,4096]{1,0:T(8,128)(2,1)S(1)} %get-tuple-element.81), channel_id=1, source_target_pairs={{0,1},{1,0},{2,3},{3,2},{4,5},{5,4},{6,7},{7,6},{8,9},{9,8},{10,11... | collective-permute-start | bytes 393224 | tf_op jit(solution)/shard_map/ppermute | solution.py:227
  37.8 22.2 %copy-start.2 = (bf16[256,1024]{1,0:T(8,128)(2,1)S(1)}, bf16[256,1024]{1,0:T(8,128)(2,1)}, u32[]{:S(2)}) copy-start(bf16[256,1024]{1,0:T(8,128)(2,1)} %residual_ref.1) | copy-start | bytes 1572868
  37.9 1.5 %collective-permute-start.9 = (bf16[16,4096]{1,0:T(8,128)(2,1)S(1)}, bf16[16,4096]{1,0:T(8,128)(2,1)S(1)}, u32[]{:S(2)}, u32[]{:S(2)}) collective-permute-start(bf16[16,4096]{1,0:T(8,128)(2,1)S(1)} %get-tuple-element.82), channel_id=1, source_target_pairs={{0,1},{1,0},{2,3},{3,2},{4,5},{5,4},{6,7},{7,6},{8,9},{9,8},{10,11... | collective-permute-start | bytes 393224 | tf_op jit(solution)/shard_map/ppermute | solution.py:227
  43.9 1.4 %collective-permute-start.13 = (bf16[16,4096]{1,0:T(8,128)(2,1)S(1)}, bf16[16,4096]{1,0:T(8,128)(2,1)S(1)}, u32[]{:S(2)}, u32[]{:S(2)}) collective-permute-start(bf16[16,4096]{1,0:T(8,128)(2,1)S(1)} %get-tuple-element.79), channel_id=1, source_target_pairs={{0,1},{1,0},{2,3},{3,2},{4,5},{5,4},{6,7},{7,6},{8,9},{9,8},{10,11... | collective-permute-start | bytes 393224 | tf_op jit(solution)/shard_map/ppermute | solution.py:227
  43.9 1.5 %collective-permute-start.12 = (bf16[16,4096]{1,0:T(8,128)(2,1)S(1)}, bf16[16,4096]{1,0:T(8,128)(2,1)S(1)}, u32[]{:S(2)}, u32[]{:S(2)}) collective-permute-start(bf16[16,4096]{1,0:T(8,128)(2,1)S(1)} %get-tuple-element.80), channel_id=1, source_target_pairs={{0,1},{1,0},{2,3},{3,2},{4,5},{5,4},{6,7},{7,6},{8,9},{9,8},{10,11... | collective-permute-start | bytes 393224 | tf_op jit(solution)/shard_map/ppermute | solution.py:227
  47.7 5.0 %collective-permute-start.14 = (f32[128,128]{1,0:T(8,128)S(1)}, f32[128,128]{1,0:T(8,128)S(1)}, u32[]{:S(2)}, u32[]{:S(2)}) collective-permute-start(f32[128,128]{1,0:T(8,128)S(1)} %get-tuple-element.59), channel_id=1, source_target_pairs={{0,2},{2,0},{1,3},{3,1},{4,6},{6,4},{5,7},{7,5},{8,10},{10,8},{9,1... | collective-permute-start | bytes 196616 | tf_op jit(solution)/shard_map/ppermute | solution.py:230
  48.8 7.9 %collective-permute-start.16 = (bf16[64,1024]{1,0:T(8,128)(2,1)S(1)}, bf16[64,1024]{1,0:T(8,128)(2,1)S(1)}, u32[]{:S(2)}, u32[]{:S(2)}) collective-permute-start(bf16[64,1024]{1,0:T(8,128)(2,1)S(1)} %get-tuple-element.61), channel_id=1, source_target_pairs={{0,2},{2,0},{1,3},{3,1},{4,6},{6,4},{5,7},{7,5},{8,10},{10,8},{9,1... | collective-permute-start | bytes 393224 | tf_op jit(solution)/shard_map/ppermute | solution.py:230
  49.8 7.9 %collective-permute-start.17 = (bf16[64,1024]{1,0:T(8,128)(2,1)S(1)}, bf16[64,1024]{1,0:T(8,128)(2,1)S(1)}, u32[]{:S(2)}, u32[]{:S(2)}) collective-permute-start(bf16[64,1024]{1,0:T(8,128)(2,1)S(1)} %get-tuple-element.62), channel_id=1, source_target_pairs={{0,2},{2,0},{1,3},{3,1},{4,6},{6,4},{5,7},{7,5},{8,10},{10,8},{9,1... | collective-permute-start | bytes 393224 | tf_op jit(solution)/shard_map/ppermute | solution.py:230
  52.7 4.0 %collective-permute-start.15 = (bf16[128,128]{1,0:T(8,128)(2,1)S(1)}, bf16[128,128]{1,0:T(8,128)(2,1)S(1)}, u32[]{:S(2)}, u32[]{:S(2)}) collective-permute-start(bf16[128,128]{1,0:T(8,128)(2,1)S(1)} %multiply_convert_fusion), channel_id=1, source_target_pairs={{0,4},{4,0},{8,12},{12,8},{1,5},{5,1},{9,13},{13,9},{2,6},{6,2},{1... | collective-permute-start | bytes 98312 | tf_op jit(solution)/shard_map/ppermute | solution.py:233
  57.7 4.8 %collective-permute-start.18 = (bf16[128,128]{1,0:T(8,128)(2,1)S(1)}, bf16[128,128]{1,0:T(8,128)(2,1)S(1)}, u32[]{:S(2)}, u32[]{:S(2)}) collective-permute-start(bf16[128,128]{1,0:T(8,128)(2,1)S(1)} %add.22.scaled_ref), channel_id=1, source_target_pairs={{0,8},{8,0},{4,12},{12,4},{1,9},{9,1},{5,13},{13,5},{2,10},{10,2},... | collective-permute-start | bytes 98312 | tf_op jit(solution)/shard_map/ppermute | solution.py:233

commit v11 on v10

--- a/solution.py
+++ b/solution.py
@@ -100,21 +100,13 @@
     return jnp.concatenate([jnp.where(first, mine, other), jnp.where(first, other, mine)])
 
 
-def low_product(rows, down_ref):
-    return lax.dot_general(
-        rows, down_ref[...], (((1,), (1,)), ((), ())), preferred_element_type=F32
-    )
-
-
 def part(flags_ref, held, value, keep_ref, send_ref, tile):
     home = flags_ref[0] == 1
     keep_ref[:, tile] = jnp.where(home, held, value)
     send_ref[:, tile] = jnp.where(home, value, held).astype(BF16)
 
 
-def own_kernel(
-    weight_ref, down_ref, rows_ref, held_ref, sum_ref, low_ref, sems
-):
+def own_kernel(weight_ref, rows_ref, held_ref, sum_ref, sems):
     tiles = column_tiles(weight_ref.shape[1])
     copies = [
         pltpu.make_async_copy(weight_ref.at[:, tile], held_ref.at[:, tile], sems.at[i])
@@ -123,33 +115,29 @@
     for copy in copies:
         copy.start()
     rows = rows_ref[...]
-    low_ref[...] = low_product(rows, down_ref)
     for copy, tile in zip(copies, tiles):
         copy.wait()
         sum_ref[:, tile] = dot(rows, held_ref[:, tile])
 
 
 def far_kernel(
-    flags_ref, weight_ref, down_ref, held_ref, mine_ref, first_ref, second_ref,
-    keep_ref, send_ref, low_ref,
+    flags_ref, weight_ref, held_ref, mine_ref, first_ref, second_ref, keep_ref, send_ref
 ):
     other = jnp.concatenate([first_ref[...], second_ref[...]])
     rows = joined(flags_ref, mine_ref[...], other)
-    low_ref[...] = low_product(rows, down_ref)
     for tile in column_tiles(weight_ref.shape[1]):
         value = dot(rows, weight_ref[:, tile])
         part(flags_ref, held_ref[:, tile], value, keep_ref, send_ref, tile)
 
 
 def near_kernel(
-    flags_ref, weight_ref, down_ref, mine_ref, first_ref, second_ref, last_ref, third_ref,
-    fourth_ref, keep_ref, send_ref, hold_ref, low_ref,
+    flags_ref, weight_ref, mine_ref, first_ref, second_ref, last_ref, third_ref, fourth_ref,
+    keep_ref, send_ref, hold_ref,
 ):
     other = jnp.concatenate([first_ref[...], second_ref[...]])
-    near = joined(flags_ref, mine_ref[...], other)
+    near = joined(flags_ref, mine_ref[: other.shape[0]], other)
     last = joined(flags_ref, last_ref[...], jnp.concatenate([third_ref[...], fourth_ref[...]]))
     rows = jnp.concatenate([near, last])
-    low_ref[...] = low_product(rows, down_ref)
     step = last_ref.shape[0]
     for tile in column_tiles(weight_ref.shape[1]):
         value = dot(rows, weight_ref[:, tile])
@@ -160,32 +148,32 @@
         )
 
 
-def last_kernel(
-    flags_ref, weight_ref, down_ref, held_ref, own_low, far_low, near_low, mine_ref, first_ref,
-    second_ref, keep_ref, send_ref, low_keep_ref, low_send_ref,
+def low_kernel(
+    flags_ref, down_ref, mine_quarter, group_quarter, core_quarter, both_quarter, rows_ref,
+    mine_ref, first_ref, second_ref, own_mask_ref, far_mask_ref, keep_ref, send_ref,
 ):
     other = jnp.concatenate([first_ref[...], second_ref[...]])
-    rows = joined(flags_ref, mine_ref[...], other)
-    low = low_product(rows, down_ref)
-    block, width = own_low.shape
-    step = mine_ref.shape[0]
-    last_low = jnp.concatenate(
-        [
-            near_low[block : block + step], low[:step],
-            near_low[block + step :], low[step:],
-        ]
-    )
-    odd, home = flags_ref[2] == 1, flags_ref[0] == 1
-    near = own_low[...], near_low[:block]
-    far = far_low[...], last_low
-    for side, here in ((0, slice(0, width)), (1, slice(width, 2 * width))):
-        near_side = jnp.where(odd, near[1 - side], near[side])
-        far_side = jnp.where(odd, far[1 - side], far[side])
-        low_keep_ref[:, here] = jnp.where(home, near_side, far_side)
-        low_send_ref[:, here] = jnp.where(home, far_side, near_side)
-    for tile in column_tiles(weight_ref.shape[1]):
-        value = dot(rows, weight_ref[:, tile])
-        part(flags_ref, held_ref[:, tile], value, keep_ref, send_ref, tile)
+    far = joined(flags_ref, mine_ref[...], other)
+
+    def half(mine, other):
+        first = flags_ref[3] == 0
+        return jnp.concatenate([jnp.where(first, mine, other), jnp.where(first, other, mine)])
+
+    core_half = half(mine_quarter[...], group_quarter[...])
+    other_half = half(core_quarter[...], both_quarter[...])
+    maps = jnp.concatenate([down_ref[...], joined(flags_ref, core_half, other_half)])
+    width = down_ref.shape[0]
+
+    def values(rows, mask_ref):
+        low = lax.dot_general(
+            rows, maps, (((1,), (1,)), ((), ())), preferred_element_type=F32
+        ) * mask_ref[...]
+        return low[:, :width] + low[:, width:]
+
+    own, far = values(rows_ref[...], own_mask_ref), values(far, far_mask_ref)
+    home = flags_ref[0] == 1
+    keep_ref[...] = jnp.where(home, own, far)
+    send_ref[...] = jnp.where(home, far, own)
 
 
 def base_kernel(flags_ref, residual_ref, *refs):
@@ -202,10 +190,10 @@
         out_ref[here, :] = residual_ref[here, :].astype(F32) + base
 
 
-def final_kernel(base_ref, scaled_ref, scaled_got_ref, hot_ref, ups_ref, out_ref):
-    scaled = scaled_ref[...] + scaled_got_ref[...]
-    width = ups_ref.shape[1]
-    scaled = jnp.concatenate([scaled[:, :width], scaled[:, width:]])
+def final_kernel(flags_ref, base_ref, scaled_ref, scaled_got_ref, hot_ref, ups_ref, out_ref):
+    mine, got = scaled_ref[...], scaled_got_ref[...]
+    odd = flags_ref[2] == 1
+    scaled = jnp.concatenate([jnp.where(odd, got, mine), jnp.where(odd, mine, got)])
     lora = dot(scaled * hot_ref[0], ups_ref[0])
     for slot in range(1, ups_ref.shape[0]):
         lora += dot(scaled * hot_ref[slot], ups_ref[slot])
@@ -214,13 +202,14 @@
 
 def line(rows, residual, weight, down, up, tenant, entry, live):
     z, x, c = lax.axis_index("blk"), lax.axis_index("split"), lax.axis_index("sub")
+    y = lax.axis_index("groups")
     block_rows = rows.shape[0]
     width = down.shape[1]
     own, cols = residual.shape
     slots = entry.shape[0]
     home = (z // 2) == x
     odd = z % 2 == 1
-    half, step = block_rows // 2, block_rows // 4
+    half, step, quarter = block_rows // 2, block_rows // 4, width // 4
     barrier = lax.optimization_barrier
 
     def over_core(value):
@@ -239,72 +228,92 @@
     def parted(count):
         return [shape((count, cols), F32), shape((count, cols), BF16)]
 
-    def lows(count):
-        return [shape((count, width), F32)]
-
     slot_all, live_all = tables(tenant, entry, live)
+    flags = jnp.stack([home, c, odd, y]).astype(jnp.int32)
+    kept_place = x * own + (z % 2) * block_rows
+    rank = lax.dynamic_slice_in_dim(live_all, kept_place, block_rows, 0)
+    live_ranks = jnp.arange(width, dtype=jnp.int32)[None, :] < rank[:, None]
+    scale = jnp.where(live_ranks, (width / rank.astype(F32))[:, None], jnp.zeros((), F32))
     slot = lax.dynamic_slice_in_dim(slot_all, x * own, own, 0)
-    rank = lax.dynamic_slice_in_dim(live_all, x * own, own, 0)
-
-    flags = jnp.stack([home, c, odd]).astype(jnp.int32)
-    kept = jnp.arange(width, dtype=jnp.int32)[None, :] < rank[:, None]
-    scale = jnp.where(kept, (width / rank.astype(F32))[:, None], jnp.zeros((), F32))
-    scale = jnp.where((slot == z)[:, None], scale, jnp.zeros((), F32))
-    scale = jnp.concatenate([scale[:block_rows], scale[block_rows:]], axis=1)
     hot = slot[None, :] == jnp.arange(slots, dtype=jnp.int32)[:, None]
     hot = jnp.broadcast_to(hot[:, :, None], (slots, own, width)).astype(BF16)
 
+    def tenant_mask(block):
+        slot = lax.dynamic_slice_in_dim(slot_all, block * block_rows, block_rows, 0)
+        entries = jnp.where(jnp.arange(2 * width) < width, z, z + 1 - 2 * (z % 2))
+        return (slot[:, None] == entries[None, :]).astype(F32)
+
+    masks = [tenant_mask(z), tenant_mask(z + 2 - 4 * (z // 2))]
+
     mine = lax.dynamic_slice_in_dim(rows, c * half, half, 0)
-    near, far = along(mine, NEAR), along(mine, FAR)
+    far = along(mine, FAR)
+    own_ranks = lax.dynamic_slice_in_dim(down[0], (2 * c + y) * quarter, quarter, 0)
+    near = along(jnp.concatenate([mine, own_ranks]), NEAR)
+    held, own_sum = call(
+        own_kernel,
+        [shape(weight.shape, BF16), shape((block_rows, cols), F32)],
+        [HBM, VMEM],
+        [weight, rows],
+        [pltpu.SemaphoreType.DMA((len(column_tiles(cols)),))],
+        FROM_HBM,
+    )
+    up, own_sum = barrier((up, own_sum))
     up_other = over_x(up)
     ups = jnp.where(x == 0, jnp.concatenate([up, up_other]), jnp.concatenate([up_other, up]))
-    held, own_sum, own_low = call(
-        own_kernel,
-        [shape(weight.shape, BF16), shape((block_rows, cols), F32)] + lows(block_rows),
-        [HBM, VMEM, VMEM],
-        [weight, down[0], rows],
-        [pltpu.SemaphoreType.DMA((len(column_tiles(cols)),))],
-        FROM_HBM,
-    )
-    near, far, own_sum, own_low, ups, hot, scale = barrier(
-        (near, far, own_sum, own_low, ups, hot, scale)
+    near, far, own_sum, ups, hot, scale, masks = barrier(
+        (near, far, own_sum, ups, hot, scale, masks)
     )
 
     last = [along(far[:step], NEAR)]
     far_others = over_core_in_two(far)
     far_second, far_others[0] = barrier((far[step:], far_others[0]))
     last.append(along(far_second, NEAR))
-    kept_a, sent_a, far_low = call(
+    kept_a, sent_a = call(
         far_kernel,
-        parted(block_rows) + lows(block_rows),
-        [SMEM] + [VMEM] * 6,
-        [flags, held, down[0], own_sum, far] + far_others,
+        parted(block_rows),
+        [SMEM] + [VMEM] * 5,
+        [flags, held, own_sum, far] + far_others,
     )
     got_a = over_x(sent_a)
-    last[0], kept_a = barrier((last[0], kept_a))
-
-    kept_c, sent_c, hold, near_low = call(
+
+    ranks, far_others[1] = barrier((near[half:], far_others[1]))
+    quarters = [
+        ranks,
+        lax.ppermute(ranks, "groups", SWAP),
+        over_core(ranks),
+        lax.ppermute(ranks, ("groups", "sub"), [(0, 3), (1, 2), (2, 1), (3, 0)]),
+    ]
+    low, low_sent = call(
+        low_kernel,
+        [shape((block_rows, width), F32)] * 2,
+        [SMEM] + [VMEM] * 11,
+        [flags, down[0]] + quarters + [rows, far] + far_others + masks,
+    )
+    low_got = over_x(low_sent)
+    last[0], kept_a, low = barrier((last[0], kept_a, low))
+
+    kept_c, sent_c, hold = call(
         near_kernel,
-        parted(half) + [shape((half, cols), F32)] + lows(block_rows + half),
-        [SMEM] + [VMEM] * 8,
-        [flags, held, down[0], near] + over_core_in_two(near)
+        parted(half) + [shape((half, cols), F32)],
+        [SMEM] + [VMEM] * 7,
+        [flags, held, near] + over_core_in_two(near[:half])
         + [last[0]] + over_core_in_two(last[0]),
     )
     got_c = over_x(sent_c)
-    last[1], hold, got_a, near_low = barrier((last[1], hold, got_a, near_low))
-
-    kept_d, sent_d, low, low_sent = call(
-        last_kernel,
-        parted(half) + [shape((block_rows, 2 * width), F32)] * 2,
-        [SMEM] + [VMEM] * 9,
-        [flags, held, down[0], hold, own_low, far_low, near_low, last[1]]
-        + over_core_in_two(last[1]),
-    )
+    last[1], hold, got_a, low, low_got = barrier((last[1], hold, got_a, low, low_got))
+
+    scaled = ((low + low_got) * scale).astype(BF16)
+    scaled_got = along(scaled, FAR)
+    kept_d, sent_d = call(
+        far_kernel,
+        parted(half),
+        [SMEM] + [VMEM] * 5,
+        [flags, held, hold, last[1]] + over_core_in_two(last[1]),
+    )
+    scaled_got, sent_d = barrier((scaled_got, sent_d))
+    scaled = scaled + scaled_got
     got_d = over_x(sent_d)
-
-    scaled = ((low + over_x(low_sent)) * scale).astype(BF16)
-    scaled = scaled + along(scaled, NEAR)
-    scaled, got_c, got_d = barrier((scaled, got_c, got_d))
+    scaled_got = along(scaled, NEAR)
     base = call(
         base_kernel,
         shape(residual.shape, F32),
@@ -314,14 +323,14 @@
     return call(
         final_kernel,
         shape(residual.shape, BF16),
-        [VMEM] * 5,
-        [base, scaled, along(scaled, FAR), hot, ups],
+        [SMEM] + [VMEM] * 5,
+        [flags, base, scaled, scaled_got, hot, ups],
     )
 
 
 def shards(rows, residual, weight, down, up, tenant, entry, live):
-    sizes = [lax.axis_size(name) for name in ("blk", "split", "sub")]
-    plan = line if sizes == [4, 2, 2] and down.shape[0] == 1 else general
+    sizes = [lax.axis_size(name) for name in ("groups", "blk", "split", "sub")]
+    plan = line if sizes == [2, 4, 2, 2] and down.shape[0] == 1 else general
     return plan(rows, residual, weight, down, up, tenant, entry, live)
 
 

time: 64.3 us -> 68.5 us (1.065)
  local copies, waits for them, and re-layouts: 3.71 us -> 10.8 us
  waiting for transfers between devices: 26.1 us -> 19.7 us
  other arithmetic: 1.38 us -> 2.88 us
  Pallas kernels: 13.7 us -> 14.8 us
  starting transfers between devices: 19 us -> 19.9 us
    ppermute x6, waiting for transfers between devices: 19.9 us -> 7.49 us  [along(): return lax.ppermute(value, 'blk', pairs)]
    ppermute x5, waiting for transfers between devices: 3.37 us -> 10.6 us  [over_x(): return lax.ppermute(value, 'split', SWAP)]
    unnamed x8 -> x24, local copies, waits for them, and re-layouts: 2.28 us -> 7.49 us
    ppermute x0 -> x2, starting transfers between devices: none -> 1.77 us  [the longest x1 1.31 us: line(): lax.ppermute(ranks, ('groups', 'sub'), [(0, 3), (1, 2), (2, 1), (3, 0)])]
    select_n x1, other arithmetic: 0.08 us -> 1.4 us  [line(): jnp.where(x == 0, jnp.concatenate([up, up_other]), jnp.concatenate([up_ot...]
    ppermute x6, starting transfers between devices: 10.9 us -> 9.65 us  [along(): return lax.ppermute(value, 'blk', pairs)]
    ppermute x8 -> x9, waiting for transfers between devices: 2.8 us -> 1.63 us  [over_core(): return lax.ppermute(value, 'sub', SWAP)]
    pallas_call x6 -> x7, Pallas kernels: 13.7 us -> 14.8 us  [call(): pl.pallas_call(kernel, out_shape=outs, in_specs=in_specs, out_specs=jax.t...]
  transfers between devices with their start and end apart: 19 -> 22, of which waited for: 14 -> 9; matrix products, arithmetic and copies ran while one was open for 2% -> 6% of each run, Pallas kernels for 16% -> 19%
where the time goes in v11:
time: 68.5 us; the launch traced here: 68.3 us
  starting transfers between devices  19.9 us (29%)
  waiting for transfers between devices  19.7 us (29%)
  Pallas kernels  14.8 us (22%)
  local copies, waits for them, and re-layouts  10.8 us (16%)
  other arithmetic  2.88 us (4%)
    pallas_call x7, Pallas kernels, call(): pl.pallas_call(kernel, out_shape=outs, in_specs=in_specs, out_specs=jax.t...  14.8 us
    ppermute x5, waiting for transfers between devices, over_x(): return lax.ppermute(value, 'split', SWAP)  10.6 us
    ppermute x6, starting transfers between devices, along(): return lax.ppermute(value, 'blk', pairs)  9.65 us
    ppermute x6, waiting for transfers between devices, along(): return lax.ppermute(value, 'blk', pairs)  7.49 us
    unnamed x24, local copies, waits for them, and re-layouts  7.49 us
    ppermute x5, starting transfers between devices, over_x(): return lax.ppermute(value, 'split', SWAP)  5.85 us
    ppermute x9, starting transfers between devices, over_core(): return lax.ppermute(value, 'sub', SWAP)  2.64 us
    ppermute x9, waiting for transfers between devices, over_core(): return lax.ppermute(value, 'sub', SWAP)  1.63 us
  transfers between devices with their start and end apart: 22, of which 9 were waited for; matrix products, arithmetic and copies ran while one was open for 6% of the time, Pallas kernels for 19%

profile of v11, /device:TPU:0, one launch (start us, length us, event | category | flops | bytes accessed | tf_op | source)
XLA Modules:
  0.0 68.3 jit_solution(6635124922506786113)
XLA Ops:
  0.0 1.2 %constant_dynamic-slice_fusion = bf16[64,4096]{1,0:T(8,128)(2,1)S(1)} fusion(bf16[128,4096]{1,0:T(8,128)(2,1)} %rows_ref.3, s32[]{:T(128)S(6)} %select_n.59), kind=kLoop, calls=%fused_computation.16 | loop fusion | bytes 1048580 | tf_op jit(solution)/shard_map/dynamic_slice | solution.py:248
  1.2 4.1 %collective-permute-start.1 = (bf16[64,4096]{1,0:T(8,128)(2,1)S(1)}, bf16[64,4096]{1,0:T(8,128)(2,1)S(1)}, u32[]{:S(2)}, u32[]{:S(2)}) collective-permute-start(bf16[64,4096]{1,0:T(8,128)(2,1)S(1)} %constant_dynamic-slice_fusion), channel_id=1, source_target_pairs={{0,8},{8,0},{4,12},{12,4},{1,9},{9,1},{5,13},{13,5},{2,10},{10,2},... | collective-permute-start | bytes 1572872 | tf_op jit(solution)/shard_map/ppermute | solution.py:222
  5.3 0.9 %dynamic-slice_bitcast_fusion = bf16[16,4096]{1,0:T(8,128)(2,1)S(1)} fusion(bf16[1,64,4096]{2,1,0:T(8,128)(2,1)} %param.11, s32[]{:T(128)S(6)} %select_n.60), kind=kLoop, calls=%fused_computation.2 | loop fusion | bytes 262148 | tf_op jit(solution)/shard_map/dynamic_slice | solution.py:250
  6.2 0.9 %pad_maximum_fusion = bf16[80,4096]{1,0:T(8,128)(2,1)} fusion(bf16[16,4096]{1,0:T(8,128)(2,1)S(1)} %dynamic-slice_bitcast_fusion, bf16[64,4096]{1,0:T(8,128)(2,1)S(1)} %constant_dynamic-slice_fusion), kind=kLoop, calls=%fused_computation | loop fusion | flops 1310720 | bytes 1310720 | tf_op jit(solution)/shard_map/concatenate | solution.py:251
  7.1 1.6 %collective-permute-start = (bf16[80,4096]{1,0:T(8,128)(2,1)}, bf16[80,4096]{1,0:T(8,128)(2,1)S(1)}, u32[]{:S(2)}, u32[]{:S(2)}) collective-permute-start(bf16[80,4096]{1,0:T(8,128)(2,1)} %pad_maximum_fusion), channel_id=1, source_target_pairs={{0,4},{4,0},{8,12},{12,8},{1,5},{5,1},{9,13},{13,9},{2,6},{6,2},{1... | collective-permute-start | bytes 1966088 | tf_op jit(solution)/shard_map/ppermute | solution.py:222
  8.8 4.4 %shard_map.82 = (bf16[4096,1024]{1,0:T(8,128)(2,1)S(1)}, f32[128,1024]{1,0:T(8,128)S(1)}) custom-call(bf16[4096,1024]{1,0:T(8,128)(2,1)} %weight_ref.1, bf16[128,4096]{1,0:T(8,128)(2,1)S(1)} %copy-done.3), custom_call_target="tpu_custom_call" | custom-call | tf_op jit(solution)/shard_map/pallas_call | solution.py:82
  13.2 3.3 %copy-done = bf16[4096,1024]{1,0:T(8,128)(2,1)} copy-done((bf16[4096,1024]{1,0:T(8,128)(2,1)}, bf16[4096,1024]{1,0:T(8,128)(2,1)S(1)}, u32[]{:S(2)}) %copy-start) | copy-done | bytes 8388632
  16.5 0.8 %copy-done.5 = f32[128,1024]{1,0:T(8,128)} copy-done((f32[128,1024]{1,0:T(8,128)}, f32[128,1024]{1,0:T(8,128)S(1)}, u32[]{:S(2)}) %copy-start.5) | copy-done | bytes 524312
  17.2 1.5 %collective-permute-start.2 = (bf16[2,64,1024]{2,1,0:T(8,128)(2,1)S(1)}, bf16[2,64,1024]{2,1,0:T(8,128)(2,1)}, u32[]{:S(2)}, u32[]{:S(2)}) collective-permute-start(bf16[2,64,1024]{2,1,0:T(8,128)(2,1)S(1)} %copy-done.8), channel_id=1, source_target_pairs={{0,2},{2,0},{1,3},{3,1},{4,6},{6,4},{5,7},{7,5},{8,10},{10,8},{9,1... | collective-permute-start | bytes 786440 | tf_op jit(solution)/shard_map/ppermute | solution.py:219
  18.7 0.1 select_reduce_fusion
  18.8 0.1 convert_divide_fusion
  18.9 0.1 dynamic_slice.23
  19.0 0.1 fusion
  19.1 0.1 fusion.6
  19.2 0.1 compare_convert_fusion
  19.3 5.5 %collective-permute-done.2 = bf16[2,64,1024]{2,1,0:T(8,128)(2,1)} collective-permute-done((bf16[2,64,1024]{2,1,0:T(8,128)(2,1)S(1)}, bf16[2,64,1024]{2,1,0:T(8,128)(2,1)}, u32[]{:S(2)}, u32[]{:S(2)}) %collective-permute-start.2) | collective-permute-done | bytes 262176 | tf_op jit(solution)/shard_map/ppermute | solution.py:219
  24.8 1.4 %maximum_select_fusion.ups_ref = bf16[4,64,1024]{2,1,0:T(8,128)(2,1)S(1)} fusion(bf16[2,64,1024]{2,1,0:T(8,128)(2,1)} %collective-permute-done.2, bf16[2,64,1024]{2,1,0:T(8,128)(2,1)} %param.12, pred[]{:T(512)S(6)} %eq.70), kind=kLoop, calls=%fused_computation.1 | loop fusion | flops 786432 | bytes 1048577 | tf_op jit(solution)/shard_map/jit(_where)/select_n | solution.py:262
  26.2 2.3 %collective-permute-done.1.mine_ref = bf16[64,4096]{1,0:T(8,128)(2,1)S(1)} collective-permute-done((bf16[64,4096]{1,0:T(8,128)(2,1)S(1)}, bf16[64,4096]{1,0:T(8,128)(2,1)S(1)}, u32[]{:S(2)}, u32[]{:S(2)}) %collective-permute-start.1) | collective-permute-done | bytes 524320 | tf_op jit(solution)/shard_map/ppermute | solution.py:222
  28.5 5.1 %collective-permute-done.mine_ref = bf16[80,4096]{1,0:T(8,128)(2,1)S(1)} collective-permute-done((bf16[80,4096]{1,0:T(8,128)(2,1)}, bf16[80,4096]{1,0:T(8,128)(2,1)S(1)}, u32[]{:S(2)}, u32[]{:S(2)}) %collective-permute-start) | collective-permute-done | bytes 655392 | tf_op jit(solution)/shard_map/ppermute | solution.py:222
  33.7 0.2 broadcast_in_dim.22.hot_ref
  33.9 0.9 %fusion.3 = (bf16[32,4096]{1,0:T(8,128)(2,1)}, bf16[32,4096]{1,0:T(8,128)(2,1)}) fusion(bf16[64,4096]{1,0:T(8,128)(2,1)S(1)} %collective-permute-done.1.mine_ref), kind=kLoop, calls=%fused_computation.18 | loop fusion | bytes 1048576 | tf_op jit(solution)/shard_map/slice | solution.py:269
  34.7 0.1 pad_add_fusion.flags_ref
  34.8 0.5 collective-permute-start.4
  35.3 1.1 %collective-permute-done.5.second_ref = bf16[32,4096]{1,0:T(8,128)(2,1)S(1)} collective-permute-done((bf16[32,4096]{1,0:T(8,128)(2,1)}, bf16[32,4096]{1,0:T(8,128)(2,1)S(1)}, u32[]{:S(2)}, u32[]{:S(2)}) %collective-permute-start.5) | collective-permute-done | bytes 262176 | tf_op jit(solution)/shard_map/ppermute | solution.py:216
  36.5 1.3 %collective-permute-start.8 = (bf16[16,4096]{1,0:T(8,128)(2,1)S(1)}, bf16[16,4096]{1,0:T(8,128)(2,1)S(1)}, u32[]{:S(2)}, u32[]{:S(2)}) collective-permute-start(bf16[16,4096]{1,0:T(8,128)(2,1)S(1)} %slice.34.mine_quarter), channel_id=1, source_target_pairs={{0,17},{1,16},{16,1},{17,0},{2,19},{3,18},{18,3},{19,2},{4,21},{5,... | collective-permute-start | bytes 393224 | tf_op jit(solution)/shard_map/ppermute | solution.py:284
  37.8 0.4 collective-permute-start.7
  38.2 0.5 collective-permute-start.6
  38.8 3.4 %copy-done.1 = bf16[4096,1024]{1,0:T(8,128)(2,1)S(1)} copy-done((bf16[4096,1024]{1,0:T(8,128)(2,1)S(1)}, bf16[4096,1024]{1,0:T(8,128)(2,1)}, u32[]{:S(2)}) %copy-start.1) | copy-done | bytes 8388632
  42.1 1.8 %shard_map.83 = (f32[128,1024]{1,0:T(8,128)S(1)}, bf16[128,1024]{1,0:T(8,128)(2,1)S(1)}) custom-call(s32[4]{0:T(128)S(1)} %pad_add_fusion.flags_ref, bf16[4096,1024]{1,0:T(8,128)(2,1)S(1)} %copy-done.1, f32[128,1024]{1,0:T(8,128)S(1)} %copy-done.6, bf16[64,4096]{1,0:T(8,128)(2,1)S(1)} %collective-permute-done.1.mine_ref, ...), custom_call_target="tpu_custom_call" | custom-call | tf_op jit(solution)/shard_map/pallas_call | solution.py:82
  44.0 0.6 collective-permute-start.10
  44.5 1.5 %collective-permute-start.14 = (bf16[128,1024]{1,0:T(8,128)(2,1)S(1)}, bf16[128,1024]{1,0:T(8,128)(2,1)S(1)}, u32[]{:S(2)}, u32[]{:S(2)}) collective-permute-start(bf16[128,1024]{1,0:T(8,128)(2,1)S(1)} %get-tuple-element.58), channel_id=1, source_target_pairs={{0,2},{2,0},{1,3},{3,1},{4,6},{6,4},{5,7},{7,5},{8,10},{10,8},{9,1... | collective-permute-start | bytes 786440 | tf_op jit(solution)/shard_map/ppermute | solution.py:219
  46.1 1.0 %collective-permute-start.9 = (bf16[32,4096]{1,0:T(8,128)(2,1)}, bf16[32,4096]{1,0:T(8,128)(2,1)S(1)}, u32[]{:S(2)}, u32[]{:S(2)}) collective-permute-start(bf16[32,4096]{1,0:T(8,128)(2,1)} %get-tuple-element.55), channel_id=1, source_target_pairs={{0,4},{4,0},{8,12},{12,8},{1,5},{5,1},{9,13},{13,9},{2,6},{6,2},{1... | collective-permute-start | bytes 786440 | tf_op jit(solution)/shard_map/ppermute | solution.py:222
  47.0 1.3 %shard_map.84 = (f32[128,64]{1,0:T(8,128)S(1)}, f32[128,64]{1,0:T(8,128)S(1)}) custom-call(s32[4]{0:T(128)S(1)} %pad_add_fusion.flags_ref, bf16[64,4096]{1,0:T(8,128)(2,1)S(1)} %bitcast.7, bf16[16,4096]{1,0:T(8,128)(2,1)S(1)} %slice.34.mine_quarter, bf16[16,4096]{1,0:T(8,128)(2,1)S(1)} %collective-permute-done.6.group_quarter, ...), custom_call_target="tpu_custom_call" | custom-call | tf_op jit(solution)/shard_map/pallas_call | solution.py:82
  48.5 0.5 collective-permute-start.12
  49.0 0.5 collective-permute-start.15
  49.5 0.3 collective-permute-done.13.fourth_ref
  49.8 0.2 collective-permute-done.12.third_ref
  50.0 2.4 %shard_map.85 = (f32[64,1024]{1,0:T(8,128)S(1)}, bf16[64,1024]{1,0:T(8,128)(2,1)S(1)}, f32[64,1024]{1,0:T(8,128)S(1)}) custom-call(s32[4]{0:T(128)S(1)} %pad_add_fusion.flags_ref, bf16[4096,1024]{1,0:T(8,128)(2,1)S(1)} %copy-done.2, bf16[80,4096]{1,0:T(8,128)(2,1)S(1)} %collective-permute-done.mine_ref, ...), custom_call_target="tpu_custom_call" | custom-call | tf_op jit(solution)/shard_map/pallas_call | solution.py:82
  52.4 1.8 %collective-permute-done.15 = f32[128,64]{1,0:T(8,128)S(1)} collective-permute-done((f32[128,64]{1,0:T(8,128)S(1)}, f32[128,64]{1,0:T(8,128)S(1)}, u32[]{:S(2)}, u32[]{:S(2)}) %collective-permute-start.15) | collective-permute-done | bytes 32800 | tf_op jit(solution)/shard_map/ppermute | solution.py:219
  54.4 0.5 collective-permute-start.17
  54.9 1.9 %collective-permute-start.19 = (bf16[128,64]{1,0:T(8,128)(2,1)S(1)}, bf16[128,64]{1,0:T(8,128)(2,1)S(1)}, u32[]{:S(2)}, u32[]{:S(2)}) collective-permute-start(bf16[128,64]{1,0:T(8,128)(2,1)S(1)} %multiply_convert_fusion), channel_id=1, source_target_pairs={{0,8},{8,0},{4,12},{12,4},{1,9},{9,1},{5,13},{13,5},{2,10},{10,2},... | collective-permute-start | bytes 49160 | tf_op jit(solution)/shard_map/ppermute | solution.py:222
  56.9 1.5 %collective-permute-start.16 = (bf16[64,1024]{1,0:T(8,128)(2,1)S(1)}, bf16[64,1024]{1,0:T(8,128)(2,1)S(1)}, u32[]{:S(2)}, u32[]{:S(2)}) collective-permute-start(bf16[64,1024]{1,0:T(8,128)(2,1)S(1)} %get-tuple-element.63), channel_id=1, source_target_pairs={{0,2},{2,0},{1,3},{3,1},{4,6},{6,4},{5,7},{7,5},{8,10},{10,8},{9,1... | collective-permute-start | bytes 393224 | tf_op jit(solution)/shard_map/ppermute | solution.py:219
  58.3 2.1 %shard_map.86 = (f32[64,1024]{1,0:T(8,128)S(1)}, bf16[64,1024]{1,0:T(8,128)(2,1)S(1)}) custom-call(s32[4]{0:T(128)S(1)} %pad_add_fusion.flags_ref, bf16[4096,1024]{1,0:T(8,128)(2,1)S(1)} %copy-done.2, f32[64,1024]{1,0:T(8,128)S(1)} %get-tuple-element.64.held_ref, bf16[32,4096]{1,0:T(8,128)(2,1)S(1)} %collective-permute-done.9.mine_ref, ...), custom_call_target="tpu_custom_call" | custom-call | tf_op jit(solution)/shard_map/pallas_call | solution.py:82
  60.5 0.8 %collective-permute-start.20 = (bf16[64,1024]{1,0:T(8,128)(2,1)S(1)}, bf16[64,1024]{1,0:T(8,128)(2,1)S(1)}, u32[]{:S(2)}, u32[]{:S(2)}) collective-permute-start(bf16[64,1024]{1,0:T(8,128)(2,1)S(1)} %get-tuple-element.71), channel_id=1, source_target_pairs={{0,2},{2,0},{1,3},{3,1},{4,6},{6,4},{5,7},{7,5},{8,10},{10,8},{9,1... | collective-permute-start | bytes 393224 | tf_op jit(solution)/shard_map/ppermute | solution.py:219
  61.3 1.0 %collective-permute-start.21 = (bf16[128,64]{1,0:T(8,128)(2,1)S(1)}, bf16[128,64]{1,0:T(8,128)(2,1)S(1)}, u32[]{:S(2)}, u32[]{:S(2)}) collective-permute-start(bf16[128,64]{1,0:T(8,128)(2,1)S(1)} %add.57.scaled_ref), channel_id=1, source_target_pairs={{0,4},{4,0},{8,12},{12,8},{1,5},{5,1},{9,13},{13,9},{2,6},{6,2},{1... | collective-permute-start | bytes 49160 | tf_op jit(solution)/shard_map/ppermute | solution.py:222
  62.3 3.2 %collective-permute-done.20.refs_5_ = bf16[64,1024]{1,0:T(8,128)(2,1)S(1)} collective-permute-done((bf16[64,1024]{1,0:T(8,128)(2,1)S(1)}, bf16[64,1024]{1,0:T(8,128)(2,1)S(1)}, u32[]{:S(2)}, u32[]{:S(2)}) %collective-permute-start.20) | collective-permute-done | bytes 131104 | tf_op jit(solution)/shard_map/ppermute | solution.py:219
  65.5 0.7 %shard_map.87.base_ref = f32[256,1024]{1,0:T(8,128)S(1)} custom-call(s32[4]{0:T(128)S(1)} %pad_add_fusion.flags_ref, bf16[256,1024]{1,0:T(8,128)(2,1)S(1)} %copy-done.7, f32[128,1024]{1,0:T(8,128)S(1)} %get-tuple-element.54.refs_0_, bf16[128,1024]{1,0:T(8,128)(2,1)S(1)} %collective-permute-done.14.refs_1_, f32[64,1024]{1,0:T(8,128)S(1)} %get-tuple-element.62.refs_2_, ...), custom_call_target="tpu_custom_call" | custom-call | tf_op jit(solution)/shard_map/pallas_call | solution.py:82
  66.3 2.0 %shard_map.88 = bf16[256,1024]{1,0:T(8,128)(2,1)} custom-call(s32[4]{0:T(128)S(1)} %pad_add_fusion.flags_ref, f32[256,1024]{1,0:T(8,128)S(1)} %shard_map.87.base_ref, bf16[128,64]{1,0:T(8,128)(2,1)S(1)} %add.57.scaled_ref, bf16[128,64]{1,0:T(8,128)(2,1)S(1)} %collective-permute-done.21.scaled_got_ref, bf16[4,256,64]{2,1,0:T(8,128)(2,1)S(1)} %broadcast_in_dim.22.hot_ref, ...), custom_call_target="tpu_custom_call" | custom-call | tf_op jit(solution)/shard_map/pallas_call | solution.py:82
  (47 shorter events, 0.5 us)
Async XLA Ops:
  0.0 8.8 %copy-start.3 = (bf16[128,4096]{1,0:T(8,128)(2,1)S(1)}, bf16[128,4096]{1,0:T(8,128)(2,1)}, u32[]{:S(2)}) copy-start(bf16[128,4096]{1,0:T(8,128)(2,1)} %rows_ref.3) | copy-start | bytes 3145732
  1.2 27.4 %collective-permute-start.1 = (bf16[64,4096]{1,0:T(8,128)(2,1)S(1)}, bf16[64,4096]{1,0:T(8,128)(2,1)S(1)}, u32[]{:S(2)}, u32[]{:S(2)}) collective-permute-start(bf16[64,4096]{1,0:T(8,128)(2,1)S(1)} %constant_dynamic-slice_fusion), channel_id=1, source_target_pairs={{0,8},{8,0},{4,12},{12,4},{1,9},{9,1},{5,13},{13,5},{2,10},{10,2},... | collective-permute-start | bytes 1572872 | tf_op jit(solution)/shard_map/ppermute | solution.py:222
  7.1 10.1 %copy-start.8 = (bf16[2,64,1024]{2,1,0:T(8,128)(2,1)S(1)}, bf16[2,64,1024]{2,1,0:T(8,128)(2,1)}, u32[]{:S(2)}) copy-start(bf16[2,64,1024]{2,1,0:T(8,128)(2,1)} %param.12) | copy-start | bytes 786436
  7.1 11.6 %copy-start.9 = (s32[512]{0:T(512)S(1)}, s32[512]{0:T(512)}, u32[]{:S(2)}) copy-start(s32[512]{0:T(512)} %param.13) | copy-start | bytes 6148
  7.1 11.6 %copy-start.10 = (s32[4]{0:T(128)S(1)}, s32[4]{0:T(128)}, u32[]{:S(2)}) copy-start(s32[4]{0:T(128)} %param.15) | copy-start | bytes 52
  7.1 11.6 %copy-start.11 = (s32[4]{0:T(128)S(1)}, s32[4]{0:T(128)}, u32[]{:S(2)}) copy-start(s32[4]{0:T(128)} %param.14) | copy-start | bytes 52
  7.1 26.5 %collective-permute-start = (bf16[80,4096]{1,0:T(8,128)(2,1)}, bf16[80,4096]{1,0:T(8,128)(2,1)S(1)}, u32[]{:S(2)}, u32[]{:S(2)}) collective-permute-start(bf16[80,4096]{1,0:T(8,128)(2,1)} %pad_maximum_fusion), channel_id=1, source_target_pairs={{0,4},{4,0},{8,12},{12,8},{1,5},{5,1},{9,13},{13,9},{2,6},{6,2},{1... | collective-permute-start | bytes 1966088 | tf_op jit(solution)/shard_map/ppermute | solution.py:222
  13.2 3.3 %copy-start = (bf16[4096,1024]{1,0:T(8,128)(2,1)}, bf16[4096,1024]{1,0:T(8,128)(2,1)S(1)}, u32[]{:S(2)}) copy-start(bf16[4096,1024]{1,0:T(8,128)(2,1)S(1)} %get-tuple-element.44.weight_ref) | copy-start | bytes 25165828
  16.4 0.8 %copy-start.5 = (f32[128,1024]{1,0:T(8,128)}, f32[128,1024]{1,0:T(8,128)S(1)}, u32[]{:S(2)}) copy-start(f32[128,1024]{1,0:T(8,128)S(1)} %get-tuple-element.45.held_ref) | copy-start | bytes 1572868
  17.2 7.6 %collective-permute-start.2 = (bf16[2,64,1024]{2,1,0:T(8,128)(2,1)S(1)}, bf16[2,64,1024]{2,1,0:T(8,128)(2,1)}, u32[]{:S(2)}, u32[]{:S(2)}) collective-permute-start(bf16[2,64,1024]{2,1,0:T(8,128)(2,1)S(1)} %copy-done.8), channel_id=1, source_target_pairs={{0,2},{2,0},{1,3},{3,1},{4,6},{6,4},{5,7},{7,5},{8,10},{10,8},{9,1... | collective-permute-start | bytes 786440 | tf_op jit(solution)/shard_map/ppermute | solution.py:219
  34.7 1.7 %collective-permute-start.5 = (bf16[32,4096]{1,0:T(8,128)(2,1)}, bf16[32,4096]{1,0:T(8,128)(2,1)S(1)}, u32[]{:S(2)}, u32[]{:S(2)}) collective-permute-start(bf16[32,4096]{1,0:T(8,128)(2,1)} %get-tuple-element.55), channel_id=1, source_target_pairs={{0,1},{1,0},{2,3},{3,2},{4,5},{5,4},{6,7},{7,6},{8,9},{9,8},{10,11... | collective-permute-start | bytes 786440 | tf_op jit(solution)/shard_map/ppermute | solution.py:216
  34.7 4.0 %copy-start.6 = (f32[128,1024]{1,0:T(8,128)S(1)}, f32[128,1024]{1,0:T(8,128)}, u32[]{:S(2)}) copy-start(f32[128,1024]{1,0:T(8,128)} %copy-done.5) | copy-start | bytes 1572868
  34.8 3.8 %collective-permute-start.4 = (bf16[32,4096]{1,0:T(8,128)(2,1)}, bf16[32,4096]{1,0:T(8,128)(2,1)S(1)}, u32[]{:S(2)}, u32[]{:S(2)}) collective-permute-start(bf16[32,4096]{1,0:T(8,128)(2,1)} %get-tuple-element.82), channel_id=1, source_target_pairs={{0,1},{1,0},{2,3},{3,2},{4,5},{5,4},{6,7},{7,6},{8,9},{9,8},{10,11... | collective-permute-start | bytes 786440 | tf_op jit(solution)/shard_map/ppermute | solution.py:216
  35.3 13.0 %collective-permute-start.3 = (bf16[32,4096]{1,0:T(8,128)(2,1)}, bf16[32,4096]{1,0:T(8,128)(2,1)S(1)}, u32[]{:S(2)}, u32[]{:S(2)}) collective-permute-start(bf16[32,4096]{1,0:T(8,128)(2,1)} %get-tuple-element.82), channel_id=1, source_target_pairs={{0,4},{4,0},{8,12},{12,8},{1,5},{5,1},{9,13},{13,9},{2,6},{6,2},{1... | collective-permute-start | bytes 786440 | tf_op jit(solution)/shard_map/ppermute | solution.py:222
  36.5 7.5 %collective-permute-start.8 = (bf16[16,4096]{1,0:T(8,128)(2,1)S(1)}, bf16[16,4096]{1,0:T(8,128)(2,1)S(1)}, u32[]{:S(2)}, u32[]{:S(2)}) collective-permute-start(bf16[16,4096]{1,0:T(8,128)(2,1)S(1)} %slice.34.mine_quarter), channel_id=1, source_target_pairs={{0,17},{1,16},{16,1},{17,0},{2,19},{3,18},{18,3},{19,2},{4,21},{5,... | collective-permute-start | bytes 393224 | tf_op jit(solution)/shard_map/ppermute | solution.py:284
  37.8 6.8 %collective-permute-start.7 = (bf16[16,4096]{1,0:T(8,128)(2,1)S(1)}, bf16[16,4096]{1,0:T(8,128)(2,1)S(1)}, u32[]{:S(2)}, u32[]{:S(2)}) collective-permute-start(bf16[16,4096]{1,0:T(8,128)(2,1)S(1)} %slice.34.mine_quarter), channel_id=1, source_target_pairs={{0,1},{1,0},{2,3},{3,2},{4,5},{5,4},{6,7},{7,6},{8,9},{9,8},{10,11... | collective-permute-start | bytes 393224 | tf_op jit(solution)/shard_map/ppermute | solution.py:216
  38.2 7.9 %collective-permute-start.6 = (bf16[16,4096]{1,0:T(8,128)(2,1)S(1)}, bf16[16,4096]{1,0:T(8,128)(2,1)S(1)}, u32[]{:S(2)}, u32[]{:S(2)}) collective-permute-start(bf16[16,4096]{1,0:T(8,128)(2,1)S(1)} %slice.34.mine_quarter), channel_id=1, source_target_pairs={{0,16},{16,0},{1,17},{17,1},{2,18},{18,2},{3,19},{19,3},{4,20},{20... | collective-permute-start | bytes 393224 | tf_op jit(solution)/shard_map/ppermute | solution.py:282
  38.7 9.8 %collective-permute-start.11 = (bf16[32,4096]{1,0:T(8,128)(2,1)S(1)}, bf16[32,4096]{1,0:T(8,128)(2,1)S(1)}, u32[]{:S(2)}, u32[]{:S(2)}) collective-permute-start(bf16[32,4096]{1,0:T(8,128)(2,1)S(1)} %get-tuple-element.79), channel_id=1, source_target_pairs={{0,1},{1,0},{2,3},{3,2},{4,5},{5,4},{6,7},{7,6},{8,9},{9,8},{10,11... | collective-permute-start | bytes 786440 | tf_op jit(solution)/shard_map/ppermute | solution.py:216
  38.8 3.4 %copy-start.1 = (bf16[4096,1024]{1,0:T(8,128)(2,1)S(1)}, bf16[4096,1024]{1,0:T(8,128)(2,1)}, u32[]{:S(2)}) copy-start(bf16[4096,1024]{1,0:T(8,128)(2,1)} %copy-done) | copy-start | bytes 25165828
  42.1 4.9 %copy-start.4 = (bf16[1,64,4096]{2,1,0:T(8,128)(2,1)S(1)}, bf16[1,64,4096]{2,1,0:T(8,128)(2,1)}, u32[]{:S(2)}) copy-start(bf16[1,64,4096]{2,1,0:T(8,128)(2,1)} %param.11) | copy-start | bytes 1572868
  42.1 7.9 %copy-start.2 = (bf16[4096,1024]{1,0:T(8,128)(2,1)S(1)}, bf16[4096,1024]{1,0:T(8,128)(2,1)}, u32[]{:S(2)}) copy-start(bf16[4096,1024]{1,0:T(8,128)(2,1)} %copy-done) | copy-start | bytes 25165828
  44.0 5.0 %collective-permute-start.10 = (bf16[32,4096]{1,0:T(8,128)(2,1)S(1)}, bf16[32,4096]{1,0:T(8,128)(2,1)S(1)}, u32[]{:S(2)}, u32[]{:S(2)}) collective-permute-start(bf16[32,4096]{1,0:T(8,128)(2,1)S(1)} %get-tuple-element.80), channel_id=1, source_target_pairs={{0,1},{1,0},{2,3},{3,2},{4,5},{5,4},{6,7},{7,6},{8,9},{9,8},{10,11... | collective-permute-start | bytes 786440 | tf_op jit(solution)/shard_map/ppermute | solution.py:216
  44.5 9.7 %collective-permute-start.14 = (bf16[128,1024]{1,0:T(8,128)(2,1)S(1)}, bf16[128,1024]{1,0:T(8,128)(2,1)S(1)}, u32[]{:S(2)}, u32[]{:S(2)}) collective-permute-start(bf16[128,1024]{1,0:T(8,128)(2,1)S(1)} %get-tuple-element.58), channel_id=1, source_target_pairs={{0,2},{2,0},{1,3},{3,1},{4,6},{6,4},{5,7},{7,5},{8,10},{10,8},{9,1... | collective-permute-start | bytes 786440 | tf_op jit(solution)/shard_map/ppermute | solution.py:219
  46.1 8.2 %collective-permute-start.9 = (bf16[32,4096]{1,0:T(8,128)(2,1)}, bf16[32,4096]{1,0:T(8,128)(2,1)S(1)}, u32[]{:S(2)}, u32[]{:S(2)}) collective-permute-start(bf16[32,4096]{1,0:T(8,128)(2,1)} %get-tuple-element.55), channel_id=1, source_target_pairs={{0,4},{4,0},{8,12},{12,8},{1,5},{5,1},{9,13},{13,9},{2,6},{6,2},{1... | collective-permute-start | bytes 786440 | tf_op jit(solution)/shard_map/ppermute | solution.py:222
  48.4 1.4 %collective-permute-start.13 = (bf16[16,4096]{1,0:T(8,128)(2,1)S(1)}, bf16[16,4096]{1,0:T(8,128)(2,1)S(1)}, u32[]{:S(2)}, u32[]{:S(2)}) collective-permute-start(bf16[16,4096]{1,0:T(8,128)(2,1)S(1)} %get-tuple-element.85), channel_id=1, source_target_pairs={{0,1},{1,0},{2,3},{3,2},{4,5},{5,4},{6,7},{7,6},{8,9},{9,8},{10,11... | collective-permute-start | bytes 393224 | tf_op jit(solution)/shard_map/ppermute | solution.py:216
  48.5 1.5 %collective-permute-start.12 = (bf16[16,4096]{1,0:T(8,128)(2,1)S(1)}, bf16[16,4096]{1,0:T(8,128)(2,1)S(1)}, u32[]{:S(2)}, u32[]{:S(2)}) collective-permute-start(bf16[16,4096]{1,0:T(8,128)(2,1)S(1)} %get-tuple-element.86), channel_id=1, source_target_pairs={{0,1},{1,0},{2,3},{3,2},{4,5},{5,4},{6,7},{7,6},{8,9},{9,8},{10,11... | collective-permute-start | bytes 393224 | tf_op jit(solution)/shard_map/ppermute | solution.py:216
  49.0 5.3 %collective-permute-start.15 = (f32[128,64]{1,0:T(8,128)S(1)}, f32[128,64]{1,0:T(8,128)S(1)}, u32[]{:S(2)}, u32[]{:S(2)}) collective-permute-start(f32[128,64]{1,0:T(8,128)S(1)} %get-tuple-element.60), channel_id=1, source_target_pairs={{0,2},{2,0},{1,3},{3,1},{4,6},{6,4},{5,7},{7,5},{8,10},{10,8},{9,1... | collective-permute-start | bytes 98312 | tf_op jit(solution)/shard_map/ppermute | solution.py:219
  54.3 4.0 %collective-permute-start.18 = (bf16[16,4096]{1,0:T(8,128)(2,1)S(1)}, bf16[16,4096]{1,0:T(8,128)(2,1)S(1)}, u32[]{:S(2)}, u32[]{:S(2)}) collective-permute-start(bf16[16,4096]{1,0:T(8,128)(2,1)S(1)} %get-tuple-element.83), channel_id=1, source_target_pairs={{0,1},{1,0},{2,3},{3,2},{4,5},{5,4},{6,7},{7,6},{8,9},{9,8},{10,11... | collective-permute-start | bytes 393224 | tf_op jit(solution)/shard_map/ppermute | solution.py:216
  54.4 3.9 %collective-permute-start.17 = (bf16[16,4096]{1,0:T(8,128)(2,1)S(1)}, bf16[16,4096]{1,0:T(8,128)(2,1)S(1)}, u32[]{:S(2)}, u32[]{:S(2)}) collective-permute-start(bf16[16,4096]{1,0:T(8,128)(2,1)S(1)} %get-tuple-element.84), channel_id=1, source_target_pairs={{0,1},{1,0},{2,3},{3,2},{4,5},{5,4},{6,7},{7,6},{8,9},{9,8},{10,11... | collective-permute-start | bytes 393224 | tf_op jit(solution)/shard_map/ppermute | solution.py:216
  54.9 5.6 %collective-permute-start.19 = (bf16[128,64]{1,0:T(8,128)(2,1)S(1)}, bf16[128,64]{1,0:T(8,128)(2,1)S(1)}, u32[]{:S(2)}, u32[]{:S(2)}) collective-permute-start(bf16[128,64]{1,0:T(8,128)(2,1)S(1)} %multiply_convert_fusion), channel_id=1, source_target_pairs={{0,8},{8,0},{4,12},{12,4},{1,9},{9,1},{5,13},{13,5},{2,10},{10,2},... | collective-permute-start | bytes 49160 | tf_op jit(solution)/shard_map/ppermute | solution.py:222
  56.9 8.7 %copy-start.7 = (bf16[256,1024]{1,0:T(8,128)(2,1)S(1)}, bf16[256,1024]{1,0:T(8,128)(2,1)}, u32[]{:S(2)}) copy-start(bf16[256,1024]{1,0:T(8,128)(2,1)} %residual_ref.1) | copy-start | bytes 1572868
  56.9 5.5 %collective-permute-start.16 = (bf16[64,1024]{1,0:T(8,128)(2,1)S(1)}, bf16[64,1024]{1,0:T(8,128)(2,1)S(1)}, u32[]{:S(2)}, u32[]{:S(2)}) collective-permute-start(bf16[64,1024]{1,0:T(8,128)(2,1)S(1)} %get-tuple-element.63), channel_id=1, source_target_pairs={{0,2},{2,0},{1,3},{3,1},{4,6},{6,4},{5,7},{7,5},{8,10},{10,8},{9,1... | collective-permute-start | bytes 393224 | tf_op jit(solution)/shard_map/ppermute | solution.py:219
  60.5 5.0 %collective-permute-start.20 = (bf16[64,1024]{1,0:T(8,128)(2,1)S(1)}, bf16[64,1024]{1,0:T(8,128)(2,1)S(1)}, u32[]{:S(2)}, u32[]{:S(2)}) collective-permute-start(bf16[64,1024]{1,0:T(8,128)(2,1)S(1)} %get-tuple-element.71), channel_id=1, source_target_pairs={{0,2},{2,0},{1,3},{3,1},{4,6},{6,4},{5,7},{7,5},{8,10},{10,8},{9,1... | collective-permute-start | bytes 393224 | tf_op jit(solution)/shard_map/ppermute | solution.py:219
  61.3 5.0 %collective-permute-start.21 = (bf16[128,64]{1,0:T(8,128)(2,1)S(1)}, bf16[128,64]{1,0:T(8,128)(2,1)S(1)}, u32[]{:S(2)}, u32[]{:S(2)}) collective-permute-start(bf16[128,64]{1,0:T(8,128)(2,1)S(1)} %add.57.scaled_ref), channel_id=1, source_target_pairs={{0,4},{4,0},{8,12},{12,8},{1,5},{5,1},{9,13},{13,9},{2,6},{6,2},{1... | collective-permute-start | bytes 49160 | tf_op jit(solution)/shard_map/ppermute | solution.py:222

commit v12 on v10

--- a/solution.py
+++ b/solution.py
@@ -62,6 +62,12 @@
 SWAP = [(0, 1), (1, 0)]
 NEAR = [(0, 1), (1, 0), (2, 3), (3, 2)]
 FAR = [(0, 2), (2, 0), (1, 3), (3, 1)]
+
+
+def by_core(first, second):
+    return [(2 * a, 2 * b) for a, b in first] + [(2 * a + 1, 2 * b + 1) for a, b in second]
+
+
 VMEM = pl.BlockSpec(memory_space=pltpu.VMEM)
 SMEM = pl.BlockSpec(memory_space=pltpu.SMEM)
 HBM = pl.BlockSpec(memory_space=pltpu.HBM)
@@ -129,39 +135,43 @@
         sum_ref[:, tile] = dot(rows, held_ref[:, tile])
 
 
-def far_kernel(
+def blocks_kernel(
+    flags_ref, weight_ref, down_ref, held_ref, mine_ref, first_ref, second_ref, third_ref,
+    fourth_ref, keep_ref, send_ref, near_ref, low_ref,
+):
+    others = [ref[...] for ref in (first_ref, second_ref, third_ref, fourth_ref)]
+    rows = jnp.concatenate([mine_ref[...]] + others)
+    first = flags_ref[1] == 0
+    count = mine_ref.shape[0]
+
+    def far_and_near(value):
+        one, two = value[:count], value[count:]
+        return jnp.where(first, one, two), jnp.where(first, two, one)
+
+    far_low, near_low = far_and_near(low_product(rows, down_ref))
+    low_ref[:count] = far_low
+    low_ref[count:] = near_low
+    for tile in column_tiles(weight_ref.shape[1]):
+        far, near = far_and_near(dot(rows, weight_ref[:, tile]))
+        part(flags_ref, held_ref[:, tile], far, keep_ref, send_ref, tile)
+        near_ref[:, tile] = near
+
+
+def piece_kernel(
     flags_ref, weight_ref, down_ref, held_ref, mine_ref, first_ref, second_ref,
     keep_ref, send_ref, low_ref,
 ):
     other = jnp.concatenate([first_ref[...], second_ref[...]])
     rows = joined(flags_ref, mine_ref[...], other)
     low_ref[...] = low_product(rows, down_ref)
+    step = mine_ref.shape[0]
     for tile in column_tiles(weight_ref.shape[1]):
-        value = dot(rows, weight_ref[:, tile])
-        part(flags_ref, held_ref[:, tile], value, keep_ref, send_ref, tile)
-
-
-def near_kernel(
-    flags_ref, weight_ref, down_ref, mine_ref, first_ref, second_ref, last_ref, third_ref,
-    fourth_ref, keep_ref, send_ref, hold_ref, low_ref,
-):
-    other = jnp.concatenate([first_ref[...], second_ref[...]])
-    near = joined(flags_ref, mine_ref[...], other)
-    last = joined(flags_ref, last_ref[...], jnp.concatenate([third_ref[...], fourth_ref[...]]))
-    rows = jnp.concatenate([near, last])
-    low_ref[...] = low_product(rows, down_ref)
-    step = last_ref.shape[0]
-    for tile in column_tiles(weight_ref.shape[1]):
-        value = dot(rows, weight_ref[:, tile])
-        held = jnp.concatenate([value[:step], value[2 * step : 3 * step]])
-        part(flags_ref, held, value[4 * step :], keep_ref, send_ref, tile)
-        hold_ref[:, tile] = jnp.concatenate(
-            [value[step : 2 * step], value[3 * step : 4 * step]]
-        )
+        held = jnp.concatenate([held_ref[:step, tile], held_ref[2 * step : 3 * step, tile]])
+        part(flags_ref, held, dot(rows, weight_ref[:, tile]), keep_ref, send_ref, tile)
 
 
 def last_kernel(
-    flags_ref, weight_ref, down_ref, held_ref, own_low, far_low, near_low, mine_ref, first_ref,
+    flags_ref, weight_ref, down_ref, held_ref, own_low, low_ref, piece_low, mine_ref, first_ref,
     second_ref, keep_ref, send_ref, low_keep_ref, low_send_ref,
 ):
     other = jnp.concatenate([first_ref[...], second_ref[...]])
@@ -171,21 +181,20 @@
     step = mine_ref.shape[0]
     last_low = jnp.concatenate(
         [
-            near_low[block : block + step], low[:step],
-            near_low[block + step :], low[step:],
+            piece_low[:step], low[:step], piece_low[step:], low[step:]
         ]
     )
     odd, home = flags_ref[2] == 1, flags_ref[0] == 1
-    near = own_low[...], near_low[:block]
-    far = far_low[...], last_low
+    near = own_low[...], low_ref[block:]
+    far = low_ref[:block], last_low
     for side, here in ((0, slice(0, width)), (1, slice(width, 2 * width))):
         near_side = jnp.where(odd, near[1 - side], near[side])
         far_side = jnp.where(odd, far[1 - side], far[side])
         low_keep_ref[:, here] = jnp.where(home, near_side, far_side)
         low_send_ref[:, here] = jnp.where(home, far_side, near_side)
     for tile in column_tiles(weight_ref.shape[1]):
-        value = dot(rows, weight_ref[:, tile])
-        part(flags_ref, held_ref[:, tile], value, keep_ref, send_ref, tile)
+        held = jnp.concatenate([held_ref[step : 2 * step, tile], held_ref[3 * step :, tile]])
+        part(flags_ref, held, dot(rows, weight_ref[:, tile]), keep_ref, send_ref, tile)
 
 
 def base_kernel(flags_ref, residual_ref, *refs):
@@ -254,10 +263,7 @@
     hot = slot[None, :] == jnp.arange(slots, dtype=jnp.int32)[:, None]
     hot = jnp.broadcast_to(hot[:, :, None], (slots, own, width)).astype(BF16)
 
-    mine = lax.dynamic_slice_in_dim(rows, c * half, half, 0)
-    near, far = along(mine, NEAR), along(mine, FAR)
-    up_other = over_x(up)
-    ups = jnp.where(x == 0, jnp.concatenate([up, up_other]), jnp.concatenate([up_other, up]))
+    got = lax.ppermute(rows, ("blk", "sub"), by_core(FAR, NEAR))
     held, own_sum, own_low = call(
         own_kernel,
         [shape(weight.shape, BF16), shape((block_rows, cols), F32)] + lows(block_rows),
@@ -266,45 +272,48 @@
         [pltpu.SemaphoreType.DMA((len(column_tiles(cols)),))],
         FROM_HBM,
     )
-    near, far, own_sum, own_low, ups, hot, scale = barrier(
-        (near, far, own_sum, own_low, ups, hot, scale)
-    )
-
-    last = [along(far[:step], NEAR)]
-    far_others = over_core_in_two(far)
-    far_second, far_others[0] = barrier((far[step:], far_others[0]))
-    last.append(along(far_second, NEAR))
-    kept_a, sent_a, far_low = call(
-        far_kernel,
-        parted(block_rows) + lows(block_rows),
-        [SMEM] + [VMEM] * 6,
-        [flags, held, down[0], own_sum, far] + far_others,
+    up, own_sum = barrier((up, own_sum))
+    up_other = over_x(up)
+    ups = jnp.where(x == 0, jnp.concatenate([up, up_other]), jnp.concatenate([up_other, up]))
+    got, own_sum, own_low, ups, hot, scale = barrier((got, own_sum, own_low, ups, hot, scale))
+
+    def cut(at):
+        return lax.dynamic_slice_in_dim(got, c * half + at * step, step, 0)
+
+    first_cut = cut(0)
+    first_cut, got = barrier((first_cut, got))
+    last = [lax.ppermute(piece, ("blk", "sub"), by_core(NEAR, FAR)) for piece in (first_cut, cut(1))]
+    others = [over_core(got[at : at + step]) for at in range(0, block_rows, step)]
+    kept_a, sent_a, near_sum, low_two = call(
+        blocks_kernel,
+        parted(block_rows) + [shape((block_rows, cols), F32)] + lows(2 * block_rows),
+        [SMEM] + [VMEM] * 8,
+        [flags, held, down[0], own_sum, got] + others,
     )
     got_a = over_x(sent_a)
     last[0], kept_a = barrier((last[0], kept_a))
 
-    kept_c, sent_c, hold, near_low = call(
-        near_kernel,
-        parted(half) + [shape((half, cols), F32)] + lows(block_rows + half),
-        [SMEM] + [VMEM] * 8,
-        [flags, held, down[0], near] + over_core_in_two(near)
-        + [last[0]] + over_core_in_two(last[0]),
+    kept_c, sent_c, piece_low = call(
+        piece_kernel,
+        parted(half) + lows(half),
+        [SMEM] + [VMEM] * 6,
+        [flags, held, down[0], near_sum, last[0]] + over_core_in_two(last[0]),
     )
     got_c = over_x(sent_c)
-    last[1], hold, got_a, near_low = barrier((last[1], hold, got_a, near_low))
+    last[1], near_sum, got_a, piece_low = barrier((last[1], near_sum, got_a, piece_low))
 
     kept_d, sent_d, low, low_sent = call(
         last_kernel,
         parted(half) + [shape((block_rows, 2 * width), F32)] * 2,
         [SMEM] + [VMEM] * 9,
-        [flags, held, down[0], hold, own_low, far_low, near_low, last[1]]
+        [flags, held, down[0], near_sum, own_low, low_two, piece_low, last[1]]
         + over_core_in_two(last[1]),
     )
     got_d = over_x(sent_d)
 
     scaled = ((low + over_x(low_sent)) * scale).astype(BF16)
     scaled = scaled + along(scaled, NEAR)
-    scaled, got_c, got_d = barrier((scaled, got_c, got_d))
+    scaled, got_c = barrier((scaled, got_c))
     base = call(
         base_kernel,
         shape(residual.shape, F32),

time: 64.3 us -> 68.2 us (1.061)
  local copies, waits for them, and re-layouts: 3.71 us -> 11 us
  waiting for transfers between devices: 26.1 us -> 19.3 us
  starting transfers between devices: 19 us -> 21.5 us
  Pallas kernels: 13.7 us -> 15.3 us
  other arithmetic: 1.38 us -> 0.69 us
    ppermute x6 -> x2, waiting for transfers between devices: 19.9 us -> 3.04 us  [along(): return lax.ppermute(value, 'blk', pairs)]
    ppermute x0 -> x3, starting transfers between devices: none -> 7.48 us  [the longest x1 4.04 us: line(): got = lax.ppermute(rows, ('blk', 'sub'), by_core(FAR, NEAR))]
    unnamed x8 -> x20, local copies, waits for them, and re-layouts: 2.28 us -> 8.93 us
    ppermute x0 -> x3, waiting for transfers between devices: none -> 6.21 us  [the longest x1 6.08 us: line(): got = lax.ppermute(rows, ('blk', 'sub'), by_core(FAR, NEAR))]
    ppermute x6 -> x2, starting transfers between devices: 10.9 us -> 5.29 us  [along(): return lax.ppermute(value, 'blk', pairs)]
    ppermute x5, waiting for transfers between devices: 3.37 us -> 7.97 us  [over_x(): return lax.ppermute(value, 'split', SWAP)]
    pallas_call x6, Pallas kernels: 13.7 us -> 15.3 us  [call(): pl.pallas_call(kernel, out_shape=outs, in_specs=in_specs, out_specs=jax.t...]
    ppermute x8, waiting for transfers between devices: 2.8 us -> 2.06 us  [over_core(): return lax.ppermute(value, 'sub', SWAP)]
  transfers between devices with their start and end apart: 19 -> 18, of which waited for: 14 -> 11; matrix products, arithmetic and copies ran while one was open for 2% -> 1% of each run, Pallas kernels for 16% -> 17%
where the time goes in v12:
time: 68.2 us; the launch traced here: 68 us
  starting transfers between devices  21.5 us (32%)
  waiting for transfers between devices  19.3 us (28%)
  Pallas kernels  15.3 us (22%)
  local copies, waits for them, and re-layouts  11 us (16%)
  other arithmetic  0.69 us (1%)
    pallas_call x6, Pallas kernels, call(): pl.pallas_call(kernel, out_shape=outs, in_specs=in_specs, out_specs=jax.t...  15.3 us
    unnamed x20, local copies, waits for them, and re-layouts  8.93 us
    ppermute x5, waiting for transfers between devices, over_x(): return lax.ppermute(value, 'split', SWAP)  7.97 us
    ppermute x5, starting transfers between devices, over_x(): return lax.ppermute(value, 'split', SWAP)  6.59 us
    ppermute x1, waiting for transfers between devices, line(): got = lax.ppermute(rows, ('blk', 'sub'), by_core(FAR, NEAR))  6.08 us
    ppermute x2, starting transfers between devices, along(): return lax.ppermute(value, 'blk', pairs)  5.29 us
    ppermute x1, starting transfers between devices, line(): got = lax.ppermute(rows, ('blk', 'sub'), by_core(FAR, NEAR))  4.04 us
    ppermute x2, starting transfers between devices, line(): lax.ppermute(piece, ('blk', 'sub'), by_core(NEAR, FAR))  3.45 us
  transfers between devices with their start and end apart: 18, of which 11 were waited for; matrix products, arithmetic and copies ran while one was open for 1% of the time, Pallas kernels for 17%

profile of v12, /device:TPU:0, one launch (start us, length us, event | category | flops | bytes accessed | tf_op | source)
XLA Modules:
  0.0 68.0 jit_solution(7753511737838390151)
XLA Ops:
  0.0 4.0 %collective-permute-start = (bf16[128,4096]{1,0:T(8,128)(2,1)}, bf16[128,4096]{1,0:T(8,128)(2,1)S(1)}, u32[]{:S(2)}, u32[]{:S(2)}) collective-permute-start(bf16[128,4096]{1,0:T(8,128)(2,1)} %rows_ref.1), channel_id=1, source_target_pairs={{0,8},{8,0},{4,12},{12,4},{1,5},{5,1},{9,13},{13,9},{2,10},{10,2},... | collective-permute-start | bytes 3145736 | tf_op jit(solution)/shard_map/ppermute | solution.py:266
  4.0 1.0 %copy-done.2 = bf16[1,64,4096]{2,1,0:T(8,128)(2,1)S(1)} copy-done((bf16[1,64,4096]{2,1,0:T(8,128)(2,1)S(1)}, bf16[1,64,4096]{2,1,0:T(8,128)(2,1)}, u32[]{:S(2)}) %copy-start.2) | copy-done | bytes 524312
  5.1 1.2 %copy-done.4 = bf16[128,4096]{1,0:T(8,128)(2,1)S(1)} copy-done((bf16[128,4096]{1,0:T(8,128)(2,1)S(1)}, bf16[128,4096]{1,0:T(8,128)(2,1)}, u32[]{:S(2)}) %copy-start.4) | copy-done | bytes 1048600
  6.3 4.5 %shard_map.82 = (bf16[4096,1024]{1,0:T(8,128)(2,1)S(1)}, f32[128,1024]{1,0:T(8,128)S(1)}, f32[128,64]{1,0:T(8,128)S(1)}) custom-call(bf16[4096,1024]{1,0:T(8,128)(2,1)} %weight_ref.1, bf16[64,4096]{1,0:T(8,128)(2,1)S(1)} %bitcast.4, bf16[128,4096]{1,0:T(8,128)(2,1)S(1)} %copy-done.4), custom_call_target="tpu_custom_call" | custom-call | tf_op jit(solution)/shard_map/pallas_call | solution.py:88
  10.8 3.3 %copy-done = bf16[4096,1024]{1,0:T(8,128)(2,1)} copy-done((bf16[4096,1024]{1,0:T(8,128)(2,1)}, bf16[4096,1024]{1,0:T(8,128)(2,1)S(1)}, u32[]{:S(2)}) %copy-start) | copy-done | bytes 8388632
  14.1 1.5 %collective-permute-start.1 = (bf16[2,64,1024]{2,1,0:T(8,128)(2,1)S(1)}, bf16[2,64,1024]{2,1,0:T(8,128)(2,1)S(1)}, u32[]{:S(2)}, u32[]{:S(2)}) collective-permute-start(bf16[2,64,1024]{2,1,0:T(8,128)(2,1)S(1)} %copy-done.6), channel_id=1, source_target_pairs={{0,2},{2,0},{1,3},{3,1},{4,6},{6,4},{5,7},{7,5},{8,10},{10,8},{9,1... | collective-permute-start | bytes 786440 | tf_op jit(solution)/shard_map/ppermute | solution.py:239
  15.6 0.1 select_reduce_fusion
  15.7 0.1 broadcast_compare_fusion
  15.8 0.1 convert_divide_fusion
  15.8 0.2 select_select_fusion
  16.0 0.1 pad_maximum_fusion
  16.1 4.7 %collective-permute-done.1 = bf16[2,64,1024]{2,1,0:T(8,128)(2,1)S(1)} collective-permute-done((bf16[2,64,1024]{2,1,0:T(8,128)(2,1)S(1)}, bf16[2,64,1024]{2,1,0:T(8,128)(2,1)S(1)}, u32[]{:S(2)}, u32[]{:S(2)}) %collective-permute-start.1) | collective-permute-done | bytes 262176 | tf_op jit(solution)/shard_map/ppermute | solution.py:239
  20.8 0.1 maximum_select_fusion.ups_ref
  20.9 6.1 %collective-permute-done.mine_ref = bf16[128,4096]{1,0:T(8,128)(2,1)S(1)} collective-permute-done((bf16[128,4096]{1,0:T(8,128)(2,1)}, bf16[128,4096]{1,0:T(8,128)(2,1)S(1)}, u32[]{:S(2)}, u32[]{:S(2)}) %collective-permute-start) | collective-permute-done | bytes 1048608 | tf_op jit(solution)/shard_map/ppermute | solution.py:266
  27.0 0.2 broadcast_in_dim.24.hot_ref
  27.2 0.7 %constant_dynamic-slice_fusion.1 = bf16[32,4096]{1,0:T(8,128)(2,1)} fusion(bf16[128,4096]{1,0:T(8,128)(2,1)S(1)} %collective-permute-done.mine_ref, s32[]{:T(128)S(6)} %select_n.44), kind=kLoop, calls=%fused_computation.14 | loop fusion | bytes 524292 | tf_op jit(solution)/shard_map/dynamic_slice | solution.py:281
  28.0 1.1 %constant_dynamic-slice_fusion = (bf16[32,4096]{1,0:T(8,128)(2,1)}, bf16[32,4096]{1,0:T(8,128)(2,1)}, bf16[32,4096]{1,0:T(8,128)(2,1)}, bf16[32,4096]{1,0:T(8,128)(2,1)}, bf16[32,4096]{1,0:T(8,128)(2,1)}) fusion(bf16[128,4096]{1,0:T(8,128)(2,1)S(1)} %collective-permute-done.mine_ref, s32[]{:T(128)S(6)} %select_n.45), kind=kLoop, calls=%fused_computation.13 | loop fusion | bytes 2621444 | tf_op jit(solution)/shard_map/dynamic_slice | solution.py:281
  29.0 0.0 collective-permute-start.6
  29.0 0.5 collective-permute-start.5
  29.5 0.5 collective-permute-start.3
  30.1 2.5 %collective-permute-start.2 = (bf16[32,4096]{1,0:T(8,128)(2,1)}, bf16[32,4096]{1,0:T(8,128)(2,1)S(1)}, u32[]{:S(2)}, u32[]{:S(2)}) collective-permute-start(bf16[32,4096]{1,0:T(8,128)(2,1)} %constant_dynamic-slice_fusion.1), channel_id=1, source_target_pairs={{0,4},{4,0},{8,12},{12,8},{1,9},{9,1},{5,13},{13,5},{2,6},{6,2},{1... | collective-permute-start | bytes 786440 | tf_op jit(solution)/shard_map/ppermute | solution.py:285
  32.5 0.1 pad_add_fusion.flags_ref
  32.6 1.0 %collective-permute-start.7 = (bf16[32,4096]{1,0:T(8,128)(2,1)}, bf16[32,4096]{1,0:T(8,128)(2,1)S(1)}, u32[]{:S(2)}, u32[]{:S(2)}) collective-permute-start(bf16[32,4096]{1,0:T(8,128)(2,1)} %get-tuple-element.75), channel_id=1, source_target_pairs={{0,4},{4,0},{8,12},{12,8},{1,9},{9,1},{5,13},{13,5},{2,6},{6,2},{1... | collective-permute-start | bytes 786440 | tf_op jit(solution)/shard_map/ppermute | solution.py:285
  33.6 3.4 %copy-done.1 = bf16[4096,1024]{1,0:T(8,128)(2,1)S(1)} copy-done((bf16[4096,1024]{1,0:T(8,128)(2,1)S(1)}, bf16[4096,1024]{1,0:T(8,128)(2,1)}, u32[]{:S(2)}) %copy-start.1) | copy-done | bytes 8388632
  37.0 4.1 %shard_map.83 = (f32[128,1024]{1,0:T(8,128)S(1)}, bf16[128,1024]{1,0:T(8,128)(2,1)S(1)}, f32[128,1024]{1,0:T(8,128)S(1)}, f32[256,64]{1,0:T(8,128)S(1)}) custom-call(s32[3]{0:T(128)S(1)} %pad_add_fusion.flags_ref, bf16[4096,1024]{1,0:T(8,128)(2,1)S(1)} %copy-done.1, bf16[64,4096]{1,0:T(8,128)(2,1)S(1)} %bitcast.5, ...), custom_call_target="tpu_custom_call" | custom-call | tf_op jit(solution)/shard_map/pallas_call | solution.py:88
  41.0 0.1 collective-permute-done.2.mine_ref
  41.2 1.5 %collective-permute-start.8 = (bf16[128,1024]{1,0:T(8,128)(2,1)S(1)}, bf16[128,1024]{1,0:T(8,128)(2,1)S(1)}, u32[]{:S(2)}, u32[]{:S(2)}) collective-permute-start(bf16[128,1024]{1,0:T(8,128)(2,1)S(1)} %get-tuple-element.49), channel_id=1, source_target_pairs={{0,2},{2,0},{1,3},{3,1},{4,6},{6,4},{5,7},{7,5},{8,10},{10,8},{9,1... | collective-permute-start | bytes 786440 | tf_op jit(solution)/shard_map/ppermute | solution.py:239
  42.7 0.1 collective-permute-start.10
  42.8 0.5 collective-permute-start.9
  43.3 0.8 %collective-permute-done.10.second_ref = bf16[16,4096]{1,0:T(8,128)(2,1)S(1)} collective-permute-done((bf16[16,4096]{1,0:T(8,128)(2,1)S(1)}, bf16[16,4096]{1,0:T(8,128)(2,1)S(1)}, u32[]{:S(2)}, u32[]{:S(2)}) %collective-permute-start.10) | collective-permute-done | bytes 131104 | tf_op jit(solution)/shard_map/ppermute | solution.py:236
  44.1 0.2 collective-permute-done.9.first_ref
  44.3 2.3 %shard_map.84 = (f32[64,1024]{1,0:T(8,128)S(1)}, bf16[64,1024]{1,0:T(8,128)(2,1)S(1)}, f32[64,64]{1,0:T(8,128)S(1)}) custom-call(s32[3]{0:T(128)S(1)} %pad_add_fusion.flags_ref, bf16[4096,1024]{1,0:T(8,128)(2,1)S(1)} %copy-done.1, bf16[64,4096]{1,0:T(8,128)(2,1)S(1)} %bitcast.6, f32[128,1024]{1,0:T(8,128)S(1)} %get-tuple-element.54.held_ref, ...), custom_call_target="tpu_custom_call" | custom-call | tf_op jit(solution)/shard_map/pallas_call | solution.py:88
  46.6 2.3 %collective-permute-done.8.refs_1_ = bf16[128,1024]{1,0:T(8,128)(2,1)S(1)} collective-permute-done((bf16[128,1024]{1,0:T(8,128)(2,1)S(1)}, bf16[128,1024]{1,0:T(8,128)(2,1)S(1)}, u32[]{:S(2)}, u32[]{:S(2)}) %collective-permute-start.8) | collective-permute-done | bytes 262176 | tf_op jit(solution)/shard_map/ppermute | solution.py:239
  48.9 0.1 collective-permute-start.12
  49.0 0.5 collective-permute-start.11
  49.5 0.8 %collective-permute-done.12.second_ref = bf16[16,4096]{1,0:T(8,128)(2,1)S(1)} collective-permute-done((bf16[16,4096]{1,0:T(8,128)(2,1)S(1)}, bf16[16,4096]{1,0:T(8,128)(2,1)S(1)}, u32[]{:S(2)}, u32[]{:S(2)}) %collective-permute-start.12) | collective-permute-done | bytes 131104 | tf_op jit(solution)/shard_map/ppermute | solution.py:236
  50.3 0.2 collective-permute-done.11.first_ref
  50.5 2.3 %shard_map.85 = (f32[64,1024]{1,0:T(8,128)S(1)}, bf16[64,1024]{1,0:T(8,128)(2,1)S(1)}, f32[128,128]{1,0:T(8,128)S(1)}, f32[128,128]{1,0:T(8,128)S(1)}) custom-call(s32[3]{0:T(128)S(1)} %pad_add_fusion.flags_ref, bf16[4096,1024]{1,0:T(8,128)(2,1)S(1)} %copy-done.1, bf16[64,4096]{1,0:T(8,128)(2,1)S(1)} %bitcast.7, f32[128,1024]{1,0:T(8,128)S(1)} %get-tuple-element.54.held_ref, ...), custom_call_target="tpu_custom_call" | custom-call | tf_op jit(solution)/shard_map/pallas_call | solution.py:88
  52.8 1.6 %collective-permute-start.13 = (f32[128,128]{1,0:T(8,128)S(1)}, f32[128,128]{1,0:T(8,128)S(1)}, u32[]{:S(2)}, u32[]{:S(2)}) collective-permute-start(f32[128,128]{1,0:T(8,128)S(1)} %get-tuple-element.60), channel_id=1, source_target_pairs={{0,2},{2,0},{1,3},{3,1},{4,6},{6,4},{5,7},{7,5},{8,10},{10,8},{9,1... | collective-permute-start | bytes 196616 | tf_op jit(solution)/shard_map/ppermute | solution.py:239
  54.3 0.5 collective-permute-start.15
  54.9 1.5 %collective-permute-start.16 = (bf16[64,1024]{1,0:T(8,128)(2,1)S(1)}, bf16[64,1024]{1,0:T(8,128)(2,1)S(1)}, u32[]{:S(2)}, u32[]{:S(2)}) collective-permute-start(bf16[64,1024]{1,0:T(8,128)(2,1)S(1)} %get-tuple-element.65), channel_id=1, source_target_pairs={{0,2},{2,0},{1,3},{3,1},{4,6},{6,4},{5,7},{7,5},{8,10},{10,8},{9,1... | collective-permute-start | bytes 393224 | tf_op jit(solution)/shard_map/ppermute | solution.py:239
  56.4 1.0 %collective-permute-done.13 = f32[128,128]{1,0:T(8,128)S(1)} collective-permute-done((f32[128,128]{1,0:T(8,128)S(1)}, f32[128,128]{1,0:T(8,128)S(1)}, u32[]{:S(2)}, u32[]{:S(2)}) %collective-permute-start.13) | collective-permute-done | bytes 65568 | tf_op jit(solution)/shard_map/ppermute | solution.py:239
  57.4 2.3 %collective-permute-start.14 = (bf16[128,128]{1,0:T(8,128)(2,1)S(1)}, bf16[128,128]{1,0:T(8,128)(2,1)S(1)}, u32[]{:S(2)}, u32[]{:S(2)}) collective-permute-start(bf16[128,128]{1,0:T(8,128)(2,1)S(1)} %multiply_convert_fusion), channel_id=1, source_target_pairs={{0,4},{4,0},{8,12},{12,8},{1,5},{5,1},{9,13},{13,9},{2,6},{6,2},{1... | collective-permute-start | bytes 98312 | tf_op jit(solution)/shard_map/ppermute | solution.py:242
  59.6 1.9 %collective-permute-done.14 = bf16[128,128]{1,0:T(8,128)(2,1)S(1)} collective-permute-done((bf16[128,128]{1,0:T(8,128)(2,1)S(1)}, bf16[128,128]{1,0:T(8,128)(2,1)S(1)}, u32[]{:S(2)}, u32[]{:S(2)}) %collective-permute-start.14) | collective-permute-done | bytes 32800 | tf_op jit(solution)/shard_map/ppermute | solution.py:242
  61.6 3.0 %collective-permute-start.17 = (bf16[128,128]{1,0:T(8,128)(2,1)S(1)}, bf16[128,128]{1,0:T(8,128)(2,1)S(1)}, u32[]{:S(2)}, u32[]{:S(2)}) collective-permute-start(bf16[128,128]{1,0:T(8,128)(2,1)S(1)} %add.32.scaled_ref), channel_id=1, source_target_pairs={{0,8},{8,0},{4,12},{12,4},{1,9},{9,1},{5,13},{13,5},{2,10},{10,2},... | collective-permute-start | bytes 98312 | tf_op jit(solution)/shard_map/ppermute | solution.py:242
  64.6 0.7 %shard_map.86.base_ref = f32[256,1024]{1,0:T(8,128)S(1)} custom-call(s32[3]{0:T(128)S(1)} %pad_add_fusion.flags_ref, bf16[256,1024]{1,0:T(8,128)(2,1)S(1)} %copy-done.5, f32[128,1024]{1,0:T(8,128)S(1)} %get-tuple-element.47.refs_0_, bf16[128,1024]{1,0:T(8,128)(2,1)S(1)} %collective-permute-done.8.refs_1_, f32[64,1024]{1,0:T(8,128)S(1)} %get-tuple-element.53.refs_2_, ...), custom_call_target="tpu_custom_call" | custom-call | tf_op jit(solution)/shard_map/pallas_call | solution.py:88
  65.3 1.1 %collective-permute-done.17.scaled_got_ref = bf16[128,128]{1,0:T(8,128)(2,1)S(1)} collective-permute-done((bf16[128,128]{1,0:T(8,128)(2,1)S(1)}, bf16[128,128]{1,0:T(8,128)(2,1)S(1)}, u32[]{:S(2)}, u32[]{:S(2)}) %collective-permute-start.17) | collective-permute-done | bytes 32800 | tf_op jit(solution)/shard_map/ppermute | solution.py:242
  66.5 1.5 %shard_map.87 = bf16[256,1024]{1,0:T(8,128)(2,1)} custom-call(f32[256,1024]{1,0:T(8,128)S(1)} %shard_map.86.base_ref, bf16[128,128]{1,0:T(8,128)(2,1)S(1)} %add.32.scaled_ref, bf16[128,128]{1,0:T(8,128)(2,1)S(1)} %collective-permute-done.17.scaled_got_ref, bf16[4,256,64]{2,1,0:T(8,128)(2,1)S(1)} %broadcast_in_dim.24.hot_ref, ...), custom_call_target="tpu_custom_call" | custom-call | tf_op jit(solution)/shard_map/pallas_call | solution.py:88
  (30 shorter events, 0.1 us)
Async XLA Ops:
  0.0 15.6 %copy-start.8 = (s32[4]{0:T(128)S(1)}, s32[4]{0:T(128)}, u32[]{:S(2)}) copy-start(s32[4]{0:T(128)} %param.15) | copy-start | bytes 52
  0.0 15.6 %copy-start.9 = (s32[4]{0:T(128)S(1)}, s32[4]{0:T(128)}, u32[]{:S(2)}) copy-start(s32[4]{0:T(128)} %param.14) | copy-start | bytes 52
  0.0 27.0 %collective-permute-start = (bf16[128,4096]{1,0:T(8,128)(2,1)}, bf16[128,4096]{1,0:T(8,128)(2,1)S(1)}, u32[]{:S(2)}, u32[]{:S(2)}) collective-permute-start(bf16[128,4096]{1,0:T(8,128)(2,1)} %rows_ref.1), channel_id=1, source_target_pairs={{0,8},{8,0},{4,12},{12,4},{1,5},{5,1},{9,13},{13,9},{2,10},{10,2},... | collective-permute-start | bytes 3145736 | tf_op jit(solution)/shard_map/ppermute | solution.py:266
  4.0 1.0 %copy-start.2 = (bf16[1,64,4096]{2,1,0:T(8,128)(2,1)S(1)}, bf16[1,64,4096]{2,1,0:T(8,128)(2,1)}, u32[]{:S(2)}) copy-start(bf16[1,64,4096]{2,1,0:T(8,128)(2,1)} %param.11) | copy-start | bytes 1572868
  5.1 1.2 %copy-start.4 = (bf16[128,4096]{1,0:T(8,128)(2,1)S(1)}, bf16[128,4096]{1,0:T(8,128)(2,1)}, u32[]{:S(2)}) copy-start(bf16[128,4096]{1,0:T(8,128)(2,1)} %rows_ref.1) | copy-start | bytes 3145732
  6.3 7.8 %copy-start.6 = (bf16[2,64,1024]{2,1,0:T(8,128)(2,1)S(1)}, bf16[2,64,1024]{2,1,0:T(8,128)(2,1)}, u32[]{:S(2)}) copy-start(bf16[2,64,1024]{2,1,0:T(8,128)(2,1)} %param.12) | copy-start | bytes 786436
  6.3 9.3 %copy-start.7 = (s32[512]{0:T(512)S(1)}, s32[512]{0:T(512)}, u32[]{:S(2)}) copy-start(s32[512]{0:T(512)} %param.13) | copy-start | bytes 6148
  6.3 27.3 %copy-start.3 = (bf16[1,64,4096]{2,1,0:T(8,128)(2,1)S(1)}, bf16[1,64,4096]{2,1,0:T(8,128)(2,1)}, u32[]{:S(2)}) copy-start(bf16[1,64,4096]{2,1,0:T(8,128)(2,1)} %param.11) | copy-start | bytes 1572868
  10.8 3.3 %copy-start = (bf16[4096,1024]{1,0:T(8,128)(2,1)}, bf16[4096,1024]{1,0:T(8,128)(2,1)S(1)}, u32[]{:S(2)}) copy-start(bf16[4096,1024]{1,0:T(8,128)(2,1)S(1)} %get-tuple-element.43.weight_ref) | copy-start | bytes 25165828
  14.1 6.8 %collective-permute-start.1 = (bf16[2,64,1024]{2,1,0:T(8,128)(2,1)S(1)}, bf16[2,64,1024]{2,1,0:T(8,128)(2,1)S(1)}, u32[]{:S(2)}, u32[]{:S(2)}) collective-permute-start(bf16[2,64,1024]{2,1,0:T(8,128)(2,1)S(1)} %copy-done.6), channel_id=1, source_target_pairs={{0,2},{2,0},{1,3},{3,1},{4,6},{6,4},{5,7},{7,5},{8,10},{10,8},{9,1... | collective-permute-start | bytes 786440 | tf_op jit(solution)/shard_map/ppermute | solution.py:239
  29.0 3.6 %collective-permute-start.6 = (bf16[32,4096]{1,0:T(8,128)(2,1)}, bf16[32,4096]{1,0:T(8,128)(2,1)S(1)}, u32[]{:S(2)}, u32[]{:S(2)}) collective-permute-start(bf16[32,4096]{1,0:T(8,128)(2,1)} %get-tuple-element.76), channel_id=1, source_target_pairs={{0,1},{1,0},{2,3},{3,2},{4,5},{5,4},{6,7},{7,6},{8,9},{9,8},{10,11... | collective-permute-start | bytes 786440 | tf_op jit(solution)/shard_map/ppermute | solution.py:236
  29.0 4.5 %collective-permute-start.5 = (bf16[32,4096]{1,0:T(8,128)(2,1)}, bf16[32,4096]{1,0:T(8,128)(2,1)}, u32[]{:S(2)}, u32[]{:S(2)}) collective-permute-start(bf16[32,4096]{1,0:T(8,128)(2,1)} %get-tuple-element.77), channel_id=1, source_target_pairs={{0,1},{1,0},{2,3},{3,2},{4,5},{5,4},{6,7},{7,6},{8,9},{9,8},{10,11... | collective-permute-start | bytes 786440 | tf_op jit(solution)/shard_map/ppermute | solution.py:236
  29.5 4.0 %collective-permute-start.4 = (bf16[32,4096]{1,0:T(8,128)(2,1)}, bf16[32,4096]{1,0:T(8,128)(2,1)}, u32[]{:S(2)}, u32[]{:S(2)}) collective-permute-start(bf16[32,4096]{1,0:T(8,128)(2,1)} %get-tuple-element.78), channel_id=1, source_target_pairs={{0,1},{1,0},{2,3},{3,2},{4,5},{5,4},{6,7},{7,6},{8,9},{9,8},{10,11... | collective-permute-start | bytes 786440 | tf_op jit(solution)/shard_map/ppermute | solution.py:236
  29.5 4.0 %collective-permute-start.3 = (bf16[32,4096]{1,0:T(8,128)(2,1)}, bf16[32,4096]{1,0:T(8,128)(2,1)}, u32[]{:S(2)}, u32[]{:S(2)}) collective-permute-start(bf16[32,4096]{1,0:T(8,128)(2,1)} %get-tuple-element.79), channel_id=1, source_target_pairs={{0,1},{1,0},{2,3},{3,2},{4,5},{5,4},{6,7},{7,6},{8,9},{9,8},{10,11... | collective-permute-start | bytes 786440 | tf_op jit(solution)/shard_map/ppermute | solution.py:236
  30.1 11.1 %collective-permute-start.2 = (bf16[32,4096]{1,0:T(8,128)(2,1)}, bf16[32,4096]{1,0:T(8,128)(2,1)S(1)}, u32[]{:S(2)}, u32[]{:S(2)}) collective-permute-start(bf16[32,4096]{1,0:T(8,128)(2,1)} %constant_dynamic-slice_fusion.1), channel_id=1, source_target_pairs={{0,4},{4,0},{8,12},{12,8},{1,9},{9,1},{5,13},{13,5},{2,6},{6,2},{1... | collective-permute-start | bytes 786440 | tf_op jit(solution)/shard_map/ppermute | solution.py:285
  32.6 14.0 %collective-permute-start.7 = (bf16[32,4096]{1,0:T(8,128)(2,1)}, bf16[32,4096]{1,0:T(8,128)(2,1)S(1)}, u32[]{:S(2)}, u32[]{:S(2)}) collective-permute-start(bf16[32,4096]{1,0:T(8,128)(2,1)} %get-tuple-element.75), channel_id=1, source_target_pairs={{0,4},{4,0},{8,12},{12,8},{1,9},{9,1},{5,13},{13,5},{2,6},{6,2},{1... | collective-permute-start | bytes 786440 | tf_op jit(solution)/shard_map/ppermute | solution.py:285
  33.6 3.4 %copy-start.1 = (bf16[4096,1024]{1,0:T(8,128)(2,1)S(1)}, bf16[4096,1024]{1,0:T(8,128)(2,1)}, u32[]{:S(2)}) copy-start(bf16[4096,1024]{1,0:T(8,128)(2,1)} %copy-done) | copy-start | bytes 25165828
  41.2 7.7 %collective-permute-start.8 = (bf16[128,1024]{1,0:T(8,128)(2,1)S(1)}, bf16[128,1024]{1,0:T(8,128)(2,1)S(1)}, u32[]{:S(2)}, u32[]{:S(2)}) collective-permute-start(bf16[128,1024]{1,0:T(8,128)(2,1)S(1)} %get-tuple-element.49), channel_id=1, source_target_pairs={{0,2},{2,0},{1,3},{3,1},{4,6},{6,4},{5,7},{7,5},{8,10},{10,8},{9,1... | collective-permute-start | bytes 786440 | tf_op jit(solution)/shard_map/ppermute | solution.py:239
  42.7 1.4 %collective-permute-start.10 = (bf16[16,4096]{1,0:T(8,128)(2,1)S(1)}, bf16[16,4096]{1,0:T(8,128)(2,1)S(1)}, u32[]{:S(2)}, u32[]{:S(2)}) collective-permute-start(bf16[16,4096]{1,0:T(8,128)(2,1)S(1)} %get-tuple-element.82), channel_id=1, source_target_pairs={{0,1},{1,0},{2,3},{3,2},{4,5},{5,4},{6,7},{7,6},{8,9},{9,8},{10,11... | collective-permute-start | bytes 393224 | tf_op jit(solution)/shard_map/ppermute | solution.py:236
  42.8 1.5 %collective-permute-start.9 = (bf16[16,4096]{1,0:T(8,128)(2,1)S(1)}, bf16[16,4096]{1,0:T(8,128)(2,1)S(1)}, u32[]{:S(2)}, u32[]{:S(2)}) collective-permute-start(bf16[16,4096]{1,0:T(8,128)(2,1)S(1)} %get-tuple-element.83), channel_id=1, source_target_pairs={{0,1},{1,0},{2,3},{3,2},{4,5},{5,4},{6,7},{7,6},{8,9},{9,8},{10,11... | collective-permute-start | bytes 393224 | tf_op jit(solution)/shard_map/ppermute | solution.py:236
  44.3 20.3 %copy-start.5 = (bf16[256,1024]{1,0:T(8,128)(2,1)S(1)}, bf16[256,1024]{1,0:T(8,128)(2,1)}, u32[]{:S(2)}) copy-start(bf16[256,1024]{1,0:T(8,128)(2,1)} %residual_ref.1) | copy-start | bytes 1572868
  48.9 1.4 %collective-permute-start.12 = (bf16[16,4096]{1,0:T(8,128)(2,1)S(1)}, bf16[16,4096]{1,0:T(8,128)(2,1)S(1)}, u32[]{:S(2)}, u32[]{:S(2)}) collective-permute-start(bf16[16,4096]{1,0:T(8,128)(2,1)S(1)} %get-tuple-element.80), channel_id=1, source_target_pairs={{0,1},{1,0},{2,3},{3,2},{4,5},{5,4},{6,7},{7,6},{8,9},{9,8},{10,11... | collective-permute-start | bytes 393224 | tf_op jit(solution)/shard_map/ppermute | solution.py:236
  49.0 1.5 %collective-permute-start.11 = (bf16[16,4096]{1,0:T(8,128)(2,1)S(1)}, bf16[16,4096]{1,0:T(8,128)(2,1)S(1)}, u32[]{:S(2)}, u32[]{:S(2)}) collective-permute-start(bf16[16,4096]{1,0:T(8,128)(2,1)S(1)} %get-tuple-element.81), channel_id=1, source_target_pairs={{0,1},{1,0},{2,3},{3,2},{4,5},{5,4},{6,7},{7,6},{8,9},{9,8},{10,11... | collective-permute-start | bytes 393224 | tf_op jit(solution)/shard_map/ppermute | solution.py:236
  52.8 4.6 %collective-permute-start.13 = (f32[128,128]{1,0:T(8,128)S(1)}, f32[128,128]{1,0:T(8,128)S(1)}, u32[]{:S(2)}, u32[]{:S(2)}) collective-permute-start(f32[128,128]{1,0:T(8,128)S(1)} %get-tuple-element.60), channel_id=1, source_target_pairs={{0,2},{2,0},{1,3},{3,1},{4,6},{6,4},{5,7},{7,5},{8,10},{10,8},{9,1... | collective-permute-start | bytes 196616 | tf_op jit(solution)/shard_map/ppermute | solution.py:239
  54.3 7.2 %collective-permute-start.15 = (bf16[64,1024]{1,0:T(8,128)(2,1)S(1)}, bf16[64,1024]{1,0:T(8,128)(2,1)S(1)}, u32[]{:S(2)}, u32[]{:S(2)}) collective-permute-start(bf16[64,1024]{1,0:T(8,128)(2,1)S(1)} %get-tuple-element.62), channel_id=1, source_target_pairs={{0,2},{2,0},{1,3},{3,1},{4,6},{6,4},{5,7},{7,5},{8,10},{10,8},{9,1... | collective-permute-start | bytes 393224 | tf_op jit(solution)/shard_map/ppermute | solution.py:239
  54.9 9.7 %collective-permute-start.16 = (bf16[64,1024]{1,0:T(8,128)(2,1)S(1)}, bf16[64,1024]{1,0:T(8,128)(2,1)S(1)}, u32[]{:S(2)}, u32[]{:S(2)}) collective-permute-start(bf16[64,1024]{1,0:T(8,128)(2,1)S(1)} %get-tuple-element.65), channel_id=1, source_target_pairs={{0,2},{2,0},{1,3},{3,1},{4,6},{6,4},{5,7},{7,5},{8,10},{10,8},{9,1... | collective-permute-start | bytes 393224 | tf_op jit(solution)/shard_map/ppermute | solution.py:239
  57.4 4.1 %collective-permute-start.14 = (bf16[128,128]{1,0:T(8,128)(2,1)S(1)}, bf16[128,128]{1,0:T(8,128)(2,1)S(1)}, u32[]{:S(2)}, u32[]{:S(2)}) collective-permute-start(bf16[128,128]{1,0:T(8,128)(2,1)S(1)} %multiply_convert_fusion), channel_id=1, source_target_pairs={{0,4},{4,0},{8,12},{12,8},{1,5},{5,1},{9,13},{13,9},{2,6},{6,2},{1... | collective-permute-start | bytes 98312 | tf_op jit(solution)/shard_map/ppermute | solution.py:242
  61.6 4.9 %collective-permute-start.17 = (bf16[128,128]{1,0:T(8,128)(2,1)S(1)}, bf16[128,128]{1,0:T(8,128)(2,1)S(1)}, u32[]{:S(2)}, u32[]{:S(2)}) collective-permute-start(bf16[128,128]{1,0:T(8,128)(2,1)S(1)} %add.32.scaled_ref), channel_id=1, source_target_pairs={{0,8},{8,0},{4,12},{12,4},{1,9},{9,1},{5,13},{13,5},{2,10},{10,2},... | collective-permute-start | bytes 98312 | tf_op jit(solution)/shard_map/ppermute | solution.py:242

commit v13 on v10

--- a/solution.py
+++ b/solution.py
@@ -62,6 +62,13 @@
 SWAP = [(0, 1), (1, 0)]
 NEAR = [(0, 1), (1, 0), (2, 3), (3, 2)]
 FAR = [(0, 2), (2, 0), (1, 3), (3, 1)]
+LAST = [(0, 3), (3, 0), (1, 2), (2, 1)]
+
+
+def by_core(first, second):
+    return [(2 * a, 2 * b) for a, b in first] + [(2 * a + 1, 2 * b + 1) for a, b in second]
+
+
 VMEM = pl.BlockSpec(memory_space=pltpu.VMEM)
 SMEM = pl.BlockSpec(memory_space=pltpu.SMEM)
 HBM = pl.BlockSpec(memory_space=pltpu.HBM)
@@ -182,7 +189,7 @@
         near_side = jnp.where(odd, near[1 - side], near[side])
         far_side = jnp.where(odd, far[1 - side], far[side])
         low_keep_ref[:, here] = jnp.where(home, near_side, far_side)
-        low_send_ref[:, here] = jnp.where(home, far_side, near_side)
+        low_send_ref[:, here] = jnp.where(home, far_side, near_side).astype(BF16)
     for tile in column_tiles(weight_ref.shape[1]):
         value = dot(rows, weight_ref[:, tile])
         part(flags_ref, held_ref[:, tile], value, keep_ref, send_ref, tile)
@@ -202,8 +209,9 @@
         out_ref[here, :] = residual_ref[here, :].astype(F32) + base
 
 
-def final_kernel(base_ref, scaled_ref, scaled_got_ref, hot_ref, ups_ref, out_ref):
-    scaled = scaled_ref[...] + scaled_got_ref[...]
+def final_kernel(base_ref, hot_ref, ups_ref, *refs):
+    *parts, out_ref = refs
+    scaled = sum(ref[...] for ref in parts)
     width = ups_ref.shape[1]
     scaled = jnp.concatenate([scaled[:, :width], scaled[:, width:]])
     lora = dot(scaled * hot_ref[0], ups_ref[0])
@@ -295,16 +303,19 @@
 
     kept_d, sent_d, low, low_sent = call(
         last_kernel,
-        parted(half) + [shape((block_rows, 2 * width), F32)] * 2,
+        parted(half) + [shape((block_rows, 2 * width), dtype) for dtype in (F32, BF16)],
         [SMEM] + [VMEM] * 9,
         [flags, held, down[0], hold, own_low, far_low, near_low, last[1]]
         + over_core_in_two(last[1]),
     )
     got_d = over_x(sent_d)
 
-    scaled = ((low + over_x(low_sent)) * scale).astype(BF16)
-    scaled = scaled + along(scaled, NEAR)
-    scaled, got_c, got_d = barrier((scaled, got_c, got_d))
+    scaled = ((low + over_x(low_sent).astype(F32)) * scale).astype(BF16)
+    scaled_got = [
+        lax.ppermute(scaled, ("blk", "sub"), by_core(NEAR, FAR)),
+        along(scaled, LAST),
+    ]
+    scaled_got.append(over_core(scaled_got[0]))
     base = call(
         base_kernel,
         shape(residual.shape, F32),
@@ -314,8 +325,8 @@
     return call(
         final_kernel,
         shape(residual.shape, BF16),
-        [VMEM] * 5,
-        [base, scaled, along(scaled, FAR), hot, ups],
+        [VMEM] * 7,
+        [base, hot, ups, scaled] + scaled_got,
     )
 
 

time: 64.3 us -> 60.2 us (0.936)
  waiting for transfers between devices: 26.1 us -> 21.1 us
  starting transfers between devices: 19 us -> 19.9 us
    ppermute x6 -> x5, waiting for transfers between devices: 19.9 us -> 15.3 us  [along(): return lax.ppermute(value, 'blk', pairs)]
    ppermute x0 -> x1, starting transfers between devices: none -> 0.86 us  [line(): lax.ppermute(scaled, ('blk', 'sub'), by_core(NEAR, FAR))]
    ppermute x6 -> x5, starting transfers between devices: 10.9 us -> 11 us  [along(): return lax.ppermute(value, 'blk', pairs)]
    ppermute x8 -> x9, starting transfers between devices: 1.93 us -> 1.93 us  [over_core(): return lax.ppermute(value, 'sub', SWAP)]
    ppermute x8 -> x9, waiting for transfers between devices: 2.8 us -> 2.8 us  [over_core(): return lax.ppermute(value, 'sub', SWAP)]
  transfers between devices with their start and end apart: 19 -> 20, of which waited for: 14 -> 13; matrix products, arithmetic and copies ran while one was open for 2% -> 2% of each run, Pallas kernels for 16% -> 17%
where the time goes in v13:
time: 60.2 us; the launch traced here: 60 us
  waiting for transfers between devices  21.1 us (35%)
  starting transfers between devices  19.9 us (33%)
  Pallas kernels  13.7 us (23%)
  local copies, waits for them, and re-layouts  3.71 us (6%)
  other arithmetic  1.37 us (2%)
    ppermute x5, waiting for transfers between devices, along(): return lax.ppermute(value, 'blk', pairs)  15.3 us
    pallas_call x6, Pallas kernels, call(): pl.pallas_call(kernel, out_shape=outs, in_specs=in_specs, out_specs=jax.t...  13.7 us
    ppermute x5, starting transfers between devices, along(): return lax.ppermute(value, 'blk', pairs)  11 us
    ppermute x5, starting transfers between devices, over_x(): return lax.ppermute(value, 'split', SWAP)  6.2 us
    ppermute x5, waiting for transfers between devices, over_x(): return lax.ppermute(value, 'split', SWAP)  2.96 us
    ppermute x9, waiting for transfers between devices, over_core(): return lax.ppermute(value, 'sub', SWAP)  2.8 us
    unnamed x8, local copies, waits for them, and re-layouts  2.28 us
    ppermute x9, starting transfers between devices, over_core(): return lax.ppermute(value, 'sub', SWAP)  1.93 us
  transfers between devices with their start and end apart: 20, of which 13 were waited for; matrix products, arithmetic and copies ran while one was open for 2% of the time, Pallas kernels for 17%

profile of v13, /device:TPU:0, one launch (start us, length us, event | category | flops | bytes accessed | tf_op | source)
XLA Modules:
  0.0 60.0 jit_solution(11763360957530950243)
XLA Ops:
  0.0 1.1 %constant_dynamic-slice_fusion = bf16[64,4096]{1,0:T(8,128)(2,1)S(1)} fusion(bf16[128,4096]{1,0:T(8,128)(2,1)} %rows_ref.1, s32[]{:T(128)S(6)} %select_n.36), kind=kLoop, calls=%fused_computation.13 | loop fusion | bytes 1048580 | tf_op jit(solution)/shard_map/dynamic_slice | solution.py:265
  1.1 4.1 %collective-permute-start.1 = (bf16[64,4096]{1,0:T(8,128)(2,1)S(1)}, bf16[64,4096]{1,0:T(8,128)(2,1)S(1)}, u32[]{:S(2)}, u32[]{:S(2)}) collective-permute-start(bf16[64,4096]{1,0:T(8,128)(2,1)S(1)} %constant_dynamic-slice_fusion), channel_id=1, source_target_pairs={{0,8},{8,0},{4,12},{12,4},{1,9},{9,1},{5,13},{13,5},{2,10},{10,2},... | collective-permute-start | bytes 1572872 | tf_op jit(solution)/shard_map/ppermute | solution.py:241
  5.2 1.6 %collective-permute-start = (bf16[64,4096]{1,0:T(8,128)(2,1)S(1)}, bf16[64,4096]{1,0:T(8,128)(2,1)S(1)}, u32[]{:S(2)}, u32[]{:S(2)}) collective-permute-start(bf16[64,4096]{1,0:T(8,128)(2,1)S(1)} %constant_dynamic-slice_fusion), channel_id=1, source_target_pairs={{0,4},{4,0},{8,12},{12,8},{1,5},{5,1},{9,13},{13,9},{2,6},{6,2},{1... | collective-permute-start | bytes 1572872 | tf_op jit(solution)/shard_map/ppermute | solution.py:241
  6.8 1.5 %collective-permute-start.2 = (bf16[2,64,1024]{2,1,0:T(8,128)(2,1)}, bf16[2,64,1024]{2,1,0:T(8,128)(2,1)S(1)}, u32[]{:S(2)}, u32[]{:S(2)}) collective-permute-start(bf16[2,64,1024]{2,1,0:T(8,128)(2,1)} %param.12), channel_id=1, source_target_pairs={{0,2},{2,0},{1,3},{3,1},{4,6},{6,4},{5,7},{7,5},{8,10},{10,8},{9,1... | collective-permute-start | bytes 786440 | tf_op jit(solution)/shard_map/ppermute | solution.py:238
  8.3 0.8 %select_reduce_fusion = (s32[512]{0:T(512)S(1)}, s32[512]{0:T(512)S(1)}) fusion(s32[4]{0:T(128)} %param.15, s32[512]{0:T(512)} %param.13, s32[4]{0:T(128)} %param.14), kind=kLoop, calls=%fused_computation.5 | loop fusion | flops 9216 | bytes 6176 | tf_op jit(solution)/shard_map/reduce_sum | solution.py:24
  9.1 0.1 convert_divide_fusion
  9.2 0.1 broadcast_compare_fusion
  9.2 0.2 select_select_fusion
  9.4 0.1 pad_maximum_fusion
  9.5 0.1 pad_add_fusion.flags_ref
  9.6 1.0 %copy-done = bf16[1,64,4096]{2,1,0:T(8,128)(2,1)S(1)} copy-done((bf16[1,64,4096]{2,1,0:T(8,128)(2,1)S(1)}, bf16[1,64,4096]{2,1,0:T(8,128)(2,1)}, u32[]{:S(2)}) %copy-start) | copy-done | bytes 524312
  10.6 1.2 %copy-done.1 = bf16[128,4096]{1,0:T(8,128)(2,1)S(1)} copy-done((bf16[128,4096]{1,0:T(8,128)(2,1)S(1)}, bf16[128,4096]{1,0:T(8,128)(2,1)}, u32[]{:S(2)}) %copy-start.1) | copy-done | bytes 1048600
  11.9 4.4 %shard_map.82 = (bf16[4096,1024]{1,0:T(8,128)(2,1)S(1)}, f32[128,1024]{1,0:T(8,128)S(1)}, f32[128,64]{1,0:T(8,128)S(1)}) custom-call(bf16[4096,1024]{1,0:T(8,128)(2,1)} %weight_ref.1, bf16[64,4096]{1,0:T(8,128)(2,1)S(1)} %bitcast.4, bf16[128,4096]{1,0:T(8,128)(2,1)S(1)} %copy-done.1), custom_call_target="tpu_custom_call" | custom-call | tf_op jit(solution)/shard_map/pallas_call | solution.py:89
  16.3 0.1 maximum_select_fusion.ups_ref
  16.4 12.1 %collective-permute-done.1.mine_ref = bf16[64,4096]{1,0:T(8,128)(2,1)S(1)} collective-permute-done((bf16[64,4096]{1,0:T(8,128)(2,1)S(1)}, bf16[64,4096]{1,0:T(8,128)(2,1)S(1)}, u32[]{:S(2)}, u32[]{:S(2)}) %collective-permute-start.1) | collective-permute-done | bytes 524320 | tf_op jit(solution)/shard_map/ppermute | solution.py:241
  28.5 0.2 collective-permute-done.mine_ref
  28.7 0.2 broadcast_in_dim.24.hot_ref
  28.9 0.1 collective-permute-start.4
  29.0 1.6 %collective-permute-start.3 = (bf16[32,4096]{1,0:T(8,128)(2,1)S(1)}, bf16[32,4096]{1,0:T(8,128)(2,1)S(1)}, u32[]{:S(2)}, u32[]{:S(2)}) collective-permute-start(bf16[32,4096]{1,0:T(8,128)(2,1)S(1)} %get-tuple-element.72), channel_id=1, source_target_pairs={{0,4},{4,0},{8,12},{12,8},{1,5},{5,1},{9,13},{13,9},{2,6},{6,2},{1... | collective-permute-start | bytes 786440 | tf_op jit(solution)/shard_map/ppermute | solution.py:241
  30.6 0.2 collective-permute-start.5
  30.8 0.4 collective-permute-start.8
  31.2 0.2 collective-permute-start.7
  31.3 0.7 %collective-permute-done.5.second_ref = bf16[32,4096]{1,0:T(8,128)(2,1)S(1)} collective-permute-done((bf16[32,4096]{1,0:T(8,128)(2,1)S(1)}, bf16[32,4096]{1,0:T(8,128)(2,1)S(1)}, u32[]{:S(2)}, u32[]{:S(2)}) %collective-permute-start.5) | collective-permute-done | bytes 262176 | tf_op jit(solution)/shard_map/ppermute | solution.py:235
  32.1 2.1 %shard_map.83 = (f32[128,1024]{1,0:T(8,128)S(1)}, bf16[128,1024]{1,0:T(8,128)(2,1)S(1)}, f32[128,64]{1,0:T(8,128)S(1)}) custom-call(s32[3]{0:T(128)S(1)} %pad_add_fusion.flags_ref, bf16[4096,1024]{1,0:T(8,128)(2,1)S(1)} %get-tuple-element.37.weight_ref, bf16[64,4096]{1,0:T(8,128)(2,1)S(1)} %bitcast.5, f32[128,1024]{1,0:T(8,128)S(1)} %get-tuple-element.38.held_ref, ...), custom_call_target="tpu_custom_call" | custom-call | tf_op jit(solution)/shard_map/pallas_call | solution.py:89
  34.2 1.6 %collective-permute-start.11 = (bf16[128,1024]{1,0:T(8,128)(2,1)S(1)}, bf16[128,1024]{1,0:T(8,128)(2,1)S(1)}, u32[]{:S(2)}, u32[]{:S(2)}) collective-permute-start(bf16[128,1024]{1,0:T(8,128)(2,1)S(1)} %get-tuple-element.46), channel_id=1, source_target_pairs={{0,2},{2,0},{1,3},{3,1},{4,6},{6,4},{5,7},{7,5},{8,10},{10,8},{9,1... | collective-permute-start | bytes 786440 | tf_op jit(solution)/shard_map/ppermute | solution.py:238
  35.7 0.6 collective-permute-start.6
  36.3 1.4 %collective-permute-done.3.last_ref = bf16[32,4096]{1,0:T(8,128)(2,1)S(1)} collective-permute-done((bf16[32,4096]{1,0:T(8,128)(2,1)S(1)}, bf16[32,4096]{1,0:T(8,128)(2,1)S(1)}, u32[]{:S(2)}, u32[]{:S(2)}) %collective-permute-start.3) | collective-permute-done | bytes 262176 | tf_op jit(solution)/shard_map/ppermute | solution.py:241
  37.9 0.5 collective-permute-start.9
  38.3 0.8 %collective-permute-done.10.fourth_ref = bf16[16,4096]{1,0:T(8,128)(2,1)S(1)} collective-permute-done((bf16[16,4096]{1,0:T(8,128)(2,1)S(1)}, bf16[16,4096]{1,0:T(8,128)(2,1)S(1)}, u32[]{:S(2)}, u32[]{:S(2)}) %collective-permute-start.10) | collective-permute-done | bytes 131104 | tf_op jit(solution)/shard_map/ppermute | solution.py:235
  39.2 0.2 collective-permute-done.9.third_ref
  39.4 2.7 %shard_map.84 = (f32[64,1024]{1,0:T(8,128)S(1)}, bf16[64,1024]{1,0:T(8,128)(2,1)S(1)}, f32[64,1024]{1,0:T(8,128)S(1)}, f32[192,64]{1,0:T(8,128)S(1)}) custom-call(s32[3]{0:T(128)S(1)} %pad_add_fusion.flags_ref, bf16[4096,1024]{1,0:T(8,128)(2,1)S(1)} %get-tuple-element.37.weight_ref, bf16[64,4096]{1,0:T(8,128)(2,1)S(1)} %bitcast.6, ...), custom_call_target="tpu_custom_call" | custom-call | tf_op jit(solution)/shard_map/pallas_call | solution.py:89
  42.1 0.5 collective-permute-done.11.refs_1_
  42.6 1.2 %collective-permute-done.6.mine_ref = bf16[32,4096]{1,0:T(8,128)(2,1)S(1)} collective-permute-done((bf16[32,4096]{1,0:T(8,128)(2,1)S(1)}, bf16[32,4096]{1,0:T(8,128)(2,1)S(1)}, u32[]{:S(2)}, u32[]{:S(2)}) %collective-permute-start.6) | collective-permute-done | bytes 262176 | tf_op jit(solution)/shard_map/ppermute | solution.py:241
  43.9 0.1 collective-permute-start.14
  43.9 0.5 collective-permute-start.13
  44.4 0.8 %collective-permute-done.14.second_ref = bf16[16,4096]{1,0:T(8,128)(2,1)S(1)} collective-permute-done((bf16[16,4096]{1,0:T(8,128)(2,1)S(1)}, bf16[16,4096]{1,0:T(8,128)(2,1)S(1)}, u32[]{:S(2)}, u32[]{:S(2)}) %collective-permute-start.14) | collective-permute-done | bytes 131104 | tf_op jit(solution)/shard_map/ppermute | solution.py:235
  45.3 0.2 collective-permute-done.13.first_ref
  45.5 2.3 %shard_map.85 = (f32[64,1024]{1,0:T(8,128)S(1)}, bf16[64,1024]{1,0:T(8,128)(2,1)S(1)}, f32[128,128]{1,0:T(8,128)S(1)}, bf16[128,128]{1,0:T(8,128)(2,1)S(1)}) custom-call(s32[3]{0:T(128)S(1)} %pad_add_fusion.flags_ref, bf16[4096,1024]{1,0:T(8,128)(2,1)S(1)} %get-tuple-element.37.weight_ref, bf16[64,4096]{1,0:T(8,128)(2,1)S(1)} %bitcast.7, ...), custom_call_target="tpu_custom_call" | custom-call | tf_op jit(solution)/shard_map/pallas_call | solution.py:89
  47.7 1.1 %collective-permute-start.16 = (bf16[128,128]{1,0:T(8,128)(2,1)S(1)}, bf16[128,128]{1,0:T(8,128)(2,1)S(1)}, u32[]{:S(2)}, u32[]{:S(2)}) collective-permute-start(bf16[128,128]{1,0:T(8,128)(2,1)S(1)} %get-tuple-element.61), channel_id=1, source_target_pairs={{0,2},{2,0},{1,3},{3,1},{4,6},{6,4},{5,7},{7,5},{8,10},{10,8},{9,1... | collective-permute-start | bytes 98312 | tf_op jit(solution)/shard_map/ppermute | solution.py:238
  48.8 1.0 %collective-permute-start.12 = (bf16[64,1024]{1,0:T(8,128)(2,1)S(1)}, bf16[64,1024]{1,0:T(8,128)(2,1)S(1)}, u32[]{:S(2)}, u32[]{:S(2)}) collective-permute-start(bf16[64,1024]{1,0:T(8,128)(2,1)S(1)} %get-tuple-element.50), channel_id=1, source_target_pairs={{0,2},{2,0},{1,3},{3,1},{4,6},{6,4},{5,7},{7,5},{8,10},{10,8},{9,1... | collective-permute-start | bytes 393224 | tf_op jit(solution)/shard_map/ppermute | solution.py:238
  49.8 1.1 %collective-permute-start.15 = (bf16[64,1024]{1,0:T(8,128)(2,1)S(1)}, bf16[64,1024]{1,0:T(8,128)(2,1)S(1)}, u32[]{:S(2)}, u32[]{:S(2)}) collective-permute-start(bf16[64,1024]{1,0:T(8,128)(2,1)S(1)} %get-tuple-element.57), channel_id=1, source_target_pairs={{0,2},{2,0},{1,3},{3,1},{4,6},{6,4},{5,7},{7,5},{8,10},{10,8},{9,1... | collective-permute-start | bytes 393224 | tf_op jit(solution)/shard_map/ppermute | solution.py:238
  50.9 1.0 %collective-permute-done.16 = bf16[128,128]{1,0:T(8,128)(2,1)S(1)} collective-permute-done((bf16[128,128]{1,0:T(8,128)(2,1)S(1)}, bf16[128,128]{1,0:T(8,128)(2,1)S(1)}, u32[]{:S(2)}, u32[]{:S(2)}) %collective-permute-start.16) | collective-permute-done | bytes 32800 | tf_op jit(solution)/shard_map/ppermute | solution.py:238
  51.9 0.9 %collective-permute-start.17 = (bf16[128,128]{1,0:T(8,128)(2,1)S(1)}, bf16[128,128]{1,0:T(8,128)(2,1)S(1)}, u32[]{:S(2)}, u32[]{:S(2)}) collective-permute-start(bf16[128,128]{1,0:T(8,128)(2,1)S(1)} %multiply_convert_fusion.refs_0_), channel_id=1, source_target_pairs={{0,4},{4,0},{8,12},{12,8},{1,9},{9,1},{5,13},{13,5},{2,6},{6,2},{1... | collective-permute-start | bytes 98312 | tf_op jit(solution)/shard_map/ppermute | solution.py:315
  52.8 3.1 %collective-permute-start.18 = (bf16[128,128]{1,0:T(8,128)(2,1)S(1)}, bf16[128,128]{1,0:T(8,128)(2,1)S(1)}, u32[]{:S(2)}, u32[]{:S(2)}) collective-permute-start(bf16[128,128]{1,0:T(8,128)(2,1)S(1)} %multiply_convert_fusion.refs_0_), channel_id=1, source_target_pairs={{0,12},{12,0},{4,8},{8,4},{1,13},{13,1},{5,9},{9,5},{2,14},{14,2},... | collective-permute-start | bytes 98312 | tf_op jit(solution)/shard_map/ppermute | solution.py:241
  55.9 1.4 %collective-permute-done.15.refs_5_ = bf16[64,1024]{1,0:T(8,128)(2,1)S(1)} collective-permute-done((bf16[64,1024]{1,0:T(8,128)(2,1)S(1)}, bf16[64,1024]{1,0:T(8,128)(2,1)S(1)}, u32[]{:S(2)}, u32[]{:S(2)}) %collective-permute-start.15) | collective-permute-done | bytes 131104 | tf_op jit(solution)/shard_map/ppermute | solution.py:238
  57.3 0.7 %shard_map.86.base_ref = f32[256,1024]{1,0:T(8,128)S(1)} custom-call(s32[3]{0:T(128)S(1)} %pad_add_fusion.flags_ref, bf16[256,1024]{1,0:T(8,128)(2,1)S(1)} %copy-done.2, f32[128,1024]{1,0:T(8,128)S(1)} %get-tuple-element.41.refs_0_, bf16[128,1024]{1,0:T(8,128)(2,1)S(1)} %collective-permute-done.11.refs_1_, f32[64,1024]{1,0:T(8,128)S(1)} %get-tuple-element.49.refs_2_, ...), custom_call_target="tpu_custom_call" | custom-call | tf_op jit(solution)/shard_map/pallas_call | solution.py:89
  58.1 0.4 collective-permute-done.18.refs_2_
  58.5 1.5 %shard_map.87 = bf16[256,1024]{1,0:T(8,128)(2,1)} custom-call(f32[256,1024]{1,0:T(8,128)S(1)} %shard_map.86.base_ref, bf16[4,256,64]{2,1,0:T(8,128)(2,1)S(1)} %broadcast_in_dim.24.hot_ref, bf16[4,64,1024]{2,1,0:T(8,128)(2,1)S(1)} %maximum_select_fusion.ups_ref, bf16[128,128]{1,0:T(8,128)(2,1)S(1)} %multiply_convert_fusion.refs_0_, ...), custom_call_target="tpu_custom_call" | custom-call | tf_op jit(solution)/shard_map/pallas_call | solution.py:89
  (22 shorter events, 0.2 us)
Async XLA Ops:
  0.0 16.3 %copy-start.3 = (bf16[2,64,1024]{2,1,0:T(8,128)(2,1)S(1)}, bf16[2,64,1024]{2,1,0:T(8,128)(2,1)}, u32[]{:S(2)}) copy-start(bf16[2,64,1024]{2,1,0:T(8,128)(2,1)} %param.12) | copy-start | bytes 786436
  1.1 27.4 %collective-permute-start.1 = (bf16[64,4096]{1,0:T(8,128)(2,1)S(1)}, bf16[64,4096]{1,0:T(8,128)(2,1)S(1)}, u32[]{:S(2)}, u32[]{:S(2)}) collective-permute-start(bf16[64,4096]{1,0:T(8,128)(2,1)S(1)} %constant_dynamic-slice_fusion), channel_id=1, source_target_pairs={{0,8},{8,0},{4,12},{12,4},{1,9},{9,1},{5,13},{13,5},{2,10},{10,2},... | collective-permute-start | bytes 1572872 | tf_op jit(solution)/shard_map/ppermute | solution.py:241
  5.2 23.5 %collective-permute-start = (bf16[64,4096]{1,0:T(8,128)(2,1)S(1)}, bf16[64,4096]{1,0:T(8,128)(2,1)S(1)}, u32[]{:S(2)}, u32[]{:S(2)}) collective-permute-start(bf16[64,4096]{1,0:T(8,128)(2,1)S(1)} %constant_dynamic-slice_fusion), channel_id=1, source_target_pairs={{0,4},{4,0},{8,12},{12,8},{1,5},{5,1},{9,13},{13,9},{2,6},{6,2},{1... | collective-permute-start | bytes 1572872 | tf_op jit(solution)/shard_map/ppermute | solution.py:241
  6.8 9.5 %collective-permute-start.2 = (bf16[2,64,1024]{2,1,0:T(8,128)(2,1)}, bf16[2,64,1024]{2,1,0:T(8,128)(2,1)S(1)}, u32[]{:S(2)}, u32[]{:S(2)}) collective-permute-start(bf16[2,64,1024]{2,1,0:T(8,128)(2,1)} %param.12), channel_id=1, source_target_pairs={{0,2},{2,0},{1,3},{3,1},{4,6},{6,4},{5,7},{7,5},{8,10},{10,8},{9,1... | collective-permute-start | bytes 786440 | tf_op jit(solution)/shard_map/ppermute | solution.py:238
  9.6 1.0 %copy-start = (bf16[1,64,4096]{2,1,0:T(8,128)(2,1)S(1)}, bf16[1,64,4096]{2,1,0:T(8,128)(2,1)}, u32[]{:S(2)}) copy-start(bf16[1,64,4096]{2,1,0:T(8,128)(2,1)} %param.11) | copy-start | bytes 1572868
  10.6 1.2 %copy-start.1 = (bf16[128,4096]{1,0:T(8,128)(2,1)S(1)}, bf16[128,4096]{1,0:T(8,128)(2,1)}, u32[]{:S(2)}) copy-start(bf16[128,4096]{1,0:T(8,128)(2,1)} %rows_ref.1) | copy-start | bytes 3145732
  28.9 2.4 %collective-permute-start.4 = (bf16[32,4096]{1,0:T(8,128)(2,1)S(1)}, bf16[32,4096]{1,0:T(8,128)(2,1)S(1)}, u32[]{:S(2)}, u32[]{:S(2)}) collective-permute-start(bf16[32,4096]{1,0:T(8,128)(2,1)S(1)} %get-tuple-element.72), channel_id=1, source_target_pairs={{0,1},{1,0},{2,3},{3,2},{4,5},{5,4},{6,7},{7,6},{8,9},{9,8},{10,11... | collective-permute-start | bytes 786440 | tf_op jit(solution)/shard_map/ppermute | solution.py:235
  29.0 8.7 %collective-permute-start.3 = (bf16[32,4096]{1,0:T(8,128)(2,1)S(1)}, bf16[32,4096]{1,0:T(8,128)(2,1)S(1)}, u32[]{:S(2)}, u32[]{:S(2)}) collective-permute-start(bf16[32,4096]{1,0:T(8,128)(2,1)S(1)} %get-tuple-element.72), channel_id=1, source_target_pairs={{0,4},{4,0},{8,12},{12,8},{1,5},{5,1},{9,13},{13,9},{2,6},{6,2},{1... | collective-permute-start | bytes 786440 | tf_op jit(solution)/shard_map/ppermute | solution.py:241
  30.6 1.5 %collective-permute-start.5 = (bf16[32,4096]{1,0:T(8,128)(2,1)S(1)}, bf16[32,4096]{1,0:T(8,128)(2,1)S(1)}, u32[]{:S(2)}, u32[]{:S(2)}) collective-permute-start(bf16[32,4096]{1,0:T(8,128)(2,1)S(1)} %get-tuple-element.42), channel_id=1, source_target_pairs={{0,1},{1,0},{2,3},{3,2},{4,5},{5,4},{6,7},{7,6},{8,9},{9,8},{10,11... | collective-permute-start | bytes 786440 | tf_op jit(solution)/shard_map/ppermute | solution.py:235
  30.8 7.1 %collective-permute-start.8 = (bf16[32,4096]{1,0:T(8,128)(2,1)S(1)}, bf16[32,4096]{1,0:T(8,128)(2,1)S(1)}, u32[]{:S(2)}, u32[]{:S(2)}) collective-permute-start(bf16[32,4096]{1,0:T(8,128)(2,1)S(1)} %get-tuple-element.69), channel_id=1, source_target_pairs={{0,1},{1,0},{2,3},{3,2},{4,5},{5,4},{6,7},{7,6},{8,9},{9,8},{10,11... | collective-permute-start | bytes 786440 | tf_op jit(solution)/shard_map/ppermute | solution.py:235
  31.2 7.2 %collective-permute-start.7 = (bf16[32,4096]{1,0:T(8,128)(2,1)S(1)}, bf16[32,4096]{1,0:T(8,128)(2,1)S(1)}, u32[]{:S(2)}, u32[]{:S(2)}) collective-permute-start(bf16[32,4096]{1,0:T(8,128)(2,1)S(1)} %get-tuple-element.70), channel_id=1, source_target_pairs={{0,1},{1,0},{2,3},{3,2},{4,5},{5,4},{6,7},{7,6},{8,9},{9,8},{10,11... | collective-permute-start | bytes 786440 | tf_op jit(solution)/shard_map/ppermute | solution.py:235
  34.2 8.4 %collective-permute-start.11 = (bf16[128,1024]{1,0:T(8,128)(2,1)S(1)}, bf16[128,1024]{1,0:T(8,128)(2,1)S(1)}, u32[]{:S(2)}, u32[]{:S(2)}) collective-permute-start(bf16[128,1024]{1,0:T(8,128)(2,1)S(1)} %get-tuple-element.46), channel_id=1, source_target_pairs={{0,2},{2,0},{1,3},{3,1},{4,6},{6,4},{5,7},{7,5},{8,10},{10,8},{9,1... | collective-permute-start | bytes 786440 | tf_op jit(solution)/shard_map/ppermute | solution.py:238
  35.7 8.1 %collective-permute-start.6 = (bf16[32,4096]{1,0:T(8,128)(2,1)S(1)}, bf16[32,4096]{1,0:T(8,128)(2,1)S(1)}, u32[]{:S(2)}, u32[]{:S(2)}) collective-permute-start(bf16[32,4096]{1,0:T(8,128)(2,1)S(1)} %get-tuple-element.42), channel_id=1, source_target_pairs={{0,4},{4,0},{8,12},{12,8},{1,5},{5,1},{9,13},{13,9},{2,6},{6,2},{1... | collective-permute-start | bytes 786440 | tf_op jit(solution)/shard_map/ppermute | solution.py:241
  37.8 1.4 %collective-permute-start.10 = (bf16[16,4096]{1,0:T(8,128)(2,1)S(1)}, bf16[16,4096]{1,0:T(8,128)(2,1)S(1)}, u32[]{:S(2)}, u32[]{:S(2)}) collective-permute-start(bf16[16,4096]{1,0:T(8,128)(2,1)S(1)} %get-tuple-element.75), channel_id=1, source_target_pairs={{0,1},{1,0},{2,3},{3,2},{4,5},{5,4},{6,7},{7,6},{8,9},{9,8},{10,11... | collective-permute-start | bytes 393224 | tf_op jit(solution)/shard_map/ppermute | solution.py:235
  37.8 19.5 %copy-start.2 = (bf16[256,1024]{1,0:T(8,128)(2,1)S(1)}, bf16[256,1024]{1,0:T(8,128)(2,1)}, u32[]{:S(2)}) copy-start(bf16[256,1024]{1,0:T(8,128)(2,1)} %residual_ref.1) | copy-start | bytes 1572868
  37.9 1.5 %collective-permute-start.9 = (bf16[16,4096]{1,0:T(8,128)(2,1)S(1)}, bf16[16,4096]{1,0:T(8,128)(2,1)S(1)}, u32[]{:S(2)}, u32[]{:S(2)}) collective-permute-start(bf16[16,4096]{1,0:T(8,128)(2,1)S(1)} %get-tuple-element.76), channel_id=1, source_target_pairs={{0,1},{1,0},{2,3},{3,2},{4,5},{5,4},{6,7},{7,6},{8,9},{9,8},{10,11... | collective-permute-start | bytes 393224 | tf_op jit(solution)/shard_map/ppermute | solution.py:235
  43.9 1.4 %collective-permute-start.14 = (bf16[16,4096]{1,0:T(8,128)(2,1)S(1)}, bf16[16,4096]{1,0:T(8,128)(2,1)S(1)}, u32[]{:S(2)}, u32[]{:S(2)}) collective-permute-start(bf16[16,4096]{1,0:T(8,128)(2,1)S(1)} %get-tuple-element.73), channel_id=1, source_target_pairs={{0,1},{1,0},{2,3},{3,2},{4,5},{5,4},{6,7},{7,6},{8,9},{9,8},{10,11... | collective-permute-start | bytes 393224 | tf_op jit(solution)/shard_map/ppermute | solution.py:235
  43.9 1.5 %collective-permute-start.13 = (bf16[16,4096]{1,0:T(8,128)(2,1)S(1)}, bf16[16,4096]{1,0:T(8,128)(2,1)S(1)}, u32[]{:S(2)}, u32[]{:S(2)}) collective-permute-start(bf16[16,4096]{1,0:T(8,128)(2,1)S(1)} %get-tuple-element.74), channel_id=1, source_target_pairs={{0,1},{1,0},{2,3},{3,2},{4,5},{5,4},{6,7},{7,6},{8,9},{9,8},{10,11... | collective-permute-start | bytes 393224 | tf_op jit(solution)/shard_map/ppermute | solution.py:235
  47.7 4.2 %collective-permute-start.16 = (bf16[128,128]{1,0:T(8,128)(2,1)S(1)}, bf16[128,128]{1,0:T(8,128)(2,1)S(1)}, u32[]{:S(2)}, u32[]{:S(2)}) collective-permute-start(bf16[128,128]{1,0:T(8,128)(2,1)S(1)} %get-tuple-element.61), channel_id=1, source_target_pairs={{0,2},{2,0},{1,3},{3,1},{4,6},{6,4},{5,7},{7,5},{8,10},{10,8},{9,1... | collective-permute-start | bytes 98312 | tf_op jit(solution)/shard_map/ppermute | solution.py:238
  48.8 7.1 %collective-permute-start.12 = (bf16[64,1024]{1,0:T(8,128)(2,1)S(1)}, bf16[64,1024]{1,0:T(8,128)(2,1)S(1)}, u32[]{:S(2)}, u32[]{:S(2)}) collective-permute-start(bf16[64,1024]{1,0:T(8,128)(2,1)S(1)} %get-tuple-element.50), channel_id=1, source_target_pairs={{0,2},{2,0},{1,3},{3,1},{4,6},{6,4},{5,7},{7,5},{8,10},{10,8},{9,1... | collective-permute-start | bytes 393224 | tf_op jit(solution)/shard_map/ppermute | solution.py:238
  49.8 7.5 %collective-permute-start.15 = (bf16[64,1024]{1,0:T(8,128)(2,1)S(1)}, bf16[64,1024]{1,0:T(8,128)(2,1)S(1)}, u32[]{:S(2)}, u32[]{:S(2)}) collective-permute-start(bf16[64,1024]{1,0:T(8,128)(2,1)S(1)} %get-tuple-element.57), channel_id=1, source_target_pairs={{0,2},{2,0},{1,3},{3,1},{4,6},{6,4},{5,7},{7,5},{8,10},{10,8},{9,1... | collective-permute-start | bytes 393224 | tf_op jit(solution)/shard_map/ppermute | solution.py:238
  51.9 4.0 %collective-permute-start.17 = (bf16[128,128]{1,0:T(8,128)(2,1)S(1)}, bf16[128,128]{1,0:T(8,128)(2,1)S(1)}, u32[]{:S(2)}, u32[]{:S(2)}) collective-permute-start(bf16[128,128]{1,0:T(8,128)(2,1)S(1)} %multiply_convert_fusion.refs_0_), channel_id=1, source_target_pairs={{0,4},{4,0},{8,12},{12,8},{1,9},{9,1},{5,13},{13,5},{2,6},{6,2},{1... | collective-permute-start | bytes 98312 | tf_op jit(solution)/shard_map/ppermute | solution.py:315
  52.8 5.7 %collective-permute-start.18 = (bf16[128,128]{1,0:T(8,128)(2,1)S(1)}, bf16[128,128]{1,0:T(8,128)(2,1)S(1)}, u32[]{:S(2)}, u32[]{:S(2)}) collective-permute-start(bf16[128,128]{1,0:T(8,128)(2,1)S(1)} %multiply_convert_fusion.refs_0_), channel_id=1, source_target_pairs={{0,12},{12,0},{4,8},{8,4},{1,13},{13,1},{5,9},{9,5},{2,14},{14,2},... | collective-permute-start | bytes 98312 | tf_op jit(solution)/shard_map/ppermute | solution.py:241
  55.9 2.6 %collective-permute-start.19 = (bf16[128,128]{1,0:T(8,128)(2,1)S(1)}, bf16[128,128]{1,0:T(8,128)(2,1)S(1)}, u32[]{:S(2)}, u32[]{:S(2)}) collective-permute-start(bf16[128,128]{1,0:T(8,128)(2,1)S(1)} %collective-permute-done.17.refs_1_), channel_id=1, source_target_pairs={{0,1},{1,0},{2,3},{3,2},{4,5},{5,4},{6,7},{7,6},{8,9},{9,8},{10,11... | collective-permute-start | bytes 98312 | tf_op jit(solution)/shard_map/ppermute | solution.py:235

commit v14 on v13

--- a/solution.py
+++ b/solution.py
@@ -1,3 +1,5 @@
+import functools
+
 import jax
 import jax.numpy as jnp
 from jax import lax
@@ -136,73 +138,75 @@
         sum_ref[:, tile] = dot(rows, held_ref[:, tile])
 
 
-def far_kernel(
-    flags_ref, weight_ref, down_ref, held_ref, mine_ref, first_ref, second_ref,
+def rows_of(piece, step):
+    return [slice((2 * core + piece) * step, (2 * core + piece + 1) * step) for core in (0, 1)]
+
+
+def in_block(first, second):
+    step = first.shape[0] // 2
+    return jnp.concatenate([first[:step], second[:step], first[step:], second[step:]])
+
+
+def piece_kernel(
+    piece, flags_ref, weight_ref, down_ref, held_ref, mine_ref, first_ref, second_ref,
     keep_ref, send_ref, low_ref,
 ):
     other = jnp.concatenate([first_ref[...], second_ref[...]])
     rows = joined(flags_ref, mine_ref[...], other)
     low_ref[...] = low_product(rows, down_ref)
+    here = rows_of(piece, mine_ref.shape[0])
+    for tile in column_tiles(weight_ref.shape[1]):
+        held = jnp.concatenate([held_ref[at, tile] for at in here])
+        part(flags_ref, held, dot(rows, weight_ref[:, tile]), keep_ref, send_ref, tile)
+
+
+def near_kernel(
+    flags_ref, weight_ref, down_ref, held_ref, mine_ref, first_ref, second_ref, near_ref,
+    near_too_ref, third_ref, fourth_ref, keep_ref, send_ref, near_sum_ref, low_ref,
+):
+    other = jnp.concatenate([first_ref[...], second_ref[...]])
+    far = joined(flags_ref, mine_ref[...], other)
+    mine = jnp.concatenate([near_ref[...], near_too_ref[...]])
+    other = jnp.concatenate([third_ref[...], fourth_ref[...]])
+    near = joined(flags_ref, mine, other)
+    rows = jnp.concatenate([near, far])
+    low_ref[...] = low_product(rows, down_ref)
+    here = rows_of(1, mine_ref.shape[0])
+    block = near.shape[0]
     for tile in column_tiles(weight_ref.shape[1]):
         value = dot(rows, weight_ref[:, tile])
-        part(flags_ref, held_ref[:, tile], value, keep_ref, send_ref, tile)
-
-
-def near_kernel(
-    flags_ref, weight_ref, down_ref, mine_ref, first_ref, second_ref, last_ref, third_ref,
-    fourth_ref, keep_ref, send_ref, hold_ref, low_ref,
-):
-    other = jnp.concatenate([first_ref[...], second_ref[...]])
-    near = joined(flags_ref, mine_ref[...], other)
-    last = joined(flags_ref, last_ref[...], jnp.concatenate([third_ref[...], fourth_ref[...]]))
-    rows = jnp.concatenate([near, last])
-    low_ref[...] = low_product(rows, down_ref)
-    step = last_ref.shape[0]
-    for tile in column_tiles(weight_ref.shape[1]):
-        value = dot(rows, weight_ref[:, tile])
-        held = jnp.concatenate([value[:step], value[2 * step : 3 * step]])
-        part(flags_ref, held, value[4 * step :], keep_ref, send_ref, tile)
-        hold_ref[:, tile] = jnp.concatenate(
-            [value[step : 2 * step], value[3 * step : 4 * step]]
-        )
+        near_sum_ref[:, tile] = value[:block]
+        held = jnp.concatenate([held_ref[at, tile] for at in here])
+        part(flags_ref, held, value[block:], keep_ref, send_ref, tile)
 
 
 def last_kernel(
-    flags_ref, weight_ref, down_ref, held_ref, own_low, far_low, near_low, mine_ref, first_ref,
+    flags_ref, weight_ref, down_ref, held_ref, own_low, low_a, low_b, low_c, mine_ref, first_ref,
     second_ref, keep_ref, send_ref, low_keep_ref, low_send_ref,
 ):
     other = jnp.concatenate([first_ref[...], second_ref[...]])
     rows = joined(flags_ref, mine_ref[...], other)
     low = low_product(rows, down_ref)
     block, width = own_low.shape
-    step = mine_ref.shape[0]
-    last_low = jnp.concatenate(
-        [
-            near_low[block : block + step], low[:step],
-            near_low[block + step :], low[step:],
-        ]
-    )
     odd, home = flags_ref[2] == 1, flags_ref[0] == 1
-    near = own_low[...], near_low[:block]
-    far = far_low[...], last_low
+    near = own_low[...], low_b[:block]
+    far = in_block(low_a[...], low_b[block:]), in_block(low_c[...], low)
     for side, here in ((0, slice(0, width)), (1, slice(width, 2 * width))):
         near_side = jnp.where(odd, near[1 - side], near[side])
         far_side = jnp.where(odd, far[1 - side], far[side])
         low_keep_ref[:, here] = jnp.where(home, near_side, far_side)
         low_send_ref[:, here] = jnp.where(home, far_side, near_side).astype(BF16)
+    here = rows_of(1, mine_ref.shape[0])
     for tile in column_tiles(weight_ref.shape[1]):
-        value = dot(rows, weight_ref[:, tile])
-        part(flags_ref, held_ref[:, tile], value, keep_ref, send_ref, tile)
+        held = jnp.concatenate([held_ref[at, tile] for at in here])
+        part(flags_ref, held, dot(rows, weight_ref[:, tile]), keep_ref, send_ref, tile)
 
 
 def base_kernel(flags_ref, residual_ref, *refs):
     *parts, out_ref = refs
     odd = flags_ref[2] == 1
-    first, left, right = [
-        keep[...] + got[...].astype(F32) for keep, got in zip(parts[::2], parts[1::2])
-    ]
-    step = left.shape[0] // 2
-    second = jnp.concatenate([left[:step], right[:step], left[step:], right[step:]])
+    sums = [keep[...] + got[...].astype(F32) for keep, got in zip(parts[::2], parts[1::2])]
+    first, second = in_block(*sums[:2]), in_block(*sums[2:])
     block = first.shape[0]
     for at, base in ((0, jnp.where(odd, second, first)), (block, jnp.where(odd, first, second))):
         here = slice(at, at + block)
@@ -262,10 +266,11 @@
     hot = slot[None, :] == jnp.arange(slots, dtype=jnp.int32)[:, None]
     hot = jnp.broadcast_to(hot[:, :, None], (slots, own, width)).astype(BF16)
 
-    mine = lax.dynamic_slice_in_dim(rows, c * half, half, 0)
-    near, far = along(mine, NEAR), along(mine, FAR)
-    up_other = over_x(up)
-    ups = jnp.where(x == 0, jnp.concatenate([up, up_other]), jnp.concatenate([up_other, up]))
+    def cut(rows, piece):
+        return lax.dynamic_slice_in_dim(rows, c * half + piece * step, step, 0)
+
+    mine = cut(rows, 0)
+    far, near = [along(mine, FAR)], [along(mine, NEAR)]
     held, own_sum, own_low = call(
         own_kernel,
         [shape(weight.shape, BF16), shape((block_rows, cols), F32)] + lows(block_rows),
@@ -274,38 +279,49 @@
         [pltpu.SemaphoreType.DMA((len(column_tiles(cols)),))],
         FROM_HBM,
     )
-    near, far, own_sum, own_low, ups, hot, scale = barrier(
-        (near, far, own_sum, own_low, ups, hot, scale)
-    )
-
-    last = [along(far[:step], NEAR)]
-    far_others = over_core_in_two(far)
-    far_second, far_others[0] = barrier((far[step:], far_others[0]))
-    last.append(along(far_second, NEAR))
-    kept_a, sent_a, far_low = call(
-        far_kernel,
-        parted(block_rows) + lows(block_rows),
-        [SMEM] + [VMEM] * 6,
-        [flags, held, down[0], own_sum, far] + far_others,
-    )
-    got_a = over_x(sent_a)
-    last[0], kept_a = barrier((last[0], kept_a))
-
-    kept_c, sent_c, hold, near_low = call(
+    up, rows, own_sum = barrier((up, rows, own_sum))
+    mine = cut(rows, 1)
+    far.append(along(mine, FAR))
+    near.append(along(mine, NEAR))
+    up_other = over_x(up)
+    ups = jnp.where(x == 0, jnp.concatenate([up, up_other]), jnp.concatenate([up_other, up]))
+    far[0], own_sum, own_low = barrier((far[0], own_sum, own_low))
+
+    def parted_piece(piece, against, value):
+        return call(
+            functools.partial(piece_kernel, piece),
+            parted(half) + lows(half),
+            [SMEM] + [VMEM] * 6,
+            [flags, held, down[0], against, value] + over_core_in_two(value),
+        )
+
+    last = [along(far[0], NEAR)]
+    kept_a, sent_a, low_a = parted_piece(0, own_sum, far[0])
+    got_a = jnp.concatenate([over_x(sent_a[:step]), over_x(sent_a[step:])])
+    near, far[1], own_sum, ups, hot, scale, got_a = barrier(
+        (near, far[1], own_sum, ups, hot, scale, got_a)
+    )
+
+    last.append(along(far[1], NEAR))
+    kept_b, sent_b, near_sum, low_b = call(
         near_kernel,
-        parted(half) + [shape((half, cols), F32)] + lows(block_rows + half),
-        [SMEM] + [VMEM] * 8,
-        [flags, held, down[0], near] + over_core_in_two(near)
-        + [last[0]] + over_core_in_two(last[0]),
-    )
+        parted(half) + [shape((block_rows, cols), F32)] + lows(block_rows + half),
+        [SMEM] + [VMEM] * 10,
+        [flags, held, down[0], own_sum, far[1]] + over_core_in_two(far[1])
+        + near + [over_core(piece) for piece in near],
+    )
+    got_b = over_x(sent_b)
+    last[0], kept_b = barrier((last[0], kept_b))
+
+    kept_c, sent_c, low_c = parted_piece(0, near_sum, last[0])
     got_c = over_x(sent_c)
-    last[1], hold, got_a, near_low = barrier((last[1], hold, got_a, near_low))
+    last[1], near_sum, got_b, low_c = barrier((last[1], near_sum, got_b, low_c))
 
     kept_d, sent_d, low, low_sent = call(
         last_kernel,
         parted(half) + [shape((block_rows, 2 * width), dtype) for dtype in (F32, BF16)],
-        [SMEM] + [VMEM] * 9,
-        [flags, held, down[0], hold, own_low, far_low, near_low, last[1]]
+        [SMEM] + [VMEM] * 10,
+        [flags, held, down[0], near_sum, own_low, low_a, low_b, low_c, last[1]]
         + over_core_in_two(last[1]),
     )
     got_d = over_x(sent_d)
@@ -319,8 +335,8 @@
     base = call(
         base_kernel,
         shape(residual.shape, F32),
-        [SMEM] + [VMEM] * 7,
-        [flags, residual, kept_a, got_a, kept_c, got_c, kept_d, got_d],
+        [SMEM] + [VMEM] * 9,
+        [flags, residual, kept_a, got_a, kept_b, got_b, kept_c, got_c, kept_d, got_d],
     )
     return call(
         final_kernel,

time: 60.2 us -> 65.2 us (1.083)
  local copies, waits for them, and re-layouts: 3.71 us -> 11.2 us
  waiting for transfers between devices: 21.1 us -> 16.4 us
  Pallas kernels: 13.7 us -> 16.2 us
  other arithmetic: 1.37 us -> 0.7 us
    ppermute x5 -> x7, waiting for transfers between devices: 15.3 us -> 5.62 us  [along(): return lax.ppermute(value, 'blk', pairs)]
    unnamed x8 -> x20, local copies, waits for them, and re-layouts: 2.28 us -> 8.94 us
    ppermute x5 -> x7, waiting for transfers between devices: 2.96 us -> 6.1 us  [over_x(): return lax.ppermute(value, 'split', SWAP)]
    pallas_call x6 -> x7, Pallas kernels: 13.7 us -> 16.2 us  [call(): pl.pallas_call(kernel, out_shape=outs, in_specs=in_specs, out_specs=jax.t...]
    ppermute x5 -> x7, starting transfers between devices: 11 us -> 8.75 us  [along(): return lax.ppermute(value, 'blk', pairs)]
    ppermute x1, waiting for transfers between devices: 0.01 us -> 1.34 us  [line(): lax.ppermute(scaled, ('blk', 'sub'), by_core(NEAR, FAR))]
    ppermute x1, starting transfers between devices: 0.86 us -> 1.82 us  [line(): lax.ppermute(scaled, ('blk', 'sub'), by_core(NEAR, FAR))]
    ppermute x9 -> x11, starting transfers between devices: 1.93 us -> 2.86 us  [over_core(): return lax.ppermute(value, 'sub', SWAP)]
  transfers between devices with their start and end apart: 20 -> 26, of which waited for: 13 -> 15; matrix products, arithmetic and copies ran while one was open for 2% -> 3% of each run, Pallas kernels for 17% -> 19%
where the time goes in v14:
time: 65.2 us; the launch traced here: 64.9 us
  starting transfers between devices  20.2 us (31%)
  waiting for transfers between devices  16.4 us (25%)
  Pallas kernels  16.2 us (25%)
  local copies, waits for them, and re-layouts  11.2 us (17%)
  other arithmetic  0.7 us (1%)
    pallas_call x7, Pallas kernels, call(): pl.pallas_call(kernel, out_shape=outs, in_specs=in_specs, out_specs=jax.t...  16.2 us
    unnamed x20, local copies, waits for them, and re-layouts  8.94 us
    ppermute x7, starting transfers between devices, along(): return lax.ppermute(value, 'blk', pairs)  8.75 us
    ppermute x7, starting transfers between devices, over_x(): return lax.ppermute(value, 'split', SWAP)  6.74 us
    ppermute x7, waiting for transfers between devices, over_x(): return lax.ppermute(value, 'split', SWAP)  6.1 us
    ppermute x7, waiting for transfers between devices, along(): return lax.ppermute(value, 'blk', pairs)  5.62 us
    ppermute x11, waiting for transfers between devices, over_core(): return lax.ppermute(value, 'sub', SWAP)  3.34 us
    ppermute x11, starting transfers between devices, over_core(): return lax.ppermute(value, 'sub', SWAP)  2.86 us
  transfers between devices with their start and end apart: 26, of which 15 were waited for; matrix products, arithmetic and copies ran while one was open for 3% of the time, Pallas kernels for 19%

profile of v14, /device:TPU:0, one launch (start us, length us, event | category | flops | bytes accessed | tf_op | source)
XLA Modules:
  0.0 64.9 jit_solution(16879387017148627801)
XLA Ops:
  0.0 1.0 %constant_dynamic-slice_fusion.1 = bf16[32,4096]{1,0:T(8,128)(2,1)S(1)} fusion(bf16[128,4096]{1,0:T(8,128)(2,1)} %rows_ref.1, s32[]{:T(128)S(6)} %select_n.39), kind=kLoop, calls=%fused_computation.15 | loop fusion | bytes 524292 | tf_op jit(solution)/shard_map/dynamic_slice | solution.py:270
  1.0 3.1 %collective-permute-start.3 = (bf16[32,4096]{1,0:T(8,128)(2,1)S(1)}, bf16[32,4096]{1,0:T(8,128)(2,1)S(1)}, u32[]{:S(2)}, u32[]{:S(2)}) collective-permute-start(bf16[32,4096]{1,0:T(8,128)(2,1)S(1)} %constant_dynamic-slice_fusion.1), channel_id=1, source_target_pairs={{0,4},{4,0},{8,12},{12,8},{1,5},{5,1},{9,13},{13,9},{2,6},{6,2},{1... | collective-permute-start | bytes 786440 | tf_op jit(solution)/shard_map/ppermute | solution.py:245
  4.1 2.6 %collective-permute-start = (bf16[32,4096]{1,0:T(8,128)(2,1)S(1)}, bf16[32,4096]{1,0:T(8,128)(2,1)S(1)}, u32[]{:S(2)}, u32[]{:S(2)}) collective-permute-start(bf16[32,4096]{1,0:T(8,128)(2,1)S(1)} %constant_dynamic-slice_fusion.1), channel_id=1, source_target_pairs={{0,8},{8,0},{4,12},{12,4},{1,9},{9,1},{5,13},{13,5},{2,10},{10,2},... | collective-permute-start | bytes 786440 | tf_op jit(solution)/shard_map/ppermute | solution.py:245
  6.7 1.0 %copy-done.2 = bf16[1,64,4096]{2,1,0:T(8,128)(2,1)S(1)} copy-done((bf16[1,64,4096]{2,1,0:T(8,128)(2,1)S(1)}, bf16[1,64,4096]{2,1,0:T(8,128)(2,1)}, u32[]{:S(2)}) %copy-start.2) | copy-done | bytes 524312
  7.8 1.2 %copy-done.4 = bf16[128,4096]{1,0:T(8,128)(2,1)S(1)} copy-done((bf16[128,4096]{1,0:T(8,128)(2,1)S(1)}, bf16[128,4096]{1,0:T(8,128)(2,1)}, u32[]{:S(2)}) %copy-start.4) | copy-done | bytes 1048600
  9.0 4.5 %shard_map.82 = (bf16[4096,1024]{1,0:T(8,128)(2,1)S(1)}, f32[128,1024]{1,0:T(8,128)S(1)}, f32[128,64]{1,0:T(8,128)S(1)}) custom-call(bf16[4096,1024]{1,0:T(8,128)(2,1)} %weight_ref.1, bf16[64,4096]{1,0:T(8,128)(2,1)S(1)} %bitcast.4, bf16[128,4096]{1,0:T(8,128)(2,1)S(1)} %copy-done.4), custom_call_target="tpu_custom_call" | custom-call | tf_op jit(solution)/shard_map/pallas_call | solution.py:91
  13.5 3.3 %copy-done = bf16[4096,1024]{1,0:T(8,128)(2,1)} copy-done((bf16[4096,1024]{1,0:T(8,128)(2,1)}, bf16[4096,1024]{1,0:T(8,128)(2,1)S(1)}, u32[]{:S(2)}) %copy-start) | copy-done | bytes 8388632
  16.7 1.0 %constant_dynamic-slice_fusion = bf16[32,4096]{1,0:T(8,128)(2,1)S(1)} fusion(bf16[128,4096]{1,0:T(8,128)(2,1)} %rows_ref.1, s32[]{:T(128)S(6)} %select_n.40), kind=kLoop, calls=%fused_computation.14 | loop fusion | bytes 524292 | tf_op jit(solution)/shard_map/dynamic_slice | solution.py:270
  17.7 0.4 collective-permute-start.5
  18.1 1.5 %collective-permute-start.6 = (bf16[2,64,1024]{2,1,0:T(8,128)(2,1)S(1)}, bf16[2,64,1024]{2,1,0:T(8,128)(2,1)S(1)}, u32[]{:S(2)}, u32[]{:S(2)}) collective-permute-start(bf16[2,64,1024]{2,1,0:T(8,128)(2,1)S(1)} %copy-done.6), channel_id=1, source_target_pairs={{0,2},{2,0},{1,3},{3,1},{4,6},{6,4},{5,7},{7,5},{8,10},{10,8},{9,1... | collective-permute-start | bytes 786440 | tf_op jit(solution)/shard_map/ppermute | solution.py:242
  20.2 0.5 collective-permute-start.1
  20.9 0.6 collective-permute-done.2.second_ref
  21.5 0.4 collective-permute-start.4
  22.0 3.4 %copy-done.1 = bf16[4096,1024]{1,0:T(8,128)(2,1)S(1)} copy-done((bf16[4096,1024]{1,0:T(8,128)(2,1)S(1)}, bf16[4096,1024]{1,0:T(8,128)(2,1)}, u32[]{:S(2)}) %copy-start.1) | copy-done | bytes 8388632
  25.4 2.2 %shard_map.83 = (f32[64,1024]{1,0:T(8,128)S(1)}, bf16[64,1024]{1,0:T(8,128)(2,1)S(1)}, f32[64,64]{1,0:T(8,128)S(1)}) custom-call(s32[3]{0:T(128)S(1)} %pad_add_fusion.flags_ref, bf16[4096,1024]{1,0:T(8,128)(2,1)S(1)} %copy-done.1, bf16[64,4096]{1,0:T(8,128)(2,1)S(1)} %bitcast.5, f32[128,1024]{1,0:T(8,128)S(1)} %get-tuple-element.53.held_ref, ...), custom_call_target="tpu_custom_call" | custom-call | tf_op jit(solution)/shard_map/pallas_call | solution.py:91
  27.6 0.3 collective-permute-start.7
  28.0 1.7 %collective-permute-start.8 = (bf16[32,1024]{1,0:T(8,128)(2,1)S(1)}, bf16[32,1024]{1,0:T(8,128)(2,1)S(1)}, u32[]{:S(2)}, u32[]{:S(2)}) collective-permute-start(bf16[32,1024]{1,0:T(8,128)(2,1)S(1)} %get-tuple-element.94), channel_id=1, source_target_pairs={{0,2},{2,0},{1,3},{3,1},{4,6},{6,4},{5,7},{7,5},{8,10},{10,8},{9,1... | collective-permute-start | bytes 196616 | tf_op jit(solution)/shard_map/ppermute | solution.py:242
  29.8 2.6 %collective-permute-done.7 = bf16[32,1024]{1,0:T(8,128)(2,1)S(1)} collective-permute-done((bf16[32,1024]{1,0:T(8,128)(2,1)S(1)}, bf16[32,1024]{1,0:T(8,128)(2,1)S(1)}, u32[]{:S(2)}, u32[]{:S(2)}) %collective-permute-start.7) | collective-permute-done | bytes 65568 | tf_op jit(solution)/shard_map/ppermute | solution.py:242
  32.5 1.4 %collective-permute-start.9 = (bf16[32,4096]{1,0:T(8,128)(2,1)S(1)}, bf16[32,4096]{1,0:T(8,128)(2,1)S(1)}, u32[]{:S(2)}, u32[]{:S(2)}) collective-permute-start(bf16[32,4096]{1,0:T(8,128)(2,1)S(1)} %collective-permute-done.mine_ref), channel_id=1, source_target_pairs={{0,4},{4,0},{8,12},{12,8},{1,5},{5,1},{9,13},{13,9},{2,6},{6,2},{1... | collective-permute-start | bytes 786440 | tf_op jit(solution)/shard_map/ppermute | solution.py:245
  33.9 2.3 %collective-permute-done.4.near_too_ref = bf16[32,4096]{1,0:T(8,128)(2,1)S(1)} collective-permute-done((bf16[32,4096]{1,0:T(8,128)(2,1)S(1)}, bf16[32,4096]{1,0:T(8,128)(2,1)S(1)}, u32[]{:S(2)}, u32[]{:S(2)}) %collective-permute-start.4) | collective-permute-done | bytes 262176 | tf_op jit(solution)/shard_map/ppermute | solution.py:245
  36.2 0.2 broadcast_in_dim.24.hot_ref
  36.5 0.5 collective-permute-start.13
  37.1 0.4 collective-permute-start.10
  37.6 1.0 %collective-permute-done.11.second_ref = bf16[16,4096]{1,0:T(8,128)(2,1)S(1)} collective-permute-done((bf16[16,4096]{1,0:T(8,128)(2,1)S(1)}, bf16[16,4096]{1,0:T(8,128)(2,1)S(1)}, u32[]{:S(2)}, u32[]{:S(2)}) %collective-permute-start.11) | collective-permute-done | bytes 131104 | tf_op jit(solution)/shard_map/ppermute | solution.py:239
  38.8 2.7 %shard_map.84 = (f32[64,1024]{1,0:T(8,128)S(1)}, bf16[64,1024]{1,0:T(8,128)(2,1)S(1)}, f32[128,1024]{1,0:T(8,128)S(1)}, f32[192,64]{1,0:T(8,128)S(1)}) custom-call(s32[3]{0:T(128)S(1)} %pad_add_fusion.flags_ref, bf16[4096,1024]{1,0:T(8,128)(2,1)S(1)} %copy-done.1, bf16[64,4096]{1,0:T(8,128)(2,1)S(1)} %bitcast.6, f32[128,1024]{1,0:T(8,128)S(1)} %get-tuple-element.53.held_ref, ...), custom_call_target="tpu_custom_call" | custom-call | tf_op jit(solution)/shard_map/pallas_call | solution.py:91
  41.5 0.2 collective-permute-start.17
  41.8 0.3 collective-permute-start.16
  42.1 0.5 collective-permute-start.15
  42.7 0.3 collective-permute-done.17.second_ref
  43.0 0.2 collective-permute-done.16.first_ref
  43.1 2.3 %shard_map.85 = (f32[64,1024]{1,0:T(8,128)S(1)}, bf16[64,1024]{1,0:T(8,128)(2,1)S(1)}, f32[64,64]{1,0:T(8,128)S(1)}) custom-call(s32[3]{0:T(128)S(1)} %pad_add_fusion.flags_ref, bf16[4096,1024]{1,0:T(8,128)(2,1)S(1)} %copy-done.1, bf16[64,4096]{1,0:T(8,128)(2,1)S(1)} %bitcast.7, f32[128,1024]{1,0:T(8,128)S(1)} %get-tuple-element.66.held_ref, ...), custom_call_target="tpu_custom_call" | custom-call | tf_op jit(solution)/shard_map/pallas_call | solution.py:91
  45.4 1.5 %collective-permute-done.14.mine_ref = bf16[32,4096]{1,0:T(8,128)(2,1)S(1)} collective-permute-done((bf16[32,4096]{1,0:T(8,128)(2,1)S(1)}, bf16[32,4096]{1,0:T(8,128)(2,1)S(1)}, u32[]{:S(2)}, u32[]{:S(2)}) %collective-permute-start.14) | collective-permute-done | bytes 262176 | tf_op jit(solution)/shard_map/ppermute | solution.py:245
  46.9 0.8 %collective-permute-done.15.refs_3_ = bf16[64,1024]{1,0:T(8,128)(2,1)S(1)} collective-permute-done((bf16[64,1024]{1,0:T(8,128)(2,1)S(1)}, bf16[64,1024]{1,0:T(8,128)(2,1)S(1)}, u32[]{:S(2)}, u32[]{:S(2)}) %collective-permute-start.15) | collective-permute-done | bytes 131104 | tf_op jit(solution)/shard_map/ppermute | solution.py:242
  47.8 0.5 collective-permute-start.19
  48.3 0.8 %collective-permute-done.20.second_ref = bf16[16,4096]{1,0:T(8,128)(2,1)S(1)} collective-permute-done((bf16[16,4096]{1,0:T(8,128)(2,1)S(1)}, bf16[16,4096]{1,0:T(8,128)(2,1)S(1)}, u32[]{:S(2)}, u32[]{:S(2)}) %collective-permute-start.20) | collective-permute-done | bytes 131104 | tf_op jit(solution)/shard_map/ppermute | solution.py:239
  49.1 0.2 collective-permute-done.19.first_ref
  49.3 2.3 %shard_map.86 = (f32[64,1024]{1,0:T(8,128)S(1)}, bf16[64,1024]{1,0:T(8,128)(2,1)S(1)}, f32[128,128]{1,0:T(8,128)S(1)}, bf16[128,128]{1,0:T(8,128)(2,1)S(1)}) custom-call(s32[3]{0:T(128)S(1)} %pad_add_fusion.flags_ref, bf16[4096,1024]{1,0:T(8,128)(2,1)S(1)} %copy-done.1, bf16[64,4096]{1,0:T(8,128)(2,1)S(1)} %bitcast.8, ...), custom_call_target="tpu_custom_call" | custom-call | tf_op jit(solution)/shard_map/pallas_call | solution.py:91
  51.6 0.6 collective-permute-start.22
  52.2 1.5 %collective-permute-start.18 = (bf16[64,1024]{1,0:T(8,128)(2,1)S(1)}, bf16[64,1024]{1,0:T(8,128)(2,1)S(1)}, u32[]{:S(2)}, u32[]{:S(2)}) collective-permute-start(bf16[64,1024]{1,0:T(8,128)(2,1)S(1)} %get-tuple-element.65), channel_id=1, source_target_pairs={{0,2},{2,0},{1,3},{3,1},{4,6},{6,4},{5,7},{7,5},{8,10},{10,8},{9,1... | collective-permute-start | bytes 393224 | tf_op jit(solution)/shard_map/ppermute | solution.py:242
  53.7 0.5 collective-permute-start.21
  54.2 1.7 %collective-permute-done.22 = bf16[128,128]{1,0:T(8,128)(2,1)S(1)} collective-permute-done((bf16[128,128]{1,0:T(8,128)(2,1)S(1)}, bf16[128,128]{1,0:T(8,128)(2,1)S(1)}, u32[]{:S(2)}, u32[]{:S(2)}) %collective-permute-start.22) | collective-permute-done | bytes 32800 | tf_op jit(solution)/shard_map/ppermute | solution.py:242
  55.9 1.8 %collective-permute-start.23 = (bf16[128,128]{1,0:T(8,128)(2,1)S(1)}, bf16[128,128]{1,0:T(8,128)(2,1)S(1)}, u32[]{:S(2)}, u32[]{:S(2)}) collective-permute-start(bf16[128,128]{1,0:T(8,128)(2,1)S(1)} %multiply_convert_fusion.refs_0_), channel_id=1, source_target_pairs={{0,4},{4,0},{8,12},{12,8},{1,9},{9,1},{5,13},{13,5},{2,6},{6,2},{1... | collective-permute-start | bytes 98312 | tf_op jit(solution)/shard_map/ppermute | solution.py:331
  57.7 0.8 %collective-permute-start.24 = (bf16[128,128]{1,0:T(8,128)(2,1)S(1)}, bf16[128,128]{1,0:T(8,128)(2,1)S(1)}, u32[]{:S(2)}, u32[]{:S(2)}) collective-permute-start(bf16[128,128]{1,0:T(8,128)(2,1)S(1)} %multiply_convert_fusion.refs_0_), channel_id=1, source_target_pairs={{0,12},{12,0},{4,8},{8,4},{1,13},{13,1},{5,9},{9,5},{2,14},{14,2},... | collective-permute-start | bytes 98312 | tf_op jit(solution)/shard_map/ppermute | solution.py:245
  58.5 1.3 %collective-permute-done.23.refs_1_ = bf16[128,128]{1,0:T(8,128)(2,1)S(1)} collective-permute-done((bf16[128,128]{1,0:T(8,128)(2,1)S(1)}, bf16[128,128]{1,0:T(8,128)(2,1)S(1)}, u32[]{:S(2)}, u32[]{:S(2)}) %collective-permute-start.23) | collective-permute-done | bytes 32800 | tf_op jit(solution)/shard_map/ppermute | solution.py:331
  59.9 1.0 %collective-permute-done.21.refs_7_ = bf16[64,1024]{1,0:T(8,128)(2,1)S(1)} collective-permute-done((bf16[64,1024]{1,0:T(8,128)(2,1)S(1)}, bf16[64,1024]{1,0:T(8,128)(2,1)S(1)}, u32[]{:S(2)}, u32[]{:S(2)}) %collective-permute-start.21) | collective-permute-done | bytes 131104 | tf_op jit(solution)/shard_map/ppermute | solution.py:242
  60.9 0.7 %shard_map.87.base_ref = f32[256,1024]{1,0:T(8,128)S(1)} custom-call(s32[3]{0:T(128)S(1)} %pad_add_fusion.flags_ref, bf16[256,1024]{1,0:T(8,128)(2,1)S(1)} %copy-done.5, f32[64,1024]{1,0:T(8,128)S(1)} %get-tuple-element.48.refs_0_, bf16[64,1024]{1,0:T(8,128)(2,1)S(1)} %pad_maximum_fusion.refs_1_, f32[64,1024]{1,0:T(8,128)S(1)} %get-tuple-element.58.refs_2_, ...), custom_call_target="tpu_custom_call" | custom-call | tf_op jit(solution)/shard_map/pallas_call | solution.py:91
  61.6 1.8 %collective-permute-done.24.refs_2_ = bf16[128,128]{1,0:T(8,128)(2,1)S(1)} collective-permute-done((bf16[128,128]{1,0:T(8,128)(2,1)S(1)}, bf16[128,128]{1,0:T(8,128)(2,1)S(1)}, u32[]{:S(2)}, u32[]{:S(2)}) %collective-permute-start.24) | collective-permute-done | bytes 32800 | tf_op jit(solution)/shard_map/ppermute | solution.py:245
  63.4 1.5 %shard_map.88 = bf16[256,1024]{1,0:T(8,128)(2,1)} custom-call(f32[256,1024]{1,0:T(8,128)S(1)} %shard_map.87.base_ref, bf16[4,256,64]{2,1,0:T(8,128)(2,1)S(1)} %broadcast_in_dim.24.hot_ref, bf16[4,64,1024]{2,1,0:T(8,128)(2,1)S(1)} %maximum_select_fusion.ups_ref, bf16[128,128]{1,0:T(8,128)(2,1)S(1)} %multiply_convert_fusion.refs_0_, ...), custom_call_target="tpu_custom_call" | custom-call | tf_op jit(solution)/shard_map/pallas_call | solution.py:91
  (50 shorter events, 1.4 us)
Async XLA Ops:
  0.0 22.0 %copy-start.3 = (bf16[1,64,4096]{2,1,0:T(8,128)(2,1)S(1)}, bf16[1,64,4096]{2,1,0:T(8,128)(2,1)}, u32[]{:S(2)}) copy-start(bf16[1,64,4096]{2,1,0:T(8,128)(2,1)} %param.11) | copy-start | bytes 1572868
  0.0 19.6 %copy-start.8 = (s32[4]{0:T(128)S(1)}, s32[4]{0:T(128)}, u32[]{:S(2)}) copy-start(s32[4]{0:T(128)} %param.15) | copy-start | bytes 52
  0.0 19.6 %copy-start.9 = (s32[4]{0:T(128)S(1)}, s32[4]{0:T(128)}, u32[]{:S(2)}) copy-start(s32[4]{0:T(128)} %param.14) | copy-start | bytes 52
  0.0 19.6 %copy-start.7 = (s32[512]{0:T(512)S(1)}, s32[512]{0:T(512)}, u32[]{:S(2)}) copy-start(s32[512]{0:T(512)} %param.13) | copy-start | bytes 6148
  1.0 32.8 %collective-permute-start.3 = (bf16[32,4096]{1,0:T(8,128)(2,1)S(1)}, bf16[32,4096]{1,0:T(8,128)(2,1)S(1)}, u32[]{:S(2)}, u32[]{:S(2)}) collective-permute-start(bf16[32,4096]{1,0:T(8,128)(2,1)S(1)} %constant_dynamic-slice_fusion.1), channel_id=1, source_target_pairs={{0,4},{4,0},{8,12},{12,8},{1,5},{5,1},{9,13},{13,9},{2,6},{6,2},{1... | collective-permute-start | bytes 786440 | tf_op jit(solution)/shard_map/ppermute | solution.py:245
  4.1 15.9 %collective-permute-start = (bf16[32,4096]{1,0:T(8,128)(2,1)S(1)}, bf16[32,4096]{1,0:T(8,128)(2,1)S(1)}, u32[]{:S(2)}, u32[]{:S(2)}) collective-permute-start(bf16[32,4096]{1,0:T(8,128)(2,1)S(1)} %constant_dynamic-slice_fusion.1), channel_id=1, source_target_pairs={{0,8},{8,0},{4,12},{12,4},{1,9},{9,1},{5,13},{13,5},{2,10},{10,2},... | collective-permute-start | bytes 786440 | tf_op jit(solution)/shard_map/ppermute | solution.py:245
  6.7 1.0 %copy-start.2 = (bf16[1,64,4096]{2,1,0:T(8,128)(2,1)S(1)}, bf16[1,64,4096]{2,1,0:T(8,128)(2,1)}, u32[]{:S(2)}) copy-start(bf16[1,64,4096]{2,1,0:T(8,128)(2,1)} %param.11) | copy-start | bytes 1572868
  7.8 1.2 %copy-start.4 = (bf16[128,4096]{1,0:T(8,128)(2,1)S(1)}, bf16[128,4096]{1,0:T(8,128)(2,1)}, u32[]{:S(2)}) copy-start(bf16[128,4096]{1,0:T(8,128)(2,1)} %rows_ref.1) | copy-start | bytes 3145732
  9.0 9.1 %copy-start.6 = (bf16[2,64,1024]{2,1,0:T(8,128)(2,1)S(1)}, bf16[2,64,1024]{2,1,0:T(8,128)(2,1)}, u32[]{:S(2)}) copy-start(bf16[2,64,1024]{2,1,0:T(8,128)(2,1)} %param.12) | copy-start | bytes 786436
  13.5 3.3 %copy-start = (bf16[4096,1024]{1,0:T(8,128)(2,1)}, bf16[4096,1024]{1,0:T(8,128)(2,1)S(1)}, u32[]{:S(2)}) copy-start(bf16[4096,1024]{1,0:T(8,128)(2,1)S(1)} %get-tuple-element.42.weight_ref) | copy-start | bytes 25165828
  17.7 16.2 %collective-permute-start.5 = (bf16[32,4096]{1,0:T(8,128)(2,1)S(1)}, bf16[32,4096]{1,0:T(8,128)(2,1)S(1)}, u32[]{:S(2)}, u32[]{:S(2)}) collective-permute-start(bf16[32,4096]{1,0:T(8,128)(2,1)S(1)} %constant_dynamic-slice_fusion), channel_id=1, source_target_pairs={{0,8},{8,0},{4,12},{12,4},{1,9},{9,1},{5,13},{13,5},{2,10},{10,2},... | collective-permute-start | bytes 786440 | tf_op jit(solution)/shard_map/ppermute | solution.py:245
  18.1 9.9 %collective-permute-start.6 = (bf16[2,64,1024]{2,1,0:T(8,128)(2,1)S(1)}, bf16[2,64,1024]{2,1,0:T(8,128)(2,1)S(1)}, u32[]{:S(2)}, u32[]{:S(2)}) collective-permute-start(bf16[2,64,1024]{2,1,0:T(8,128)(2,1)S(1)} %copy-done.6), channel_id=1, source_target_pairs={{0,2},{2,0},{1,3},{3,1},{4,6},{6,4},{5,7},{7,5},{8,10},{10,8},{9,1... | collective-permute-start | bytes 786440 | tf_op jit(solution)/shard_map/ppermute | solution.py:242
  20.1 1.4 %collective-permute-start.2 = (bf16[16,4096]{1,0:T(8,128)(2,1)S(1)}, bf16[16,4096]{1,0:T(8,128)(2,1)S(1)}, u32[]{:S(2)}, u32[]{:S(2)}) collective-permute-start(bf16[16,4096]{1,0:T(8,128)(2,1)S(1)} %get-tuple-element.91), channel_id=1, source_target_pairs={{0,1},{1,0},{2,3},{3,2},{4,5},{5,4},{6,7},{7,6},{8,9},{9,8},{10,11... | collective-permute-start | bytes 393224 | tf_op jit(solution)/shard_map/ppermute | solution.py:239
  20.2 1.8 %collective-permute-start.1 = (bf16[16,4096]{1,0:T(8,128)(2,1)S(1)}, bf16[16,4096]{1,0:T(8,128)(2,1)S(1)}, u32[]{:S(2)}, u32[]{:S(2)}) collective-permute-start(bf16[16,4096]{1,0:T(8,128)(2,1)S(1)} %get-tuple-element.92), channel_id=1, source_target_pairs={{0,1},{1,0},{2,3},{3,2},{4,5},{5,4},{6,7},{7,6},{8,9},{9,8},{10,11... | collective-permute-start | bytes 393224 | tf_op jit(solution)/shard_map/ppermute | solution.py:239
  21.5 14.7 %collective-permute-start.4 = (bf16[32,4096]{1,0:T(8,128)(2,1)S(1)}, bf16[32,4096]{1,0:T(8,128)(2,1)S(1)}, u32[]{:S(2)}, u32[]{:S(2)}) collective-permute-start(bf16[32,4096]{1,0:T(8,128)(2,1)S(1)} %constant_dynamic-slice_fusion), channel_id=1, source_target_pairs={{0,4},{4,0},{8,12},{12,8},{1,5},{5,1},{9,13},{13,9},{2,6},{6,2},{1... | collective-permute-start | bytes 786440 | tf_op jit(solution)/shard_map/ppermute | solution.py:245
  22.0 3.4 %copy-start.1 = (bf16[4096,1024]{1,0:T(8,128)(2,1)S(1)}, bf16[4096,1024]{1,0:T(8,128)(2,1)}, u32[]{:S(2)}) copy-start(bf16[4096,1024]{1,0:T(8,128)(2,1)} %copy-done) | copy-start | bytes 25165828
  27.6 4.8 %collective-permute-start.7 = (bf16[32,1024]{1,0:T(8,128)(2,1)S(1)}, bf16[32,1024]{1,0:T(8,128)(2,1)S(1)}, u32[]{:S(2)}, u32[]{:S(2)}) collective-permute-start(bf16[32,1024]{1,0:T(8,128)(2,1)S(1)} %get-tuple-element.93), channel_id=1, source_target_pairs={{0,2},{2,0},{1,3},{3,1},{4,6},{6,4},{5,7},{7,5},{8,10},{10,8},{9,1... | collective-permute-start | bytes 196616 | tf_op jit(solution)/shard_map/ppermute | solution.py:242
  28.0 5.9 %collective-permute-start.8 = (bf16[32,1024]{1,0:T(8,128)(2,1)S(1)}, bf16[32,1024]{1,0:T(8,128)(2,1)S(1)}, u32[]{:S(2)}, u32[]{:S(2)}) collective-permute-start(bf16[32,1024]{1,0:T(8,128)(2,1)S(1)} %get-tuple-element.94), channel_id=1, source_target_pairs={{0,2},{2,0},{1,3},{3,1},{4,6},{6,4},{5,7},{7,5},{8,10},{10,8},{9,1... | collective-permute-start | bytes 196616 | tf_op jit(solution)/shard_map/ppermute | solution.py:242
  32.5 9.0 %collective-permute-start.9 = (bf16[32,4096]{1,0:T(8,128)(2,1)S(1)}, bf16[32,4096]{1,0:T(8,128)(2,1)S(1)}, u32[]{:S(2)}, u32[]{:S(2)}) collective-permute-start(bf16[32,4096]{1,0:T(8,128)(2,1)S(1)} %collective-permute-done.mine_ref), channel_id=1, source_target_pairs={{0,4},{4,0},{8,12},{12,8},{1,5},{5,1},{9,13},{13,9},{2,6},{6,2},{1... | collective-permute-start | bytes 786440 | tf_op jit(solution)/shard_map/ppermute | solution.py:245
  36.4 2.4 %collective-permute-start.12 = (bf16[32,4096]{1,0:T(8,128)(2,1)S(1)}, bf16[32,4096]{1,0:T(8,128)(2,1)S(1)}, u32[]{:S(2)}, u32[]{:S(2)}) collective-permute-start(bf16[32,4096]{1,0:T(8,128)(2,1)S(1)} %collective-permute-done.3.near_ref), channel_id=1, source_target_pairs={{0,1},{1,0},{2,3},{3,2},{4,5},{5,4},{6,7},{7,6},{8,9},{9,8},{10,11... | collective-permute-start | bytes 786440 | tf_op jit(solution)/shard_map/ppermute | solution.py:239
  36.5 2.3 %collective-permute-start.13 = (bf16[32,4096]{1,0:T(8,128)(2,1)S(1)}, bf16[32,4096]{1,0:T(8,128)(2,1)S(1)}, u32[]{:S(2)}, u32[]{:S(2)}) collective-permute-start(bf16[32,4096]{1,0:T(8,128)(2,1)S(1)} %collective-permute-done.4.near_too_ref), channel_id=1, source_target_pairs={{0,1},{1,0},{2,3},{3,2},{4,5},{5,4},{6,7},{7,6},{8,9},{9,8},{10,11... | collective-permute-start | bytes 786440 | tf_op jit(solution)/shard_map/ppermute | solution.py:239
  37.0 1.6 %collective-permute-start.11 = (bf16[16,4096]{1,0:T(8,128)(2,1)S(1)}, bf16[16,4096]{1,0:T(8,128)(2,1)S(1)}, u32[]{:S(2)}, u32[]{:S(2)}) collective-permute-start(bf16[16,4096]{1,0:T(8,128)(2,1)S(1)} %get-tuple-element.89), channel_id=1, source_target_pairs={{0,1},{1,0},{2,3},{3,2},{4,5},{5,4},{6,7},{7,6},{8,9},{9,8},{10,11... | collective-permute-start | bytes 393224 | tf_op jit(solution)/shard_map/ppermute | solution.py:239
  37.1 1.6 %collective-permute-start.10 = (bf16[16,4096]{1,0:T(8,128)(2,1)S(1)}, bf16[16,4096]{1,0:T(8,128)(2,1)S(1)}, u32[]{:S(2)}, u32[]{:S(2)}) collective-permute-start(bf16[16,4096]{1,0:T(8,128)(2,1)S(1)} %get-tuple-element.90), channel_id=1, source_target_pairs={{0,1},{1,0},{2,3},{3,2},{4,5},{5,4},{6,7},{7,6},{8,9},{9,8},{10,11... | collective-permute-start | bytes 393224 | tf_op jit(solution)/shard_map/ppermute | solution.py:239
  38.6 8.3 %collective-permute-start.14 = (bf16[32,4096]{1,0:T(8,128)(2,1)S(1)}, bf16[32,4096]{1,0:T(8,128)(2,1)S(1)}, u32[]{:S(2)}, u32[]{:S(2)}) collective-permute-start(bf16[32,4096]{1,0:T(8,128)(2,1)S(1)} %collective-permute-done.5.mine_ref), channel_id=1, source_target_pairs={{0,4},{4,0},{8,12},{12,8},{1,5},{5,1},{9,13},{13,9},{2,6},{6,2},{1... | collective-permute-start | bytes 786440 | tf_op jit(solution)/shard_map/ppermute | solution.py:245
  41.5 1.4 %collective-permute-start.17 = (bf16[16,4096]{1,0:T(8,128)(2,1)S(1)}, bf16[16,4096]{1,0:T(8,128)(2,1)S(1)}, u32[]{:S(2)}, u32[]{:S(2)}) collective-permute-start(bf16[16,4096]{1,0:T(8,128)(2,1)S(1)} %get-tuple-element.87), channel_id=1, source_target_pairs={{0,1},{1,0},{2,3},{3,2},{4,5},{5,4},{6,7},{7,6},{8,9},{9,8},{10,11... | collective-permute-start | bytes 393224 | tf_op jit(solution)/shard_map/ppermute | solution.py:239
  41.8 1.4 %collective-permute-start.16 = (bf16[16,4096]{1,0:T(8,128)(2,1)S(1)}, bf16[16,4096]{1,0:T(8,128)(2,1)S(1)}, u32[]{:S(2)}, u32[]{:S(2)}) collective-permute-start(bf16[16,4096]{1,0:T(8,128)(2,1)S(1)} %get-tuple-element.88), channel_id=1, source_target_pairs={{0,1},{1,0},{2,3},{3,2},{4,5},{5,4},{6,7},{7,6},{8,9},{9,8},{10,11... | collective-permute-start | bytes 393224 | tf_op jit(solution)/shard_map/ppermute | solution.py:239
  42.1 5.6 %collective-permute-start.15 = (bf16[64,1024]{1,0:T(8,128)(2,1)S(1)}, bf16[64,1024]{1,0:T(8,128)(2,1)S(1)}, u32[]{:S(2)}, u32[]{:S(2)}) collective-permute-start(bf16[64,1024]{1,0:T(8,128)(2,1)S(1)} %get-tuple-element.60), channel_id=1, source_target_pairs={{0,2},{2,0},{1,3},{3,1},{4,6},{6,4},{5,7},{7,5},{8,10},{10,8},{9,1... | collective-permute-start | bytes 393224 | tf_op jit(solution)/shard_map/ppermute | solution.py:242
  43.1 17.7 %copy-start.5 = (bf16[256,1024]{1,0:T(8,128)(2,1)S(1)}, bf16[256,1024]{1,0:T(8,128)(2,1)}, u32[]{:S(2)}) copy-start(bf16[256,1024]{1,0:T(8,128)(2,1)} %residual_ref.1) | copy-start | bytes 1572868
  47.7 1.4 %collective-permute-start.20 = (bf16[16,4096]{1,0:T(8,128)(2,1)S(1)}, bf16[16,4096]{1,0:T(8,128)(2,1)S(1)}, u32[]{:S(2)}, u32[]{:S(2)}) collective-permute-start(bf16[16,4096]{1,0:T(8,128)(2,1)S(1)} %get-tuple-element.85), channel_id=1, source_target_pairs={{0,1},{1,0},{2,3},{3,2},{4,5},{5,4},{6,7},{7,6},{8,9},{9,8},{10,11... | collective-permute-start | bytes 393224 | tf_op jit(solution)/shard_map/ppermute | solution.py:239
  47.8 1.5 %collective-permute-start.19 = (bf16[16,4096]{1,0:T(8,128)(2,1)S(1)}, bf16[16,4096]{1,0:T(8,128)(2,1)S(1)}, u32[]{:S(2)}, u32[]{:S(2)}) collective-permute-start(bf16[16,4096]{1,0:T(8,128)(2,1)S(1)} %get-tuple-element.86), channel_id=1, source_target_pairs={{0,1},{1,0},{2,3},{3,2},{4,5},{5,4},{6,7},{7,6},{8,9},{9,8},{10,11... | collective-permute-start | bytes 393224 | tf_op jit(solution)/shard_map/ppermute | solution.py:239
  51.6 4.3 %collective-permute-start.22 = (bf16[128,128]{1,0:T(8,128)(2,1)S(1)}, bf16[128,128]{1,0:T(8,128)(2,1)S(1)}, u32[]{:S(2)}, u32[]{:S(2)}) collective-permute-start(bf16[128,128]{1,0:T(8,128)(2,1)S(1)} %get-tuple-element.77), channel_id=1, source_target_pairs={{0,2},{2,0},{1,3},{3,1},{4,6},{6,4},{5,7},{7,5},{8,10},{10,8},{9,1... | collective-permute-start | bytes 98312 | tf_op jit(solution)/shard_map/ppermute | solution.py:242
  52.2 7.7 %collective-permute-start.18 = (bf16[64,1024]{1,0:T(8,128)(2,1)S(1)}, bf16[64,1024]{1,0:T(8,128)(2,1)S(1)}, u32[]{:S(2)}, u32[]{:S(2)}) collective-permute-start(bf16[64,1024]{1,0:T(8,128)(2,1)S(1)} %get-tuple-element.65), channel_id=1, source_target_pairs={{0,2},{2,0},{1,3},{3,1},{4,6},{6,4},{5,7},{7,5},{8,10},{10,8},{9,1... | collective-permute-start | bytes 393224 | tf_op jit(solution)/shard_map/ppermute | solution.py:242
  53.7 7.2 %collective-permute-start.21 = (bf16[64,1024]{1,0:T(8,128)(2,1)S(1)}, bf16[64,1024]{1,0:T(8,128)(2,1)S(1)}, u32[]{:S(2)}, u32[]{:S(2)}) collective-permute-start(bf16[64,1024]{1,0:T(8,128)(2,1)S(1)} %get-tuple-element.73), channel_id=1, source_target_pairs={{0,2},{2,0},{1,3},{3,1},{4,6},{6,4},{5,7},{7,5},{8,10},{10,8},{9,1... | collective-permute-start | bytes 393224 | tf_op jit(solution)/shard_map/ppermute | solution.py:242
  55.9 4.0 %collective-permute-start.23 = (bf16[128,128]{1,0:T(8,128)(2,1)S(1)}, bf16[128,128]{1,0:T(8,128)(2,1)S(1)}, u32[]{:S(2)}, u32[]{:S(2)}) collective-permute-start(bf16[128,128]{1,0:T(8,128)(2,1)S(1)} %multiply_convert_fusion.refs_0_), channel_id=1, source_target_pairs={{0,4},{4,0},{8,12},{12,8},{1,9},{9,1},{5,13},{13,5},{2,6},{6,2},{1... | collective-permute-start | bytes 98312 | tf_op jit(solution)/shard_map/ppermute | solution.py:331
  57.7 5.7 %collective-permute-start.24 = (bf16[128,128]{1,0:T(8,128)(2,1)S(1)}, bf16[128,128]{1,0:T(8,128)(2,1)S(1)}, u32[]{:S(2)}, u32[]{:S(2)}) collective-permute-start(bf16[128,128]{1,0:T(8,128)(2,1)S(1)} %multiply_convert_fusion.refs_0_), channel_id=1, source_target_pairs={{0,12},{12,0},{4,8},{8,4},{1,13},{13,1},{5,9},{9,5},{2,14},{14,2},... | collective-permute-start | bytes 98312 | tf_op jit(solution)/shard_map/ppermute | solution.py:245
  59.9 3.6 %collective-permute-start.25 = (bf16[128,128]{1,0:T(8,128)(2,1)S(1)}, bf16[128,128]{1,0:T(8,128)(2,1)S(1)}, u32[]{:S(2)}, u32[]{:S(2)}) collective-permute-start(bf16[128,128]{1,0:T(8,128)(2,1)S(1)} %collective-permute-done.23.refs_1_), channel_id=1, source_target_pairs={{0,1},{1,0},{2,3},{3,2},{4,5},{5,4},{6,7},{7,6},{8,9},{9,8},{10,11... | collective-permute-start | bytes 98312 | tf_op jit(solution)/shard_map/ppermute | solution.py:239

commit v15 on v14

--- a/solution.py
+++ b/solution.py
@@ -270,6 +270,7 @@
         return lax.dynamic_slice_in_dim(rows, c * half + piece * step, step, 0)
 
     mine = cut(rows, 0)
+    rows, hot, scale = barrier((rows, hot, scale))
     far, near = [along(mine, FAR)], [along(mine, NEAR)]
     held, own_sum, own_low = call(
         own_kernel,
@@ -297,10 +298,8 @@
 
     last = [along(far[0], NEAR)]
     kept_a, sent_a, low_a = parted_piece(0, own_sum, far[0])
-    got_a = jnp.concatenate([over_x(sent_a[:step]), over_x(sent_a[step:])])
-    near, far[1], own_sum, ups, hot, scale, got_a = barrier(
-        (near, far[1], own_sum, ups, hot, scale, got_a)
-    )
+    got_a = over_x(sent_a)
+    near, far[1], own_sum, ups, kept_a = barrier((near, far[1], own_sum, ups, kept_a))
 
     last.append(along(far[1], NEAR))
     kept_b, sent_b, near_sum, low_b = call(
@@ -310,6 +309,7 @@
         [flags, held, down[0], own_sum, far[1]] + over_core_in_two(far[1])
         + near + [over_core(piece) for piece in near],
     )
+    sent_b, got_a = barrier((sent_b, got_a))
     got_b = over_x(sent_b)
     last[0], kept_b = barrier((last[0], kept_b))
 

time: 65.2 us -> 65.6 us (level)
  waiting for transfers between devices: 16.4 us -> 11.5 us
  starting transfers between devices: 20.2 us -> 23.1 us
  other arithmetic: 0.7 us -> 2.4 us
  local copies, waits for them, and re-layouts: 11.2 us -> 11.9 us
    ppermute x7, waiting for transfers between devices: 5.62 us -> 0.81 us  [along(): return lax.ppermute(value, 'blk', pairs)]
    ppermute x7 -> x6, waiting for transfers between devices: 6.1 us -> 8.66 us  [over_x(): return lax.ppermute(value, 'split', SWAP)]
    ppermute x7, starting transfers between devices: 8.75 us -> 10.8 us  [along(): return lax.ppermute(value, 'blk', pairs)]
    ppermute x7 -> x6, starting transfers between devices: 6.74 us -> 8.3 us  [over_x(): return lax.ppermute(value, 'split', SWAP)]
    ppermute x1, waiting for transfers between devices: 1.34 us -> 0.01 us  [line(): lax.ppermute(scaled, ('blk', 'sub'), by_core(NEAR, FAR))]
    ppermute x11, waiting for transfers between devices: 3.34 us -> 2.03 us  [over_core(): return lax.ppermute(value, 'sub', SWAP)]
    select_n x1, other arithmetic: 0.08 us -> 1.12 us  [line(): jnp.where(x == 0, jnp.concatenate([up, up_other]), jnp.concatenate([up_ot...]
    slice x4, local copies, waits for them, and re-layouts: 0.07 us -> 0.77 us  [over_core_in_two(): return [over_core(piece[:count]), over_core(piece[count:])]]
  transfers between devices with their start and end apart: 26 -> 25, of which waited for: 15 -> 9; matrix products, arithmetic and copies ran while one was open for 3% -> 7% of each run, Pallas kernels for 19% -> 19%
where the time goes in v15:
time: 65.6 us; the launch traced here: 65.2 us
  starting transfers between devices  23.1 us (35%)
  Pallas kernels  16.1 us (25%)
  local copies, waits for them, and re-layouts  11.9 us (18%)
  waiting for transfers between devices  11.5 us (18%)
  other arithmetic  2.4 us (4%)
    pallas_call x7, Pallas kernels, call(): pl.pallas_call(kernel, out_shape=outs, in_specs=in_specs, out_specs=jax.t...  16.1 us
    ppermute x7, starting transfers between devices, along(): return lax.ppermute(value, 'blk', pairs)  10.8 us
    unnamed x14, local copies, waits for them, and re-layouts  8.93 us
    ppermute x6, waiting for transfers between devices, over_x(): return lax.ppermute(value, 'split', SWAP)  8.66 us
    ppermute x6, starting transfers between devices, over_x(): return lax.ppermute(value, 'split', SWAP)  8.3 us
    ppermute x11, starting transfers between devices, over_core(): return lax.ppermute(value, 'sub', SWAP)  2.29 us
    ppermute x11, waiting for transfers between devices, over_core(): return lax.ppermute(value, 'sub', SWAP)  2.03 us
    dynamic_slice x2, local copies, waits for them, and re-layouts, cut(): return lax.dynamic_slice_in_dim(rows, c * half + piece * step, step, 0)  2.01 us
  transfers between devices with their start and end apart: 25, of which 9 were waited for; matrix products, arithmetic and copies ran while one was open for 7% of the time, Pallas kernels for 19%

profile of v15, /device:TPU:0, one launch (start us, length us, event | category | flops | bytes accessed | tf_op | source)
XLA Modules:
  0.0 65.2 jit_solution(8084076281634243824)
XLA Ops:
  0.0 1.0 %constant_dynamic-slice_fusion.1 = bf16[32,4096]{1,0:T(8,128)(2,1)S(1)} fusion(bf16[128,4096]{1,0:T(8,128)(2,1)} %rows_ref, s32[]{:T(128)S(6)} %select_n.39), kind=kLoop, calls=%fused_computation.14 | loop fusion | bytes 524292 | tf_op jit(solution)/shard_map/dynamic_slice | solution.py:270
  1.0 4.1 %collective-permute-start.3 = (bf16[32,4096]{1,0:T(8,128)(2,1)S(1)}, bf16[32,4096]{1,0:T(8,128)(2,1)S(1)}, u32[]{:S(2)}, u32[]{:S(2)}) collective-permute-start(bf16[32,4096]{1,0:T(8,128)(2,1)S(1)} %constant_dynamic-slice_fusion.1), channel_id=1, source_target_pairs={{0,8},{8,0},{4,12},{12,4},{1,9},{9,1},{5,13},{13,5},{2,10},{10,2},... | collective-permute-start | bytes 786440 | tf_op jit(solution)/shard_map/ppermute | solution.py:245
  5.2 1.6 %collective-permute-start = (bf16[32,4096]{1,0:T(8,128)(2,1)S(1)}, bf16[32,4096]{1,0:T(8,128)(2,1)S(1)}, u32[]{:S(2)}, u32[]{:S(2)}) collective-permute-start(bf16[32,4096]{1,0:T(8,128)(2,1)S(1)} %constant_dynamic-slice_fusion.1), channel_id=1, source_target_pairs={{0,4},{4,0},{8,12},{12,8},{1,5},{5,1},{9,13},{13,9},{2,6},{6,2},{1... | collective-permute-start | bytes 786440 | tf_op jit(solution)/shard_map/ppermute | solution.py:245
  6.7 0.8 %select_reduce_fusion = (s32[512]{0:T(512)S(1)}, s32[512]{0:T(512)S(1)}) fusion(s32[4]{0:T(128)} %param.15, s32[512]{0:T(512)} %param.13, s32[4]{0:T(128)} %param.14), kind=kLoop, calls=%fused_computation.5 | loop fusion | flops 9216 | bytes 6176 | tf_op jit(solution)/shard_map/reduce_sum | solution.py:26
  7.5 0.1 convert_divide_fusion
  7.7 0.2 select_select_fusion
  8.0 0.2 broadcast_in_dim.24.hot_ref
  8.2 1.0 %copy-done.2 = bf16[1,64,4096]{2,1,0:T(8,128)(2,1)S(1)} copy-done((bf16[1,64,4096]{2,1,0:T(8,128)(2,1)S(1)}, bf16[1,64,4096]{2,1,0:T(8,128)(2,1)}, u32[]{:S(2)}) %copy-start.2) | copy-done | bytes 524312
  9.2 1.2 %copy-done.4 = bf16[128,4096]{1,0:T(8,128)(2,1)S(1)} copy-done((bf16[128,4096]{1,0:T(8,128)(2,1)S(1)}, bf16[128,4096]{1,0:T(8,128)(2,1)}, u32[]{:S(2)}) %copy-start.4) | copy-done | bytes 1048600
  10.4 4.4 %shard_map.82 = (bf16[4096,1024]{1,0:T(8,128)(2,1)S(1)}, f32[128,1024]{1,0:T(8,128)S(1)}, f32[128,64]{1,0:T(8,128)S(1)}) custom-call(bf16[4096,1024]{1,0:T(8,128)(2,1)} %weight_ref.1, bf16[64,4096]{1,0:T(8,128)(2,1)S(1)} %bitcast.4, bf16[128,4096]{1,0:T(8,128)(2,1)S(1)} %copy-done.4), custom_call_target="tpu_custom_call" | custom-call | tf_op jit(solution)/shard_map/pallas_call | solution.py:91
  14.9 3.3 %copy-done = bf16[4096,1024]{1,0:T(8,128)(2,1)} copy-done((bf16[4096,1024]{1,0:T(8,128)(2,1)}, bf16[4096,1024]{1,0:T(8,128)(2,1)S(1)}, u32[]{:S(2)}) %copy-start) | copy-done | bytes 8388632
  18.1 1.0 %constant_dynamic-slice_fusion = bf16[32,4096]{1,0:T(8,128)(2,1)S(1)} fusion(bf16[128,4096]{1,0:T(8,128)(2,1)} %rows_ref, s32[]{:T(128)S(6)} %select_n.43), kind=kLoop, calls=%fused_computation.13 | loop fusion | bytes 524292 | tf_op jit(solution)/shard_map/dynamic_slice | solution.py:270
  19.1 0.4 collective-permute-start.2
  19.5 0.2 collective-permute-start.1
  19.7 1.7 %collective-permute-start.4 = (bf16[2,64,1024]{2,1,0:T(8,128)(2,1)S(1)}, bf16[2,64,1024]{2,1,0:T(8,128)(2,1)}, u32[]{:S(2)}, u32[]{:S(2)}) collective-permute-start(bf16[2,64,1024]{2,1,0:T(8,128)(2,1)S(1)} %copy-done.6), channel_id=1, source_target_pairs={{0,2},{2,0},{1,3},{3,1},{4,6},{6,4},{5,7},{7,5},{8,10},{10,8},{9,1... | collective-permute-start | bytes 786440 | tf_op jit(solution)/shard_map/ppermute | solution.py:242
  21.5 0.7 %fusion.4 = (bf16[16,4096]{1,0:T(8,128)(2,1)}, bf16[16,4096]{1,0:T(8,128)(2,1)}) fusion(bf16[32,4096]{1,0:T(8,128)(2,1)S(1)} %collective-permute-done.3.mine_ref), kind=kLoop, calls=%fused_computation.18 | loop fusion | bytes 524288 | tf_op jit(solution)/shard_map/slice | solution.py:249
  22.2 4.8 %collective-permute-done.4 = bf16[2,64,1024]{2,1,0:T(8,128)(2,1)} collective-permute-done((bf16[2,64,1024]{2,1,0:T(8,128)(2,1)S(1)}, bf16[2,64,1024]{2,1,0:T(8,128)(2,1)}, u32[]{:S(2)}, u32[]{:S(2)}) %collective-permute-start.4) | collective-permute-done | bytes 262176 | tf_op jit(solution)/shard_map/ppermute | solution.py:242
  27.1 1.1 %maximum_select_fusion.ups_ref = bf16[4,64,1024]{2,1,0:T(8,128)(2,1)S(1)} fusion(bf16[2,64,1024]{2,1,0:T(8,128)(2,1)} %collective-permute-done.4, bf16[2,64,1024]{2,1,0:T(8,128)(2,1)S(1)} %copy-done.6, pred[]{:T(512)S(6)} %eq.57), kind=kLoop, calls=%fused_computation | loop fusion | flops 786432 | bytes 1048577 | tf_op jit(solution)/shard_map/jit(_where)/select_n | solution.py:288
  28.2 1.6 %collective-permute-start.12 = (bf16[32,4096]{1,0:T(8,128)(2,1)S(1)}, bf16[32,4096]{1,0:T(8,128)(2,1)S(1)}, u32[]{:S(2)}, u32[]{:S(2)}) collective-permute-start(bf16[32,4096]{1,0:T(8,128)(2,1)S(1)} %collective-permute-done.3.mine_ref), channel_id=1, source_target_pairs={{0,4},{4,0},{8,12},{12,8},{1,5},{5,1},{9,13},{13,9},{2,6},{6,2},{1... | collective-permute-start | bytes 786440 | tf_op jit(solution)/shard_map/ppermute | solution.py:245
  29.9 3.4 %copy-done.1 = bf16[4096,1024]{1,0:T(8,128)(2,1)S(1)} copy-done((bf16[4096,1024]{1,0:T(8,128)(2,1)S(1)}, bf16[4096,1024]{1,0:T(8,128)(2,1)}, u32[]{:S(2)}) %copy-start.1) | copy-done | bytes 8388632
  33.3 2.2 %shard_map.83 = (f32[64,1024]{1,0:T(8,128)S(1)}, bf16[64,1024]{1,0:T(8,128)(2,1)S(1)}, f32[64,64]{1,0:T(8,128)S(1)}) custom-call(s32[3]{0:T(128)S(1)} %pad_add_fusion.flags_ref, bf16[4096,1024]{1,0:T(8,128)(2,1)S(1)} %copy-done.1, bf16[64,4096]{1,0:T(8,128)(2,1)S(1)} %bitcast.5, f32[128,1024]{1,0:T(8,128)S(1)} %get-tuple-element.56.held_ref, ...), custom_call_target="tpu_custom_call" | custom-call | tf_op jit(solution)/shard_map/pallas_call | solution.py:91
  35.5 0.3 collective-permute-start.9
  35.8 0.3 collective-permute-start.10
  36.1 0.3 collective-permute-start.8
  36.4 0.3 collective-permute-start.7
  36.7 1.0 %collective-permute-done.8.second_ref = bf16[16,4096]{1,0:T(8,128)(2,1)S(1)} collective-permute-done((bf16[16,4096]{1,0:T(8,128)(2,1)S(1)}, bf16[16,4096]{1,0:T(8,128)(2,1)S(1)}, u32[]{:S(2)}, u32[]{:S(2)}) %collective-permute-start.8) | collective-permute-done | bytes 131104 | tf_op jit(solution)/shard_map/ppermute | solution.py:239
  37.7 0.4 collective-permute-start.13
  38.2 1.5 %collective-permute-start.11 = (bf16[64,1024]{1,0:T(8,128)(2,1)S(1)}, bf16[64,1024]{1,0:T(8,128)(2,1)S(1)}, u32[]{:S(2)}, u32[]{:S(2)}) collective-permute-start(bf16[64,1024]{1,0:T(8,128)(2,1)S(1)} %get-tuple-element.61), channel_id=1, source_target_pairs={{0,2},{2,0},{1,3},{3,1},{4,6},{6,4},{5,7},{7,5},{8,10},{10,8},{9,1... | collective-permute-start | bytes 393224 | tf_op jit(solution)/shard_map/ppermute | solution.py:242
  39.7 2.7 %shard_map.84 = (f32[64,1024]{1,0:T(8,128)S(1)}, bf16[64,1024]{1,0:T(8,128)(2,1)S(1)}, f32[128,1024]{1,0:T(8,128)S(1)}, f32[192,64]{1,0:T(8,128)S(1)}) custom-call(s32[3]{0:T(128)S(1)} %pad_add_fusion.flags_ref, bf16[4096,1024]{1,0:T(8,128)(2,1)S(1)} %copy-done.1, bf16[64,4096]{1,0:T(8,128)(2,1)S(1)} %bitcast.6, f32[128,1024]{1,0:T(8,128)S(1)} %get-tuple-element.56.held_ref, ...), custom_call_target="tpu_custom_call" | custom-call | tf_op jit(solution)/shard_map/pallas_call | solution.py:91
  42.5 0.5 collective-permute-start.15
  43.0 0.5 collective-permute-done.11.refs_1_
  43.5 1.5 %collective-permute-start.14 = (bf16[64,1024]{1,0:T(8,128)(2,1)S(1)}, bf16[64,1024]{1,0:T(8,128)(2,1)S(1)}, u32[]{:S(2)}, u32[]{:S(2)}) collective-permute-start(bf16[64,1024]{1,0:T(8,128)(2,1)S(1)} %get-tuple-element.66), channel_id=1, source_target_pairs={{0,2},{2,0},{1,3},{3,1},{4,6},{6,4},{5,7},{7,5},{8,10},{10,8},{9,1... | collective-permute-start | bytes 393224 | tf_op jit(solution)/shard_map/ppermute | solution.py:242
  45.0 2.3 %shard_map.85 = (f32[64,1024]{1,0:T(8,128)S(1)}, bf16[64,1024]{1,0:T(8,128)(2,1)S(1)}, f32[64,64]{1,0:T(8,128)S(1)}) custom-call(s32[3]{0:T(128)S(1)} %pad_add_fusion.flags_ref, bf16[4096,1024]{1,0:T(8,128)(2,1)S(1)} %copy-done.1, bf16[64,4096]{1,0:T(8,128)(2,1)S(1)} %bitcast.7, f32[128,1024]{1,0:T(8,128)S(1)} %get-tuple-element.72.held_ref, ...), custom_call_target="tpu_custom_call" | custom-call | tf_op jit(solution)/shard_map/pallas_call | solution.py:91
  47.3 1.2 %collective-permute-done.14.refs_3_ = bf16[64,1024]{1,0:T(8,128)(2,1)S(1)} collective-permute-done((bf16[64,1024]{1,0:T(8,128)(2,1)S(1)}, bf16[64,1024]{1,0:T(8,128)(2,1)S(1)}, u32[]{:S(2)}, u32[]{:S(2)}) %collective-permute-start.14) | collective-permute-done | bytes 131104 | tf_op jit(solution)/shard_map/ppermute | solution.py:242
  48.6 0.5 collective-permute-start.18
  49.1 0.8 %collective-permute-done.19.second_ref = bf16[16,4096]{1,0:T(8,128)(2,1)S(1)} collective-permute-done((bf16[16,4096]{1,0:T(8,128)(2,1)S(1)}, bf16[16,4096]{1,0:T(8,128)(2,1)S(1)}, u32[]{:S(2)}, u32[]{:S(2)}) %collective-permute-start.19) | collective-permute-done | bytes 131104 | tf_op jit(solution)/shard_map/ppermute | solution.py:239
  49.9 0.2 collective-permute-done.18.first_ref
  50.1 2.3 %shard_map.86 = (f32[64,1024]{1,0:T(8,128)S(1)}, bf16[64,1024]{1,0:T(8,128)(2,1)S(1)}, f32[128,128]{1,0:T(8,128)S(1)}, bf16[128,128]{1,0:T(8,128)(2,1)S(1)}) custom-call(s32[3]{0:T(128)S(1)} %pad_add_fusion.flags_ref, bf16[4096,1024]{1,0:T(8,128)(2,1)S(1)} %copy-done.1, bf16[64,4096]{1,0:T(8,128)(2,1)S(1)} %bitcast.8, ...), custom_call_target="tpu_custom_call" | custom-call | tf_op jit(solution)/shard_map/pallas_call | solution.py:91
  52.4 1.6 %collective-permute-start.21 = (bf16[128,128]{1,0:T(8,128)(2,1)S(1)}, bf16[128,128]{1,0:T(8,128)(2,1)S(1)}, u32[]{:S(2)}, u32[]{:S(2)}) collective-permute-start(bf16[128,128]{1,0:T(8,128)(2,1)S(1)} %get-tuple-element.83), channel_id=1, source_target_pairs={{0,2},{2,0},{1,3},{3,1},{4,6},{6,4},{5,7},{7,5},{8,10},{10,8},{9,1... | collective-permute-start | bytes 98312 | tf_op jit(solution)/shard_map/ppermute | solution.py:242
  53.9 0.5 collective-permute-start.17
  54.5 1.5 %collective-permute-start.20 = (bf16[64,1024]{1,0:T(8,128)(2,1)S(1)}, bf16[64,1024]{1,0:T(8,128)(2,1)S(1)}, u32[]{:S(2)}, u32[]{:S(2)}) collective-permute-start(bf16[64,1024]{1,0:T(8,128)(2,1)S(1)} %get-tuple-element.79), channel_id=1, source_target_pairs={{0,2},{2,0},{1,3},{3,1},{4,6},{6,4},{5,7},{7,5},{8,10},{10,8},{9,1... | collective-permute-start | bytes 393224 | tf_op jit(solution)/shard_map/ppermute | solution.py:242
  56.0 0.4 collective-permute-done.21
  56.4 1.6 %collective-permute-start.22 = (bf16[128,128]{1,0:T(8,128)(2,1)S(1)}, bf16[128,128]{1,0:T(8,128)(2,1)S(1)}, u32[]{:S(2)}, u32[]{:S(2)}) collective-permute-start(bf16[128,128]{1,0:T(8,128)(2,1)S(1)} %multiply_convert_fusion.refs_0_), channel_id=1, source_target_pairs={{0,4},{4,0},{8,12},{12,8},{1,9},{9,1},{5,13},{13,5},{2,6},{6,2},{1... | collective-permute-start | bytes 98312 | tf_op jit(solution)/shard_map/ppermute | solution.py:331
  58.0 2.5 %collective-permute-start.23 = (bf16[128,128]{1,0:T(8,128)(2,1)S(1)}, bf16[128,128]{1,0:T(8,128)(2,1)S(1)}, u32[]{:S(2)}, u32[]{:S(2)}) collective-permute-start(bf16[128,128]{1,0:T(8,128)(2,1)S(1)} %multiply_convert_fusion.refs_0_), channel_id=1, source_target_pairs={{0,12},{12,0},{4,8},{8,4},{1,13},{13,1},{5,9},{9,5},{2,14},{14,2},... | collective-permute-start | bytes 98312 | tf_op jit(solution)/shard_map/ppermute | solution.py:245
  60.5 1.7 %collective-permute-done.20.refs_7_ = bf16[64,1024]{1,0:T(8,128)(2,1)S(1)} collective-permute-done((bf16[64,1024]{1,0:T(8,128)(2,1)S(1)}, bf16[64,1024]{1,0:T(8,128)(2,1)S(1)}, u32[]{:S(2)}, u32[]{:S(2)}) %collective-permute-start.20) | collective-permute-done | bytes 131104 | tf_op jit(solution)/shard_map/ppermute | solution.py:242
  62.2 0.7 %shard_map.87.base_ref = f32[256,1024]{1,0:T(8,128)S(1)} custom-call(s32[3]{0:T(128)S(1)} %pad_add_fusion.flags_ref, bf16[256,1024]{1,0:T(8,128)(2,1)S(1)} %copy-done.5, f32[64,1024]{1,0:T(8,128)S(1)} %get-tuple-element.55.refs_0_, bf16[64,1024]{1,0:T(8,128)(2,1)S(1)} %collective-permute-done.11.refs_1_, f32[64,1024]{1,0:T(8,128)S(1)} %get-tuple-element.64.refs_2_, ...), custom_call_target="tpu_custom_call" | custom-call | tf_op jit(solution)/shard_map/pallas_call | solution.py:91
  62.9 0.8 %collective-permute-done.23.refs_2_ = bf16[128,128]{1,0:T(8,128)(2,1)S(1)} collective-permute-done((bf16[128,128]{1,0:T(8,128)(2,1)S(1)}, bf16[128,128]{1,0:T(8,128)(2,1)S(1)}, u32[]{:S(2)}, u32[]{:S(2)}) %collective-permute-start.23) | collective-permute-done | bytes 32800 | tf_op jit(solution)/shard_map/ppermute | solution.py:245
  63.7 1.5 %shard_map.88 = bf16[256,1024]{1,0:T(8,128)(2,1)} custom-call(f32[256,1024]{1,0:T(8,128)S(1)} %shard_map.87.base_ref, bf16[4,256,64]{2,1,0:T(8,128)(2,1)S(1)} %broadcast_in_dim.24.hot_ref, bf16[4,64,1024]{2,1,0:T(8,128)(2,1)S(1)} %maximum_select_fusion.ups_ref, bf16[128,128]{1,0:T(8,128)(2,1)S(1)} %multiply_convert_fusion.refs_0_, ...), custom_call_target="tpu_custom_call" | custom-call | tf_op jit(solution)/shard_map/pallas_call | solution.py:91
  (40 shorter events, 0.5 us)
Async XLA Ops:
  0.0 29.9 %copy-start.3 = (bf16[1,64,4096]{2,1,0:T(8,128)(2,1)S(1)}, bf16[1,64,4096]{2,1,0:T(8,128)(2,1)}, u32[]{:S(2)}) copy-start(bf16[1,64,4096]{2,1,0:T(8,128)(2,1)} %param.11) | copy-start | bytes 1572868
  0.0 19.7 %copy-start.6 = (bf16[2,64,1024]{2,1,0:T(8,128)(2,1)S(1)}, bf16[2,64,1024]{2,1,0:T(8,128)(2,1)}, u32[]{:S(2)}) copy-start(bf16[2,64,1024]{2,1,0:T(8,128)(2,1)} %param.12) | copy-start | bytes 786436
  1.0 20.4 %collective-permute-start.3 = (bf16[32,4096]{1,0:T(8,128)(2,1)S(1)}, bf16[32,4096]{1,0:T(8,128)(2,1)S(1)}, u32[]{:S(2)}, u32[]{:S(2)}) collective-permute-start(bf16[32,4096]{1,0:T(8,128)(2,1)S(1)} %constant_dynamic-slice_fusion.1), channel_id=1, source_target_pairs={{0,8},{8,0},{4,12},{12,4},{1,9},{9,1},{5,13},{13,5},{2,10},{10,2},... | collective-permute-start | bytes 786440 | tf_op jit(solution)/shard_map/ppermute | solution.py:245
  5.2 30.4 %collective-permute-start = (bf16[32,4096]{1,0:T(8,128)(2,1)S(1)}, bf16[32,4096]{1,0:T(8,128)(2,1)S(1)}, u32[]{:S(2)}, u32[]{:S(2)}) collective-permute-start(bf16[32,4096]{1,0:T(8,128)(2,1)S(1)} %constant_dynamic-slice_fusion.1), channel_id=1, source_target_pairs={{0,4},{4,0},{8,12},{12,8},{1,5},{5,1},{9,13},{13,9},{2,6},{6,2},{1... | collective-permute-start | bytes 786440 | tf_op jit(solution)/shard_map/ppermute | solution.py:245
  8.2 1.0 %copy-start.2 = (bf16[1,64,4096]{2,1,0:T(8,128)(2,1)S(1)}, bf16[1,64,4096]{2,1,0:T(8,128)(2,1)}, u32[]{:S(2)}) copy-start(bf16[1,64,4096]{2,1,0:T(8,128)(2,1)} %param.11) | copy-start | bytes 1572868
  9.2 1.2 %copy-start.4 = (bf16[128,4096]{1,0:T(8,128)(2,1)S(1)}, bf16[128,4096]{1,0:T(8,128)(2,1)}, u32[]{:S(2)}) copy-start(bf16[128,4096]{1,0:T(8,128)(2,1)} %rows_ref) | copy-start | bytes 3145732
  14.9 3.3 %copy-start = (bf16[4096,1024]{1,0:T(8,128)(2,1)}, bf16[4096,1024]{1,0:T(8,128)(2,1)S(1)}, u32[]{:S(2)}) copy-start(bf16[4096,1024]{1,0:T(8,128)(2,1)S(1)} %get-tuple-element.52.weight_ref) | copy-start | bytes 25165828
  19.1 16.4 %collective-permute-start.2 = (bf16[32,4096]{1,0:T(8,128)(2,1)S(1)}, bf16[32,4096]{1,0:T(8,128)(2,1)S(1)}, u32[]{:S(2)}, u32[]{:S(2)}) collective-permute-start(bf16[32,4096]{1,0:T(8,128)(2,1)S(1)} %constant_dynamic-slice_fusion), channel_id=1, source_target_pairs={{0,8},{8,0},{4,12},{12,4},{1,9},{9,1},{5,13},{13,5},{2,10},{10,2},... | collective-permute-start | bytes 786440 | tf_op jit(solution)/shard_map/ppermute | solution.py:245
  19.5 16.0 %collective-permute-start.1 = (bf16[32,4096]{1,0:T(8,128)(2,1)S(1)}, bf16[32,4096]{1,0:T(8,128)(2,1)S(1)}, u32[]{:S(2)}, u32[]{:S(2)}) collective-permute-start(bf16[32,4096]{1,0:T(8,128)(2,1)S(1)} %constant_dynamic-slice_fusion), channel_id=1, source_target_pairs={{0,4},{4,0},{8,12},{12,8},{1,5},{5,1},{9,13},{13,9},{2,6},{6,2},{1... | collective-permute-start | bytes 786440 | tf_op jit(solution)/shard_map/ppermute | solution.py:245
  19.7 7.3 %collective-permute-start.4 = (bf16[2,64,1024]{2,1,0:T(8,128)(2,1)S(1)}, bf16[2,64,1024]{2,1,0:T(8,128)(2,1)}, u32[]{:S(2)}, u32[]{:S(2)}) collective-permute-start(bf16[2,64,1024]{2,1,0:T(8,128)(2,1)S(1)} %copy-done.6), channel_id=1, source_target_pairs={{0,2},{2,0},{1,3},{3,1},{4,6},{6,4},{5,7},{7,5},{8,10},{10,8},{9,1... | collective-permute-start | bytes 786440 | tf_op jit(solution)/shard_map/ppermute | solution.py:242
  22.2 6.0 %collective-permute-start.6 = (bf16[16,4096]{1,0:T(8,128)(2,1)}, bf16[16,4096]{1,0:T(8,128)(2,1)S(1)}, u32[]{:S(2)}, u32[]{:S(2)}) collective-permute-start(bf16[16,4096]{1,0:T(8,128)(2,1)} %get-tuple-element.97), channel_id=1, source_target_pairs={{0,1},{1,0},{2,3},{3,2},{4,5},{5,4},{6,7},{7,6},{8,9},{9,8},{10,11... | collective-permute-start | bytes 393224 | tf_op jit(solution)/shard_map/ppermute | solution.py:239
  27.0 2.9 %collective-permute-start.5 = (bf16[16,4096]{1,0:T(8,128)(2,1)}, bf16[16,4096]{1,0:T(8,128)(2,1)S(1)}, u32[]{:S(2)}, u32[]{:S(2)}) collective-permute-start(bf16[16,4096]{1,0:T(8,128)(2,1)} %get-tuple-element.98), channel_id=1, source_target_pairs={{0,1},{1,0},{2,3},{3,2},{4,5},{5,4},{6,7},{7,6},{8,9},{9,8},{10,11... | collective-permute-start | bytes 393224 | tf_op jit(solution)/shard_map/ppermute | solution.py:239
  28.2 14.2 %collective-permute-start.12 = (bf16[32,4096]{1,0:T(8,128)(2,1)S(1)}, bf16[32,4096]{1,0:T(8,128)(2,1)S(1)}, u32[]{:S(2)}, u32[]{:S(2)}) collective-permute-start(bf16[32,4096]{1,0:T(8,128)(2,1)S(1)} %collective-permute-done.3.mine_ref), channel_id=1, source_target_pairs={{0,4},{4,0},{8,12},{12,8},{1,5},{5,1},{9,13},{13,9},{2,6},{6,2},{1... | collective-permute-start | bytes 786440 | tf_op jit(solution)/shard_map/ppermute | solution.py:245
  29.9 3.4 %copy-start.1 = (bf16[4096,1024]{1,0:T(8,128)(2,1)S(1)}, bf16[4096,1024]{1,0:T(8,128)(2,1)}, u32[]{:S(2)}) copy-start(bf16[4096,1024]{1,0:T(8,128)(2,1)} %copy-done) | copy-start | bytes 25165828
  35.5 4.1 %collective-permute-start.9 = (bf16[32,4096]{1,0:T(8,128)(2,1)S(1)}, bf16[32,4096]{1,0:T(8,128)(2,1)S(1)}, u32[]{:S(2)}, u32[]{:S(2)}) collective-permute-start(bf16[32,4096]{1,0:T(8,128)(2,1)S(1)} %collective-permute-done.near_ref), channel_id=1, source_target_pairs={{0,1},{1,0},{2,3},{3,2},{4,5},{5,4},{6,7},{7,6},{8,9},{9,8},{10,11... | collective-permute-start | bytes 786440 | tf_op jit(solution)/shard_map/ppermute | solution.py:239
  35.8 3.8 %collective-permute-start.10 = (bf16[32,4096]{1,0:T(8,128)(2,1)S(1)}, bf16[32,4096]{1,0:T(8,128)(2,1)S(1)}, u32[]{:S(2)}, u32[]{:S(2)}) collective-permute-start(bf16[32,4096]{1,0:T(8,128)(2,1)S(1)} %collective-permute-done.1.near_too_ref), channel_id=1, source_target_pairs={{0,1},{1,0},{2,3},{3,2},{4,5},{5,4},{6,7},{7,6},{8,9},{9,8},{10,11... | collective-permute-start | bytes 786440 | tf_op jit(solution)/shard_map/ppermute | solution.py:239
  36.1 1.6 %collective-permute-start.8 = (bf16[16,4096]{1,0:T(8,128)(2,1)S(1)}, bf16[16,4096]{1,0:T(8,128)(2,1)S(1)}, u32[]{:S(2)}, u32[]{:S(2)}) collective-permute-start(bf16[16,4096]{1,0:T(8,128)(2,1)S(1)} %get-tuple-element.95), channel_id=1, source_target_pairs={{0,1},{1,0},{2,3},{3,2},{4,5},{5,4},{6,7},{7,6},{8,9},{9,8},{10,11... | collective-permute-start | bytes 393224 | tf_op jit(solution)/shard_map/ppermute | solution.py:239
  36.4 1.7 %collective-permute-start.7 = (bf16[16,4096]{1,0:T(8,128)(2,1)S(1)}, bf16[16,4096]{1,0:T(8,128)(2,1)S(1)}, u32[]{:S(2)}, u32[]{:S(2)}) collective-permute-start(bf16[16,4096]{1,0:T(8,128)(2,1)S(1)} %get-tuple-element.96), channel_id=1, source_target_pairs={{0,1},{1,0},{2,3},{3,2},{4,5},{5,4},{6,7},{7,6},{8,9},{9,8},{10,11... | collective-permute-start | bytes 393224 | tf_op jit(solution)/shard_map/ppermute | solution.py:239
  37.7 9.6 %collective-permute-start.13 = (bf16[32,4096]{1,0:T(8,128)(2,1)S(1)}, bf16[32,4096]{1,0:T(8,128)(2,1)S(1)}, u32[]{:S(2)}, u32[]{:S(2)}) collective-permute-start(bf16[32,4096]{1,0:T(8,128)(2,1)S(1)} %collective-permute-done.2.mine_ref), channel_id=1, source_target_pairs={{0,4},{4,0},{8,12},{12,8},{1,5},{5,1},{9,13},{13,9},{2,6},{6,2},{1... | collective-permute-start | bytes 786440 | tf_op jit(solution)/shard_map/ppermute | solution.py:245
  38.2 5.4 %collective-permute-start.11 = (bf16[64,1024]{1,0:T(8,128)(2,1)S(1)}, bf16[64,1024]{1,0:T(8,128)(2,1)S(1)}, u32[]{:S(2)}, u32[]{:S(2)}) collective-permute-start(bf16[64,1024]{1,0:T(8,128)(2,1)S(1)} %get-tuple-element.61), channel_id=1, source_target_pairs={{0,2},{2,0},{1,3},{3,1},{4,6},{6,4},{5,7},{7,5},{8,10},{10,8},{9,1... | collective-permute-start | bytes 393224 | tf_op jit(solution)/shard_map/ppermute | solution.py:242
  42.4 2.6 %collective-permute-start.16 = (bf16[16,4096]{1,0:T(8,128)(2,1)S(1)}, bf16[16,4096]{1,0:T(8,128)(2,1)S(1)}, u32[]{:S(2)}, u32[]{:S(2)}) collective-permute-start(bf16[16,4096]{1,0:T(8,128)(2,1)S(1)} %get-tuple-element.93), channel_id=1, source_target_pairs={{0,1},{1,0},{2,3},{3,2},{4,5},{5,4},{6,7},{7,6},{8,9},{9,8},{10,11... | collective-permute-start | bytes 393224 | tf_op jit(solution)/shard_map/ppermute | solution.py:239
  42.5 2.5 %collective-permute-start.15 = (bf16[16,4096]{1,0:T(8,128)(2,1)S(1)}, bf16[16,4096]{1,0:T(8,128)(2,1)S(1)}, u32[]{:S(2)}, u32[]{:S(2)}) collective-permute-start(bf16[16,4096]{1,0:T(8,128)(2,1)S(1)} %get-tuple-element.94), channel_id=1, source_target_pairs={{0,1},{1,0},{2,3},{3,2},{4,5},{5,4},{6,7},{7,6},{8,9},{9,8},{10,11... | collective-permute-start | bytes 393224 | tf_op jit(solution)/shard_map/ppermute | solution.py:239
  43.5 5.0 %collective-permute-start.14 = (bf16[64,1024]{1,0:T(8,128)(2,1)S(1)}, bf16[64,1024]{1,0:T(8,128)(2,1)S(1)}, u32[]{:S(2)}, u32[]{:S(2)}) collective-permute-start(bf16[64,1024]{1,0:T(8,128)(2,1)S(1)} %get-tuple-element.66), channel_id=1, source_target_pairs={{0,2},{2,0},{1,3},{3,1},{4,6},{6,4},{5,7},{7,5},{8,10},{10,8},{9,1... | collective-permute-start | bytes 393224 | tf_op jit(solution)/shard_map/ppermute | solution.py:242
  45.0 17.2 %copy-start.5 = (bf16[256,1024]{1,0:T(8,128)(2,1)S(1)}, bf16[256,1024]{1,0:T(8,128)(2,1)}, u32[]{:S(2)}) copy-start(bf16[256,1024]{1,0:T(8,128)(2,1)} %residual_ref.1) | copy-start | bytes 1572868
  48.5 1.4 %collective-permute-start.19 = (bf16[16,4096]{1,0:T(8,128)(2,1)S(1)}, bf16[16,4096]{1,0:T(8,128)(2,1)S(1)}, u32[]{:S(2)}, u32[]{:S(2)}) collective-permute-start(bf16[16,4096]{1,0:T(8,128)(2,1)S(1)} %get-tuple-element.91), channel_id=1, source_target_pairs={{0,1},{1,0},{2,3},{3,2},{4,5},{5,4},{6,7},{7,6},{8,9},{9,8},{10,11... | collective-permute-start | bytes 393224 | tf_op jit(solution)/shard_map/ppermute | solution.py:239
  48.6 1.5 %collective-permute-start.18 = (bf16[16,4096]{1,0:T(8,128)(2,1)S(1)}, bf16[16,4096]{1,0:T(8,128)(2,1)S(1)}, u32[]{:S(2)}, u32[]{:S(2)}) collective-permute-start(bf16[16,4096]{1,0:T(8,128)(2,1)S(1)} %get-tuple-element.92), channel_id=1, source_target_pairs={{0,1},{1,0},{2,3},{3,2},{4,5},{5,4},{6,7},{7,6},{8,9},{9,8},{10,11... | collective-permute-start | bytes 393224 | tf_op jit(solution)/shard_map/ppermute | solution.py:239
  52.4 4.0 %collective-permute-start.21 = (bf16[128,128]{1,0:T(8,128)(2,1)S(1)}, bf16[128,128]{1,0:T(8,128)(2,1)S(1)}, u32[]{:S(2)}, u32[]{:S(2)}) collective-permute-start(bf16[128,128]{1,0:T(8,128)(2,1)S(1)} %get-tuple-element.83), channel_id=1, source_target_pairs={{0,2},{2,0},{1,3},{3,1},{4,6},{6,4},{5,7},{7,5},{8,10},{10,8},{9,1... | collective-permute-start | bytes 98312 | tf_op jit(solution)/shard_map/ppermute | solution.py:242
  53.9 6.6 %collective-permute-start.17 = (bf16[64,1024]{1,0:T(8,128)(2,1)S(1)}, bf16[64,1024]{1,0:T(8,128)(2,1)S(1)}, u32[]{:S(2)}, u32[]{:S(2)}) collective-permute-start(bf16[64,1024]{1,0:T(8,128)(2,1)S(1)} %get-tuple-element.71), channel_id=1, source_target_pairs={{0,2},{2,0},{1,3},{3,1},{4,6},{6,4},{5,7},{7,5},{8,10},{10,8},{9,1... | collective-permute-start | bytes 393224 | tf_op jit(solution)/shard_map/ppermute | solution.py:242
  54.5 7.7 %collective-permute-start.20 = (bf16[64,1024]{1,0:T(8,128)(2,1)S(1)}, bf16[64,1024]{1,0:T(8,128)(2,1)S(1)}, u32[]{:S(2)}, u32[]{:S(2)}) collective-permute-start(bf16[64,1024]{1,0:T(8,128)(2,1)S(1)} %get-tuple-element.79), channel_id=1, source_target_pairs={{0,2},{2,0},{1,3},{3,1},{4,6},{6,4},{5,7},{7,5},{8,10},{10,8},{9,1... | collective-permute-start | bytes 393224 | tf_op jit(solution)/shard_map/ppermute | solution.py:242
  56.4 4.1 %collective-permute-start.22 = (bf16[128,128]{1,0:T(8,128)(2,1)S(1)}, bf16[128,128]{1,0:T(8,128)(2,1)S(1)}, u32[]{:S(2)}, u32[]{:S(2)}) collective-permute-start(bf16[128,128]{1,0:T(8,128)(2,1)S(1)} %multiply_convert_fusion.refs_0_), channel_id=1, source_target_pairs={{0,4},{4,0},{8,12},{12,8},{1,9},{9,1},{5,13},{13,5},{2,6},{6,2},{1... | collective-permute-start | bytes 98312 | tf_op jit(solution)/shard_map/ppermute | solution.py:331
  58.0 5.7 %collective-permute-start.23 = (bf16[128,128]{1,0:T(8,128)(2,1)S(1)}, bf16[128,128]{1,0:T(8,128)(2,1)S(1)}, u32[]{:S(2)}, u32[]{:S(2)}) collective-permute-start(bf16[128,128]{1,0:T(8,128)(2,1)S(1)} %multiply_convert_fusion.refs_0_), channel_id=1, source_target_pairs={{0,12},{12,0},{4,8},{8,4},{1,13},{13,1},{5,9},{9,5},{2,14},{14,2},... | collective-permute-start | bytes 98312 | tf_op jit(solution)/shard_map/ppermute | solution.py:245
  60.5 3.3 %collective-permute-start.24 = (bf16[128,128]{1,0:T(8,128)(2,1)S(1)}, bf16[128,128]{1,0:T(8,128)(2,1)S(1)}, u32[]{:S(2)}, u32[]{:S(2)}) collective-permute-start(bf16[128,128]{1,0:T(8,128)(2,1)S(1)} %collective-permute-done.22.refs_1_), channel_id=1, source_target_pairs={{0,1},{1,0},{2,3},{3,2},{4,5},{5,4},{6,7},{7,6},{8,9},{9,8},{10,11... | collective-permute-start | bytes 98312 | tf_op jit(solution)/shard_map/ppermute | solution.py:239

commit v16 on v15

--- a/solution.py
+++ b/solution.py
@@ -266,12 +266,12 @@
     hot = slot[None, :] == jnp.arange(slots, dtype=jnp.int32)[:, None]
     hot = jnp.broadcast_to(hot[:, :, None], (slots, own, width)).astype(BF16)
 
-    def cut(rows, piece):
-        return lax.dynamic_slice_in_dim(rows, c * half + piece * step, step, 0)
-
-    mine = cut(rows, 0)
-    rows, hot, scale = barrier((rows, hot, scale))
+    mine = lax.dynamic_slice_in_dim(rows, c * half, step, 0)
     far, near = [along(mine, FAR)], [along(mine, NEAR)]
+    offset = [(c * half + step).astype(jnp.uint32), jnp.zeros((), jnp.uint32)]
+    rows, hot, scale, flags, offset, first_slots = barrier(
+        (rows, hot, scale, flags, offset, x == 0)
+    )
     held, own_sum, own_low = call(
         own_kernel,
         [shape(weight.shape, BF16), shape((block_rows, cols), F32)] + lows(block_rows),
@@ -281,11 +281,11 @@
         FROM_HBM,
     )
     up, rows, own_sum = barrier((up, rows, own_sum))
-    mine = cut(rows, 1)
+    mine = lax.dynamic_slice(rows, offset, (step, rows.shape[1]))
     far.append(along(mine, FAR))
     near.append(along(mine, NEAR))
     up_other = over_x(up)
-    ups = jnp.where(x == 0, jnp.concatenate([up, up_other]), jnp.concatenate([up_other, up]))
+    ups = jnp.where(first_slots, jnp.concatenate([up, up_other]), jnp.concatenate([up_other, up]))
     far[0], own_sum, own_low = barrier((far[0], own_sum, own_low))
 
     def parted_piece(piece, against, value):

time: 65.6 us -> 59.8 us (0.912)
  local copies, waits for them, and re-layouts: 11.9 us -> 3.64 us
  waiting for transfers between devices: 11.5 us -> 14.9 us
  other arithmetic: 2.4 us -> 1.37 us
    unnamed x14 -> x8, local copies, waits for them, and re-layouts: 8.93 us -> 2.27 us
    ppermute x7, waiting for transfers between devices: 0.81 us -> 2.36 us  [along(): return lax.ppermute(value, 'blk', pairs)]
    ppermute x7, starting transfers between devices: 10.8 us -> 12.3 us  [along(): return lax.ppermute(value, 'blk', pairs)]
    ppermute x1, waiting for transfers between devices: 0.01 us -> 1.22 us  [line(): lax.ppermute(scaled, ('blk', 'sub'), by_core(NEAR, FAR))]
    ppermute x1, starting transfers between devices: 1.64 us -> 0.44 us  [line(): lax.ppermute(scaled, ('blk', 'sub'), by_core(NEAR, FAR))]
    select_n x1, other arithmetic: 1.12 us -> 0.08 us  [line(): jnp.where(first_slots, jnp.concatenate([up, up_other]), jnp.concatenate([...]
    dynamic_slice x2, local copies, waits for them, and re-layouts: 2.01 us -> 1.09 us  [the longest x1 1.01 us: line(): mine = lax.dynamic_slice_in_dim(rows, c * half, step, 0)]
    slice x4, local copies, waits for them, and re-layouts: 0.77 us -> 0.07 us  [over_core_in_two(): return [over_core(piece[:count]), over_core(piece[count:])]]
  transfers between devices with their start and end apart: 25 -> 25, of which waited for: 9 -> 10; matrix products, arithmetic and copies ran while one was open for 7% -> 3% of each run, Pallas kernels for 19% -> 21%
where the time goes in v16:
time: 59.8 us; the launch traced here: 59.5 us
  starting transfers between devices  23.3 us (39%)
  Pallas kernels  16.2 us (27%)
  waiting for transfers between devices  14.9 us (25%)
  local copies, waits for them, and re-layouts  3.64 us (6%)
  other arithmetic  1.37 us (2%)
    pallas_call x7, Pallas kernels, call(): pl.pallas_call(kernel, out_shape=outs, in_specs=in_specs, out_specs=jax.t...  16.2 us
    ppermute x7, starting transfers between devices, along(): return lax.ppermute(value, 'blk', pairs)  12.3 us
    ppermute x6, waiting for transfers between devices, over_x(): return lax.ppermute(value, 'split', SWAP)  9.29 us
    ppermute x6, starting transfers between devices, over_x(): return lax.ppermute(value, 'split', SWAP)  8.19 us
    ppermute x7, waiting for transfers between devices, along(): return lax.ppermute(value, 'blk', pairs)  2.36 us
    ppermute x11, starting transfers between devices, over_core(): return lax.ppermute(value, 'sub', SWAP)  2.29 us
    unnamed x8, local copies, waits for them, and re-layouts  2.27 us
    ppermute x11, waiting for transfers between devices, over_core(): return lax.ppermute(value, 'sub', SWAP)  2.03 us
  transfers between devices with their start and end apart: 25, of which 10 were waited for; matrix products, arithmetic and copies ran while one was open for 3% of the time, Pallas kernels for 21%

profile of v16, /device:TPU:0, one launch (start us, length us, event | category | flops | bytes accessed | tf_op | source)
XLA Modules:
  0.0 59.5 jit_solution(2932846682818109880)
XLA Ops:
  0.0 1.0 %constant_dynamic-slice_fusion.1 = bf16[32,4096]{1,0:T(8,128)(2,1)S(1)} fusion(bf16[128,4096]{1,0:T(8,128)(2,1)} %rows_ref, s32[]{:T(128)S(6)} %select_n.39), kind=kLoop, calls=%fused_computation.14 | loop fusion | bytes 524292 | tf_op jit(solution)/shard_map/dynamic_slice | solution.py:269
  1.0 4.1 %collective-permute-start.3 = (bf16[32,4096]{1,0:T(8,128)(2,1)S(1)}, bf16[32,4096]{1,0:T(8,128)(2,1)S(1)}, u32[]{:S(2)}, u32[]{:S(2)}) collective-permute-start(bf16[32,4096]{1,0:T(8,128)(2,1)S(1)} %constant_dynamic-slice_fusion.1), channel_id=1, source_target_pairs={{0,8},{8,0},{4,12},{12,4},{1,9},{9,1},{5,13},{13,5},{2,10},{10,2},... | collective-permute-start | bytes 786440 | tf_op jit(solution)/shard_map/ppermute | solution.py:245
  5.1 1.6 %collective-permute-start = (bf16[32,4096]{1,0:T(8,128)(2,1)S(1)}, bf16[32,4096]{1,0:T(8,128)(2,1)S(1)}, u32[]{:S(2)}, u32[]{:S(2)}) collective-permute-start(bf16[32,4096]{1,0:T(8,128)(2,1)S(1)} %constant_dynamic-slice_fusion.1), channel_id=1, source_target_pairs={{0,4},{4,0},{8,12},{12,8},{1,5},{5,1},{9,13},{13,9},{2,6},{6,2},{1... | collective-permute-start | bytes 786440 | tf_op jit(solution)/shard_map/ppermute | solution.py:245
  6.7 0.8 %select_reduce_fusion = (s32[512]{0:T(512)S(1)}, s32[512]{0:T(512)S(1)}) fusion(s32[4]{0:T(128)} %param.15, s32[512]{0:T(512)} %param.13, s32[4]{0:T(128)} %param.14), kind=kLoop, calls=%fused_computation.5 | loop fusion | flops 9216 | bytes 6176 | tf_op jit(solution)/shard_map/reduce_sum | solution.py:26
  7.5 0.1 convert_divide_fusion
  7.6 0.1 broadcast_compare_fusion
  7.6 0.2 select_select_fusion
  7.8 0.1 pad_maximum_fusion
  7.9 0.1 pad_add_fusion.flags_ref
  8.0 0.2 broadcast_in_dim.24.hot_ref
  8.2 1.0 %copy-done = bf16[1,64,4096]{2,1,0:T(8,128)(2,1)S(1)} copy-done((bf16[1,64,4096]{2,1,0:T(8,128)(2,1)S(1)}, bf16[1,64,4096]{2,1,0:T(8,128)(2,1)}, u32[]{:S(2)}) %copy-start) | copy-done | bytes 524312
  9.3 1.2 %copy-done.1 = bf16[128,4096]{1,0:T(8,128)(2,1)S(1)} copy-done((bf16[128,4096]{1,0:T(8,128)(2,1)S(1)}, bf16[128,4096]{1,0:T(8,128)(2,1)}, u32[]{:S(2)}) %copy-start.1) | copy-done | bytes 1048600
  10.5 4.4 %shard_map.82 = (bf16[4096,1024]{1,0:T(8,128)(2,1)S(1)}, f32[128,1024]{1,0:T(8,128)S(1)}, f32[128,64]{1,0:T(8,128)S(1)}) custom-call(bf16[4096,1024]{1,0:T(8,128)(2,1)} %weight_ref.1, bf16[64,4096]{1,0:T(8,128)(2,1)S(1)} %bitcast.4, bf16[128,4096]{1,0:T(8,128)(2,1)S(1)} %copy-done.1), custom_call_target="tpu_custom_call" | custom-call | tf_op jit(solution)/shard_map/pallas_call | solution.py:91
  14.9 0.1 constant_dynamic-slice_fusion
  15.0 0.4 collective-permute-start.2
  15.4 0.2 collective-permute-start.1
  15.6 1.8 %collective-permute-start.4 = (bf16[2,64,1024]{2,1,0:T(8,128)(2,1)S(1)}, bf16[2,64,1024]{2,1,0:T(8,128)(2,1)S(1)}, u32[]{:S(2)}, u32[]{:S(2)}) collective-permute-start(bf16[2,64,1024]{2,1,0:T(8,128)(2,1)S(1)} %copy-done.3), channel_id=1, source_target_pairs={{0,2},{2,0},{1,3},{3,1},{4,6},{6,4},{5,7},{7,5},{8,10},{10,8},{9,1... | collective-permute-start | bytes 786440 | tf_op jit(solution)/shard_map/ppermute | solution.py:242
  17.4 5.4 %collective-permute-done.4 = bf16[2,64,1024]{2,1,0:T(8,128)(2,1)S(1)} collective-permute-done((bf16[2,64,1024]{2,1,0:T(8,128)(2,1)S(1)}, bf16[2,64,1024]{2,1,0:T(8,128)(2,1)S(1)}, u32[]{:S(2)}, u32[]{:S(2)}) %collective-permute-start.4) | collective-permute-done | bytes 262176 | tf_op jit(solution)/shard_map/ppermute | solution.py:242
  22.8 0.1 maximum_select_fusion.ups_ref
  22.9 1.6 %collective-permute-start.12 = (bf16[32,4096]{1,0:T(8,128)(2,1)S(1)}, bf16[32,4096]{1,0:T(8,128)(2,1)S(1)}, u32[]{:S(2)}, u32[]{:S(2)}) collective-permute-start(bf16[32,4096]{1,0:T(8,128)(2,1)S(1)} %collective-permute-done.3.mine_ref), channel_id=1, source_target_pairs={{0,4},{4,0},{8,12},{12,8},{1,5},{5,1},{9,13},{13,9},{2,6},{6,2},{1... | collective-permute-start | bytes 786440 | tf_op jit(solution)/shard_map/ppermute | solution.py:245
  24.5 2.3 %shard_map.83 = (f32[64,1024]{1,0:T(8,128)S(1)}, bf16[64,1024]{1,0:T(8,128)(2,1)S(1)}, f32[64,64]{1,0:T(8,128)S(1)}) custom-call(s32[3]{0:T(128)S(1)} %pad_add_fusion.flags_ref, bf16[4096,1024]{1,0:T(8,128)(2,1)S(1)} %get-tuple-element.58.weight_ref, bf16[64,4096]{1,0:T(8,128)(2,1)S(1)} %bitcast.5, f32[128,1024]{1,0:T(8,128)S(1)} %get-tuple-element.62.held_ref, ...), custom_call_target="tpu_custom_call" | custom-call | tf_op jit(solution)/shard_map/pallas_call | solution.py:91
  26.8 2.3 %collective-permute-done.2.mine_ref = bf16[32,4096]{1,0:T(8,128)(2,1)S(1)} collective-permute-done((bf16[32,4096]{1,0:T(8,128)(2,1)S(1)}, bf16[32,4096]{1,0:T(8,128)(2,1)S(1)}, u32[]{:S(2)}, u32[]{:S(2)}) %collective-permute-start.2) | collective-permute-done | bytes 262176 | tf_op jit(solution)/shard_map/ppermute | solution.py:245
  29.1 0.5 collective-permute-start.10
  29.7 0.1 collective-permute-start.8
  29.8 0.5 collective-permute-start.7
  30.2 1.0 %collective-permute-done.8.second_ref = bf16[16,4096]{1,0:T(8,128)(2,1)S(1)} collective-permute-done((bf16[16,4096]{1,0:T(8,128)(2,1)S(1)}, bf16[16,4096]{1,0:T(8,128)(2,1)S(1)}, u32[]{:S(2)}, u32[]{:S(2)}) %collective-permute-start.8) | collective-permute-done | bytes 131104 | tf_op jit(solution)/shard_map/ppermute | solution.py:239
  31.2 2.1 %collective-permute-start.13 = (bf16[32,4096]{1,0:T(8,128)(2,1)S(1)}, bf16[32,4096]{1,0:T(8,128)(2,1)S(1)}, u32[]{:S(2)}, u32[]{:S(2)}) collective-permute-start(bf16[32,4096]{1,0:T(8,128)(2,1)S(1)} %collective-permute-done.2.mine_ref), channel_id=1, source_target_pairs={{0,4},{4,0},{8,12},{12,8},{1,5},{5,1},{9,13},{13,9},{2,6},{6,2},{1... | collective-permute-start | bytes 786440 | tf_op jit(solution)/shard_map/ppermute | solution.py:245
  33.4 1.5 %collective-permute-start.11 = (bf16[64,1024]{1,0:T(8,128)(2,1)S(1)}, bf16[64,1024]{1,0:T(8,128)(2,1)S(1)}, u32[]{:S(2)}, u32[]{:S(2)}) collective-permute-start(bf16[64,1024]{1,0:T(8,128)(2,1)S(1)} %get-tuple-element.67), channel_id=1, source_target_pairs={{0,2},{2,0},{1,3},{3,1},{4,6},{6,4},{5,7},{7,5},{8,10},{10,8},{9,1... | collective-permute-start | bytes 393224 | tf_op jit(solution)/shard_map/ppermute | solution.py:242
  34.9 2.7 %shard_map.84 = (f32[64,1024]{1,0:T(8,128)S(1)}, bf16[64,1024]{1,0:T(8,128)(2,1)S(1)}, f32[128,1024]{1,0:T(8,128)S(1)}, f32[192,64]{1,0:T(8,128)S(1)}) custom-call(s32[3]{0:T(128)S(1)} %pad_add_fusion.flags_ref, bf16[4096,1024]{1,0:T(8,128)(2,1)S(1)} %get-tuple-element.58.weight_ref, bf16[64,4096]{1,0:T(8,128)(2,1)S(1)} %bitcast.6, ...), custom_call_target="tpu_custom_call" | custom-call | tf_op jit(solution)/shard_map/pallas_call | solution.py:91
  37.7 0.5 collective-permute-start.15
  38.2 0.4 collective-permute-done.11.refs_1_
  38.6 1.5 %collective-permute-start.14 = (bf16[64,1024]{1,0:T(8,128)(2,1)S(1)}, bf16[64,1024]{1,0:T(8,128)(2,1)S(1)}, u32[]{:S(2)}, u32[]{:S(2)}) collective-permute-start(bf16[64,1024]{1,0:T(8,128)(2,1)S(1)} %get-tuple-element.72), channel_id=1, source_target_pairs={{0,2},{2,0},{1,3},{3,1},{4,6},{6,4},{5,7},{7,5},{8,10},{10,8},{9,1... | collective-permute-start | bytes 393224 | tf_op jit(solution)/shard_map/ppermute | solution.py:242
  40.1 2.3 %shard_map.85 = (f32[64,1024]{1,0:T(8,128)S(1)}, bf16[64,1024]{1,0:T(8,128)(2,1)S(1)}, f32[64,64]{1,0:T(8,128)S(1)}) custom-call(s32[3]{0:T(128)S(1)} %pad_add_fusion.flags_ref, bf16[4096,1024]{1,0:T(8,128)(2,1)S(1)} %get-tuple-element.58.weight_ref, bf16[64,4096]{1,0:T(8,128)(2,1)S(1)} %bitcast.7, f32[128,1024]{1,0:T(8,128)S(1)} %get-tuple-element.78.held_ref, ...), custom_call_target="tpu_custom_call" | custom-call | tf_op jit(solution)/shard_map/pallas_call | solution.py:91
  42.4 1.3 %collective-permute-done.14.refs_3_ = bf16[64,1024]{1,0:T(8,128)(2,1)S(1)} collective-permute-done((bf16[64,1024]{1,0:T(8,128)(2,1)S(1)}, bf16[64,1024]{1,0:T(8,128)(2,1)S(1)}, u32[]{:S(2)}, u32[]{:S(2)}) %collective-permute-start.14) | collective-permute-done | bytes 131104 | tf_op jit(solution)/shard_map/ppermute | solution.py:242
  43.8 0.5 collective-permute-start.18
  44.3 0.8 %collective-permute-done.19.second_ref = bf16[16,4096]{1,0:T(8,128)(2,1)S(1)} collective-permute-done((bf16[16,4096]{1,0:T(8,128)(2,1)S(1)}, bf16[16,4096]{1,0:T(8,128)(2,1)S(1)}, u32[]{:S(2)}, u32[]{:S(2)}) %collective-permute-start.19) | collective-permute-done | bytes 131104 | tf_op jit(solution)/shard_map/ppermute | solution.py:239
  45.1 0.2 collective-permute-done.18.first_ref
  45.3 2.3 %shard_map.86 = (f32[64,1024]{1,0:T(8,128)S(1)}, bf16[64,1024]{1,0:T(8,128)(2,1)S(1)}, f32[128,128]{1,0:T(8,128)S(1)}, bf16[128,128]{1,0:T(8,128)(2,1)S(1)}) custom-call(s32[3]{0:T(128)S(1)} %pad_add_fusion.flags_ref, bf16[4096,1024]{1,0:T(8,128)(2,1)S(1)} %get-tuple-element.58.weight_ref, bf16[64,4096]{1,0:T(8,128)(2,1)S(1)} %bitcast.8, ...), custom_call_target="tpu_custom_call" | custom-call | tf_op jit(solution)/shard_map/pallas_call | solution.py:91
  47.6 1.4 %collective-permute-start.21 = (bf16[128,128]{1,0:T(8,128)(2,1)S(1)}, bf16[128,128]{1,0:T(8,128)(2,1)S(1)}, u32[]{:S(2)}, u32[]{:S(2)}) collective-permute-start(bf16[128,128]{1,0:T(8,128)(2,1)S(1)} %get-tuple-element.89), channel_id=1, source_target_pairs={{0,2},{2,0},{1,3},{3,1},{4,6},{6,4},{5,7},{7,5},{8,10},{10,8},{9,1... | collective-permute-start | bytes 98312 | tf_op jit(solution)/shard_map/ppermute | solution.py:242
  49.0 0.7 %collective-permute-start.17 = (bf16[64,1024]{1,0:T(8,128)(2,1)S(1)}, bf16[64,1024]{1,0:T(8,128)(2,1)S(1)}, u32[]{:S(2)}, u32[]{:S(2)}) collective-permute-start(bf16[64,1024]{1,0:T(8,128)(2,1)S(1)} %get-tuple-element.77), channel_id=1, source_target_pairs={{0,2},{2,0},{1,3},{3,1},{4,6},{6,4},{5,7},{7,5},{8,10},{10,8},{9,1... | collective-permute-start | bytes 393224 | tf_op jit(solution)/shard_map/ppermute | solution.py:242
  49.7 1.4 %collective-permute-start.20 = (bf16[64,1024]{1,0:T(8,128)(2,1)S(1)}, bf16[64,1024]{1,0:T(8,128)(2,1)S(1)}, u32[]{:S(2)}, u32[]{:S(2)}) collective-permute-start(bf16[64,1024]{1,0:T(8,128)(2,1)S(1)} %get-tuple-element.85), channel_id=1, source_target_pairs={{0,2},{2,0},{1,3},{3,1},{4,6},{6,4},{5,7},{7,5},{8,10},{10,8},{9,1... | collective-permute-start | bytes 393224 | tf_op jit(solution)/shard_map/ppermute | solution.py:242
  51.0 0.5 collective-permute-done.21
  51.6 0.4 collective-permute-start.22
  52.0 2.3 %collective-permute-start.23 = (bf16[128,128]{1,0:T(8,128)(2,1)S(1)}, bf16[128,128]{1,0:T(8,128)(2,1)S(1)}, u32[]{:S(2)}, u32[]{:S(2)}) collective-permute-start(bf16[128,128]{1,0:T(8,128)(2,1)S(1)} %multiply_convert_fusion.refs_0_), channel_id=1, source_target_pairs={{0,12},{12,0},{4,8},{8,4},{1,13},{13,1},{5,9},{9,5},{2,14},{14,2},... | collective-permute-start | bytes 98312 | tf_op jit(solution)/shard_map/ppermute | solution.py:245
  54.3 1.2 %collective-permute-done.22.refs_1_ = bf16[128,128]{1,0:T(8,128)(2,1)S(1)} collective-permute-done((bf16[128,128]{1,0:T(8,128)(2,1)S(1)}, bf16[128,128]{1,0:T(8,128)(2,1)S(1)}, u32[]{:S(2)}, u32[]{:S(2)}) %collective-permute-start.22) | collective-permute-done | bytes 32800 | tf_op jit(solution)/shard_map/ppermute | solution.py:331
  55.6 1.7 %collective-permute-done.20.refs_7_ = bf16[64,1024]{1,0:T(8,128)(2,1)S(1)} collective-permute-done((bf16[64,1024]{1,0:T(8,128)(2,1)S(1)}, bf16[64,1024]{1,0:T(8,128)(2,1)S(1)}, u32[]{:S(2)}, u32[]{:S(2)}) %collective-permute-start.20) | collective-permute-done | bytes 131104 | tf_op jit(solution)/shard_map/ppermute | solution.py:242
  57.3 0.7 %shard_map.87.base_ref = f32[256,1024]{1,0:T(8,128)S(1)} custom-call(s32[3]{0:T(128)S(1)} %pad_add_fusion.flags_ref, bf16[256,1024]{1,0:T(8,128)(2,1)S(1)} %copy-done.2, f32[64,1024]{1,0:T(8,128)S(1)} %get-tuple-element.61.refs_0_, bf16[64,1024]{1,0:T(8,128)(2,1)S(1)} %collective-permute-done.11.refs_1_, f32[64,1024]{1,0:T(8,128)S(1)} %get-tuple-element.70.refs_2_, ...), custom_call_target="tpu_custom_call" | custom-call | tf_op jit(solution)/shard_map/pallas_call | solution.py:91
  58.0 1.5 %shard_map.88 = bf16[256,1024]{1,0:T(8,128)(2,1)} custom-call(f32[256,1024]{1,0:T(8,128)S(1)} %shard_map.87.base_ref, bf16[4,256,64]{2,1,0:T(8,128)(2,1)S(1)} %broadcast_in_dim.24.hot_ref, bf16[4,64,1024]{2,1,0:T(8,128)(2,1)S(1)} %maximum_select_fusion.ups_ref, bf16[128,128]{1,0:T(8,128)(2,1)S(1)} %multiply_convert_fusion.refs_0_, ...), custom_call_target="tpu_custom_call" | custom-call | tf_op jit(solution)/shard_map/pallas_call | solution.py:91
  (34 shorter events, 0.4 us)
Async XLA Ops:
  0.0 15.6 %copy-start.3 = (bf16[2,64,1024]{2,1,0:T(8,128)(2,1)S(1)}, bf16[2,64,1024]{2,1,0:T(8,128)(2,1)}, u32[]{:S(2)}) copy-start(bf16[2,64,1024]{2,1,0:T(8,128)(2,1)} %param.12) | copy-start | bytes 786436
  1.0 16.3 %collective-permute-start.3 = (bf16[32,4096]{1,0:T(8,128)(2,1)S(1)}, bf16[32,4096]{1,0:T(8,128)(2,1)S(1)}, u32[]{:S(2)}, u32[]{:S(2)}) collective-permute-start(bf16[32,4096]{1,0:T(8,128)(2,1)S(1)} %constant_dynamic-slice_fusion.1), channel_id=1, source_target_pairs={{0,8},{8,0},{4,12},{12,4},{1,9},{9,1},{5,13},{13,5},{2,10},{10,2},... | collective-permute-start | bytes 786440 | tf_op jit(solution)/shard_map/ppermute | solution.py:245
  5.1 21.7 %collective-permute-start = (bf16[32,4096]{1,0:T(8,128)(2,1)S(1)}, bf16[32,4096]{1,0:T(8,128)(2,1)S(1)}, u32[]{:S(2)}, u32[]{:S(2)}) collective-permute-start(bf16[32,4096]{1,0:T(8,128)(2,1)S(1)} %constant_dynamic-slice_fusion.1), channel_id=1, source_target_pairs={{0,4},{4,0},{8,12},{12,8},{1,5},{5,1},{9,13},{13,9},{2,6},{6,2},{1... | collective-permute-start | bytes 786440 | tf_op jit(solution)/shard_map/ppermute | solution.py:245
  8.2 1.0 %copy-start = (bf16[1,64,4096]{2,1,0:T(8,128)(2,1)S(1)}, bf16[1,64,4096]{2,1,0:T(8,128)(2,1)}, u32[]{:S(2)}) copy-start(bf16[1,64,4096]{2,1,0:T(8,128)(2,1)} %param.11) | copy-start | bytes 1572868
  9.3 1.2 %copy-start.1 = (bf16[128,4096]{1,0:T(8,128)(2,1)S(1)}, bf16[128,4096]{1,0:T(8,128)(2,1)}, u32[]{:S(2)}) copy-start(bf16[128,4096]{1,0:T(8,128)(2,1)} %rows_ref) | copy-start | bytes 3145732
  15.0 14.2 %collective-permute-start.2 = (bf16[32,4096]{1,0:T(8,128)(2,1)S(1)}, bf16[32,4096]{1,0:T(8,128)(2,1)S(1)}, u32[]{:S(2)}, u32[]{:S(2)}) collective-permute-start(bf16[32,4096]{1,0:T(8,128)(2,1)S(1)} %constant_dynamic-slice_fusion), channel_id=1, source_target_pairs={{0,8},{8,0},{4,12},{12,4},{1,9},{9,1},{5,13},{13,5},{2,10},{10,2},... | collective-permute-start | bytes 786440 | tf_op jit(solution)/shard_map/ppermute | solution.py:245
  15.4 13.8 %collective-permute-start.1 = (bf16[32,4096]{1,0:T(8,128)(2,1)S(1)}, bf16[32,4096]{1,0:T(8,128)(2,1)S(1)}, u32[]{:S(2)}, u32[]{:S(2)}) collective-permute-start(bf16[32,4096]{1,0:T(8,128)(2,1)S(1)} %constant_dynamic-slice_fusion), channel_id=1, source_target_pairs={{0,4},{4,0},{8,12},{12,8},{1,5},{5,1},{9,13},{13,9},{2,6},{6,2},{1... | collective-permute-start | bytes 786440 | tf_op jit(solution)/shard_map/ppermute | solution.py:245
  15.6 7.2 %collective-permute-start.4 = (bf16[2,64,1024]{2,1,0:T(8,128)(2,1)S(1)}, bf16[2,64,1024]{2,1,0:T(8,128)(2,1)S(1)}, u32[]{:S(2)}, u32[]{:S(2)}) collective-permute-start(bf16[2,64,1024]{2,1,0:T(8,128)(2,1)S(1)} %copy-done.3), channel_id=1, source_target_pairs={{0,2},{2,0},{1,3},{3,1},{4,6},{6,4},{5,7},{7,5},{8,10},{10,8},{9,1... | collective-permute-start | bytes 786440 | tf_op jit(solution)/shard_map/ppermute | solution.py:242
  17.4 5.5 %collective-permute-start.6 = (bf16[16,4096]{1,0:T(8,128)(2,1)S(1)}, bf16[16,4096]{1,0:T(8,128)(2,1)S(1)}, u32[]{:S(2)}, u32[]{:S(2)}) collective-permute-start(bf16[16,4096]{1,0:T(8,128)(2,1)S(1)} %get-tuple-element.103), channel_id=1, source_target_pairs={{0,1},{1,0},{2,3},{3,2},{4,5},{5,4},{6,7},{7,6},{8,9},{9,8},{10,11... | collective-permute-start | bytes 393224 | tf_op jit(solution)/shard_map/ppermute | solution.py:239
  22.8 1.7 %collective-permute-start.5 = (bf16[16,4096]{1,0:T(8,128)(2,1)S(1)}, bf16[16,4096]{1,0:T(8,128)(2,1)S(1)}, u32[]{:S(2)}, u32[]{:S(2)}) collective-permute-start(bf16[16,4096]{1,0:T(8,128)(2,1)S(1)} %get-tuple-element.104), channel_id=1, source_target_pairs={{0,1},{1,0},{2,3},{3,2},{4,5},{5,4},{6,7},{7,6},{8,9},{9,8},{10,11... | collective-permute-start | bytes 393224 | tf_op jit(solution)/shard_map/ppermute | solution.py:239
  22.9 14.7 %collective-permute-start.12 = (bf16[32,4096]{1,0:T(8,128)(2,1)S(1)}, bf16[32,4096]{1,0:T(8,128)(2,1)S(1)}, u32[]{:S(2)}, u32[]{:S(2)}) collective-permute-start(bf16[32,4096]{1,0:T(8,128)(2,1)S(1)} %collective-permute-done.3.mine_ref), channel_id=1, source_target_pairs={{0,4},{4,0},{8,12},{12,8},{1,5},{5,1},{9,13},{13,9},{2,6},{6,2},{1... | collective-permute-start | bytes 786440 | tf_op jit(solution)/shard_map/ppermute | solution.py:245
  29.1 5.7 %collective-permute-start.9 = (bf16[32,4096]{1,0:T(8,128)(2,1)S(1)}, bf16[32,4096]{1,0:T(8,128)(2,1)S(1)}, u32[]{:S(2)}, u32[]{:S(2)}) collective-permute-start(bf16[32,4096]{1,0:T(8,128)(2,1)S(1)} %collective-permute-done.near_ref), channel_id=1, source_target_pairs={{0,1},{1,0},{2,3},{3,2},{4,5},{5,4},{6,7},{7,6},{8,9},{9,8},{10,11... | collective-permute-start | bytes 786440 | tf_op jit(solution)/shard_map/ppermute | solution.py:239
  29.1 5.7 %collective-permute-start.10 = (bf16[32,4096]{1,0:T(8,128)(2,1)S(1)}, bf16[32,4096]{1,0:T(8,128)(2,1)S(1)}, u32[]{:S(2)}, u32[]{:S(2)}) collective-permute-start(bf16[32,4096]{1,0:T(8,128)(2,1)S(1)} %collective-permute-done.1.near_too_ref), channel_id=1, source_target_pairs={{0,1},{1,0},{2,3},{3,2},{4,5},{5,4},{6,7},{7,6},{8,9},{9,8},{10,11... | collective-permute-start | bytes 786440 | tf_op jit(solution)/shard_map/ppermute | solution.py:239
  29.7 1.6 %collective-permute-start.8 = (bf16[16,4096]{1,0:T(8,128)(2,1)S(1)}, bf16[16,4096]{1,0:T(8,128)(2,1)S(1)}, u32[]{:S(2)}, u32[]{:S(2)}) collective-permute-start(bf16[16,4096]{1,0:T(8,128)(2,1)S(1)} %get-tuple-element.101), channel_id=1, source_target_pairs={{0,1},{1,0},{2,3},{3,2},{4,5},{5,4},{6,7},{7,6},{8,9},{9,8},{10,11... | collective-permute-start | bytes 393224 | tf_op jit(solution)/shard_map/ppermute | solution.py:239
  29.8 3.6 %collective-permute-start.7 = (bf16[16,4096]{1,0:T(8,128)(2,1)S(1)}, bf16[16,4096]{1,0:T(8,128)(2,1)S(1)}, u32[]{:S(2)}, u32[]{:S(2)}) collective-permute-start(bf16[16,4096]{1,0:T(8,128)(2,1)S(1)} %get-tuple-element.102), channel_id=1, source_target_pairs={{0,1},{1,0},{2,3},{3,2},{4,5},{5,4},{6,7},{7,6},{8,9},{9,8},{10,11... | collective-permute-start | bytes 393224 | tf_op jit(solution)/shard_map/ppermute | solution.py:239
  31.2 11.1 %collective-permute-start.13 = (bf16[32,4096]{1,0:T(8,128)(2,1)S(1)}, bf16[32,4096]{1,0:T(8,128)(2,1)S(1)}, u32[]{:S(2)}, u32[]{:S(2)}) collective-permute-start(bf16[32,4096]{1,0:T(8,128)(2,1)S(1)} %collective-permute-done.2.mine_ref), channel_id=1, source_target_pairs={{0,4},{4,0},{8,12},{12,8},{1,5},{5,1},{9,13},{13,9},{2,6},{6,2},{1... | collective-permute-start | bytes 786440 | tf_op jit(solution)/shard_map/ppermute | solution.py:245
  33.4 5.3 %collective-permute-start.11 = (bf16[64,1024]{1,0:T(8,128)(2,1)S(1)}, bf16[64,1024]{1,0:T(8,128)(2,1)S(1)}, u32[]{:S(2)}, u32[]{:S(2)}) collective-permute-start(bf16[64,1024]{1,0:T(8,128)(2,1)S(1)} %get-tuple-element.67), channel_id=1, source_target_pairs={{0,2},{2,0},{1,3},{3,1},{4,6},{6,4},{5,7},{7,5},{8,10},{10,8},{9,1... | collective-permute-start | bytes 393224 | tf_op jit(solution)/shard_map/ppermute | solution.py:242
  37.6 2.5 %collective-permute-start.16 = (bf16[16,4096]{1,0:T(8,128)(2,1)S(1)}, bf16[16,4096]{1,0:T(8,128)(2,1)S(1)}, u32[]{:S(2)}, u32[]{:S(2)}) collective-permute-start(bf16[16,4096]{1,0:T(8,128)(2,1)S(1)} %get-tuple-element.99), channel_id=1, source_target_pairs={{0,1},{1,0},{2,3},{3,2},{4,5},{5,4},{6,7},{7,6},{8,9},{9,8},{10,11... | collective-permute-start | bytes 393224 | tf_op jit(solution)/shard_map/ppermute | solution.py:239
  37.7 2.4 %collective-permute-start.15 = (bf16[16,4096]{1,0:T(8,128)(2,1)S(1)}, bf16[16,4096]{1,0:T(8,128)(2,1)S(1)}, u32[]{:S(2)}, u32[]{:S(2)}) collective-permute-start(bf16[16,4096]{1,0:T(8,128)(2,1)S(1)} %get-tuple-element.100), channel_id=1, source_target_pairs={{0,1},{1,0},{2,3},{3,2},{4,5},{5,4},{6,7},{7,6},{8,9},{9,8},{10,11... | collective-permute-start | bytes 393224 | tf_op jit(solution)/shard_map/ppermute | solution.py:239
  38.6 5.1 %collective-permute-start.14 = (bf16[64,1024]{1,0:T(8,128)(2,1)S(1)}, bf16[64,1024]{1,0:T(8,128)(2,1)S(1)}, u32[]{:S(2)}, u32[]{:S(2)}) collective-permute-start(bf16[64,1024]{1,0:T(8,128)(2,1)S(1)} %get-tuple-element.72), channel_id=1, source_target_pairs={{0,2},{2,0},{1,3},{3,1},{4,6},{6,4},{5,7},{7,5},{8,10},{10,8},{9,1... | collective-permute-start | bytes 393224 | tf_op jit(solution)/shard_map/ppermute | solution.py:242
  40.1 17.2 %copy-start.2 = (bf16[256,1024]{1,0:T(8,128)(2,1)S(1)}, bf16[256,1024]{1,0:T(8,128)(2,1)}, u32[]{:S(2)}) copy-start(bf16[256,1024]{1,0:T(8,128)(2,1)} %residual_ref.1) | copy-start | bytes 1572868
  43.7 1.4 %collective-permute-start.19 = (bf16[16,4096]{1,0:T(8,128)(2,1)S(1)}, bf16[16,4096]{1,0:T(8,128)(2,1)S(1)}, u32[]{:S(2)}, u32[]{:S(2)}) collective-permute-start(bf16[16,4096]{1,0:T(8,128)(2,1)S(1)} %get-tuple-element.97), channel_id=1, source_target_pairs={{0,1},{1,0},{2,3},{3,2},{4,5},{5,4},{6,7},{7,6},{8,9},{9,8},{10,11... | collective-permute-start | bytes 393224 | tf_op jit(solution)/shard_map/ppermute | solution.py:239
  43.8 1.5 %collective-permute-start.18 = (bf16[16,4096]{1,0:T(8,128)(2,1)S(1)}, bf16[16,4096]{1,0:T(8,128)(2,1)S(1)}, u32[]{:S(2)}, u32[]{:S(2)}) collective-permute-start(bf16[16,4096]{1,0:T(8,128)(2,1)S(1)} %get-tuple-element.98), channel_id=1, source_target_pairs={{0,1},{1,0},{2,3},{3,2},{4,5},{5,4},{6,7},{7,6},{8,9},{9,8},{10,11... | collective-permute-start | bytes 393224 | tf_op jit(solution)/shard_map/ppermute | solution.py:239
  47.6 4.0 %collective-permute-start.21 = (bf16[128,128]{1,0:T(8,128)(2,1)S(1)}, bf16[128,128]{1,0:T(8,128)(2,1)S(1)}, u32[]{:S(2)}, u32[]{:S(2)}) collective-permute-start(bf16[128,128]{1,0:T(8,128)(2,1)S(1)} %get-tuple-element.89), channel_id=1, source_target_pairs={{0,2},{2,0},{1,3},{3,1},{4,6},{6,4},{5,7},{7,5},{8,10},{10,8},{9,1... | collective-permute-start | bytes 98312 | tf_op jit(solution)/shard_map/ppermute | solution.py:242
  49.0 6.5 %collective-permute-start.17 = (bf16[64,1024]{1,0:T(8,128)(2,1)S(1)}, bf16[64,1024]{1,0:T(8,128)(2,1)S(1)}, u32[]{:S(2)}, u32[]{:S(2)}) collective-permute-start(bf16[64,1024]{1,0:T(8,128)(2,1)S(1)} %get-tuple-element.77), channel_id=1, source_target_pairs={{0,2},{2,0},{1,3},{3,1},{4,6},{6,4},{5,7},{7,5},{8,10},{10,8},{9,1... | collective-permute-start | bytes 393224 | tf_op jit(solution)/shard_map/ppermute | solution.py:242
  49.7 7.6 %collective-permute-start.20 = (bf16[64,1024]{1,0:T(8,128)(2,1)S(1)}, bf16[64,1024]{1,0:T(8,128)(2,1)S(1)}, u32[]{:S(2)}, u32[]{:S(2)}) collective-permute-start(bf16[64,1024]{1,0:T(8,128)(2,1)S(1)} %get-tuple-element.85), channel_id=1, source_target_pairs={{0,2},{2,0},{1,3},{3,1},{4,6},{6,4},{5,7},{7,5},{8,10},{10,8},{9,1... | collective-permute-start | bytes 393224 | tf_op jit(solution)/shard_map/ppermute | solution.py:242
  51.6 4.0 %collective-permute-start.22 = (bf16[128,128]{1,0:T(8,128)(2,1)S(1)}, bf16[128,128]{1,0:T(8,128)(2,1)S(1)}, u32[]{:S(2)}, u32[]{:S(2)}) collective-permute-start(bf16[128,128]{1,0:T(8,128)(2,1)S(1)} %multiply_convert_fusion.refs_0_), channel_id=1, source_target_pairs={{0,4},{4,0},{8,12},{12,8},{1,9},{9,1},{5,13},{13,5},{2,6},{6,2},{1... | collective-permute-start | bytes 98312 | tf_op jit(solution)/shard_map/ppermute | solution.py:331
  52.0 6.0 %collective-permute-start.23 = (bf16[128,128]{1,0:T(8,128)(2,1)S(1)}, bf16[128,128]{1,0:T(8,128)(2,1)S(1)}, u32[]{:S(2)}, u32[]{:S(2)}) collective-permute-start(bf16[128,128]{1,0:T(8,128)(2,1)S(1)} %multiply_convert_fusion.refs_0_), channel_id=1, source_target_pairs={{0,12},{12,0},{4,8},{8,4},{1,13},{13,1},{5,9},{9,5},{2,14},{14,2},... | collective-permute-start | bytes 98312 | tf_op jit(solution)/shard_map/ppermute | solution.py:245
  55.6 2.5 %collective-permute-start.24 = (bf16[128,128]{1,0:T(8,128)(2,1)S(1)}, bf16[128,128]{1,0:T(8,128)(2,1)S(1)}, u32[]{:S(2)}, u32[]{:S(2)}) collective-permute-start(bf16[128,128]{1,0:T(8,128)(2,1)S(1)} %collective-permute-done.22.refs_1_), channel_id=1, source_target_pairs={{0,1},{1,0},{2,3},{3,2},{4,5},{5,4},{6,7},{7,6},{8,9},{9,8},{10,11... | collective-permute-start | bytes 98312 | tf_op jit(solution)/shard_map/ppermute | solution.py:239

commit v17 on v16

--- a/solution.py
+++ b/solution.py
@@ -309,13 +309,12 @@
         [flags, held, down[0], own_sum, far[1]] + over_core_in_two(far[1])
         + near + [over_core(piece) for piece in near],
     )
-    sent_b, got_a = barrier((sent_b, got_a))
+    last[0], kept_b = barrier((last[0], kept_b))
+
+    kept_c, sent_c, low_c = parted_piece(0, near_sum, last[0])
+    sent_b = jnp.concatenate([sent_b, sent_c])
     got_b = over_x(sent_b)
-    last[0], kept_b = barrier((last[0], kept_b))
-
-    kept_c, sent_c, low_c = parted_piece(0, near_sum, last[0])
-    got_c = over_x(sent_c)
-    last[1], near_sum, got_b, low_c = barrier((last[1], near_sum, got_b, low_c))
+    last[1], near_sum, got_a, low_c, sent_b = barrier((last[1], near_sum, got_a, low_c, sent_b))
 
     kept_d, sent_d, low, low_sent = call(
         last_kernel,
@@ -327,6 +326,8 @@
     got_d = over_x(sent_d)
 
     scaled = ((low + over_x(low_sent).astype(F32)) * scale).astype(BF16)
+    scaled, got_b = barrier((scaled, got_b))
+    got_b, got_c = got_b[:half], got_b[half:]
     scaled_got = [
         lax.ppermute(scaled, ("blk", "sub"), by_core(NEAR, FAR)),
         along(scaled, LAST),

time: 59.8 us -> 61.1 us (1.022)
  waiting for transfers between devices: 14.9 us -> 17.1 us
  starting transfers between devices: 23.3 us -> 22.4 us
    ppermute x6 -> x5, waiting for transfers between devices: 9.29 us -> 12.5 us  [over_x(): return lax.ppermute(value, 'split', SWAP)]
    ppermute x1, waiting for transfers between devices: 1.22 us -> 0.01 us  [line(): lax.ppermute(scaled, ('blk', 'sub'), by_core(NEAR, FAR))]
    ppermute x7, waiting for transfers between devices: 2.36 us -> 3.49 us  [along(): return lax.ppermute(value, 'blk', pairs)]
    ppermute x11, waiting for transfers between devices: 2.03 us -> 1.02 us  [over_core(): return lax.ppermute(value, 'sub', SWAP)]
    ppermute x6 -> x5, starting transfers between devices: 8.19 us -> 7.3 us  [over_x(): return lax.ppermute(value, 'split', SWAP)]
    unnamed x8 -> x9, local copies, waits for them, and re-layouts: 2.27 us -> 2.28 us
  transfers between devices with their start and end apart: 25 -> 24, of which waited for: 10 -> 7; matrix products, arithmetic and copies ran while one was open for 3% -> 3% of each run, Pallas kernels for 21% -> 24%
where the time goes in v17:
time: 61.1 us; the launch traced here: 60.9 us
  starting transfers between devices  22.4 us (37%)
  waiting for transfers between devices  17.1 us (28%)
  Pallas kernels  16.2 us (27%)
  local copies, waits for them, and re-layouts  3.68 us (6%)
  other arithmetic  1.37 us (2%)
    pallas_call x7, Pallas kernels, call(): pl.pallas_call(kernel, out_shape=outs, in_specs=in_specs, out_specs=jax.t...  16.2 us
    ppermute x5, waiting for transfers between devices, over_x(): return lax.ppermute(value, 'split', SWAP)  12.5 us
    ppermute x7, starting transfers between devices, along(): return lax.ppermute(value, 'blk', pairs)  12.5 us
    ppermute x5, starting transfers between devices, over_x(): return lax.ppermute(value, 'split', SWAP)  7.3 us
    ppermute x7, waiting for transfers between devices, along(): return lax.ppermute(value, 'blk', pairs)  3.49 us
    ppermute x11, starting transfers between devices, over_core(): return lax.ppermute(value, 'sub', SWAP)  2.29 us
    unnamed x9, local copies, waits for them, and re-layouts  2.28 us
  transfers between devices with their start and end apart: 24, of which 7 were waited for; matrix products, arithmetic and copies ran while one was open for 3% of the time, Pallas kernels for 24%

profile of v17, /device:TPU:0, one launch (start us, length us, event | category | flops | bytes accessed | tf_op | source)
XLA Modules:
  0.0 60.9 jit_solution(6017883138621863076)
XLA Ops:
  0.0 1.0 %constant_dynamic-slice_fusion.1 = bf16[32,4096]{1,0:T(8,128)(2,1)S(1)} fusion(bf16[128,4096]{1,0:T(8,128)(2,1)} %rows_ref, s32[]{:T(128)S(6)} %select_n.39), kind=kLoop, calls=%fused_computation.16 | loop fusion | bytes 524292 | tf_op jit(solution)/shard_map/dynamic_slice | solution.py:269
  1.0 4.1 %collective-permute-start.3 = (bf16[32,4096]{1,0:T(8,128)(2,1)S(1)}, bf16[32,4096]{1,0:T(8,128)(2,1)S(1)}, u32[]{:S(2)}, u32[]{:S(2)}) collective-permute-start(bf16[32,4096]{1,0:T(8,128)(2,1)S(1)} %constant_dynamic-slice_fusion.1), channel_id=1, source_target_pairs={{0,8},{8,0},{4,12},{12,4},{1,9},{9,1},{5,13},{13,5},{2,10},{10,2},... | collective-permute-start | bytes 786440 | tf_op jit(solution)/shard_map/ppermute | solution.py:245
  5.1 1.6 %collective-permute-start = (bf16[32,4096]{1,0:T(8,128)(2,1)S(1)}, bf16[32,4096]{1,0:T(8,128)(2,1)S(1)}, u32[]{:S(2)}, u32[]{:S(2)}) collective-permute-start(bf16[32,4096]{1,0:T(8,128)(2,1)S(1)} %constant_dynamic-slice_fusion.1), channel_id=1, source_target_pairs={{0,4},{4,0},{8,12},{12,8},{1,5},{5,1},{9,13},{13,9},{2,6},{6,2},{1... | collective-permute-start | bytes 786440 | tf_op jit(solution)/shard_map/ppermute | solution.py:245
  6.7 0.8 %select_reduce_fusion = (s32[512]{0:T(512)S(1)}, s32[512]{0:T(512)S(1)}) fusion(s32[4]{0:T(128)} %param.15, s32[512]{0:T(512)} %param.13, s32[4]{0:T(128)} %param.14), kind=kLoop, calls=%fused_computation.5 | loop fusion | flops 9216 | bytes 6176 | tf_op jit(solution)/shard_map/reduce_sum | solution.py:26
  7.5 0.1 convert_divide_fusion
  7.6 0.1 broadcast_compare_fusion
  7.6 0.2 select_select_fusion
  7.8 0.1 pad_maximum_fusion
  7.9 0.1 pad_add_fusion.flags_ref
  8.0 0.2 broadcast_in_dim.24.hot_ref
  8.2 1.0 %copy-done = bf16[1,64,4096]{2,1,0:T(8,128)(2,1)S(1)} copy-done((bf16[1,64,4096]{2,1,0:T(8,128)(2,1)S(1)}, bf16[1,64,4096]{2,1,0:T(8,128)(2,1)}, u32[]{:S(2)}) %copy-start) | copy-done | bytes 524312
  9.3 1.2 %copy-done.1 = bf16[128,4096]{1,0:T(8,128)(2,1)S(1)} copy-done((bf16[128,4096]{1,0:T(8,128)(2,1)S(1)}, bf16[128,4096]{1,0:T(8,128)(2,1)}, u32[]{:S(2)}) %copy-start.1) | copy-done | bytes 1048600
  10.5 4.4 %shard_map.82 = (bf16[4096,1024]{1,0:T(8,128)(2,1)S(1)}, f32[128,1024]{1,0:T(8,128)S(1)}, f32[128,64]{1,0:T(8,128)S(1)}) custom-call(bf16[4096,1024]{1,0:T(8,128)(2,1)} %weight_ref.1, bf16[64,4096]{1,0:T(8,128)(2,1)S(1)} %bitcast.4, bf16[128,4096]{1,0:T(8,128)(2,1)S(1)} %copy-done.1), custom_call_target="tpu_custom_call" | custom-call | tf_op jit(solution)/shard_map/pallas_call | solution.py:91
  14.9 0.1 constant_dynamic-slice_fusion
  15.0 0.4 collective-permute-start.2
  15.4 0.2 collective-permute-start.1
  15.6 1.8 %collective-permute-start.4 = (bf16[2,64,1024]{2,1,0:T(8,128)(2,1)S(1)}, bf16[2,64,1024]{2,1,0:T(8,128)(2,1)S(1)}, u32[]{:S(2)}, u32[]{:S(2)}) collective-permute-start(bf16[2,64,1024]{2,1,0:T(8,128)(2,1)S(1)} %copy-done.3), channel_id=1, source_target_pairs={{0,2},{2,0},{1,3},{3,1},{4,6},{6,4},{5,7},{7,5},{8,10},{10,8},{9,1... | collective-permute-start | bytes 786440 | tf_op jit(solution)/shard_map/ppermute | solution.py:242
  17.4 0.1 collective-permute-start.6
  17.4 5.4 %collective-permute-done.4 = bf16[2,64,1024]{2,1,0:T(8,128)(2,1)S(1)} collective-permute-done((bf16[2,64,1024]{2,1,0:T(8,128)(2,1)S(1)}, bf16[2,64,1024]{2,1,0:T(8,128)(2,1)S(1)}, u32[]{:S(2)}, u32[]{:S(2)}) %collective-permute-start.4) | collective-permute-done | bytes 262176 | tf_op jit(solution)/shard_map/ppermute | solution.py:242
  22.8 0.1 maximum_select_fusion.ups_ref
  22.9 1.6 %collective-permute-start.13 = (bf16[32,4096]{1,0:T(8,128)(2,1)S(1)}, bf16[32,4096]{1,0:T(8,128)(2,1)S(1)}, u32[]{:S(2)}, u32[]{:S(2)}) collective-permute-start(bf16[32,4096]{1,0:T(8,128)(2,1)S(1)} %collective-permute-done.3.mine_ref), channel_id=1, source_target_pairs={{0,4},{4,0},{8,12},{12,8},{1,5},{5,1},{9,13},{13,9},{2,6},{6,2},{1... | collective-permute-start | bytes 786440 | tf_op jit(solution)/shard_map/ppermute | solution.py:245
  24.5 2.3 %shard_map.83 = (f32[64,1024]{1,0:T(8,128)S(1)}, bf16[64,1024]{1,0:T(8,128)(2,1)S(1)}, f32[64,64]{1,0:T(8,128)S(1)}) custom-call(s32[3]{0:T(128)S(1)} %pad_add_fusion.flags_ref, bf16[4096,1024]{1,0:T(8,128)(2,1)S(1)} %get-tuple-element.58.weight_ref, bf16[64,4096]{1,0:T(8,128)(2,1)S(1)} %bitcast.5, f32[128,1024]{1,0:T(8,128)S(1)} %get-tuple-element.63.held_ref, ...), custom_call_target="tpu_custom_call" | custom-call | tf_op jit(solution)/shard_map/pallas_call | solution.py:91
  26.8 2.3 %collective-permute-done.2.mine_ref = bf16[32,4096]{1,0:T(8,128)(2,1)S(1)} collective-permute-done((bf16[32,4096]{1,0:T(8,128)(2,1)S(1)}, bf16[32,4096]{1,0:T(8,128)(2,1)S(1)}, u32[]{:S(2)}, u32[]{:S(2)}) %collective-permute-start.2) | collective-permute-done | bytes 262176 | tf_op jit(solution)/shard_map/ppermute | solution.py:245
  29.1 0.5 collective-permute-start.11
  29.7 0.1 collective-permute-start.9
  29.8 0.5 collective-permute-start.8
  30.2 1.0 %collective-permute-done.9.second_ref = bf16[16,4096]{1,0:T(8,128)(2,1)S(1)} collective-permute-done((bf16[16,4096]{1,0:T(8,128)(2,1)S(1)}, bf16[16,4096]{1,0:T(8,128)(2,1)S(1)}, u32[]{:S(2)}, u32[]{:S(2)}) %collective-permute-start.9) | collective-permute-done | bytes 131104 | tf_op jit(solution)/shard_map/ppermute | solution.py:239
  31.2 2.1 %collective-permute-start.7 = (bf16[32,4096]{1,0:T(8,128)(2,1)S(1)}, bf16[32,4096]{1,0:T(8,128)(2,1)S(1)}, u32[]{:S(2)}, u32[]{:S(2)}) collective-permute-start(bf16[32,4096]{1,0:T(8,128)(2,1)S(1)} %collective-permute-done.2.mine_ref), channel_id=1, source_target_pairs={{0,4},{4,0},{8,12},{12,8},{1,5},{5,1},{9,13},{13,9},{2,6},{6,2},{1... | collective-permute-start | bytes 786440 | tf_op jit(solution)/shard_map/ppermute | solution.py:245
  33.4 2.7 %shard_map.84 = (f32[64,1024]{1,0:T(8,128)S(1)}, bf16[64,1024]{1,0:T(8,128)(2,1)S(1)}, f32[128,1024]{1,0:T(8,128)S(1)}, f32[192,64]{1,0:T(8,128)S(1)}) custom-call(s32[3]{0:T(128)S(1)} %pad_add_fusion.flags_ref, bf16[4096,1024]{1,0:T(8,128)(2,1)S(1)} %get-tuple-element.58.weight_ref, bf16[64,4096]{1,0:T(8,128)(2,1)S(1)} %bitcast.6, ...), custom_call_target="tpu_custom_call" | custom-call | tf_op jit(solution)/shard_map/pallas_call | solution.py:91
  36.2 0.1 collective-permute-start.15
  36.2 0.5 collective-permute-start.14
  36.7 1.5 %collective-permute-start.12 = (bf16[64,1024]{1,0:T(8,128)(2,1)S(1)}, bf16[64,1024]{1,0:T(8,128)(2,1)S(1)}, u32[]{:S(2)}, u32[]{:S(2)}) collective-permute-start(bf16[64,1024]{1,0:T(8,128)(2,1)S(1)} %get-tuple-element.67), channel_id=1, source_target_pairs={{0,2},{2,0},{1,3},{3,1},{4,6},{6,4},{5,7},{7,5},{8,10},{10,8},{9,1... | collective-permute-start | bytes 393224 | tf_op jit(solution)/shard_map/ppermute | solution.py:242
  38.3 0.0 copy-start.2
  38.3 2.3 %shard_map.85 = (f32[64,1024]{1,0:T(8,128)S(1)}, bf16[64,1024]{1,0:T(8,128)(2,1)S(1)}, f32[64,64]{1,0:T(8,128)S(1)}) custom-call(s32[3]{0:T(128)S(1)} %pad_add_fusion.flags_ref, bf16[4096,1024]{1,0:T(8,128)(2,1)S(1)} %get-tuple-element.58.weight_ref, bf16[64,4096]{1,0:T(8,128)(2,1)S(1)} %bitcast.7, f32[128,1024]{1,0:T(8,128)S(1)} %get-tuple-element.75.held_ref, ...), custom_call_target="tpu_custom_call" | custom-call | tf_op jit(solution)/shard_map/pallas_call | solution.py:91
  40.5 1.7 %collective-permute-done.12.refs_1_ = bf16[64,1024]{1,0:T(8,128)(2,1)S(1)} collective-permute-done((bf16[64,1024]{1,0:T(8,128)(2,1)S(1)}, bf16[64,1024]{1,0:T(8,128)(2,1)S(1)}, u32[]{:S(2)}, u32[]{:S(2)}) %collective-permute-start.12) | collective-permute-done | bytes 131104 | tf_op jit(solution)/shard_map/ppermute | solution.py:242
  42.2 0.1 collective-permute-start.17
  42.3 0.5 collective-permute-start.16
  42.8 1.5 %collective-permute-start.19 = (bf16[128,1024]{1,0:T(8,128)(2,1)S(1)}, bf16[128,1024]{1,0:T(8,128)(2,1)S(1)}, u32[]{:S(2)}, u32[]{:S(2)}) collective-permute-start(bf16[128,1024]{1,0:T(8,128)(2,1)S(1)} %constant_dynamic-update-slice_fusion), channel_id=1, source_target_pairs={{0,2},{2,0},{1,3},{3,1},{4,6},{6,4},{5,7},{7,5},{8,10},{10,8},{9,1... | collective-permute-start | bytes 786440 | tf_op jit(solution)/shard_map/ppermute | solution.py:242
  44.3 2.3 %shard_map.86 = (f32[64,1024]{1,0:T(8,128)S(1)}, bf16[64,1024]{1,0:T(8,128)(2,1)S(1)}, f32[128,128]{1,0:T(8,128)S(1)}, bf16[128,128]{1,0:T(8,128)(2,1)S(1)}) custom-call(s32[3]{0:T(128)S(1)} %pad_add_fusion.flags_ref, bf16[4096,1024]{1,0:T(8,128)(2,1)S(1)} %get-tuple-element.58.weight_ref, bf16[64,4096]{1,0:T(8,128)(2,1)S(1)} %bitcast.8, ...), custom_call_target="tpu_custom_call" | custom-call | tf_op jit(solution)/shard_map/pallas_call | solution.py:91
  46.6 1.1 %collective-permute-start.18 = (bf16[128,128]{1,0:T(8,128)(2,1)S(1)}, bf16[128,128]{1,0:T(8,128)(2,1)S(1)}, u32[]{:S(2)}, u32[]{:S(2)}) collective-permute-start(bf16[128,128]{1,0:T(8,128)(2,1)S(1)} %get-tuple-element.82), channel_id=1, source_target_pairs={{0,2},{2,0},{1,3},{3,1},{4,6},{6,4},{5,7},{7,5},{8,10},{10,8},{9,1... | collective-permute-start | bytes 98312 | tf_op jit(solution)/shard_map/ppermute | solution.py:242
  47.7 4.1 %collective-permute-done.18 = bf16[128,128]{1,0:T(8,128)(2,1)S(1)} collective-permute-done((bf16[128,128]{1,0:T(8,128)(2,1)S(1)}, bf16[128,128]{1,0:T(8,128)(2,1)S(1)}, u32[]{:S(2)}, u32[]{:S(2)}) %collective-permute-start.18) | collective-permute-done | bytes 32800 | tf_op jit(solution)/shard_map/ppermute | solution.py:242
  51.8 0.3 collective-permute-start.21
  52.2 1.5 %collective-permute-start.20 = (bf16[64,1024]{1,0:T(8,128)(2,1)S(1)}, bf16[64,1024]{1,0:T(8,128)(2,1)S(1)}, u32[]{:S(2)}, u32[]{:S(2)}) collective-permute-start(bf16[64,1024]{1,0:T(8,128)(2,1)S(1)} %get-tuple-element.87), channel_id=1, source_target_pairs={{0,2},{2,0},{1,3},{3,1},{4,6},{6,4},{5,7},{7,5},{8,10},{10,8},{9,1... | collective-permute-start | bytes 393224 | tf_op jit(solution)/shard_map/ppermute | solution.py:242
  53.7 2.4 %collective-permute-start.22 = (bf16[128,128]{1,0:T(8,128)(2,1)S(1)}, bf16[128,128]{1,0:T(8,128)(2,1)S(1)}, u32[]{:S(2)}, u32[]{:S(2)}) collective-permute-start(bf16[128,128]{1,0:T(8,128)(2,1)S(1)} %multiply_convert_fusion.refs_0_), channel_id=1, source_target_pairs={{0,12},{12,0},{4,8},{8,4},{1,13},{13,1},{5,9},{9,5},{2,14},{14,2},... | collective-permute-start | bytes 98312 | tf_op jit(solution)/shard_map/ppermute | solution.py:245
  56.1 1.4 %collective-permute-done.20.refs_7_ = bf16[64,1024]{1,0:T(8,128)(2,1)S(1)} collective-permute-done((bf16[64,1024]{1,0:T(8,128)(2,1)S(1)}, bf16[64,1024]{1,0:T(8,128)(2,1)S(1)}, u32[]{:S(2)}, u32[]{:S(2)}) %collective-permute-start.20) | collective-permute-done | bytes 131104 | tf_op jit(solution)/shard_map/ppermute | solution.py:242
  57.5 0.7 %shard_map.87.base_ref = f32[256,1024]{1,0:T(8,128)S(1)} custom-call(s32[3]{0:T(128)S(1)} %pad_add_fusion.flags_ref, bf16[256,1024]{1,0:T(8,128)(2,1)S(1)} %copy-done.2, f32[64,1024]{1,0:T(8,128)S(1)} %get-tuple-element.61.refs_0_, bf16[64,1024]{1,0:T(8,128)(2,1)S(1)} %collective-permute-done.12.refs_1_, f32[64,1024]{1,0:T(8,128)S(1)} %get-tuple-element.74.refs_2_, ...), custom_call_target="tpu_custom_call" | custom-call | tf_op jit(solution)/shard_map/pallas_call | solution.py:91
  58.2 1.1 %collective-permute-done.22.refs_2_ = bf16[128,128]{1,0:T(8,128)(2,1)S(1)} collective-permute-done((bf16[128,128]{1,0:T(8,128)(2,1)S(1)}, bf16[128,128]{1,0:T(8,128)(2,1)S(1)}, u32[]{:S(2)}, u32[]{:S(2)}) %collective-permute-start.22) | collective-permute-done | bytes 32800 | tf_op jit(solution)/shard_map/ppermute | solution.py:245
  59.4 1.5 %shard_map.88 = bf16[256,1024]{1,0:T(8,128)(2,1)} custom-call(f32[256,1024]{1,0:T(8,128)S(1)} %shard_map.87.base_ref, bf16[4,256,64]{2,1,0:T(8,128)(2,1)S(1)} %broadcast_in_dim.24.hot_ref, bf16[4,64,1024]{2,1,0:T(8,128)(2,1)S(1)} %maximum_select_fusion.ups_ref, bf16[128,128]{1,0:T(8,128)(2,1)S(1)} %multiply_convert_fusion.refs_0_, ...), custom_call_target="tpu_custom_call" | custom-call | tf_op jit(solution)/shard_map/pallas_call | solution.py:91
  (35 shorter events, 0.2 us)
Async XLA Ops:
  0.0 15.6 %copy-start.3 = (bf16[2,64,1024]{2,1,0:T(8,128)(2,1)S(1)}, bf16[2,64,1024]{2,1,0:T(8,128)(2,1)}, u32[]{:S(2)}) copy-start(bf16[2,64,1024]{2,1,0:T(8,128)(2,1)} %param.12) | copy-start | bytes 786436
  1.0 16.3 %collective-permute-start.3 = (bf16[32,4096]{1,0:T(8,128)(2,1)S(1)}, bf16[32,4096]{1,0:T(8,128)(2,1)S(1)}, u32[]{:S(2)}, u32[]{:S(2)}) collective-permute-start(bf16[32,4096]{1,0:T(8,128)(2,1)S(1)} %constant_dynamic-slice_fusion.1), channel_id=1, source_target_pairs={{0,8},{8,0},{4,12},{12,4},{1,9},{9,1},{5,13},{13,5},{2,10},{10,2},... | collective-permute-start | bytes 786440 | tf_op jit(solution)/shard_map/ppermute | solution.py:245
  5.1 21.7 %collective-permute-start = (bf16[32,4096]{1,0:T(8,128)(2,1)S(1)}, bf16[32,4096]{1,0:T(8,128)(2,1)S(1)}, u32[]{:S(2)}, u32[]{:S(2)}) collective-permute-start(bf16[32,4096]{1,0:T(8,128)(2,1)S(1)} %constant_dynamic-slice_fusion.1), channel_id=1, source_target_pairs={{0,4},{4,0},{8,12},{12,8},{1,5},{5,1},{9,13},{13,9},{2,6},{6,2},{1... | collective-permute-start | bytes 786440 | tf_op jit(solution)/shard_map/ppermute | solution.py:245
  8.2 1.0 %copy-start = (bf16[1,64,4096]{2,1,0:T(8,128)(2,1)S(1)}, bf16[1,64,4096]{2,1,0:T(8,128)(2,1)}, u32[]{:S(2)}) copy-start(bf16[1,64,4096]{2,1,0:T(8,128)(2,1)} %param.11) | copy-start | bytes 1572868
  9.3 1.2 %copy-start.1 = (bf16[128,4096]{1,0:T(8,128)(2,1)S(1)}, bf16[128,4096]{1,0:T(8,128)(2,1)}, u32[]{:S(2)}) copy-start(bf16[128,4096]{1,0:T(8,128)(2,1)} %rows_ref) | copy-start | bytes 3145732
  15.0 14.2 %collective-permute-start.2 = (bf16[32,4096]{1,0:T(8,128)(2,1)S(1)}, bf16[32,4096]{1,0:T(8,128)(2,1)S(1)}, u32[]{:S(2)}, u32[]{:S(2)}) collective-permute-start(bf16[32,4096]{1,0:T(8,128)(2,1)S(1)} %constant_dynamic-slice_fusion), channel_id=1, source_target_pairs={{0,8},{8,0},{4,12},{12,4},{1,9},{9,1},{5,13},{13,5},{2,10},{10,2},... | collective-permute-start | bytes 786440 | tf_op jit(solution)/shard_map/ppermute | solution.py:245
  15.4 13.8 %collective-permute-start.1 = (bf16[32,4096]{1,0:T(8,128)(2,1)S(1)}, bf16[32,4096]{1,0:T(8,128)(2,1)S(1)}, u32[]{:S(2)}, u32[]{:S(2)}) collective-permute-start(bf16[32,4096]{1,0:T(8,128)(2,1)S(1)} %constant_dynamic-slice_fusion), channel_id=1, source_target_pairs={{0,4},{4,0},{8,12},{12,8},{1,5},{5,1},{9,13},{13,9},{2,6},{6,2},{1... | collective-permute-start | bytes 786440 | tf_op jit(solution)/shard_map/ppermute | solution.py:245
  15.6 7.2 %collective-permute-start.4 = (bf16[2,64,1024]{2,1,0:T(8,128)(2,1)S(1)}, bf16[2,64,1024]{2,1,0:T(8,128)(2,1)S(1)}, u32[]{:S(2)}, u32[]{:S(2)}) collective-permute-start(bf16[2,64,1024]{2,1,0:T(8,128)(2,1)S(1)} %copy-done.3), channel_id=1, source_target_pairs={{0,2},{2,0},{1,3},{3,1},{4,6},{6,4},{5,7},{7,5},{8,10},{10,8},{9,1... | collective-permute-start | bytes 786440 | tf_op jit(solution)/shard_map/ppermute | solution.py:242
  17.4 5.5 %collective-permute-start.6 = (bf16[16,4096]{1,0:T(8,128)(2,1)S(1)}, bf16[16,4096]{1,0:T(8,128)(2,1)S(1)}, u32[]{:S(2)}, u32[]{:S(2)}) collective-permute-start(bf16[16,4096]{1,0:T(8,128)(2,1)S(1)} %get-tuple-element.105), channel_id=1, source_target_pairs={{0,1},{1,0},{2,3},{3,2},{4,5},{5,4},{6,7},{7,6},{8,9},{9,8},{10,11... | collective-permute-start | bytes 393224 | tf_op jit(solution)/shard_map/ppermute | solution.py:239
  22.8 1.7 %collective-permute-start.5 = (bf16[16,4096]{1,0:T(8,128)(2,1)S(1)}, bf16[16,4096]{1,0:T(8,128)(2,1)S(1)}, u32[]{:S(2)}, u32[]{:S(2)}) collective-permute-start(bf16[16,4096]{1,0:T(8,128)(2,1)S(1)} %get-tuple-element.106), channel_id=1, source_target_pairs={{0,1},{1,0},{2,3},{3,2},{4,5},{5,4},{6,7},{7,6},{8,9},{9,8},{10,11... | collective-permute-start | bytes 393224 | tf_op jit(solution)/shard_map/ppermute | solution.py:239
  22.9 13.2 %collective-permute-start.13 = (bf16[32,4096]{1,0:T(8,128)(2,1)S(1)}, bf16[32,4096]{1,0:T(8,128)(2,1)S(1)}, u32[]{:S(2)}, u32[]{:S(2)}) collective-permute-start(bf16[32,4096]{1,0:T(8,128)(2,1)S(1)} %collective-permute-done.3.mine_ref), channel_id=1, source_target_pairs={{0,4},{4,0},{8,12},{12,8},{1,5},{5,1},{9,13},{13,9},{2,6},{6,2},{1... | collective-permute-start | bytes 786440 | tf_op jit(solution)/shard_map/ppermute | solution.py:245
  29.1 4.2 %collective-permute-start.10 = (bf16[32,4096]{1,0:T(8,128)(2,1)S(1)}, bf16[32,4096]{1,0:T(8,128)(2,1)S(1)}, u32[]{:S(2)}, u32[]{:S(2)}) collective-permute-start(bf16[32,4096]{1,0:T(8,128)(2,1)S(1)} %collective-permute-done.near_ref), channel_id=1, source_target_pairs={{0,1},{1,0},{2,3},{3,2},{4,5},{5,4},{6,7},{7,6},{8,9},{9,8},{10,11... | collective-permute-start | bytes 786440 | tf_op jit(solution)/shard_map/ppermute | solution.py:239
  29.1 4.2 %collective-permute-start.11 = (bf16[32,4096]{1,0:T(8,128)(2,1)S(1)}, bf16[32,4096]{1,0:T(8,128)(2,1)S(1)}, u32[]{:S(2)}, u32[]{:S(2)}) collective-permute-start(bf16[32,4096]{1,0:T(8,128)(2,1)S(1)} %collective-permute-done.1.near_too_ref), channel_id=1, source_target_pairs={{0,1},{1,0},{2,3},{3,2},{4,5},{5,4},{6,7},{7,6},{8,9},{9,8},{10,11... | collective-permute-start | bytes 786440 | tf_op jit(solution)/shard_map/ppermute | solution.py:239
  29.7 1.6 %collective-permute-start.9 = (bf16[16,4096]{1,0:T(8,128)(2,1)S(1)}, bf16[16,4096]{1,0:T(8,128)(2,1)S(1)}, u32[]{:S(2)}, u32[]{:S(2)}) collective-permute-start(bf16[16,4096]{1,0:T(8,128)(2,1)S(1)} %get-tuple-element.103), channel_id=1, source_target_pairs={{0,1},{1,0},{2,3},{3,2},{4,5},{5,4},{6,7},{7,6},{8,9},{9,8},{10,11... | collective-permute-start | bytes 393224 | tf_op jit(solution)/shard_map/ppermute | solution.py:239
  29.8 3.6 %collective-permute-start.8 = (bf16[16,4096]{1,0:T(8,128)(2,1)S(1)}, bf16[16,4096]{1,0:T(8,128)(2,1)S(1)}, u32[]{:S(2)}, u32[]{:S(2)}) collective-permute-start(bf16[16,4096]{1,0:T(8,128)(2,1)S(1)} %get-tuple-element.104), channel_id=1, source_target_pairs={{0,1},{1,0},{2,3},{3,2},{4,5},{5,4},{6,7},{7,6},{8,9},{9,8},{10,11... | collective-permute-start | bytes 393224 | tf_op jit(solution)/shard_map/ppermute | solution.py:239
  31.2 11.0 %collective-permute-start.7 = (bf16[32,4096]{1,0:T(8,128)(2,1)S(1)}, bf16[32,4096]{1,0:T(8,128)(2,1)S(1)}, u32[]{:S(2)}, u32[]{:S(2)}) collective-permute-start(bf16[32,4096]{1,0:T(8,128)(2,1)S(1)} %collective-permute-done.2.mine_ref), channel_id=1, source_target_pairs={{0,4},{4,0},{8,12},{12,8},{1,5},{5,1},{9,13},{13,9},{2,6},{6,2},{1... | collective-permute-start | bytes 786440 | tf_op jit(solution)/shard_map/ppermute | solution.py:245
  36.2 2.1 %collective-permute-start.15 = (bf16[16,4096]{1,0:T(8,128)(2,1)S(1)}, bf16[16,4096]{1,0:T(8,128)(2,1)S(1)}, u32[]{:S(2)}, u32[]{:S(2)}) collective-permute-start(bf16[16,4096]{1,0:T(8,128)(2,1)S(1)} %get-tuple-element.101), channel_id=1, source_target_pairs={{0,1},{1,0},{2,3},{3,2},{4,5},{5,4},{6,7},{7,6},{8,9},{9,8},{10,11... | collective-permute-start | bytes 393224 | tf_op jit(solution)/shard_map/ppermute | solution.py:239
  36.2 2.0 %collective-permute-start.14 = (bf16[16,4096]{1,0:T(8,128)(2,1)S(1)}, bf16[16,4096]{1,0:T(8,128)(2,1)S(1)}, u32[]{:S(2)}, u32[]{:S(2)}) collective-permute-start(bf16[16,4096]{1,0:T(8,128)(2,1)S(1)} %get-tuple-element.102), channel_id=1, source_target_pairs={{0,1},{1,0},{2,3},{3,2},{4,5},{5,4},{6,7},{7,6},{8,9},{9,8},{10,11... | collective-permute-start | bytes 393224 | tf_op jit(solution)/shard_map/ppermute | solution.py:239
  36.7 5.5 %collective-permute-start.12 = (bf16[64,1024]{1,0:T(8,128)(2,1)S(1)}, bf16[64,1024]{1,0:T(8,128)(2,1)S(1)}, u32[]{:S(2)}, u32[]{:S(2)}) collective-permute-start(bf16[64,1024]{1,0:T(8,128)(2,1)S(1)} %get-tuple-element.67), channel_id=1, source_target_pairs={{0,2},{2,0},{1,3},{3,1},{4,6},{6,4},{5,7},{7,5},{8,10},{10,8},{9,1... | collective-permute-start | bytes 393224 | tf_op jit(solution)/shard_map/ppermute | solution.py:242
  38.3 19.2 %copy-start.2 = (bf16[256,1024]{1,0:T(8,128)(2,1)S(1)}, bf16[256,1024]{1,0:T(8,128)(2,1)}, u32[]{:S(2)}) copy-start(bf16[256,1024]{1,0:T(8,128)(2,1)} %residual_ref.1) | copy-start | bytes 1572868
  42.2 2.1 %collective-permute-start.17 = (bf16[16,4096]{1,0:T(8,128)(2,1)S(1)}, bf16[16,4096]{1,0:T(8,128)(2,1)S(1)}, u32[]{:S(2)}, u32[]{:S(2)}) collective-permute-start(bf16[16,4096]{1,0:T(8,128)(2,1)S(1)} %get-tuple-element.99), channel_id=1, source_target_pairs={{0,1},{1,0},{2,3},{3,2},{4,5},{5,4},{6,7},{7,6},{8,9},{9,8},{10,11... | collective-permute-start | bytes 393224 | tf_op jit(solution)/shard_map/ppermute | solution.py:239
  42.3 2.0 %collective-permute-start.16 = (bf16[16,4096]{1,0:T(8,128)(2,1)S(1)}, bf16[16,4096]{1,0:T(8,128)(2,1)S(1)}, u32[]{:S(2)}, u32[]{:S(2)}) collective-permute-start(bf16[16,4096]{1,0:T(8,128)(2,1)S(1)} %get-tuple-element.100), channel_id=1, source_target_pairs={{0,1},{1,0},{2,3},{3,2},{4,5},{5,4},{6,7},{7,6},{8,9},{9,8},{10,11... | collective-permute-start | bytes 393224 | tf_op jit(solution)/shard_map/ppermute | solution.py:239
  42.8 9.0 %collective-permute-start.19 = (bf16[128,1024]{1,0:T(8,128)(2,1)S(1)}, bf16[128,1024]{1,0:T(8,128)(2,1)S(1)}, u32[]{:S(2)}, u32[]{:S(2)}) collective-permute-start(bf16[128,1024]{1,0:T(8,128)(2,1)S(1)} %constant_dynamic-update-slice_fusion), channel_id=1, source_target_pairs={{0,2},{2,0},{1,3},{3,1},{4,6},{6,4},{5,7},{7,5},{8,10},{10,8},{9,1... | collective-permute-start | bytes 786440 | tf_op jit(solution)/shard_map/ppermute | solution.py:242
  46.6 5.2 %collective-permute-start.18 = (bf16[128,128]{1,0:T(8,128)(2,1)S(1)}, bf16[128,128]{1,0:T(8,128)(2,1)S(1)}, u32[]{:S(2)}, u32[]{:S(2)}) collective-permute-start(bf16[128,128]{1,0:T(8,128)(2,1)S(1)} %get-tuple-element.82), channel_id=1, source_target_pairs={{0,2},{2,0},{1,3},{3,1},{4,6},{6,4},{5,7},{7,5},{8,10},{10,8},{9,1... | collective-permute-start | bytes 98312 | tf_op jit(solution)/shard_map/ppermute | solution.py:242
  51.8 4.3 %collective-permute-start.21 = (bf16[128,128]{1,0:T(8,128)(2,1)S(1)}, bf16[128,128]{1,0:T(8,128)(2,1)S(1)}, u32[]{:S(2)}, u32[]{:S(2)}) collective-permute-start(bf16[128,128]{1,0:T(8,128)(2,1)S(1)} %multiply_convert_fusion.refs_0_), channel_id=1, source_target_pairs={{0,4},{4,0},{8,12},{12,8},{1,9},{9,1},{5,13},{13,5},{2,6},{6,2},{1... | collective-permute-start | bytes 98312 | tf_op jit(solution)/shard_map/ppermute | solution.py:332
  52.2 5.3 %collective-permute-start.20 = (bf16[64,1024]{1,0:T(8,128)(2,1)S(1)}, bf16[64,1024]{1,0:T(8,128)(2,1)S(1)}, u32[]{:S(2)}, u32[]{:S(2)}) collective-permute-start(bf16[64,1024]{1,0:T(8,128)(2,1)S(1)} %get-tuple-element.87), channel_id=1, source_target_pairs={{0,2},{2,0},{1,3},{3,1},{4,6},{6,4},{5,7},{7,5},{8,10},{10,8},{9,1... | collective-permute-start | bytes 393224 | tf_op jit(solution)/shard_map/ppermute | solution.py:242
  53.7 5.7 %collective-permute-start.22 = (bf16[128,128]{1,0:T(8,128)(2,1)S(1)}, bf16[128,128]{1,0:T(8,128)(2,1)S(1)}, u32[]{:S(2)}, u32[]{:S(2)}) collective-permute-start(bf16[128,128]{1,0:T(8,128)(2,1)S(1)} %multiply_convert_fusion.refs_0_), channel_id=1, source_target_pairs={{0,12},{12,0},{4,8},{8,4},{1,13},{13,1},{5,9},{9,5},{2,14},{14,2},... | collective-permute-start | bytes 98312 | tf_op jit(solution)/shard_map/ppermute | solution.py:245
  56.1 3.3 %collective-permute-start.23 = (bf16[128,128]{1,0:T(8,128)(2,1)S(1)}, bf16[128,128]{1,0:T(8,128)(2,1)S(1)}, u32[]{:S(2)}, u32[]{:S(2)}) collective-permute-start(bf16[128,128]{1,0:T(8,128)(2,1)S(1)} %collective-permute-done.21.refs_1_), channel_id=1, source_target_pairs={{0,1},{1,0},{2,3},{3,2},{4,5},{5,4},{6,7},{7,6},{8,9},{9,8},{10,11... | collective-permute-start | bytes 98312 | tf_op jit(solution)/shard_map/ppermute | solution.py:239
